TPU v7x, 256 devices: a whole 4x4x8 slice. The times are simulated.
256 devices in a mesh: wide: 16 (over y_lo, x, core), narrow: 16 (over z, y_hi).
Axes of the slice: x: 4, y: 4 (y_hi: 2, y_lo: 2; y = y_hi * 2 + y_lo), z: 8, core: 2. Of those that a mesh axis runs over, the one named last changes fastest.
Arguments:
- batch_index: int32 [1024], P('narrow'), may hold values from 0 to 255
- train_features: float32 [4096, 1024], P('narrow'), may hold values from -6 to 6
- train_labels: float32 [4096, 1000], P('narrow'), may hold values from -12 to 12
- centers: float32 [65536, 1024], P(('wide', 'narrow')), may hold values from -6 to 6
- weights: float32 [65536, 1000], P(('wide', 'narrow')), may hold values from -6 to 6
Outputs:
- new_weights: float32 [65536, 1000], P(('wide', 'narrow'))
- residual: float32 [1024, 1000], P('narrow')
Inputs may be any that keep to these rules, and one draw needn't show every extreme that they name: `batch_index`: entry i names a row of the training shard held by narrow index i // 64.
All inputs are finite; a program needn't handle non-finite values.
Results may differ from a plain program's by a relative error of at most 0.0001.
Values sent between devices are 32-bit elements; how exact they have to be, the bound alone decides.
No kernel may reach another device: no remote copies, remote signals or barrier semaphores. Data moves between devices by JAX's collectives and lax.ppermute only.
A program may use at most 64 MiB of HBM per device.

v0:
```python
import math

import jax
import jax.numpy as jnp
from jax import lax
from jax.sharding import Mesh
from jax.sharding import PartitionSpec as P

NARROW = ("narrow_0", "narrow_1")
WIDE_NARROW = ("wide", "narrow_0", "narrow_1")


step_size = 1.0


def gather_axes(array, axes, dim):
    for axis in reversed(axes):
        array = lax.all_gather(array, axis, axis=dim, tiled=True)
    return array


def per_device(batch_index, train_features, train_labels, centers, weights):
    block = batch_index.shape[0]
    rows = jnp.take(train_features, batch_index, axis=0)
    targets = jnp.take(train_labels, batch_index, axis=0)
    features = centers.shape[1]
    center_sq = jnp.sum(centers * centers, axis=1)
    count = centers.shape[0] * lax.axis_size("wide") * lax.axis_size(NARROW)
    scale = 1.0 / math.sqrt(count)
    piece = gather_axes(rows, NARROW, 0)
    inner = jnp.dot(
        piece, centers.T, precision=lax.Precision.HIGHEST, preferred_element_type=jnp.float32
    )
    piece_sq = jnp.sum(piece * piece, axis=1)
    kernel = jnp.exp(
        (2.0 * features - piece_sq[:, None] - center_sq[None, :] + 2.0 * inner) / 128.0
    )
    batch = kernel.shape[0]
    partial_value = jnp.dot(
        kernel, weights, precision=lax.Precision.HIGHEST, preferred_element_type=jnp.float32
    )
    owner = jnp.where(lax.axis_index("wide") == 0, 1.0, 0.0).astype(jnp.float32)
    placed = lax.dynamic_update_slice_in_dim(
        jnp.zeros((batch, targets.shape[1]), jnp.float32),
        targets * owner,
        lax.axis_index(NARROW) * block,
        0,
    )
    resid_all = lax.psum(partial_value * scale - placed, WIDE_NARROW)
    residual = lax.dynamic_slice_in_dim(resid_all, lax.axis_index(NARROW) * block, block, 0)
    delta = lax.dot_general(
        kernel,
        resid_all,
        (((0,), (0,)), ((), ())),
        precision=lax.Precision.HIGHEST,
        preferred_element_type=jnp.float32,
    )
    new_weights = weights - step_size / batch * delta
    return (new_weights, residual)


def solution(mesh):
    split = Mesh(mesh.devices.reshape(mesh.shape["wide"], 8, 2), ("wide", "narrow_0", "narrow_1"))
    placed = (
        P(NARROW),
        P(NARROW, None),
        P(NARROW, None),
        P(WIDE_NARROW, None),
        P(WIDE_NARROW, None),
    )
    return jax.shard_map(
        per_device,
        mesh=split,
        in_specs=placed,
        out_specs=(P(WIDE_NARROW, None), P(NARROW, None)),
        check_vma=False,
    )
```

profile of v0, /device:TPU:1, one launch (start us, length us, event | category | flops | bytes accessed | tf_op | source)
XLA Modules:
  0.0 374.2 jit_solution(9159140242311068464)
XLA Ops:
  7.2 0.0 copy-start
  7.2 0.0 copy-start.6
  7.2 0.0 all-gather.2.cloned.1.call-start
  7.2 0.8 compare_select_fusion
  8.0 0.7 compare_and_fusion
  8.7 0.0 copy-done
  8.7 0.7 gather_fusion
  9.4 0.1 broadcast_select_fusion
  9.5 9.4 %all_gather.6 = f32[128,1024]{1,0:T(8,128)} all-gather(f32[64,1024]{1,0:T(8,128)S(1)} %broadcast_select_fusion), channel_id=1, replica_groups=mesh['wide'=16,'narrow_0'=8,'narrow_1'=2] {'narrow_1'}, dimensions={0}, use_global_device_ids=true | all-gather | bytes 786432 | tf_op jit(solution)/shard_map/all_gather | solution.py:18
  18.9 0.0 all-gather.2.cloned.1.call-update
  18.9 0.0 all-reduce.2.cloned.1.call-start
  19.0 0.0 copy-done.6
  19.0 0.3 copy.7
  19.3 0.0 copy-start.3
  19.3 0.7 gather_fusion.1
  20.0 0.2 copy.8
  20.3 2.5 broadcast_in_dim.30
  22.7 3.5 dynamic_update_slice.3
  26.2 0.0 copy-done.3
  26.2 0.1 multiply_reduce_fusion.1
  26.4 52.3 %all-gather.2.cloned.1.call-done = f32[1024,1024]{1,0:T(8,128)} async-done(((f32[128,1024]{1,0:T(8,128)}), f32[1024,1024]{1,0:T(8,128)}) %all-gather.2.cloned.1.call-update) | async-done | bytes 4194320 | tf_op jit(solution)/shard_map/all_gather | solution.py:18
  78.6 2.7 multiply_reduce_fusion
  81.3 0.0 copy-start.4
  81.3 0.7 copy-done.1
  82.1 3.5 fusion.2
  85.6 5.3 %multiply_subtract_fusion = f32[1024,1000]{0,1:T(8,128)} fusion(f32[1024,1000]{0,1:T(8,128)S(1)} %copy-done.2, f32[1024,256]{1,0:T(8,128)S(1)} %fusion.2, f32[256,1000]{0,1:T(8,128)S(1)} %copy-done.4), kind=kOutput, calls=%fused_computation.3 | convolution fusion | flops 3147776000 | bytes 10264576 | tf_op jit(solution)/shard_map/dot_general | solution.py:39
  91.0 0.0 all-reduce.2.cloned.1.call-update
  91.0 266.0 %all-reduce.2.cloned.1.call-done = f32[1024,1000]{0,1:T(8,128)} async-done(((f32[1024,1000]{0,1:T(8,128)}), f32[1024,1000]{0,1:T(8,128)}) %all-reduce.2.cloned.1.call-update) | async-done | bytes 4096016 | tf_op jit(solution)/shard_map/psum | solution.py:49
  357.0 2.0 constant_dynamic-slice_fusion
  359.0 1.9 copy.9
  360.9 0.0 copy-done.5
  360.9 6.5 %fusion.3 = f32[256,1000]{0,1:T(8,128)} fusion(f32[256,1000]{0,1:T(8,128)S(1)} %copy-done.5, f32[1024,256]{1,0:T(8,128)S(1)} %fusion.2, f32[1024,1000]{0,1:T(8,128)} %all-reduce.2.cloned.1.call-done), kind=kOutput, calls=%fused_computation.9 | convolution fusion | flops 3146240000 | bytes 7192576 | tf_op jit(solution)/shard_map/dot_general | solution.py:51
  (8 shorter events, 0.1 us)
Async XLA Ops:
  7.2 1.5 copy-start
  7.2 11.8 %copy-start.6 = (f32[256,1000]{0,1:T(8,128)S(1)}, f32[256,1000]{0,1:T(8,128)}, u32[]{:S(2)}) copy-start(f32[256,1000]{0,1:T(8,128)} %param.7) | copy-start | bytes 3072004
  7.2 71.4 %all-gather.2.cloned.1.call-start = ((), (), s32[]{:S(2)}) async-start(), calls=%async_computation | async-start | bytes 4718592 | tf_op jit(solution)/shard_map/all_gather | solution.py:18
  18.9 338.1 %all-reduce.2.cloned.1.call-start = ((), (), s32[]{:S(2)}) async-start(), calls=%async_computation.1 | async-start | bytes 8192000 | tf_op jit(solution)/shard_map/psum | solution.py:49
  19.3 6.9 %copy-start.3 = (f32[256,1024]{1,0:T(8,128)S(1)}, f32[256,1024]{1,0:T(8,128)}, u32[]{:S(2)}) copy-start(f32[256,1024]{1,0:T(8,128)} %param.8) | copy-start | bytes 3145732
  78.6 3.4 copy-start.1
  81.3 4.3 %copy-start.2 = (f32[1024,1000]{0,1:T(8,128)S(1)}, f32[1024,1000]{0,1:T(8,128)}, u32[]{:S(2)}) copy-start(f32[1024,1000]{0,1:T(8,128)} %dynamic_update_slice.3) | copy-start | bytes 12288004
  81.3 4.3 %copy-start.4 = (f32[256,1000]{0,1:T(8,128)S(1)}, f32[256,1000]{0,1:T(8,128)}, u32[]{:S(2)}) copy-start(f32[256,1000]{0,1:T(8,128)} %param.9) | copy-start | bytes 3072004
  91.0 270.0 %copy-start.5 = (f32[256,1000]{0,1:T(8,128)S(1)}, f32[256,1000]{0,1:T(8,128)}, u32[]{:S(2)}) copy-start(f32[256,1000]{0,1:T(8,128)} %param.9) | copy-start | bytes 3072004
Sparse Core Ops, SparseCore 0:
  19.0 59.5 all-gather.1
  91.1 265.8 all-reduce.1
where the time goes:
time: 375 us; the launch traced here: 374 us
  waiting for transfers between devices  318 us (85%)
  matrix products  15.3 us (4%)
  between operations  14.2 us (4%)
  local copies, waits for them, and re-layouts  12.5 us (3%)
  blocking collectives  9.4 us (3%)
  other arithmetic  4.42 us (1%)
    psum x1, waiting for transfers between devices, per_device(): resid_all = lax.psum(partial_value * scale - placed, WIDE_NARROW)  266 us
    all_gather x1, waiting for transfers between devices, gather_axes(): array = lax.all_gather(array, axis, axis=dim, tiled=True)  52.3 us
    all_gather x1, blocking collectives, gather_axes(): array = lax.all_gather(array, axis, axis=dim, tiled=True)  9.4 us
  transfers between devices with their start and end apart: 2, of which 2 were waited for; matrix products, arithmetic and copies ran while one was open for 2% of the time, Pallas kernels for 0%

commit v1 on v0

v1 whole, which is shorter than its diff:
```python
import math

import jax
import jax.numpy as jnp
from jax import lax
from jax.sharding import Mesh
from jax.sharding import PartitionSpec as P

AXES = ("y_lo", "x", "core", "z", "y_hi")
SIZES = (2, 4, 2, 8, 2)
WIDE_NARROW = AXES
NARROW = ("z", "y_hi")
PLANE = ("y_lo", "y_hi", "x")
SWAP = ((0, 1), (1, 0))

step_size = 1.0


def group_size(axes):
    return math.prod(lax.axis_size(axis) for axis in axes)


def exchange(array, axes):
    return lax.all_to_all(array, axes, 0, 0, tiled=True)


def spread(array, axes):
    count = group_size(axes)
    copies = jnp.broadcast_to(array[None], (count,) + array.shape)
    return exchange(copies.reshape((-1,) + array.shape[1:]), axes)


def scatter_sum(array, axes):
    count = group_size(axes)
    return exchange(array, axes).reshape((count, -1) + array.shape[1:]).sum(axis=0)


def pick(array, index):
    return array.at[index].get(mode="promise_in_bounds")


def per_device(batch_index, train_features, train_labels, centers, weights):
    block = batch_index.shape[0]
    features = centers.shape[1]
    outputs = weights.shape[1]
    wide = lax.axis_size("y_lo") * lax.axis_size("x") * lax.axis_size("core")
    devices = wide * group_size(NARROW)
    batch = block * group_size(NARROW)
    count = centers.shape[0] * devices
    scale = 1.0 / math.sqrt(count)
    core = lax.axis_index("core")
    own = block // wide
    start = (core * (wide // 2) + lax.axis_index(("y_lo", "x"))) * own
    index = lax.dynamic_slice_in_dim(batch_index, start, own, 0)
    rows = pick(train_features, index)
    targets = pick(train_labels, index)

    other_centers = lax.ppermute(centers, "core", SWAP)
    other_weights = lax.ppermute(weights, "core", SWAP)
    pair_centers = jnp.concatenate([centers, other_centers], axis=0)
    pair_weights = jnp.concatenate([weights, other_weights], axis=0)
    center_sq = jnp.sum(pair_centers * pair_centers, axis=1)

    rows_all = spread(spread(rows, ("z",)), PLANE)
    inner = lax.dot_general(
        rows_all,
        pair_centers,
        (((1,), (1,)), ((), ())),
        precision=lax.Precision.HIGH,
        preferred_element_type=jnp.float32,
    )
    row_sq = jnp.sum(rows_all * rows_all, axis=1)
    kernel = jnp.exp(
        (2.0 * features - row_sq[:, None] - center_sq[None, :] + 2.0 * inner) / 128.0
    )
    partial_value = jnp.dot(
        kernel, pair_weights, precision=lax.Precision.HIGH, preferred_element_type=jnp.float32
    )
    value = scatter_sum(scatter_sum(partial_value, PLANE), ("z",))
    resid = value * scale - targets
    resid_all = spread(spread(resid, ("z",)), PLANE)

    shaped = resid_all.reshape(
        lax.axis_size("y_lo"),
        lax.axis_size("y_hi"),
        lax.axis_size("x"),
        lax.axis_size("z"),
        own,
        outputs,
    )
    mine = lax.dynamic_index_in_dim(shaped, lax.axis_index("y_hi"), 1, keepdims=False)
    mine = lax.dynamic_index_in_dim(mine, lax.axis_index("z"), 2, keepdims=False)
    mine = mine.reshape(block // 2, outputs)
    theirs = lax.ppermute(mine, "core", SWAP)
    residual = jnp.where(
        core == 0,
        jnp.concatenate([mine, theirs], axis=0),
        jnp.concatenate([theirs, mine], axis=0),
    )
    delta = lax.dot_general(
        kernel,
        resid_all,
        (((0,), (0,)), ((), ())),
        precision=lax.Precision.HIGH,
        preferred_element_type=jnp.float32,
    )
    here = centers.shape[0]
    received = lax.ppermute(delta[here:], "core", SWAP)
    new_weights = weights - step_size / batch * (delta[:here] + received)
    return (new_weights, residual)


def solution(mesh):
    split = Mesh(mesh.devices.reshape(SIZES), AXES)
    placed = (
        P(NARROW),
        P(NARROW, None),
        P(NARROW, None),
        P(WIDE_NARROW, None),
        P(WIDE_NARROW, None),
    )
    return jax.shard_map(
        per_device,
        mesh=split,
        in_specs=placed,
        out_specs=(P(WIDE_NARROW, None), P(NARROW, None)),
        check_vma=False,
    )
```

time: 375 us -> 163 us (0.43)
  waiting for transfers between devices: 318 us -> 28.4 us
  blocking collectives: 9.4 us -> 87.8 us
  starting transfers between devices: 0.08 us -> 18 us
  between operations: 14.2 us -> 0.86 us
  matrix products: 15.3 us -> 9.11 us
    psum x1 -> x0, waiting for transfers between devices: 266 us -> none  [per_device(): resid_all = lax.psum(partial_value * scale - placed, WIDE_NARROW)]
    all_to_all x0 -> x4, blocking collectives: none -> 87.8 us  [exchange(): return lax.all_to_all(array, axes, 0, 0, tiled=True)]
    all_gather x1 -> x0, waiting for transfers between devices: 52.3 us -> none  [gather_axes(): array = lax.all_gather(array, axis, axis=dim, tiled=True)]
    all_to_all x0 -> x2, waiting for transfers between devices: none -> 25.5 us  [exchange(): return lax.all_to_all(array, axes, 0, 0, tiled=True)]
    all_to_all x0 -> x2, starting transfers between devices: none -> 10.1 us  [exchange(): return lax.all_to_all(array, axes, 0, 0, tiled=True)]
    all_gather x1 -> x0, blocking collectives: 9.4 us -> none  [gather_axes(): array = lax.all_gather(array, axis, axis=dim, tiled=True)]
    ppermute x0 -> x4, starting transfers between devices: none -> 7.86 us  [the longest x1 5.02 us: per_device(): received = lax.ppermute(delta[here:], 'core', SWAP)]
    dot_general x1, matrix products: 6.47 us -> 2.08 us  [per_device(): lax.dot_general(kernel, resid_all, (((0,), (0,)), ((), ())), precision=la...]
  transfers between devices with their start and end apart: 2 -> 6, of which waited for: 2 -> 4; matrix products, arithmetic and copies ran while one was open for 2% -> 7% of each run, Pallas kernels for 0% -> 0%
where the time goes in v1:
time: 163 us
  blocking collectives  87.8 us (54%)
  waiting for transfers between devices  28.4 us (17%)
  starting transfers between devices  18 us (11%)
  local copies, waits for them, and re-layouts  13.5 us (8%)
  matrix products  9.11 us (6%)
  other arithmetic  5.12 us (3%)
    all_to_all x4, blocking collectives, exchange(): return lax.all_to_all(array, axes, 0, 0, tiled=True)  87.8 us
    all_to_all x2, waiting for transfers between devices, exchange(): return lax.all_to_all(array, axes, 0, 0, tiled=True)  25.5 us
    all_to_all x2, starting transfers between devices, exchange(): return lax.all_to_all(array, axes, 0, 0, tiled=True)  10.1 us
    unnamed x14, local copies, waits for them, and re-layouts  5.86 us
    ppermute x1, starting transfers between devices, per_device(): received = lax.ppermute(delta[here:], 'core', SWAP)  5.02 us
    dot_general x1, matrix products, per_device(): jnp.dot(kernel, pair_weights, precision=lax.Precision.HIGH, preferred_ele...  3.53 us
    dot_general x1, matrix products, per_device(): lax.dot_general(rows_all, pair_centers, (((1,), (1,)), ((), ())), precisi...  3.51 us
  transfers between devices with their start and end apart: 6, of which 4 were waited for; matrix products, arithmetic and copies ran while one was open for 7% of the time, Pallas kernels for 0%

profile of v1, /device:TPU:1, one launch (start us, length us, event | category | flops | bytes accessed | tf_op | source)
XLA Modules:
  0.0 162.8 jit_solution(17644137596451975100)
XLA Ops:
  0.7 0.8 compare_select_fusion
  1.5 0.4 copy-done
  1.9 0.6 gather_fusion
  2.5 16.6 %all_to_all.48 = f32[8,4,1024]{2,1,0:T(4,128)S(1)} all-to-all(f32[8,4,1024]{2,1,0:T(4,128)S(1)} %broadcast_in_dim.15), channel_id=1, replica_groups=mesh['y_lo'=2,'x'=4,'core'=2,'z'=8,'y_hi'=2] {'z'}, dimensions={0} | all-to-all | bytes 262144 | tf_op jit(solution)/shard_map/all_to_all | solution.py:24
  19.1 1.6 broadcast_in_dim.17
  20.7 6.8 %all-to-all-start.1 = ((f32[16,32,1024]{2,1,0:T(8,128)}), f32[16,32,1024]{2,1,0:T(8,128)S(1)}, u32[]{:S(2)}, u32[]{:S(2)}) async-start(f32[16,32,1024]{2,1,0:T(8,128)} %broadcast_in_dim.17), calls=%async_computation.1 | async-start | bytes 4194304 | tf_op jit(solution)/shard_map/all_to_all | solution.py:24
  27.5 2.6 %collective-permute-start = (f32[256,1024]{1,0:T(8,128)}, f32[256,1024]{1,0:T(8,128)S(1)}, u32[]{:S(2)}, u32[]{:S(2)}) collective-permute-start(f32[256,1024]{1,0:T(8,128)} %param.8), channel_id=1, source_target_pairs={{0,16},{16,0},{1,17},{17,1},{2,18},{18,2},{3,19},{19,3},{4,20},{20... | collective-permute-start | bytes 3145736 | tf_op jit(solution)/shard_map/ppermute | solution.py:58
  30.2 1.3 constant_dynamic-update-slice_fusion.1
  31.5 1.5 collective-permute-done
  33.2 1.3 copy-done.1
  34.5 0.2 multiply_reduce_fusion
  34.7 19.8 %all-to-all-done.1 = f32[16,32,1024]{2,1,0:T(8,128)S(1)} async-done(((f32[16,32,1024]{2,1,0:T(8,128)}), f32[16,32,1024]{2,1,0:T(8,128)S(1)}, u32[]{:S(2)}, u32[]{:S(2)}) %all-to-all-start.1) | async-done | bytes 2097184 | tf_op jit(solution)/shard_map/all_to_all | solution.py:24
  54.8 3.5 %convolution_multiply_fusion = f32[512,512]{1,0:T(8,128)S(1)} fusion(f32[512,1024]{1,0:T(8,128)S(1)} %bitcast.7, f32[512,1024]{1,0:T(8,128)} %copy-done.1), kind=kOutput, calls=%fused_computation.8 | convolution fusion | flops 1610874880 | bytes 5242880 | tf_op jit(solution)/shard_map/dot_general | solution.py:65
  58.4 3.5 %fusion = f32[512,1000]{1,0:T(8,128)S(1)} fusion(f32[256,1000]{0,1:T(8,128)} %collective-permute-done.1, f32[256,1000]{0,1:T(8,128)S(1)} %copy-done.5, f32[512,512]{1,0:T(8,128)S(1)} %convolution_multiply_fusion, f32[512]{0:T(512)S(1)} %multiply_reduce_fusion, f32[512]{0:T(512)S(1)} %sub.39), kind=kOutput, calls=%fused_computation.4 | convolution fusion | flops 1574162432 | bytes 5148672 | tf_op jit(solution)/shard_map/dot_general | solution.py:76
  61.9 33.7 %all_to_all.49 = f32[16,32,1000]{2,1,0:T(8,128)S(1)} all-to-all(f32[16,32,1000]{2,1,0:T(8,128)S(1)} %bitcast.8), channel_id=1, replica_groups=mesh['y_lo'=2,'x'=4,'core'=2,'z'=8,'y_hi'=2] {'y_lo','y_hi','x'}, dimensions={0} | all-to-all | bytes 4096000 | tf_op jit(solution)/shard_map/all_to_all | solution.py:24
  95.8 0.7 all_to_all.37
  96.5 3.4 %all-to-all-start.3 = ((f32[8,4,1000]{2,1,0:T(4,128)}), f32[8,4,1000]{2,1,0:T(4,128)S(1)}, u32[]{:S(2)}, u32[]{:S(2)}) async-start(f32[8,4,1000]{2,1,0:T(4,128)} %all_to_all.37), calls=%async_computation.3 | async-start | bytes 262144 | tf_op jit(solution)/shard_map/all_to_all | solution.py:24
  99.8 1.5 copy.14
  101.4 0.6 gather_fusion.1
  102.0 5.7 %all-to-all-done.3 = f32[8,4,1000]{2,1,0:T(4,128)S(1)} async-done(((f32[8,4,1000]{2,1,0:T(4,128)}), f32[8,4,1000]{2,1,0:T(4,128)S(1)}, u32[]{:S(2)}, u32[]{:S(2)}) %all-to-all-start.3) | async-done | bytes 128032 | tf_op jit(solution)/shard_map/all_to_all | solution.py:24
  107.8 10.3 %all_to_all.50 = f32[8,4,1000]{2,1,0:T(4,128)S(1)} all-to-all(f32[8,4,1000]{2,1,0:T(4,128)S(1)} %broadcast_in_dim.18), channel_id=1, replica_groups=mesh['y_lo'=2,'x'=4,'core'=2,'z'=8,'y_hi'=2] {'z'}, dimensions={0} | all-to-all | bytes 256000 | tf_op jit(solution)/shard_map/all_to_all | solution.py:24
  118.1 0.2 broadcast_in_dim.40
  118.4 27.2 %all_to_all.51 = f32[16,32,1000]{2,1,0:T(8,128)S(1)} all-to-all(f32[16,32,1000]{2,1,0:T(8,128)S(1)} %broadcast_in_dim.40), channel_id=1, replica_groups=mesh['y_lo'=2,'x'=4,'core'=2,'z'=8,'y_hi'=2] {'y_lo','y_hi','x'}, dimensions={0} | all-to-all | bytes 4096000 | tf_op jit(solution)/shard_map/all_to_all | solution.py:24
  145.6 2.1 %fusion.6 = f32[512,1000]{0,1:T(8,128)S(1)} fusion(f32[512,1000]{1,0:T(8,128)S(1)} %bitcast.6, f32[512,512]{1,0:T(8,128)S(1)} %copy-done.3, f32[512]{0:T(512)S(1)} %multiply_reduce_fusion, f32[512]{0:T(512)S(1)} %sub.39), kind=kOutput, calls=%fused_computation.13 | convolution fusion | flops 1573650432 | bytes 5148672 | tf_op jit(solution)/shard_map/dot_general | solution.py:100
  147.6 1.3 copy-done.4
  148.9 1.1 slice.13
  150.0 5.0 %collective-permute-start.2 = (f32[256,1000]{0,1:T(8,128)}, f32[256,1000]{0,1:T(8,128)}, u32[]{:S(2)}, u32[]{:S(2)}) collective-permute-start(f32[256,1000]{0,1:T(8,128)} %slice.13), channel_id=1, source_target_pairs={{0,16},{16,0},{1,17},{17,1},{2,18},{18,2},{3,19},{19,3},{4,20},{20... | collective-permute-start | bytes 3072008 | tf_op jit(solution)/shard_map/ppermute | solution.py:108
  155.0 1.7 %reshape.60 = f32[2,2,4,8,4,1000]{5,4,3,2,1,0:T(4,128)} reshape(f32[16,32,1000]{2,1,0:T(8,128)S(1)} %all_to_all.51) | data formatting | bytes 4096000 | tf_op jit(solution)/shard_map/reshape | solution.py:83
  156.7 0.9 constant_dynamic-slice_fusion
  157.7 1.3 collective-permute-done.3
  159.1 0.7 maximum_select_fusion
  159.8 3.0 %fusion.5 = f32[256,1000]{0,1:T(8,128)} fusion(f32[256,1000]{0,1:T(8,128)} %param.9, f32[256,1000]{0,1:T(8,128)} %collective-permute-done.2, f32[512,1000]{0,1:T(8,128)} %copy-done.4), kind=kLoop, calls=%fused_computation.12 | loop fusion | flops 768000 | bytes 4096000 | tf_op jit(solution)/shard_map/sub | solution.py:109
  (26 shorter events, 0.9 us)
Async XLA Ops:
  0.6 1.2 copy-start
  20.7 33.8 %all-to-all-start.1 = ((f32[16,32,1024]{2,1,0:T(8,128)}), f32[16,32,1024]{2,1,0:T(8,128)S(1)}, u32[]{:S(2)}, u32[]{:S(2)}) async-start(f32[16,32,1024]{2,1,0:T(8,128)} %broadcast_in_dim.17), calls=%async_computation.1 | async-start | bytes 4194304 | tf_op jit(solution)/shard_map/all_to_all | solution.py:24
  27.5 5.6 %collective-permute-start = (f32[256,1024]{1,0:T(8,128)}, f32[256,1024]{1,0:T(8,128)S(1)}, u32[]{:S(2)}, u32[]{:S(2)}) collective-permute-start(f32[256,1024]{1,0:T(8,128)} %param.8), channel_id=1, source_target_pairs={{0,16},{16,0},{1,17},{17,1},{2,18},{18,2},{3,19},{19,3},{4,20},{20... | collective-permute-start | bytes 3145736 | tf_op jit(solution)/shard_map/ppermute | solution.py:58
  30.1 28.2 %collective-permute-start.1 = (f32[256,1000]{0,1:T(8,128)}, f32[256,1000]{0,1:T(8,128)}, u32[]{:S(2)}, u32[]{:S(2)}) collective-permute-start(f32[256,1000]{0,1:T(8,128)} %param.9), channel_id=1, source_target_pairs={{0,16},{16,0},{1,17},{17,1},{2,18},{18,2},{3,19},{19,3},{4,20},{20... | collective-permute-start | bytes 3072008 | tf_op jit(solution)/shard_map/ppermute | solution.py:59
  33.2 1.3 copy-start.1
  54.8 3.5 %copy-start.5 = (f32[256,1000]{0,1:T(8,128)S(1)}, f32[256,1000]{0,1:T(8,128)}, u32[]{:S(2)}) copy-start(f32[256,1000]{0,1:T(8,128)} %param.9) | copy-start | bytes 3072004
  58.3 3.6 %copy-start.2 = (f32[512,512]{1,0:T(8,128)}, f32[512,512]{1,0:T(8,128)S(1)}, u32[]{:S(2)}) copy-start(f32[512,512]{1,0:T(8,128)S(1)} %convolution_multiply_fusion) | copy-start | bytes 3145732
  96.5 11.2 %all-to-all-start.3 = ((f32[8,4,1000]{2,1,0:T(4,128)}), f32[8,4,1000]{2,1,0:T(4,128)S(1)}, u32[]{:S(2)}, u32[]{:S(2)}) async-start(f32[8,4,1000]{2,1,0:T(4,128)} %all_to_all.37), calls=%async_computation.3 | async-start | bytes 262144 | tf_op jit(solution)/shard_map/all_to_all | solution.py:24
  118.4 27.2 %copy-start.3 = (f32[512,512]{1,0:T(8,128)S(1)}, f32[512,512]{1,0:T(8,128)}, u32[]{:S(2)}) copy-start(f32[512,512]{1,0:T(8,128)} %copy-done.2) | copy-start | bytes 3145732
  147.6 1.3 copy-start.4
  150.0 9.8 %collective-permute-start.2 = (f32[256,1000]{0,1:T(8,128)}, f32[256,1000]{0,1:T(8,128)}, u32[]{:S(2)}, u32[]{:S(2)}) collective-permute-start(f32[256,1000]{0,1:T(8,128)} %slice.13), channel_id=1, source_target_pairs={{0,16},{16,0},{1,17},{17,1},{2,18},{18,2},{3,19},{19,3},{4,20},{20... | collective-permute-start | bytes 3072008 | tf_op jit(solution)/shard_map/ppermute | solution.py:108
  157.6 1.4 collective-permute-start.3

commit v2 on v1

--- a/solution.py
+++ b/solution.py
@@ -12,6 +12,7 @@
 NARROW = ("z", "y_hi")
 PLANE = ("y_lo", "y_hi", "x")
 SWAP = ((0, 1), (1, 0))
+LANE = 128
 
 step_size = 1.0
 
@@ -53,60 +54,76 @@
     start = (core * (wide // 2) + lax.axis_index(("y_lo", "x"))) * own
     index = lax.dynamic_slice_in_dim(batch_index, start, own, 0)
     rows = pick(train_features, index)
-    targets = pick(train_labels, index)
+    lanes = -(-outputs // LANE) * LANE
+    fill = ((0, 0), (0, lanes - outputs))
+    targets = jnp.pad(pick(train_labels, index), fill)
 
     other_centers = lax.ppermute(centers, "core", SWAP)
-    other_weights = lax.ppermute(weights, "core", SWAP)
-    pair_centers = jnp.concatenate([centers, other_centers], axis=0)
-    pair_weights = jnp.concatenate([weights, other_weights], axis=0)
-    center_sq = jnp.sum(pair_centers * pair_centers, axis=1)
+    other_weights = jnp.pad(lax.ppermute(weights, "core", SWAP), fill)
+    own_weights = jnp.pad(weights, fill)
 
     rows_all = spread(spread(rows, ("z",)), PLANE)
-    inner = lax.dot_general(
-        rows_all,
-        pair_centers,
-        (((1,), (1,)), ((), ())),
-        precision=lax.Precision.HIGH,
-        preferred_element_type=jnp.float32,
-    )
     row_sq = jnp.sum(rows_all * rows_all, axis=1)
-    kernel = jnp.exp(
-        (2.0 * features - row_sq[:, None] - center_sq[None, :] + 2.0 * inner) / 128.0
-    )
-    partial_value = jnp.dot(
-        kernel, pair_weights, precision=lax.Precision.HIGH, preferred_element_type=jnp.float32
-    )
+
+    def kernel_of(block_centers):
+        inner = lax.dot_general(
+            rows_all,
+            block_centers,
+            (((1,), (1,)), ((), ())),
+            precision=lax.Precision.HIGH,
+            preferred_element_type=jnp.float32,
+        )
+        center_sq = jnp.sum(block_centers * block_centers, axis=1)
+        return jnp.exp(
+            (2.0 * features - row_sq[:, None] - center_sq[None, :] + 2.0 * inner) / 128.0
+        )
+
+    def product(kernel, block_weights):
+        return jnp.dot(
+            kernel,
+            block_weights,
+            precision=lax.Precision.HIGH,
+            preferred_element_type=jnp.float32,
+        )
+
+    own_kernel = kernel_of(centers)
+    other_kernel = kernel_of(other_centers)
+    partial_value = product(own_kernel, own_weights) + product(other_kernel, other_weights)
     value = scatter_sum(scatter_sum(partial_value, PLANE), ("z",))
     resid = value * scale - targets
     resid_all = spread(spread(resid, ("z",)), PLANE)
 
-    shaped = resid_all.reshape(
-        lax.axis_size("y_lo"),
-        lax.axis_size("y_hi"),
-        lax.axis_size("x"),
-        lax.axis_size("z"),
-        own,
-        outputs,
-    )
-    mine = lax.dynamic_index_in_dim(shaped, lax.axis_index("y_hi"), 1, keepdims=False)
-    mine = lax.dynamic_index_in_dim(mine, lax.axis_index("z"), 2, keepdims=False)
-    mine = mine.reshape(block // 2, outputs)
+    def delta_of(kernel):
+        return lax.dot_general(
+            resid_all,
+            kernel,
+            (((0,), (0,)), ((), ())),
+            precision=lax.Precision.HIGH,
+            preferred_element_type=jnp.float32,
+        )[:outputs]
+
+    received = lax.ppermute(delta_of(other_kernel), "core", SWAP)
+    delta = delta_of(own_kernel)
+    new_weights = weights - step_size / batch * (delta + received).T
+
+    plane = own * lax.axis_size("z")
+    place = lax.axis_index("z") * own + lax.axis_index("y_hi") * lax.axis_size("x") * plane
+    mine = jnp.concatenate(
+        [
+            lax.dynamic_slice_in_dim(
+                resid_all, place + (y * lax.axis_size("y_hi") * lax.axis_size("x") + x) * plane, own, 0
+            )
+            for y in range(lax.axis_size("y_lo"))
+            for x in range(lax.axis_size("x"))
+        ],
+        axis=0,
+    )[:, :outputs]
     theirs = lax.ppermute(mine, "core", SWAP)
     residual = jnp.where(
         core == 0,
         jnp.concatenate([mine, theirs], axis=0),
         jnp.concatenate([theirs, mine], axis=0),
     )
-    delta = lax.dot_general(
-        kernel,
-        resid_all,
-        (((0,), (0,)), ((), ())),
-        precision=lax.Precision.HIGH,
-        preferred_element_type=jnp.float32,
-    )
-    here = centers.shape[0]
-    received = lax.ppermute(delta[here:], "core", SWAP)
-    new_weights = weights - step_size / batch * (delta[:here] + received)
     return (new_weights, residual)
 
 

time: 163 us -> 163 us (level)
  local copies, waits for them, and re-layouts: 13.5 us -> 7.94 us
  matrix products: 9.11 us -> 14.3 us
  other arithmetic: 5.12 us -> 3.43 us
    dot_general x3 -> x6, matrix products: 9.11 us -> 14.3 us  [the longest x2 7.32 us: delta_of(): lax.dot_general(resid_all, kernel, (((0,), (0,)), ((), ())), precision=la...]
    sub x2 -> x1, other arithmetic: 2.99 us -> 0.01 us  [kernel_of(): 2.0 * features - row_sq[:, None] - center_sq[None, :] + 2.0 * inner]
    unnamed x14 -> x15, local copies, waits for them, and re-layouts: 5.86 us -> 3.92 us
    reshape x2 -> x0, local copies, waits for them, and re-layouts: 1.72 us -> none  [the longest x1 1.67 us: per_device(): resid_all.reshape(lax.axis_size('y_lo'), lax.axis_size('y_hi'), lax.axis_...]
  transfers between devices with their start and end apart: 6 -> 6, of which waited for: 4 -> 4; matrix products, arithmetic and copies ran while one was open for 7% -> 6% of each run, Pallas kernels for 0% -> 0%
where the time goes in v2:
time: 163 us; the launch traced here: 162 us
  blocking collectives  87.8 us (54%)
  waiting for transfers between devices  29.7 us (18%)
  starting transfers between devices  18 us (11%)
  matrix products  14.3 us (9%)
  local copies, waits for them, and re-layouts  7.94 us (5%)
  other arithmetic  3.43 us (2%)
    all_to_all x4, blocking collectives, exchange(): return lax.all_to_all(array, axes, 0, 0, tiled=True)  87.8 us
    all_to_all x2, waiting for transfers between devices, exchange(): return lax.all_to_all(array, axes, 0, 0, tiled=True)  26 us
    all_to_all x2, starting transfers between devices, exchange(): return lax.all_to_all(array, axes, 0, 0, tiled=True)  10.1 us
    dot_general x2, matrix products, delta_of(): lax.dot_general(resid_all, kernel, (((0,), (0,)), ((), ())), precision=la...  7.32 us
    ppermute x1, starting transfers between devices, per_device(): received = lax.ppermute(delta_of(other_kernel), 'core', SWAP)  5.02 us
    unnamed x15, local copies, waits for them, and re-layouts  3.92 us
    dot_general x2, matrix products, product(): jnp.dot(kernel, block_weights, precision=lax.Precision.HIGH, preferred_el...  3.52 us
    dot_general x2, matrix products, kernel_of(): lax.dot_general(rows_all, block_centers, (((1,), (1,)), ((), ())), precis...  3.41 us
  transfers between devices with their start and end apart: 6, of which 4 were waited for; matrix products, arithmetic and copies ran while one was open for 6% of the time, Pallas kernels for 0%

profile of v2, /device:TPU:1, one launch (start us, length us, event | category | flops | bytes accessed | tf_op | source)
XLA Modules:
  0.0 162.0 jit_solution(86433619644536647)
XLA Ops:
  0.7 0.8 compare_select_fusion
  1.5 0.4 copy-done
  1.9 0.6 gather_fusion
  2.5 16.6 %all_to_all.48 = f32[8,4,1024]{2,1,0:T(4,128)S(1)} all-to-all(f32[8,4,1024]{2,1,0:T(4,128)S(1)} %broadcast_in_dim.15), channel_id=1, replica_groups=mesh['y_lo'=2,'x'=4,'core'=2,'z'=8,'y_hi'=2] {'z'}, dimensions={0} | all-to-all | bytes 262144 | tf_op jit(solution)/shard_map/all_to_all | solution.py:25
  19.1 1.6 broadcast_in_dim.17
  20.7 6.8 %all-to-all-start.1 = ((f32[16,32,1024]{2,1,0:T(8,128)}), f32[16,32,1024]{2,1,0:T(8,128)S(1)}, u32[]{:S(2)}, u32[]{:S(2)}) async-start(f32[16,32,1024]{2,1,0:T(8,128)} %broadcast_in_dim.17), calls=%async_computation.1 | async-start | bytes 4194304 | tf_op jit(solution)/shard_map/all_to_all | solution.py:25
  27.5 2.6 %collective-permute-start = (f32[256,1024]{1,0:T(8,128)}, f32[256,1024]{1,0:T(8,128)S(1)}, u32[]{:S(2)}, u32[]{:S(2)}) collective-permute-start(f32[256,1024]{1,0:T(8,128)} %param.8), channel_id=1, source_target_pairs={{0,16},{16,0},{1,17},{17,1},{2,18},{18,2},{3,19},{19,3},{4,20},{20... | collective-permute-start | bytes 3145736 | tf_op jit(solution)/shard_map/ppermute | solution.py:61
  30.2 1.4 multiply_reduce_fusion.2
  31.6 1.5 collective-permute-done
  33.1 1.0 copy-done.4
  34.2 20.3 %all-to-all-done.1 = f32[16,32,1024]{2,1,0:T(8,128)S(1)} async-done(((f32[16,32,1024]{2,1,0:T(8,128)}), f32[16,32,1024]{2,1,0:T(8,128)S(1)}, u32[]{:S(2)}, u32[]{:S(2)}) %all-to-all-start.1) | async-done | bytes 2097184 | tf_op jit(solution)/shard_map/all_to_all | solution.py:25
  54.5 0.2 multiply_reduce_fusion
  54.8 2.4 %fusion.18 = f32[512,256]{1,0:T(8,128)S(1)} fusion(f32[512,1024]{1,0:T(8,128)S(1)} %bitcast.14, f32[256,1024]{1,0:T(8,128)} %param.8, f32[256]{0:T(256)S(1)} %multiply_reduce_fusion.2, f32[512]{0:T(512)S(1)} %sub.43), kind=kOutput, calls=%fused_computation.16 | convolution fusion | flops 805830656 | bytes 3673088 | tf_op jit(solution)/shard_map/dot_general | solution.py:69
  57.2 0.8 copy-done.3
  58.0 1.1 fusion.20
  59.1 0.2 copy-done.5
  59.3 1.0 convolution_multiply_fusion
  60.3 2.5 %convolution_add_fusion = f32[512,1024]{1,0:T(8,128)S(1)} fusion(f32[512,1024]{1,0:T(8,128)S(1)} %fusion.20, f32[256,1000]{0,1:T(8,128)} %collective-permute-done.1, f32[512,256]{1,0:T(8,128)S(1)} %convolution_multiply_fusion, f32[256]{0:T(256)S(1)} %multiply_reduce_fusion.1, f32[512]{0:T(512)S(1)} %sub.43), kind=kOutput, calls=%fused_computation.7 | convolution fusion | flops 806223872 | bytes 5745664 | tf_op jit(solution)/shard_map/dot_general | solution.py:82
  62.8 33.7 %all_to_all.49 = f32[16,32,1024]{2,1,0:T(8,128)S(1)} all-to-all(f32[16,32,1024]{2,1,0:T(8,128)S(1)} %bitcast.19), channel_id=1, replica_groups=mesh['y_lo'=2,'x'=4,'core'=2,'z'=8,'y_hi'=2] {'y_lo','y_hi','x'}, dimensions={0} | all-to-all | bytes 4194304 | tf_op jit(solution)/shard_map/all_to_all | solution.py:25
  96.6 0.7 all_to_all.37
  97.3 3.4 %all-to-all-start.3 = ((f32[8,4,1024]{2,1,0:T(4,128)}), f32[8,4,1024]{2,1,0:T(4,128)S(1)}, u32[]{:S(2)}, u32[]{:S(2)}) async-start(f32[8,4,1024]{2,1,0:T(4,128)} %all_to_all.37), calls=%async_computation.3 | async-start | bytes 262144 | tf_op jit(solution)/shard_map/all_to_all | solution.py:25
  100.7 1.5 copy.10
  102.3 0.6 gather_fusion.1
  102.8 5.7 %all-to-all-done.3 = f32[8,4,1024]{2,1,0:T(4,128)S(1)} async-done(((f32[8,4,1024]{2,1,0:T(4,128)}), f32[8,4,1024]{2,1,0:T(4,128)S(1)}, u32[]{:S(2)}, u32[]{:S(2)}) %all-to-all-start.3) | async-done | bytes 131104 | tf_op jit(solution)/shard_map/all_to_all | solution.py:25
  108.6 10.3 %all_to_all.50 = f32[8,4,1024]{2,1,0:T(4,128)S(1)} all-to-all(f32[8,4,1024]{2,1,0:T(4,128)S(1)} %broadcast_in_dim.18), channel_id=1, replica_groups=mesh['y_lo'=2,'x'=4,'core'=2,'z'=8,'y_hi'=2] {'z'}, dimensions={0} | all-to-all | bytes 262144 | tf_op jit(solution)/shard_map/all_to_all | solution.py:25
  119.0 0.2 broadcast_in_dim.20
  119.3 27.2 %all_to_all.51 = f32[16,32,1024]{2,1,0:T(8,128)S(1)} all-to-all(f32[16,32,1024]{2,1,0:T(8,128)S(1)} %broadcast_in_dim.20), channel_id=1, replica_groups=mesh['y_lo'=2,'x'=4,'core'=2,'z'=8,'y_hi'=2] {'y_lo','y_hi','x'}, dimensions={0} | all-to-all | bytes 4194304 | tf_op jit(solution)/shard_map/all_to_all | solution.py:25
  146.4 2.9 %fusion = f32[1000,256]{1,0:T(8,128)} fusion(f32[512,1024]{1,0:T(8,128)S(1)} %bitcast.16, f32[512,256]{1,0:T(8,128)S(1)} %copy-done.2, f32[256]{0:T(256)S(1)} %multiply_reduce_fusion.1, f32[512]{0:T(512)S(1)} %sub.43), kind=kOutput, calls=%fused_computation.3 | convolution fusion | flops 786825216 | bytes 3648512 | tf_op jit(solution)/shard_map/dot_general | solution.py:97
  149.3 5.0 %collective-permute-start.2 = (f32[1000,256]{1,0:T(8,128)}, f32[1000,256]{1,0:T(8,128)}, u32[]{:S(2)}, u32[]{:S(2)}) collective-permute-start(f32[1000,256]{1,0:T(8,128)} %fusion), channel_id=1, source_target_pairs={{0,16},{16,0},{1,17},{17,1},{2,18},{18,2},{3,19},{19,3},{4,20},{20... | collective-permute-start | bytes 3072008 | tf_op jit(solution)/shard_map/ppermute | solution.py:105
  154.6 2.2 %collective-permute-done.3 = f32[32,1000]{1,0:T(8,128)S(1)} collective-permute-done((f32[32,1000]{1,0:T(8,128)S(1)}, f32[32,1000]{1,0:T(8,128)S(1)}, u32[]{:S(2)}, u32[]{:S(2)}) %collective-permute-start.3) | collective-permute-done | bytes 128032 | tf_op jit(solution)/shard_map/ppermute | solution.py:121
  156.8 0.7 maximum_select_fusion
  157.5 4.5 %fusion.13 = f32[256,1000]{0,1:T(8,128)} fusion(f32[256,1000]{0,1:T(8,128)} %param.9, f32[1000,256]{1,0:T(8,128)} %collective-permute-done.2, f32[512,256]{1,0:T(8,128)} %copy-done.3, f32[512,1024]{1,0:T(8,128)S(1)} %bitcast.18), kind=kOutput, calls=%fused_computation.11 | convolution fusion | flops 787200000 | bytes 5693440 | tf_op jit(solution)/shard_map/dot_general | solution.py:97
  (27 shorter events, 0.9 us)
Async XLA Ops:
  0.6 1.2 copy-start
  20.7 33.8 %all-to-all-start.1 = ((f32[16,32,1024]{2,1,0:T(8,128)}), f32[16,32,1024]{2,1,0:T(8,128)S(1)}, u32[]{:S(2)}, u32[]{:S(2)}) async-start(f32[16,32,1024]{2,1,0:T(8,128)} %broadcast_in_dim.17), calls=%async_computation.1 | async-start | bytes 4194304 | tf_op jit(solution)/shard_map/all_to_all | solution.py:25
  27.5 5.6 %collective-permute-start = (f32[256,1024]{1,0:T(8,128)}, f32[256,1024]{1,0:T(8,128)S(1)}, u32[]{:S(2)}, u32[]{:S(2)}) collective-permute-start(f32[256,1024]{1,0:T(8,128)} %param.8), channel_id=1, source_target_pairs={{0,16},{16,0},{1,17},{17,1},{2,18},{18,2},{3,19},{19,3},{4,20},{20... | collective-permute-start | bytes 3145736 | tf_op jit(solution)/shard_map/ppermute | solution.py:61
  30.1 30.2 %collective-permute-start.1 = (f32[256,1000]{0,1:T(8,128)}, f32[256,1000]{0,1:T(8,128)}, u32[]{:S(2)}, u32[]{:S(2)}) collective-permute-start(f32[256,1000]{0,1:T(8,128)} %param.9), channel_id=1, source_target_pairs={{0,16},{16,0},{1,17},{17,1},{2,18},{18,2},{3,19},{19,3},{4,20},{20... | collective-permute-start | bytes 3072008 | tf_op jit(solution)/shard_map/ppermute | solution.py:62
  33.1 1.0 copy-start.4
  54.8 3.2 %copy-start.6 = (f32[256,1000]{0,1:T(8,128)S(1)}, f32[256,1000]{0,1:T(8,128)}, u32[]{:S(2)}) copy-start(f32[256,1000]{0,1:T(8,128)} %param.9) | copy-start | bytes 3072004
  57.2 0.8 copy-start.3
  58.0 1.2 copy-start.5
  60.3 2.5 %copy-start.1 = (f32[512,256]{1,0:T(8,128)}, f32[512,256]{1,0:T(8,128)S(1)}, u32[]{:S(2)}) copy-start(f32[512,256]{1,0:T(8,128)S(1)} %convolution_multiply_fusion) | copy-start | bytes 1572868
  97.3 11.2 %all-to-all-start.3 = ((f32[8,4,1024]{2,1,0:T(4,128)}), f32[8,4,1024]{2,1,0:T(4,128)S(1)}, u32[]{:S(2)}, u32[]{:S(2)}) async-start(f32[8,4,1024]{2,1,0:T(4,128)} %all_to_all.37), calls=%async_computation.3 | async-start | bytes 262144 | tf_op jit(solution)/shard_map/all_to_all | solution.py:25
  119.3 27.2 %copy-start.2 = (f32[512,256]{1,0:T(8,128)S(1)}, f32[512,256]{1,0:T(8,128)}, u32[]{:S(2)}) copy-start(f32[512,256]{1,0:T(8,128)} %copy-done.1) | copy-start | bytes 1572868
  149.3 8.2 %collective-permute-start.2 = (f32[1000,256]{1,0:T(8,128)}, f32[1000,256]{1,0:T(8,128)}, u32[]{:S(2)}, u32[]{:S(2)}) collective-permute-start(f32[1000,256]{1,0:T(8,128)} %fusion), channel_id=1, source_target_pairs={{0,16},{16,0},{1,17},{17,1},{2,18},{18,2},{3,19},{19,3},{4,20},{20... | collective-permute-start | bytes 3072008 | tf_op jit(solution)/shard_map/ppermute | solution.py:105
  154.5 2.3 %collective-permute-start.3 = (f32[32,1000]{1,0:T(8,128)S(1)}, f32[32,1000]{1,0:T(8,128)S(1)}, u32[]{:S(2)}, u32[]{:S(2)}) collective-permute-start(f32[32,1000]{1,0:T(8,128)S(1)} %bitcast.20), channel_id=1, source_target_pairs={{0,16},{16,0},{1,17},{17,1},{2,18},{18,2},{3,19},{19,3},{4,20},{20... | collective-permute-start | bytes 384008 | tf_op jit(solution)/shard_map/ppermute | solution.py:121

commit v3 on v0

v3 whole, which is shorter than its diff:
```python
import math

import jax
import jax.numpy as jnp
from jax import lax
from jax.sharding import Mesh
from jax.sharding import PartitionSpec as P

AXES = ("y_lo", "x", "core", "z", "y_hi")
SIZES = (2, 4, 2, 8, 2)
WIDE_NARROW = AXES
NARROW = ("z", "y_hi")
RING = 4
LEVELS = 8
LANE = 128
ORDER = (2, 1, 3)

step_size = 1.0


def position(x, y, z, core):
    x, y = x % RING, y % RING
    return (((y % 2 * RING + x) * 2 + core) * LEVELS + z) * 2 + y // 2


def everywhere():
    return [
        (x, y, z, core)
        for x in range(RING)
        for y in range(RING)
        for z in range(LEVELS)
        for core in range(2)
    ]


def bulk_shift(offset):
    return [
        (
            position(x, y, z, core),
            position(x + offset, y, z, 0) if core == 0 else position(x, y + offset, z, 1),
        )
        for x, y, z, core in everywhere()
    ]


SWAP = [(position(x, y, z, core), position(x, y, z, 1 - core)) for x, y, z, core in everywhere()]
COLUMNS = [
    [position(x, y, z, core) for z in range(LEVELS)]
    for x in range(RING)
    for y in range(RING)
    for core in range(2)
]
RINGS = [
    [position(i, k, z, 0) if core == 0 else position(k, i, z, 1) for k in range(RING)]
    for i in range(RING)
    for z in range(LEVELS)
    for core in range(2)
]


def permute(array, pairs):
    return lax.ppermute(array, AXES, pairs)


def exchange(array, groups):
    return lax.all_to_all(array, AXES, 0, 0, axis_index_groups=groups, tiled=True)


def spread(array, groups):
    count = len(groups[0])
    copies = jnp.broadcast_to(array[None], (count,) + array.shape)
    return exchange(copies.reshape((-1,) + array.shape[1:]), groups)


def scatter_sum(array, groups):
    count = len(groups[0])
    return exchange(array, groups).reshape((count, -1) + array.shape[1:]).sum(axis=0)


def quarters(own):
    received = {offset: permute(own, bulk_shift(-offset)) for offset in ORDER}
    received[0] = own
    return received


def pick(array, index):
    return array.at[index].get(mode="promise_in_bounds")


def dot(left, right, contract):
    return lax.dot_general(
        left,
        right,
        (contract, ((), ())),
        precision=lax.Precision.HIGH,
        preferred_element_type=jnp.float32,
    )


def per_device(batch_index, train_features, train_labels, centers, weights):
    block = batch_index.shape[0]
    features = centers.shape[1]
    outputs = weights.shape[1]
    here = centers.shape[0]
    devices = math.prod(SIZES)
    batch = block * LEVELS * 2
    scale = 1.0 / math.sqrt(here * devices)
    x, core, z = lax.axis_index("x"), lax.axis_index("core"), lax.axis_index("z")
    y_lo, y_hi = lax.axis_index("y_lo"), lax.axis_index("y_hi")
    y = y_hi * 2 + y_lo
    own = block // (2 * RING * 2)
    start = (core * 2 * RING + y_lo * RING + x) * own
    index = lax.dynamic_slice_in_dim(batch_index, start, own, 0)
    rows = pick(train_features, index)
    lanes = -(-outputs // LANE) * LANE
    fill = ((0, 0), (0, lanes - outputs))
    targets = jnp.pad(pick(train_labels, index), fill)

    pair_centers = jnp.concatenate([centers, permute(centers, SWAP)], axis=0)
    pair_weights = jnp.pad(jnp.concatenate([weights, permute(weights, SWAP)], axis=0), fill)
    center_sq = jnp.sum(pair_centers * pair_centers, axis=1)

    rows_of = quarters(spread(spread(rows, COLUMNS), RINGS))
    kernel_of = {}
    for offset, part in rows_of.items():
        row_sq = jnp.sum(part * part, axis=1)
        inner = dot(part, pair_centers, ((1,), (1,)))
        kernel_of[offset] = jnp.exp(
            (2.0 * features - row_sq[:, None] - center_sq[None, :] + 2.0 * inner) / 128.0
        )
    value = dot(kernel_of[0], pair_weights, ((1,), (0,)))
    for offset in ORDER:
        value = value + permute(
            dot(kernel_of[offset], pair_weights, ((1,), (0,))), bulk_shift(offset)
        )
    value = scatter_sum(scatter_sum(value, RINGS), COLUMNS)
    resid_of = quarters(spread(spread(value * scale - targets, COLUMNS), RINGS))

    def delta_of(low, high):
        return sum(
            dot(resid_of[offset], kernel_of[offset][:, low:high], ((0,), (0,)))
            for offset in (0,) + ORDER
        )[:outputs]

    received = permute(delta_of(here, 2 * here), SWAP)
    delta = delta_of(0, here)
    new_weights = weights - step_size / batch * (delta + received).T

    quarter = RING * LEVELS * own
    resid_all = jnp.concatenate([resid_of[offset] for offset in range(RING)], axis=0)
    pieces = []
    for low in range(2):
        for column in range(RING):
            line = y_hi * 2 + low
            offset = jnp.where(core == 0, column - x, line - y) % RING
            slot = jnp.where(core == 0, line, column)
            place = offset * quarter + (slot * LEVELS + z) * own
            pieces.append(lax.dynamic_slice_in_dim(resid_all, place, own, 0))
    mine = jnp.concatenate(pieces, axis=0)[:, :outputs]
    theirs = permute(mine, SWAP)
    residual = jnp.where(
        core == 0,
        jnp.concatenate([mine, theirs], axis=0),
        jnp.concatenate([theirs, mine], axis=0),
    )
    return (new_weights, residual)


def solution(mesh):
    split = Mesh(mesh.devices.reshape(SIZES), AXES)
    placed = (
        P(NARROW),
        P(NARROW, None),
        P(NARROW, None),
        P(WIDE_NARROW, None),
        P(WIDE_NARROW, None),
    )
    return jax.shard_map(
        per_device,
        mesh=split,
        in_specs=placed,
        out_specs=(P(WIDE_NARROW, None), P(NARROW, None)),
        check_vma=False,
    )
```

time: 375 us -> 153 us (0.41)
  waiting for transfers between devices: 318 us -> 32.5 us
  blocking collectives: 9.4 us -> 45.3 us
  starting transfers between devices: 0.08 us -> 33.2 us
  between operations: 14.2 us -> 1.25 us
  matrix products: 15.3 us -> 28.2 us
  local copies, waits for them, and re-layouts: 12.5 us -> 4.85 us
    psum x1 -> x0, waiting for transfers between devices: 266 us -> none  [per_device(): resid_all = lax.psum(partial_value * scale - placed, WIDE_NARROW)]
    all_gather x1 -> x0, waiting for transfers between devices: 52.3 us -> none  [gather_axes(): array = lax.all_gather(array, axis, axis=dim, tiled=True)]
    all_to_all x0 -> x4, blocking collectives: none -> 45.3 us  [exchange(): lax.all_to_all(array, AXES, 0, 0, axis_index_groups=groups, tiled=True)]
    ppermute x0 -> x13, starting transfers between devices: none -> 26.1 us  [permute(): return lax.ppermute(array, AXES, pairs)]
    ppermute x0 -> x13, waiting for transfers between devices: none -> 18.9 us  [permute(): return lax.ppermute(array, AXES, pairs)]
    all_to_all x0 -> x2, waiting for transfers between devices: none -> 13.7 us  [exchange(): lax.all_to_all(array, AXES, 0, 0, axis_index_groups=groups, tiled=True)]
    dot_general x3 -> x16, matrix products: 15.3 us -> 28.2 us  [dot(): lax.dot_general(left, right, (contract, ((), ())), precision=lax.Precisio...]
    all_gather x1 -> x0, blocking collectives: 9.4 us -> none  [gather_axes(): array = lax.all_gather(array, axis, axis=dim, tiled=True)]
  transfers between devices with their start and end apart: 2 -> 15, of which waited for: 2 -> 5; matrix products, arithmetic and copies ran while one was open for 2% -> 20% of each run, Pallas kernels for 0% -> 0%
where the time goes in v3:
time: 153 us; the launch traced here: 152 us
  blocking collectives  45.3 us (30%)
  starting transfers between devices  33.2 us (22%)
  waiting for transfers between devices  32.5 us (21%)
  matrix products  28.2 us (18%)
  other arithmetic  6.48 us (4%)
  local copies, waits for them, and re-layouts  4.85 us (3%)
    all_to_all x4, blocking collectives, exchange(): lax.all_to_all(array, AXES, 0, 0, axis_index_groups=groups, tiled=True)  45.3 us
    dot_general x16, matrix products, dot(): lax.dot_general(left, right, (contract, ((), ())), precision=lax.Precisio...  28.2 us
    ppermute x13, starting transfers between devices, permute(): return lax.ppermute(array, AXES, pairs)  26.1 us
    ppermute x13, waiting for transfers between devices, permute(): return lax.ppermute(array, AXES, pairs)  18.9 us
    all_to_all x2, waiting for transfers between devices, exchange(): lax.all_to_all(array, AXES, 0, 0, axis_index_groups=groups, tiled=True)  13.7 us
    all_to_all x2, starting transfers between devices, exchange(): lax.all_to_all(array, AXES, 0, 0, axis_index_groups=groups, tiled=True)  7.06 us
  transfers between devices with their start and end apart: 15, of which 5 were waited for; matrix products, arithmetic and copies ran while one was open for 20% of the time, Pallas kernels for 0%

profile of v3, /device:TPU:1, one launch (start us, length us, event | category | flops | bytes accessed | tf_op | source)
XLA Modules:
  0.0 151.8 jit_solution(17583731288730784424)
XLA Ops:
  0.6 3.3 %collective-permute-start = (f32[256,1024]{1,0:T(8,128)}, f32[256,1024]{1,0:T(8,128)}, u32[]{:S(2)}, u32[]{:S(2)}) collective-permute-start(f32[256,1024]{1,0:T(8,128)} %param.8), channel_id=1, source_target_pairs={{0,16},{16,0},{2,18},{18,2},{4,20},{20,4},{6,22},{22,6},{8,24},{24... | collective-permute-start | bytes 3145736 | tf_op jit(solution)/shard_map/ppermute | solution.py:62
  5.3 14.1 %all_to_all.48 = f32[8,4,1024]{2,1,0:T(4,128)S(1)} all-to-all(f32[8,4,1024]{2,1,0:T(4,128)S(1)} %broadcast_in_dim.15), channel_id=1, replica_groups={{0,2,4,6,8,10,12,14},{16,18,20,22,24,26,28,30},{128,130,132,134,136,138..., dimensions={0} | all-to-all | bytes 262144 | tf_op jit(solution)/shard_map/all_to_all | solution.py:66
  19.5 10.9 %all_to_all.49 = f32[4,32,1024]{2,1,0:T(8,128)S(1)} all-to-all(f32[4,32,1024]{2,1,0:T(8,128)S(1)} %broadcast_in_dim.17), channel_id=1, replica_groups={{0,128,1,129},{16,48,80,112},{2,130,3,131},{18,50,82,114},{4,132,5,133}..., dimensions={0} | all-to-all | bytes 1048576 | tf_op jit(solution)/shard_map/all_to_all | solution.py:66
  30.4 1.3 collective-permute-start.6
  31.7 4.0 %collective-permute-start.1 = (f32[256,1000]{0,1:T(8,128)}, f32[256,1000]{0,1:T(8,128)S(1)}, u32[]{:S(2)}, u32[]{:S(2)}) collective-permute-start(f32[256,1000]{0,1:T(8,128)} %param.9), channel_id=1, source_target_pairs={{0,16},{16,0},{2,18},{18,2},{4,20},{20,4},{6,22},{22,6},{8,24},{24... | collective-permute-start | bytes 3072008 | tf_op jit(solution)/shard_map/ppermute | solution.py:62
  37.9 1.3 constant_dynamic-update-slice_fusion
  40.3 1.2 multiply_exponential_fusion
  41.5 3.5 %fusion.24 = f32[128,1024]{1,0:T(8,128)} fusion(f32[128,512]{1,0:T(8,128)S(1)} %multiply_exponential_fusion, f32[256,1000]{0,1:T(8,128)S(1)} %collective-permute-done.1, f32[256,1000]{0,1:T(8,128)} %param.9), kind=kOutput, calls=%fused_computation.67 | convolution fusion | flops 404750336 | bytes 2834432 | tf_op jit(solution)/shard_map/dot_general | solution.py:91
  45.0 1.5 collective-permute-start.7
  46.6 1.2 multiply_exponential_fusion.1
  47.8 3.2 %fusion.22 = f32[128,1024]{1,0:T(8,128)} fusion(f32[128,512]{1,0:T(8,128)S(1)} %multiply_exponential_fusion.1, f32[256,1000]{0,1:T(8,128)S(1)} %collective-permute-done.1, f32[256,1000]{0,1:T(8,128)} %param.9), kind=kOutput, calls=%fused_computation.65 | convolution fusion | flops 404750336 | bytes 2834432 | tf_op jit(solution)/shard_map/dot_general | solution.py:91
  51.0 3.6 %collective-permute-start.5 = (f32[128,1024]{1,0:T(8,128)}, f32[128,1024]{1,0:T(8,128)}, u32[]{:S(2)}, u32[]{:S(2)}) collective-permute-start(f32[128,1024]{1,0:T(8,128)} %fusion.22), channel_id=1, source_target_pairs={{0,32},{16,144},{2,34},{18,146},{4,36},{20,148},{6,38},{22,150},{8... | collective-permute-start | bytes 1572872 | tf_op jit(solution)/shard_map/ppermute | solution.py:62
  54.7 1.2 multiply_exponential_fusion.2
  56.0 3.2 %fusion.23 = f32[128,1024]{1,0:T(8,128)} fusion(f32[128,512]{1,0:T(8,128)S(1)} %multiply_exponential_fusion.2, f32[256,1000]{0,1:T(8,128)S(1)} %collective-permute-done.1, f32[256,1000]{0,1:T(8,128)} %param.9), kind=kOutput, calls=%fused_computation.66 | convolution fusion | flops 404750336 | bytes 2834432 | tf_op jit(solution)/shard_map/dot_general | solution.py:91
  59.4 2.3 %multiply_exponential_fusion.3 = f32[128,512]{1,0:T(8,128)S(1)} fusion(f32[128,1024]{1,0:T(8,128)} %bitcast.37, f32[512,1024]{1,0:T(8,128)S(1)} %constant_dynamic-update-slice_fusion, f32[512]{0:T(512)S(1)} %multiply_reduce_fusion, f32[128]{0:T(128)S(1)} %sub.116), kind=kOutput, calls=%fused_computation.31 | convolution fusion | flops 402915328 | bytes 2886144 | tf_op jit(solution)/shard_map/dot_general | solution.py:91
  61.8 7.5 %collective-permute-done.3 = f32[128,1024]{1,0:T(8,128)} collective-permute-done((f32[128,1024]{1,0:T(8,128)}, f32[128,1024]{1,0:T(8,128)}, u32[]{:S(2)}, u32[]{:S(2)}) %collective-permute-start.3) | collective-permute-done | bytes 524320 | tf_op jit(solution)/shard_map/ppermute | solution.py:62
  69.3 2.7 %fusion.1 = f32[128,1024]{1,0:T(8,128)S(1)} fusion(f32[128,1024]{1,0:T(8,128)} %collective-permute-done.7, f32[128,1024]{1,0:T(8,128)} %collective-permute-done.5, f32[128,1024]{1,0:T(8,128)} %collective-permute-done.3, f32[128,512]{1,0:T(8,128)S(1)} %multiply_exponential_fusion.3, f32[256,1000]{0,1:T(8,128)S(1)} %copy-done.11, f32[256,1000]{0,1:T(8,128)} %param.9), kind=kOutput, calls=%fused_computation.8 | convolution fusion | flops 405143552 | bytes 4407296 | tf_op jit(solution)/shard_map/dot_general | solution.py:91
  72.1 10.0 %all_to_all.50 = f32[4,32,1024]{2,1,0:T(8,128)S(1)} all-to-all(f32[4,32,1024]{2,1,0:T(8,128)S(1)} %bitcast.40), channel_id=1, replica_groups={{0,128,1,129},{16,48,80,112},{2,130,3,131},{18,50,82,114},{4,132,5,133}..., dimensions={0} | all-to-all | bytes 1048576 | tf_op jit(solution)/shard_map/all_to_all | solution.py:66
  82.8 3.6 %all-to-all-start.3 = ((f32[8,4,1024]{2,1,0:T(4,128)}), f32[8,4,1024]{2,1,0:T(4,128)S(1)}, u32[]{:S(2)}, u32[]{:S(2)}) async-start(f32[8,4,1024]{2,1,0:T(4,128)} %all_to_all.37), calls=%async_computation.3 | async-start | bytes 262144 | tf_op jit(solution)/shard_map/all_to_all | solution.py:66
  87.3 7.0 %all-to-all-done.3 = f32[8,4,1024]{2,1,0:T(4,128)S(1)} async-done(((f32[8,4,1024]{2,1,0:T(4,128)}), f32[8,4,1024]{2,1,0:T(4,128)S(1)}, u32[]{:S(2)}, u32[]{:S(2)}) %all-to-all-start.3) | async-done | bytes 131104 | tf_op jit(solution)/shard_map/all_to_all | solution.py:66
  94.4 10.3 %all_to_all.51 = f32[8,4,1024]{2,1,0:T(4,128)S(1)} all-to-all(f32[8,4,1024]{2,1,0:T(4,128)S(1)} %broadcast_in_dim.18), channel_id=1, replica_groups={{0,2,4,6,8,10,12,14},{16,18,20,22,24,26,28,30},{128,130,132,134,136,138..., dimensions={0} | all-to-all | bytes 262144 | tf_op jit(solution)/shard_map/all_to_all | solution.py:66
  105.6 3.5 %all-to-all-start.5 = ((f32[4,32,1024]{2,1,0:T(8,128)}), f32[4,32,1024]{2,1,0:T(8,128)S(1)}, u32[]{:S(2)}, u32[]{:S(2)}) async-start(f32[4,32,1024]{2,1,0:T(8,128)} %broadcast_in_dim.20), calls=%async_computation.5 | async-start | bytes 1048576 | tf_op jit(solution)/shard_map/all_to_all | solution.py:66
  109.3 6.7 %all-to-all-done.5 = f32[4,32,1024]{2,1,0:T(8,128)S(1)} async-done(((f32[4,32,1024]{2,1,0:T(8,128)}), f32[4,32,1024]{2,1,0:T(8,128)S(1)}, u32[]{:S(2)}, u32[]{:S(2)}) %all-to-all-start.5) | async-done | bytes 524320 | tf_op jit(solution)/shard_map/all_to_all | solution.py:66
  116.1 2.6 %collective-permute-start.9 = (f32[128,1024]{1,0:T(8,128)S(1)}, f32[128,1024]{1,0:T(8,128)S(1)}, u32[]{:S(2)}, u32[]{:S(2)}) collective-permute-start(f32[128,1024]{1,0:T(8,128)S(1)} %bitcast.29), channel_id=1, source_target_pairs={{0,96},{16,145},{2,98},{18,147},{4,100},{20,149},{6,102},{22,151},... | collective-permute-start | bytes 1572872 | tf_op jit(solution)/shard_map/ppermute | solution.py:62
  119.0 1.5 fusion.12
  120.6 2.5 %fusion.20 = f32[1024,256]{1,0:T(8,128)} fusion(f32[128,1024]{1,0:T(8,128)S(1)} %bitcast.32, f32[128,512]{1,0:T(8,128)} %copy-done.8), kind=kOutput, calls=%fused_computation.46 | convolution fusion | flops 201326592 | bytes 1703936 | tf_op jit(solution)/shard_map/dot_general | solution.py:91
  123.1 10.6 %collective-permute-done.10 = f32[128,1024]{1,0:T(8,128)S(1)} collective-permute-done((f32[128,1024]{1,0:T(8,128)S(1)}, f32[128,1024]{1,0:T(8,128)S(1)}, u32[]{:S(2)}, u32[]{:S(2)}) %collective-permute-start.10) | collective-permute-done | bytes 524320 | tf_op jit(solution)/shard_map/ppermute | solution.py:62
  135.6 1.2 slice_add_fusion
  136.8 7.1 %collective-permute-start.11 = (f32[1000,256]{1,0:T(8,128)}, f32[1000,256]{1,0:T(8,128)}, u32[]{:S(2)}, u32[]{:S(2)}) collective-permute-start(f32[1000,256]{1,0:T(8,128)} %slice_add_fusion), channel_id=1, source_target_pairs={{0,16},{16,0},{2,18},{18,2},{4,20},{20,4},{6,22},{22,6},{8,24},{24... | collective-permute-start | bytes 3072008 | tf_op jit(solution)/shard_map/ppermute | solution.py:62
  145.0 1.6 %fusion.16 = f32[1024,256]{1,0:T(8,128)S(1)} fusion(f32[128,1024]{1,0:T(8,128)S(1)} %collective-permute-done.9, f32[128,512]{1,0:T(8,128)} %copy-done.4), kind=kOutput, calls=%fused_computation.42 | convolution fusion | flops 201326592 | bytes 1703936 | tf_op jit(solution)/shard_map/dot_general | solution.py:91
  146.6 1.5 fusion.18
  148.9 2.9 %fusion.5 = f32[256,1000]{0,1:T(8,128)} fusion(f32[256,1000]{0,1:T(8,128)} %param.9, f32[1000,256]{1,0:T(8,128)} %collective-permute-done.11, f32[1024,256]{1,0:T(8,128)S(1)} %fusion.14, f32[1024,256]{1,0:T(8,128)S(1)} %fusion.16, f32[1024,256]{1,0:T(8,128)S(1)} %fusion.18, f32[1024,256]{1,0:T(8,128)S(1)} %copy-done.2), kind=kLoop, calls=%fused_computation.20 | loop fusion | flops 1536000 | bytes 7168000 | tf_op jit(solution)/shard_map/sub | solution.py:147
  (75 shorter events, 11.8 us)
Async XLA Ops:
  0.6 4.1 %copy-start = (f32[256,1024]{1,0:T(8,128)S(1)}, f32[256,1024]{1,0:T(8,128)}, u32[]{:S(2)}) copy-start(f32[256,1024]{1,0:T(8,128)} %param.6) | copy-start | bytes 3145732
  0.6 37.3 %collective-permute-start = (f32[256,1024]{1,0:T(8,128)}, f32[256,1024]{1,0:T(8,128)}, u32[]{:S(2)}, u32[]{:S(2)}) collective-permute-start(f32[256,1024]{1,0:T(8,128)} %param.8), channel_id=1, source_target_pairs={{0,16},{16,0},{2,18},{18,2},{4,20},{20,4},{6,22},{22,6},{8,24},{24... | collective-permute-start | bytes 3145736 | tf_op jit(solution)/shard_map/ppermute | solution.py:62
  19.4 16.2 %copy-start.3 = (f32[256,1024]{1,0:T(8,128)S(1)}, f32[256,1024]{1,0:T(8,128)}, u32[]{:S(2)}) copy-start(f32[256,1024]{1,0:T(8,128)} %param.8) | copy-start | bytes 3145732
  30.4 28.8 %copy-start.1 = (f32[4,32,1024]{2,1,0:T(8,128)}, f32[4,32,1024]{2,1,0:T(8,128)S(1)}, u32[]{:S(2)}) copy-start(f32[4,32,1024]{2,1,0:T(8,128)S(1)} %all_to_all.49) | copy-start | bytes 1572868
  30.4 9.7 %collective-permute-start.6 = (f32[128,1024]{1,0:T(8,128)S(1)}, f32[128,1024]{1,0:T(8,128)S(1)}, u32[]{:S(2)}, u32[]{:S(2)}) collective-permute-start(f32[128,1024]{1,0:T(8,128)S(1)} %bitcast.34), channel_id=1, source_target_pairs={{0,32},{16,144},{2,34},{18,146},{4,36},{20,148},{6,38},{22,150},{8... | collective-permute-start | bytes 1572872 | tf_op jit(solution)/shard_map/ppermute | solution.py:62
  31.7 9.8 %collective-permute-start.1 = (f32[256,1000]{0,1:T(8,128)}, f32[256,1000]{0,1:T(8,128)S(1)}, u32[]{:S(2)}, u32[]{:S(2)}) collective-permute-start(f32[256,1000]{0,1:T(8,128)} %param.9), channel_id=1, source_target_pairs={{0,16},{16,0},{2,18},{18,2},{4,20},{20,4},{6,22},{22,6},{8,24},{24... | collective-permute-start | bytes 3072008 | tf_op jit(solution)/shard_map/ppermute | solution.py:62
  35.7 10.7 %collective-permute-start.4 = (f32[128,1024]{1,0:T(8,128)S(1)}, f32[128,1024]{1,0:T(8,128)S(1)}, u32[]{:S(2)}, u32[]{:S(2)}) collective-permute-start(f32[128,1024]{1,0:T(8,128)S(1)} %bitcast.35), channel_id=1, source_target_pairs={{0,96},{16,145},{2,98},{18,147},{4,100},{20,149},{6,102},{22,151},... | collective-permute-start | bytes 1572872 | tf_op jit(solution)/shard_map/ppermute | solution.py:62
  36.7 17.9 %collective-permute-start.2 = (f32[128,1024]{1,0:T(8,128)S(1)}, f32[128,1024]{1,0:T(8,128)S(1)}, u32[]{:S(2)}, u32[]{:S(2)}) collective-permute-start(f32[128,1024]{1,0:T(8,128)S(1)} %bitcast.36), channel_id=1, source_target_pairs={{0,64},{16,17},{2,66},{18,19},{4,68},{20,21},{6,70},{22,23},{8,72}... | collective-permute-start | bytes 1572872 | tf_op jit(solution)/shard_map/ppermute | solution.py:62
  41.5 14.5 %copy-start.10 = (f32[256,1000]{0,1:T(8,128)}, f32[256,1000]{0,1:T(8,128)S(1)}, u32[]{:S(2)}) copy-start(f32[256,1000]{0,1:T(8,128)S(1)} %collective-permute-done.1) | copy-start | bytes 3072004
  45.0 16.8 %collective-permute-start.7 = (f32[128,1024]{1,0:T(8,128)}, f32[128,1024]{1,0:T(8,128)}, u32[]{:S(2)}, u32[]{:S(2)}) collective-permute-start(f32[128,1024]{1,0:T(8,128)} %fusion.24), channel_id=1, source_target_pairs={{0,96},{16,145},{2,98},{18,147},{4,100},{20,149},{6,102},{22,151},... | collective-permute-start | bytes 1572872 | tf_op jit(solution)/shard_map/ppermute | solution.py:62
  47.8 11.5 %copy-start.4 = (f32[128,512]{1,0:T(8,128)}, f32[128,512]{1,0:T(8,128)S(1)}, u32[]{:S(2)}) copy-start(f32[128,512]{1,0:T(8,128)S(1)} %multiply_exponential_fusion.1) | copy-start | bytes 786436
  51.0 10.8 %collective-permute-start.5 = (f32[128,1024]{1,0:T(8,128)}, f32[128,1024]{1,0:T(8,128)}, u32[]{:S(2)}, u32[]{:S(2)}) collective-permute-start(f32[128,1024]{1,0:T(8,128)} %fusion.22), channel_id=1, source_target_pairs={{0,32},{16,144},{2,34},{18,146},{4,36},{20,148},{6,38},{22,150},{8... | collective-permute-start | bytes 1572872 | tf_op jit(solution)/shard_map/ppermute | solution.py:62
  56.0 3.3 %copy-start.6 = (f32[128,512]{1,0:T(8,128)}, f32[128,512]{1,0:T(8,128)S(1)}, u32[]{:S(2)}) copy-start(f32[128,512]{1,0:T(8,128)S(1)} %multiply_exponential_fusion.2) | copy-start | bytes 786436
  59.2 10.1 %collective-permute-start.3 = (f32[128,1024]{1,0:T(8,128)}, f32[128,1024]{1,0:T(8,128)}, u32[]{:S(2)}, u32[]{:S(2)}) collective-permute-start(f32[128,1024]{1,0:T(8,128)} %fusion.23), channel_id=1, source_target_pairs={{0,64},{16,17},{2,66},{18,19},{4,68},{20,21},{6,70},{22,23},{8,72}... | collective-permute-start | bytes 1572872 | tf_op jit(solution)/shard_map/ppermute | solution.py:62
  59.4 9.9 %copy-start.11 = (f32[256,1000]{0,1:T(8,128)S(1)}, f32[256,1000]{0,1:T(8,128)}, u32[]{:S(2)}) copy-start(f32[256,1000]{0,1:T(8,128)} %copy-done.10) | copy-start | bytes 3072004
  61.8 10.3 %copy-start.8 = (f32[128,512]{1,0:T(8,128)}, f32[128,512]{1,0:T(8,128)S(1)}, u32[]{:S(2)}) copy-start(f32[128,512]{1,0:T(8,128)S(1)} %multiply_exponential_fusion.3) | copy-start | bytes 786436
  72.1 14.3 %copy-start.9 = (f32[256,1000]{0,1:T(8,128)S(1)}, f32[256,1000]{0,1:T(8,128)}, u32[]{:S(2)}) copy-start(f32[256,1000]{0,1:T(8,128)} %param.7) | copy-start | bytes 3072004
  82.8 11.5 %all-to-all-start.3 = ((f32[8,4,1024]{2,1,0:T(4,128)}), f32[8,4,1024]{2,1,0:T(4,128)S(1)}, u32[]{:S(2)}, u32[]{:S(2)}) async-start(f32[8,4,1024]{2,1,0:T(4,128)} %all_to_all.37), calls=%async_computation.3 | async-start | bytes 262144 | tf_op jit(solution)/shard_map/all_to_all | solution.py:66
  105.6 10.4 %all-to-all-start.5 = ((f32[4,32,1024]{2,1,0:T(8,128)}), f32[4,32,1024]{2,1,0:T(8,128)S(1)}, u32[]{:S(2)}, u32[]{:S(2)}) async-start(f32[4,32,1024]{2,1,0:T(8,128)} %broadcast_in_dim.20), calls=%async_computation.5 | async-start | bytes 1048576 | tf_op jit(solution)/shard_map/all_to_all | solution.py:66
  116.0 17.7 %collective-permute-start.10 = (f32[128,1024]{1,0:T(8,128)S(1)}, f32[128,1024]{1,0:T(8,128)S(1)}, u32[]{:S(2)}, u32[]{:S(2)}) collective-permute-start(f32[128,1024]{1,0:T(8,128)S(1)} %bitcast.28), channel_id=1, source_target_pairs={{0,32},{16,144},{2,34},{18,146},{4,36},{20,148},{6,38},{22,150},{8... | collective-permute-start | bytes 1572872 | tf_op jit(solution)/shard_map/ppermute | solution.py:62
  116.1 18.2 %collective-permute-start.9 = (f32[128,1024]{1,0:T(8,128)S(1)}, f32[128,1024]{1,0:T(8,128)S(1)}, u32[]{:S(2)}, u32[]{:S(2)}) collective-permute-start(f32[128,1024]{1,0:T(8,128)S(1)} %bitcast.29), channel_id=1, source_target_pairs={{0,96},{16,145},{2,98},{18,147},{4,100},{20,149},{6,102},{22,151},... | collective-permute-start | bytes 1572872 | tf_op jit(solution)/shard_map/ppermute | solution.py:62
  118.7 16.3 %collective-permute-start.8 = (f32[128,1024]{1,0:T(8,128)S(1)}, f32[128,1024]{1,0:T(8,128)S(1)}, u32[]{:S(2)}, u32[]{:S(2)}) collective-permute-start(f32[128,1024]{1,0:T(8,128)S(1)} %bitcast.30), channel_id=1, source_target_pairs={{0,64},{16,17},{2,66},{18,19},{4,68},{20,21},{6,70},{22,23},{8,72}... | collective-permute-start | bytes 1572872 | tf_op jit(solution)/shard_map/ppermute | solution.py:62
  120.6 13.8 %copy-start.5 = (f32[128,512]{1,0:T(8,128)S(1)}, f32[128,512]{1,0:T(8,128)}, u32[]{:S(2)}) copy-start(f32[128,512]{1,0:T(8,128)} %copy-done.4) | copy-start | bytes 786436
  123.1 11.9 %copy-start.7 = (f32[128,512]{1,0:T(8,128)S(1)}, f32[128,512]{1,0:T(8,128)}, u32[]{:S(2)}) copy-start(f32[128,512]{1,0:T(8,128)} %copy-done.6) | copy-start | bytes 786436
  136.8 12.1 %collective-permute-start.11 = (f32[1000,256]{1,0:T(8,128)}, f32[1000,256]{1,0:T(8,128)}, u32[]{:S(2)}, u32[]{:S(2)}) collective-permute-start(f32[1000,256]{1,0:T(8,128)} %slice_add_fusion), channel_id=1, source_target_pairs={{0,16},{16,0},{2,18},{18,2},{4,20},{20,4},{6,22},{22,6},{8,24},{24... | collective-permute-start | bytes 3072008 | tf_op jit(solution)/shard_map/ppermute | solution.py:62
  144.3 3.9 %collective-permute-start.12 = (f32[32,1000]{1,0:T(8,128)S(1)}, f32[32,1000]{1,0:T(8,128)S(1)}, u32[]{:S(2)}, u32[]{:S(2)}) collective-permute-start(f32[32,1000]{1,0:T(8,128)S(1)} %bitcast.38), channel_id=1, source_target_pairs={{0,16},{16,0},{2,18},{18,2},{4,20},{20,4},{6,22},{22,6},{8,24},{24... | collective-permute-start | bytes 384008 | tf_op jit(solution)/shard_map/ppermute | solution.py:62
  145.0 3.9 %copy-start.2 = (f32[1024,256]{1,0:T(8,128)S(1)}, f32[1024,256]{1,0:T(8,128)}, u32[]{:S(2)}) copy-start(f32[1024,256]{1,0:T(8,128)} %fusion.20) | copy-start | bytes 3145732

commit v4 on v3

--- a/solution.py
+++ b/solution.py
@@ -44,16 +44,13 @@
 
 
 SWAP = [(position(x, y, z, core), position(x, y, z, 1 - core)) for x, y, z, core in everywhere()]
-COLUMNS = [
-    [position(x, y, z, core) for z in range(LEVELS)]
-    for x in range(RING)
-    for y in range(RING)
-    for core in range(2)
-]
-RINGS = [
-    [position(i, k, z, 0) if core == 0 else position(k, i, z, 1) for k in range(RING)]
+SHEETS = [
+    [
+        position(i, k, z, 0) if core == 0 else position(k, i, z, 1)
+        for k in range(RING)
+        for z in range(LEVELS)
+    ]
     for i in range(RING)
-    for z in range(LEVELS)
     for core in range(2)
 ]
 
@@ -118,36 +115,38 @@
 
     pair_centers = jnp.concatenate([centers, permute(centers, SWAP)], axis=0)
     pair_weights = jnp.pad(jnp.concatenate([weights, permute(weights, SWAP)], axis=0), fill)
+    pair_centers, pair_weights = lax.optimization_barrier((pair_centers, pair_weights))
     center_sq = jnp.sum(pair_centers * pair_centers, axis=1)
 
-    rows_of = quarters(spread(spread(rows, COLUMNS), RINGS))
-    kernel_of = {}
-    for offset, part in rows_of.items():
+    def kernel_of(part):
         row_sq = jnp.sum(part * part, axis=1)
         inner = dot(part, pair_centers, ((1,), (1,)))
-        kernel_of[offset] = jnp.exp(
+        kernel = jnp.exp(
             (2.0 * features - row_sq[:, None] - center_sq[None, :] + 2.0 * inner) / 128.0
         )
-    value = dot(kernel_of[0], pair_weights, ((1,), (0,)))
-    for offset in ORDER:
+        return lax.optimization_barrier(kernel)
+
+    rows_of = quarters(spread(rows, SHEETS))
+    kernels = {0: kernel_of(rows_of[0])}
+    value = dot(kernels[0], pair_weights, ((1,), (0,)))
+    later = [rows_of[offset] for offset in ORDER]
+    *later, value = lax.optimization_barrier((*later, value))
+    for offset, part in zip(ORDER, later):
+        kernels[offset] = kernel_of(part)
         value = value + permute(
-            dot(kernel_of[offset], pair_weights, ((1,), (0,))), bulk_shift(offset)
+            dot(kernels[offset], pair_weights, ((1,), (0,))), bulk_shift(offset)
         )
-    value = scatter_sum(scatter_sum(value, RINGS), COLUMNS)
-    resid_of = quarters(spread(spread(value * scale - targets, COLUMNS), RINGS))
+    value = scatter_sum(value, SHEETS)
+    resid_of = quarters(spread(value * scale - targets, SHEETS))
+    resid_all = jnp.concatenate([resid_of[offset] for offset in range(RING)], axis=0)
+    kernel_all = jnp.concatenate([kernels[offset] for offset in range(RING)], axis=0)
+    resid_all, kernel_all = lax.optimization_barrier((resid_all, kernel_all))
 
-    def delta_of(low, high):
-        return sum(
-            dot(resid_of[offset], kernel_of[offset][:, low:high], ((0,), (0,)))
-            for offset in (0,) + ORDER
-        )[:outputs]
-
-    received = permute(delta_of(here, 2 * here), SWAP)
-    delta = delta_of(0, here)
+    received = permute(dot(resid_all, kernel_all[:, here:], ((0,), (0,)))[:outputs], SWAP)
+    delta = dot(resid_all, kernel_all[:, :here], ((0,), (0,)))[:outputs]
     new_weights = weights - step_size / batch * (delta + received).T
 
     quarter = RING * LEVELS * own
-    resid_all = jnp.concatenate([resid_of[offset] for offset in range(RING)], axis=0)
     pieces = []
     for low in range(2):
         for column in range(RING):

time: 153 us -> 149 us (0.974)
  blocking collectives: 45.3 us -> 19.1 us
  waiting for transfers between devices: 32.5 us -> 47.4 us
  starting transfers between devices: 33.2 us -> 42.7 us
  matrix products: 28.2 us -> 21.4 us
  local copies, waits for them, and re-layouts: 4.85 us -> 8.85 us
  other arithmetic: 6.48 us -> 8.36 us
    all_to_all x4 -> x1, blocking collectives: 45.3 us -> 19.1 us  [exchange(): lax.all_to_all(array, AXES, 0, 0, axis_index_groups=groups, tiled=True)]
    all_to_all x2, starting transfers between devices: 7.06 us -> 19.1 us  [exchange(): lax.all_to_all(array, AXES, 0, 0, axis_index_groups=groups, tiled=True)]
    ppermute x13, waiting for transfers between devices: 18.9 us -> 27.5 us  [permute(): return lax.ppermute(array, AXES, pairs)]
    dot_general x16 -> x10, matrix products: 28.2 us -> 21.4 us  [dot(): lax.dot_general(left, right, (contract, ((), ())), precision=lax.Precisio...]
    all_to_all x2, waiting for transfers between devices: 13.7 us -> 19.8 us  [exchange(): lax.all_to_all(array, AXES, 0, 0, axis_index_groups=groups, tiled=True)]
    sub x6 -> x5, other arithmetic: 2.91 us -> 0.03 us  [the longest x4 0.02 us: kernel_of(): 2.0 * features - row_sq[:, None] - center_sq[None, :] + 2.0 * inner]
    ppermute x13, starting transfers between devices: 26.1 us -> 23.6 us  [permute(): return lax.ppermute(array, AXES, pairs)]
    unnamed x26 -> x21, local copies, waits for them, and re-layouts: 0.46 us -> 2.96 us
  transfers between devices with their start and end apart: 15 -> 15, of which waited for: 5 -> 8; matrix products, arithmetic and copies ran while one was open for 20% -> 9% of each run, Pallas kernels for 0% -> 0%
where the time goes in v4:
time: 149 us
  waiting for transfers between devices  47.4 us (32%)
  starting transfers between devices  42.7 us (29%)
  matrix products  21.4 us (14%)
  blocking collectives  19.1 us (13%)
  local copies, waits for them, and re-layouts  8.85 us (6%)
  other arithmetic  8.36 us (6%)
    ppermute x13, waiting for transfers between devices, permute(): return lax.ppermute(array, AXES, pairs)  27.5 us
    ppermute x13, starting transfers between devices, permute(): return lax.ppermute(array, AXES, pairs)  23.6 us
    dot_general x10, matrix products, dot(): lax.dot_general(left, right, (contract, ((), ())), precision=lax.Precisio...  21.4 us
    all_to_all x2, waiting for transfers between devices, exchange(): lax.all_to_all(array, AXES, 0, 0, axis_index_groups=groups, tiled=True)  19.8 us
    all_to_all x2, starting transfers between devices, exchange(): lax.all_to_all(array, AXES, 0, 0, axis_index_groups=groups, tiled=True)  19.1 us
    all_to_all x1, blocking collectives, exchange(): lax.all_to_all(array, AXES, 0, 0, axis_index_groups=groups, tiled=True)  19.1 us
  transfers between devices with their start and end apart: 15, of which 8 were waited for; matrix products, arithmetic and copies ran while one was open for 9% of the time, Pallas kernels for 0%

profile of v4, /device:TPU:1, one launch (start us, length us, event | category | flops | bytes accessed | tf_op | source)
XLA Modules:
  0.0 148.7 jit_solution(8684848170932807741)
XLA Ops:
  3.4 11.9 %all-to-all-start = ((f32[32,4,1024]{2,1,0:T(4,128)}), f32[32,4,1024]{2,1,0:T(4,128)S(1)}, u32[]{:S(2)}, u32[]{:S(2)}) async-start(f32[32,4,1024]{2,1,0:T(4,128)} %broadcast_in_dim.7), calls=%async_computation | async-start | bytes 1048576 | tf_op jit(solution)/shard_map/all_to_all | solution.py:63
  16.5 12.4 %all-to-all-done = f32[32,4,1024]{2,1,0:T(4,128)S(1)} async-done(((f32[32,4,1024]{2,1,0:T(4,128)}), f32[32,4,1024]{2,1,0:T(4,128)S(1)}, u32[]{:S(2)}, u32[]{:S(2)}) %all-to-all-start) | async-done | bytes 524320 | tf_op jit(solution)/shard_map/all_to_all | solution.py:63
  29.9 3.3 %collective-permute-start = (f32[128,1024]{1,0:T(8,128)}, f32[128,1024]{1,0:T(8,128)}, u32[]{:S(2)}, u32[]{:S(2)}) collective-permute-start(f32[128,1024]{1,0:T(8,128)} %all_to_all.19), channel_id=1, source_target_pairs={{0,64},{16,17},{2,66},{18,19},{4,68},{20,21},{6,70},{22,23},{8,72}... | collective-permute-start | bytes 1572872 | tf_op jit(solution)/shard_map/ppermute | solution.py:59
  35.2 1.9 %select_maximum_fusion = f32[512,1024]{0,1:T(8,128)S(1)} fusion(f32[256,1000]{0,1:T(8,128)} %collective-permute-done.4, f32[256,1000]{0,1:T(8,128)} %param.9), kind=kLoop, calls=%fused_computation.2 | loop fusion | flops 2097152 | bytes 4145152 | tf_op jit(solution)/shard_map/concatenate | solution.py:117
  37.5 2.3 %fusion.21 = f32[128,512]{1,0:T(8,128)S(1)} fusion(f32[128,1024]{1,0:T(8,128)} %all_to_all.19, f32[512,1024]{1,0:T(8,128)S(1)} %pad_maximum_fusion, f32[512]{0:T(512)S(1)} %multiply_reduce_fusion, f32[128]{0:T(128)S(1)} %sub.116), kind=kOutput, calls=%fused_computation.24 | convolution fusion | flops 402915328 | bytes 2886144 | tf_op jit(solution)/shard_map/dot_general | solution.py:88
  41.0 5.8 %collective-permute-done.1 = f32[128,1024]{1,0:T(8,128)} collective-permute-done((f32[128,1024]{1,0:T(8,128)}, f32[128,1024]{1,0:T(8,128)}, u32[]{:S(2)}, u32[]{:S(2)}) %collective-permute-start.1) | collective-permute-done | bytes 524320 | tf_op jit(solution)/shard_map/ppermute | solution.py:59
  48.0 2.3 %fusion.23 = f32[128,512]{1,0:T(8,128)S(1)} fusion(f32[128,1024]{1,0:T(8,128)} %collective-permute-done, f32[512,1024]{1,0:T(8,128)S(1)} %pad_maximum_fusion, f32[128]{0:T(128)S(1)} %broadcast_subtract_fusion.3, f32[512]{0:T(512)S(1)} %multiply_reduce_fusion), kind=kOutput, calls=%fused_computation.26 | convolution fusion | flops 402915328 | bytes 2886144 | tf_op jit(solution)/shard_map/dot_general | solution.py:88
  50.3 1.4 multiply_reduce_fusion.1
  51.8 2.3 %fusion.25 = f32[128,512]{1,0:T(8,128)S(1)} fusion(f32[128,1024]{1,0:T(8,128)} %collective-permute-done.1, f32[512,1024]{1,0:T(8,128)S(1)} %pad_maximum_fusion, f32[128]{0:T(128)S(1)} %broadcast_subtract_fusion.2, f32[512]{0:T(512)S(1)} %multiply_reduce_fusion), kind=kOutput, calls=%fused_computation.28 | convolution fusion | flops 402915328 | bytes 2886144 | tf_op jit(solution)/shard_map/dot_general | solution.py:88
  54.1 2.4 %fusion.27 = f32[128,512]{1,0:T(8,128)S(1)} fusion(f32[128,1024]{1,0:T(8,128)} %collective-permute-done.2, f32[512,1024]{1,0:T(8,128)S(1)} %pad_maximum_fusion, f32[128]{0:T(128)S(1)} %broadcast_subtract_fusion.1, f32[512]{0:T(512)S(1)} %multiply_reduce_fusion), kind=kOutput, calls=%fused_computation.30 | convolution fusion | flops 402915328 | bytes 2886144 | tf_op jit(solution)/shard_map/dot_general | solution.py:88
  56.5 1.2 fusion.32
  57.7 2.4 %collective-permute-start.5 = (f32[128,1024]{1,0:T(8,128)S(1)}, f32[128,1024]{1,0:T(8,128)S(1)}, u32[]{:S(2)}, u32[]{:S(2)}) collective-permute-start(f32[128,1024]{1,0:T(8,128)S(1)} %fusion.32), channel_id=1, source_target_pairs={{0,64},{16,17},{2,66},{18,19},{4,68},{20,21},{6,70},{22,23},{8,72}... | collective-permute-start | bytes 1572872 | tf_op jit(solution)/shard_map/ppermute | solution.py:59
  60.1 1.2 fusion.33
  62.3 1.2 fusion.34
  63.5 1.9 %collective-permute-start.7 = (f32[128,1024]{1,0:T(8,128)S(1)}, f32[128,1024]{1,0:T(8,128)S(1)}, u32[]{:S(2)}, u32[]{:S(2)}) collective-permute-start(f32[128,1024]{1,0:T(8,128)S(1)} %fusion.34), channel_id=1, source_target_pairs={{0,96},{16,145},{2,98},{18,147},{4,100},{20,149},{6,102},{22,151},... | collective-permute-start | bytes 1572872 | tf_op jit(solution)/shard_map/ppermute | solution.py:59
  65.4 2.5 %collective-permute-done.5 = f32[128,1024]{1,0:T(8,128)S(1)} collective-permute-done((f32[128,1024]{1,0:T(8,128)S(1)}, f32[128,1024]{1,0:T(8,128)S(1)}, u32[]{:S(2)}, u32[]{:S(2)}) %collective-permute-start.5) | collective-permute-done | bytes 524320 | tf_op jit(solution)/shard_map/ppermute | solution.py:59
  67.9 5.6 %collective-permute-done.6 = f32[128,1024]{1,0:T(8,128)S(1)} collective-permute-done((f32[128,1024]{1,0:T(8,128)S(1)}, f32[128,1024]{1,0:T(8,128)S(1)}, u32[]{:S(2)}, u32[]{:S(2)}) %collective-permute-start.6) | collective-permute-done | bytes 524320 | tf_op jit(solution)/shard_map/ppermute | solution.py:59
  74.6 7.3 %all-to-all-start.1 = ((f32[32,4,1024]{2,1,0:T(4,128)}), f32[32,4,1024]{2,1,0:T(4,128)S(1)}, u32[]{:S(2)}, u32[]{:S(2)}) async-start(f32[32,4,1024]{2,1,0:T(4,128)} %all_to_all.20), calls=%async_computation.1 | async-start | bytes 1048576 | tf_op jit(solution)/shard_map/all_to_all | solution.py:63
  81.8 2.5 %copy.18 = f32[256,1000]{1,0:T(8,128)} copy(f32[256,1000]{0,1:T(8,128)} %param.7) | data formatting | bytes 2048000 | tf_op args[2]
  84.4 1.9 %gather_fusion.1 = f32[4,1000]{1,0:T(4,128)S(1)} fusion(f32[256,1000]{1,0:T(8,128)} %copy.18, s32[1024]{0:T(1024)S(1)} %pad_clamp_fusion), kind=kCustom, calls=%fused_computation.1 | custom fusion | bytes 32016 | tf_op jit(solution)/shard_map/gather | solution.py:84
  86.2 7.4 %all-to-all-done.1 = f32[32,4,1024]{2,1,0:T(4,128)S(1)} async-done(((f32[32,4,1024]{2,1,0:T(4,128)}), f32[32,4,1024]{2,1,0:T(4,128)S(1)}, u32[]{:S(2)}, u32[]{:S(2)}) %all-to-all-start.1) | async-done | bytes 524320 | tf_op jit(solution)/shard_map/all_to_all | solution.py:63
  93.9 19.1 %all_to_all.27 = f32[32,4,1024]{2,1,0:T(4,128)S(1)} all-to-all(f32[32,4,1024]{2,1,0:T(4,128)S(1)} %broadcast_in_dim.8), channel_id=1, replica_groups={{0,2,4,6,8,10,12,14,128,130,132,134,136,138,140,142,1,3,5,7,9,11,13,15,..., dimensions={0} | all-to-all | bytes 1048576 | tf_op jit(solution)/shard_map/all_to_all | solution.py:63
  113.2 1.2 collective-permute-start.10
  114.4 1.5 %collective-permute-start.8 = (f32[128,1024]{1,0:T(8,128)S(1)}, f32[128,1024]{1,0:T(8,128)S(1)}, u32[]{:S(2)}, u32[]{:S(2)}) collective-permute-start(f32[128,1024]{1,0:T(8,128)S(1)} %all_to_all.23), channel_id=1, source_target_pairs={{0,96},{16,145},{2,98},{18,147},{4,100},{20,149},{6,102},{22,151},... | collective-permute-start | bytes 1572872 | tf_op jit(solution)/shard_map/ppermute | solution.py:59
  115.9 1.4 collective-permute-start.9
  117.4 5.7 %collective-permute-done.10 = f32[128,1024]{1,0:T(8,128)S(1)} collective-permute-done((f32[128,1024]{1,0:T(8,128)S(1)}, f32[128,1024]{1,0:T(8,128)S(1)}, u32[]{:S(2)}, u32[]{:S(2)}) %collective-permute-start.10) | collective-permute-done | bytes 524320 | tf_op jit(solution)/shard_map/ppermute | solution.py:59
  123.1 5.8 %collective-permute-done.9 = f32[128,1024]{1,0:T(8,128)S(1)} collective-permute-done((f32[128,1024]{1,0:T(8,128)S(1)}, f32[128,1024]{1,0:T(8,128)S(1)}, u32[]{:S(2)}, u32[]{:S(2)}) %collective-permute-start.9) | collective-permute-done | bytes 524320 | tf_op jit(solution)/shard_map/ppermute | solution.py:59
  128.9 1.3 pad_maximum_fusion.1
  130.2 2.8 %fusion = f32[1000,256]{1,0:T(8,128)} fusion(f32[512,1024]{1,0:T(8,128)S(1)} %pad_maximum_fusion.1, f32[512,512]{1,0:T(8,128)S(1)} %pad_maximum_fusion.2), kind=kOutput, calls=%fused_computation.7 | convolution fusion | flops 786432000 | bytes 3645440 | tf_op jit(solution)/shard_map/dot_general | solution.py:88
  133.0 8.1 %collective-permute-start.11 = (f32[1000,256]{1,0:T(8,128)}, f32[1000,256]{1,0:T(8,128)}, u32[]{:S(2)}, u32[]{:S(2)}) collective-permute-start(f32[1000,256]{1,0:T(8,128)} %fusion), channel_id=1, source_target_pairs={{0,16},{16,0},{2,18},{18,2},{4,20},{20,4},{6,22},{22,6},{8,24},{24... | collective-permute-start | bytes 3072008 | tf_op jit(solution)/shard_map/ppermute | solution.py:59
  141.3 2.2 %collective-permute-done.12 = f32[32,1000]{1,0:T(8,128)S(1)} collective-permute-done((f32[32,1000]{1,0:T(8,128)S(1)}, f32[32,1000]{1,0:T(8,128)S(1)}, u32[]{:S(2)}, u32[]{:S(2)}) %collective-permute-start.12) | collective-permute-done | bytes 128032 | tf_op jit(solution)/shard_map/ppermute | solution.py:59
  144.2 4.5 %fusion.13 = f32[256,1000]{0,1:T(8,128)} fusion(f32[256,1000]{0,1:T(8,128)} %param.9, f32[1000,256]{1,0:T(8,128)} %collective-permute-done.11, f32[512,1024]{1,0:T(8,128)S(1)} %pad_maximum_fusion.1, f32[512,512]{1,0:T(8,128)} %copy-done.1), kind=kOutput, calls=%fused_computation.14 | convolution fusion | flops 787200000 | bytes 5693440 | tf_op jit(solution)/shard_map/dot_general | solution.py:88
  (59 shorter events, 13.2 us)
Async XLA Ops:
  0.6 1.2 copy-start
  3.4 25.6 %all-to-all-start = ((f32[32,4,1024]{2,1,0:T(4,128)}), f32[32,4,1024]{2,1,0:T(4,128)S(1)}, u32[]{:S(2)}, u32[]{:S(2)}) async-start(f32[32,4,1024]{2,1,0:T(4,128)} %broadcast_in_dim.7), calls=%async_computation | async-start | bytes 1048576 | tf_op jit(solution)/shard_map/all_to_all | solution.py:63
  15.2 20.0 %collective-permute-start.4 = (f32[256,1000]{0,1:T(8,128)}, f32[256,1000]{0,1:T(8,128)}, u32[]{:S(2)}, u32[]{:S(2)}) collective-permute-start(f32[256,1000]{0,1:T(8,128)} %param.9), channel_id=1, source_target_pairs={{0,16},{16,0},{2,18},{18,2},{4,20},{20,4},{6,22},{22,6},{8,24},{24... | collective-permute-start | bytes 3072008 | tf_op jit(solution)/shard_map/ppermute | solution.py:59
  16.4 20.6 %collective-permute-start.3 = (f32[256,1024]{1,0:T(8,128)}, f32[256,1024]{1,0:T(8,128)S(1)}, u32[]{:S(2)}, u32[]{:S(2)}) collective-permute-start(f32[256,1024]{1,0:T(8,128)} %param.8), channel_id=1, source_target_pairs={{0,16},{16,0},{2,18},{18,2},{4,20},{20,4},{6,22},{22,6},{8,24},{24... | collective-permute-start | bytes 3145736 | tf_op jit(solution)/shard_map/ppermute | solution.py:59
  29.9 11.1 %collective-permute-start = (f32[128,1024]{1,0:T(8,128)}, f32[128,1024]{1,0:T(8,128)}, u32[]{:S(2)}, u32[]{:S(2)}) collective-permute-start(f32[128,1024]{1,0:T(8,128)} %all_to_all.19), channel_id=1, source_target_pairs={{0,64},{16,17},{2,66},{18,19},{4,68},{20,21},{6,70},{22,23},{8,72}... | collective-permute-start | bytes 1572872 | tf_op jit(solution)/shard_map/ppermute | solution.py:59
  33.2 13.7 %collective-permute-start.1 = (f32[128,1024]{1,0:T(8,128)}, f32[128,1024]{1,0:T(8,128)}, u32[]{:S(2)}, u32[]{:S(2)}) collective-permute-start(f32[128,1024]{1,0:T(8,128)} %all_to_all.19), channel_id=1, source_target_pairs={{0,96},{16,145},{2,98},{18,147},{4,100},{20,149},{6,102},{22,151},... | collective-permute-start | bytes 1572872 | tf_op jit(solution)/shard_map/ppermute | solution.py:59
  33.8 13.0 %collective-permute-start.2 = (f32[128,1024]{1,0:T(8,128)}, f32[128,1024]{1,0:T(8,128)}, u32[]{:S(2)}, u32[]{:S(2)}) collective-permute-start(f32[128,1024]{1,0:T(8,128)} %all_to_all.19), channel_id=1, source_target_pairs={{0,32},{16,144},{2,34},{18,146},{4,36},{20,148},{6,38},{22,150},{8... | collective-permute-start | bytes 1572872 | tf_op jit(solution)/shard_map/ppermute | solution.py:59
  35.0 2.1 %copy-start.9 = (f32[256,1024]{1,0:T(8,128)S(1)}, f32[256,1024]{1,0:T(8,128)}, u32[]{:S(2)}) copy-start(f32[256,1024]{1,0:T(8,128)} %param.8) | copy-start | bytes 3145732
  50.3 6.2 %copy-start.2 = (f32[128,512]{1,0:T(8,128)}, f32[128,512]{1,0:T(8,128)S(1)}, u32[]{:S(2)}) copy-start(f32[128,512]{1,0:T(8,128)S(1)} %fusion.23) | copy-start | bytes 786436
  54.1 6.1 %copy-start.4 = (f32[128,512]{1,0:T(8,128)}, f32[128,512]{1,0:T(8,128)S(1)}, u32[]{:S(2)}) copy-start(f32[128,512]{1,0:T(8,128)S(1)} %fusion.25) | copy-start | bytes 786436
  56.5 5.7 %copy-start.6 = (f32[128,512]{1,0:T(8,128)}, f32[128,512]{1,0:T(8,128)S(1)}, u32[]{:S(2)}) copy-start(f32[128,512]{1,0:T(8,128)S(1)} %fusion.27) | copy-start | bytes 786436
  57.7 10.1 %collective-permute-start.5 = (f32[128,1024]{1,0:T(8,128)S(1)}, f32[128,1024]{1,0:T(8,128)S(1)}, u32[]{:S(2)}, u32[]{:S(2)}) collective-permute-start(f32[128,1024]{1,0:T(8,128)S(1)} %fusion.32), channel_id=1, source_target_pairs={{0,64},{16,17},{2,66},{18,19},{4,68},{20,21},{6,70},{22,23},{8,72}... | collective-permute-start | bytes 1572872 | tf_op jit(solution)/shard_map/ppermute | solution.py:59
  61.4 12.1 %collective-permute-start.6 = (f32[128,1024]{1,0:T(8,128)S(1)}, f32[128,1024]{1,0:T(8,128)S(1)}, u32[]{:S(2)}, u32[]{:S(2)}) collective-permute-start(f32[128,1024]{1,0:T(8,128)S(1)} %fusion.33), channel_id=1, source_target_pairs={{0,32},{16,144},{2,34},{18,146},{4,36},{20,148},{6,38},{22,150},{8... | collective-permute-start | bytes 1572872 | tf_op jit(solution)/shard_map/ppermute | solution.py:59
  63.5 10.0 %collective-permute-start.7 = (f32[128,1024]{1,0:T(8,128)S(1)}, f32[128,1024]{1,0:T(8,128)S(1)}, u32[]{:S(2)}, u32[]{:S(2)}) collective-permute-start(f32[128,1024]{1,0:T(8,128)S(1)} %fusion.34), channel_id=1, source_target_pairs={{0,96},{16,145},{2,98},{18,147},{4,100},{20,149},{6,102},{22,151},... | collective-permute-start | bytes 1572872 | tf_op jit(solution)/shard_map/ppermute | solution.py:59
  74.6 19.1 %all-to-all-start.1 = ((f32[32,4,1024]{2,1,0:T(4,128)}), f32[32,4,1024]{2,1,0:T(4,128)S(1)}, u32[]{:S(2)}, u32[]{:S(2)}) async-start(f32[32,4,1024]{2,1,0:T(4,128)} %all_to_all.20), calls=%async_computation.1 | async-start | bytes 1048576 | tf_op jit(solution)/shard_map/all_to_all | solution.py:63
  84.3 33.0 %copy-start.3 = (f32[128,512]{1,0:T(8,128)S(1)}, f32[128,512]{1,0:T(8,128)}, u32[]{:S(2)}) copy-start(f32[128,512]{1,0:T(8,128)} %copy-done.2) | copy-start | bytes 786436
  84.3 33.0 %copy-start.5 = (f32[128,512]{1,0:T(8,128)S(1)}, f32[128,512]{1,0:T(8,128)}, u32[]{:S(2)}) copy-start(f32[128,512]{1,0:T(8,128)} %copy-done.4) | copy-start | bytes 786436
  84.3 33.0 %copy-start.7 = (f32[128,512]{1,0:T(8,128)S(1)}, f32[128,512]{1,0:T(8,128)}, u32[]{:S(2)}) copy-start(f32[128,512]{1,0:T(8,128)} %copy-done.6) | copy-start | bytes 786436
  113.2 10.0 %copy-start.8 = (f32[128,1024]{1,0:T(8,128)}, f32[128,1024]{1,0:T(8,128)S(1)}, u32[]{:S(2)}) copy-start(f32[128,1024]{1,0:T(8,128)S(1)} %all_to_all.23) | copy-start | bytes 1572868
  113.2 9.9 %collective-permute-start.10 = (f32[128,1024]{1,0:T(8,128)S(1)}, f32[128,1024]{1,0:T(8,128)S(1)}, u32[]{:S(2)}, u32[]{:S(2)}) collective-permute-start(f32[128,1024]{1,0:T(8,128)S(1)} %all_to_all.23), channel_id=1, source_target_pairs={{0,32},{16,144},{2,34},{18,146},{4,36},{20,148},{6,38},{22,150},{8... | collective-permute-start | bytes 1572872 | tf_op jit(solution)/shard_map/ppermute | solution.py:59
  114.4 8.7 %collective-permute-start.8 = (f32[128,1024]{1,0:T(8,128)S(1)}, f32[128,1024]{1,0:T(8,128)S(1)}, u32[]{:S(2)}, u32[]{:S(2)}) collective-permute-start(f32[128,1024]{1,0:T(8,128)S(1)} %all_to_all.23), channel_id=1, source_target_pairs={{0,96},{16,145},{2,98},{18,147},{4,100},{20,149},{6,102},{22,151},... | collective-permute-start | bytes 1572872 | tf_op jit(solution)/shard_map/ppermute | solution.py:59
  115.9 13.0 %collective-permute-start.9 = (f32[128,1024]{1,0:T(8,128)S(1)}, f32[128,1024]{1,0:T(8,128)S(1)}, u32[]{:S(2)}, u32[]{:S(2)}) collective-permute-start(f32[128,1024]{1,0:T(8,128)S(1)} %all_to_all.23), channel_id=1, source_target_pairs={{0,64},{16,17},{2,66},{18,19},{4,68},{20,21},{6,70},{22,23},{8,72}... | collective-permute-start | bytes 1572872 | tf_op jit(solution)/shard_map/ppermute | solution.py:59
  117.4 12.8 %copy-start.1 = (f32[512,512]{1,0:T(8,128)}, f32[512,512]{1,0:T(8,128)S(1)}, u32[]{:S(2)}) copy-start(f32[512,512]{1,0:T(8,128)S(1)} %pad_maximum_fusion.2) | copy-start | bytes 3145732
  133.0 11.2 %collective-permute-start.11 = (f32[1000,256]{1,0:T(8,128)}, f32[1000,256]{1,0:T(8,128)}, u32[]{:S(2)}, u32[]{:S(2)}) collective-permute-start(f32[1000,256]{1,0:T(8,128)} %fusion), channel_id=1, source_target_pairs={{0,16},{16,0},{2,18},{18,2},{4,20},{20,4},{6,22},{22,6},{8,24},{24... | collective-permute-start | bytes 3072008 | tf_op jit(solution)/shard_map/ppermute | solution.py:59
  141.2 2.3 %collective-permute-start.12 = (f32[32,1000]{1,0:T(8,128)S(1)}, f32[32,1000]{1,0:T(8,128)S(1)}, u32[]{:S(2)}, u32[]{:S(2)}) collective-permute-start(f32[32,1000]{1,0:T(8,128)S(1)} %bitcast.21), channel_id=1, source_target_pairs={{0,16},{16,0},{2,18},{18,2},{4,20},{20,4},{6,22},{22,6},{8,24},{24... | collective-permute-start | bytes 384008 | tf_op jit(solution)/shard_map/ppermute | solution.py:59

commit v5 on v4

--- a/solution.py
+++ b/solution.py
@@ -3,6 +3,8 @@
 import jax
 import jax.numpy as jnp
 from jax import lax
+from jax.experimental import pallas as pl
+from jax.experimental.pallas import tpu as pltpu
 from jax.sharding import Mesh
 from jax.sharding import PartitionSpec as P
 
@@ -14,6 +16,8 @@
 LEVELS = 8
 LANE = 128
 ORDER = (2, 1, 3)
+
+VMEM_BYTES = 24 * 1024 * 1024
 
 step_size = 1.0
 
@@ -84,14 +88,57 @@
     return array.at[index].get(mode="promise_in_bounds")
 
 
-def dot(left, right, contract):
-    return lax.dot_general(
-        left,
-        right,
-        (contract, ((), ())),
-        precision=lax.Precision.HIGH,
-        preferred_element_type=jnp.float32,
-    )
+def parts(array):
+    high = array.astype(jnp.bfloat16)
+    return high, (array - high.astype(jnp.float32)).astype(jnp.bfloat16)
+
+
+def rounded_parts(array):
+    high = lax.reduce_precision(array, 8, 7)
+    return high.astype(jnp.bfloat16), (array - high).astype(jnp.bfloat16)
+
+
+def product(left, right, contract):
+    def one(a, b):
+        return lax.dot_general(
+            a, b, (contract, ((), ())), preferred_element_type=jnp.float32
+        )
+
+    return one(left[0], right[0]) + (one(left[0], right[1]) + one(left[1], right[0]))
+
+
+def quarter_kernel(
+    rows, centers_high, centers_low, center_sq, weights_high, weights_low, value, high, low
+):
+    features = rows.shape[1]
+    part = rows[...]
+    row_sq = jnp.sum(part * part, axis=1, keepdims=True)
+    inner = product(parts(part), (centers_high[...], centers_low[...]), ((1,), (0,)))
+    kernel = parts(jnp.exp((2.0 * features - row_sq - center_sq[...] + 2.0 * inner) / 128.0))
+    high[...], low[...] = kernel
+    value[...] = product(kernel, (weights_high[...], weights_low[...]), ((1,), (0,)))
+
+
+def first_delta_kernel(resid_0, resid_1, resid_2, resid_3, high, low, delta, out_high, out_low):
+    quarter = resid_0.shape[0]
+    for i, resid in enumerate((resid_0, resid_1, resid_2, resid_3)):
+        place = pl.ds(i * quarter, quarter)
+        out_high[place, :], out_low[place, :] = parts(resid[...])
+    found = product((high[...], low[...]), (out_high[...], out_low[...]), ((0,), (0,)))
+    delta[...] = found.T[: delta.shape[0]]
+
+
+def second_delta_kernel(resid_high, resid_low, high, low, delta):
+    found = product((high[...], low[...]), (resid_high[...], resid_low[...]), ((0,), (0,)))
+    delta[...] = found.T[: delta.shape[0]]
+
+
+def call(kernel, outs, *operands):
+    return pl.pallas_call(
+        kernel,
+        out_shape=[jax.ShapeDtypeStruct(shape, dtype) for shape, dtype in outs],
+        compiler_params=pltpu.CompilerParams(vmem_limit_bytes=VMEM_BYTES),
+    )(*operands)
 
 
 def per_device(batch_index, train_features, train_labels, centers, weights):
@@ -115,38 +162,67 @@
 
     pair_centers = jnp.concatenate([centers, permute(centers, SWAP)], axis=0)
     pair_weights = jnp.pad(jnp.concatenate([weights, permute(weights, SWAP)], axis=0), fill)
-    pair_centers, pair_weights = lax.optimization_barrier((pair_centers, pair_weights))
-    center_sq = jnp.sum(pair_centers * pair_centers, axis=1)
-
-    def kernel_of(part):
-        row_sq = jnp.sum(part * part, axis=1)
-        inner = dot(part, pair_centers, ((1,), (1,)))
-        kernel = jnp.exp(
-            (2.0 * features - row_sq[:, None] - center_sq[None, :] + 2.0 * inner) / 128.0
-        )
-        return lax.optimization_barrier(kernel)
+    held = lax.optimization_barrier(
+        (
+            *rounded_parts(pair_centers.T),
+            jnp.sum(pair_centers * pair_centers, axis=1)[None, :],
+            *rounded_parts(pair_weights),
+        )
+    )
+    quarter = RING * LEVELS * own
+    pair = 2 * here
+
+    def quarter_of(part):
+        return call(
+            quarter_kernel,
+            (
+                ((quarter, lanes), jnp.float32),
+                ((quarter, pair), jnp.bfloat16),
+                ((quarter, pair), jnp.bfloat16),
+            ),
+            part,
+            *held,
+        )
 
     rows_of = quarters(spread(rows, SHEETS))
-    kernels = {0: kernel_of(rows_of[0])}
-    value = dot(kernels[0], pair_weights, ((1,), (0,)))
+    done = {0: quarter_of(rows_of[0])}
+    value = done[0][0]
     later = [rows_of[offset] for offset in ORDER]
     *later, value = lax.optimization_barrier((*later, value))
     for offset, part in zip(ORDER, later):
-        kernels[offset] = kernel_of(part)
-        value = value + permute(
-            dot(kernels[offset], pair_weights, ((1,), (0,))), bulk_shift(offset)
-        )
+        done[offset] = quarter_of(part)
+        value = value + permute(done[offset][0], bulk_shift(offset))
+    high = jnp.concatenate([done[offset][1] for offset in range(RING)], axis=0)
+    low = jnp.concatenate([done[offset][2] for offset in range(RING)], axis=0)
     value = scatter_sum(value, SHEETS)
     resid_of = quarters(spread(value * scale - targets, SHEETS))
-    resid_all = jnp.concatenate([resid_of[offset] for offset in range(RING)], axis=0)
-    kernel_all = jnp.concatenate([kernels[offset] for offset in range(RING)], axis=0)
-    resid_all, kernel_all = lax.optimization_barrier((resid_all, kernel_all))
-
-    received = permute(dot(resid_all, kernel_all[:, here:], ((0,), (0,)))[:outputs], SWAP)
-    delta = dot(resid_all, kernel_all[:, :here], ((0,), (0,)))[:outputs]
-    new_weights = weights - step_size / batch * (delta + received).T
-
-    quarter = RING * LEVELS * own
+    resid_list = [resid_of[offset] for offset in range(RING)]
+
+    batch_rows = RING * quarter
+    first, resid_high, resid_low = call(
+        first_delta_kernel,
+        (
+            ((outputs, here), jnp.float32),
+            ((batch_rows, lanes), jnp.bfloat16),
+            ((batch_rows, lanes), jnp.bfloat16),
+        ),
+        *resid_list,
+        high[:, here:],
+        low[:, here:],
+    )
+    received = permute(first, SWAP)
+    (second,) = call(
+        second_delta_kernel,
+        (((outputs, here), jnp.float32),),
+        resid_high,
+        resid_low,
+        high[:, :here],
+        low[:, :here],
+    )
+    new_weights = (weights.T - step_size / batch * (second + received)).T
+
+    *resid_list, _ = lax.optimization_barrier((*resid_list, first))
+    resid_all = jnp.concatenate(resid_list, axis=0)
     pieces = []
     for low in range(2):
         for column in range(RING):

time: 149 us -> 146 us (0.980)
  matrix products: 21.4 us -> 0 us
  blocking collectives: 19.1 us -> 0 us
  local copies, waits for them, and re-layouts: 8.85 us -> 24.4 us
  waiting for transfers between devices: 47.4 us -> 58.8 us
  Pallas kernels: 0 us -> 8.04 us
  other arithmetic: 8.36 us -> 9.85 us
    dot_general x10 -> x0, matrix products: 21.4 us -> none  [dot(): lax.dot_general(left, right, (contract, ((), ())), precision=lax.Precisio...]
    all_to_all x1 -> x0, blocking collectives: 19.1 us -> none  [exchange(): lax.all_to_all(array, AXES, 0, 0, axis_index_groups=groups, tiled=True)]
    all_to_all x2 -> x3, waiting for transfers between devices: 19.8 us -> 35.5 us  [exchange(): lax.all_to_all(array, AXES, 0, 0, axis_index_groups=groups, tiled=True)]
    unnamed x21 -> x31, local copies, waits for them, and re-layouts: 2.96 us -> 12.7 us
    pallas_call x0 -> x6, Pallas kernels: none -> 8.04 us  [call(): pl.pallas_call(kernel, out_shape=[jax.ShapeDtypeStruct(shape, dtype) for...]
    all_to_all x2 -> x3, starting transfers between devices: 19.1 us -> 26 us  [exchange(): lax.all_to_all(array, AXES, 0, 0, axis_index_groups=groups, tiled=True)]
    ppermute x13, starting transfers between devices: 23.6 us -> 16.9 us  [permute(): return lax.ppermute(array, AXES, pairs)]
    ppermute x13, waiting for transfers between devices: 27.5 us -> 23.3 us  [permute(): return lax.ppermute(array, AXES, pairs)]
  transfers between devices with their start and end apart: 15 -> 16, of which waited for: 8 -> 8; matrix products, arithmetic and copies ran while one was open for 9% -> 14% of each run, Pallas kernels for 0% -> 3%
where the time goes in v5:
time: 146 us; the launch traced here: 145 us
  waiting for transfers between devices  58.8 us (40%)
  starting transfers between devices  43 us (29%)
  local copies, waits for them, and re-layouts  24.4 us (17%)
  other arithmetic  9.85 us (7%)
  Pallas kernels  8.04 us (6%)
    all_to_all x3, waiting for transfers between devices, exchange(): lax.all_to_all(array, AXES, 0, 0, axis_index_groups=groups, tiled=True)  35.5 us
    all_to_all x3, starting transfers between devices, exchange(): lax.all_to_all(array, AXES, 0, 0, axis_index_groups=groups, tiled=True)  26 us
    ppermute x13, waiting for transfers between devices, permute(): return lax.ppermute(array, AXES, pairs)  23.3 us
    ppermute x13, starting transfers between devices, permute(): return lax.ppermute(array, AXES, pairs)  16.9 us
    unnamed x31, local copies, waits for them, and re-layouts  12.7 us
    pallas_call x6, Pallas kernels, call(): pl.pallas_call(kernel, out_shape=[jax.ShapeDtypeStruct(shape, dtype) for...  8.04 us
    convert_element_type x2, other arithmetic, rounded_parts(): return (high.astype(jnp.bfloat16), (array - high).astype(jnp.bfloat16))  3.83 us
  transfers between devices with their start and end apart: 16, of which 8 were waited for; matrix products, arithmetic and copies ran while one was open for 14% of the time, Pallas kernels for 3%

profile of v5, /device:TPU:1, one launch (start us, length us, event | category | flops | bytes accessed | tf_op | source)
XLA Modules:
  0.0 145.0 jit_solution(17042816635767442832)
XLA Ops:
  3.4 11.9 %all-to-all-start = ((f32[32,4,1024]{2,1,0:T(4,128)}), f32[32,4,1024]{2,1,0:T(4,128)S(1)}, u32[]{:S(2)}, u32[]{:S(2)}) async-start(f32[32,4,1024]{2,1,0:T(4,128)} %broadcast_in_dim.9), calls=%async_computation | async-start | bytes 1048576 | tf_op jit(solution)/shard_map/all_to_all | solution.py:67
  15.2 1.2 collective-permute-start.4
  16.4 1.3 copy.13
  17.8 11.1 %all-to-all-done = f32[32,4,1024]{2,1,0:T(4,128)S(1)} async-done(((f32[32,4,1024]{2,1,0:T(4,128)}), f32[32,4,1024]{2,1,0:T(4,128)S(1)}, u32[]{:S(2)}, u32[]{:S(2)}) %all-to-all-start) | async-done | bytes 524320 | tf_op jit(solution)/shard_map/all_to_all | solution.py:67
  29.1 3.3 %collective-permute-start = (f32[128,1024]{1,0:T(8,128)S(1)}, f32[128,1024]{1,0:T(8,128)S(1)}, u32[]{:S(2)}, u32[]{:S(2)}) collective-permute-start(f32[128,1024]{1,0:T(8,128)S(1)} %all_to_all.17.rows), channel_id=1, source_target_pairs={{0,64},{16,17},{2,66},{18,19},{4,68},{20,21},{6,70},{22,23},{8,72}... | collective-permute-start | bytes 1572872 | tf_op jit(solution)/shard_map/ppermute | solution.py:63
  33.9 2.5 %copy.14 = f32[256,1000]{1,0:T(8,128)} copy(f32[256,1000]{0,1:T(8,128)} %param.9) | data formatting | bytes 2048000 | tf_op args[4]
  36.5 2.6 %copy.15 = f32[256,1000]{1,0:T(8,128)} copy(f32[256,1000]{0,1:T(8,128)} %collective-permute-done.4) | data formatting | bytes 2048000 | tf_op jit(solution)/shard_map/ppermute | solution.py:63
  39.0 2.0 %fusion.1 = (bf16[512,1024]{1,0:T(8,128)(2,1)S(1)}, bf16[512,1024]{1,0:T(8,128)(2,1)S(1)}) fusion(f32[256,1000]{1,0:T(8,128)} %copy.15, f32[256,1000]{1,0:T(8,128)} %copy.14), kind=kLoop, calls=%fused_computation.7 | loop fusion | flops 4194304 | bytes 4145152 | tf_op jit(solution)/shard_map/convert_element_type | solution.py:98
  41.0 1.8 %multiply_reduce_fusion = f32[512]{0:T(512)S(1)} fusion(f32[256,1024]{0,1:T(8,128)} %collective-permute-done.3, f32[256,1024]{0,1:T(8,128)} %copy.13), kind=kLoop, calls=%fused_computation.11 | loop fusion | flops 1572352 | bytes 2099200 | tf_op jit(solution)/shard_map/reduce_sum | solution.py:168
  42.8 1.9 %fusion = (bf16[1024,512]{1,0:T(8,128)(2,1)S(1)}, bf16[1024,512]{1,0:T(8,128)(2,1)S(1)}) fusion(f32[256,1024]{0,1:T(8,128)} %collective-permute-done.3, f32[256,1024]{0,1:T(8,128)} %copy.13), kind=kLoop, calls=%fused_computation.6 | loop fusion | flops 2621440 | bytes 4194304 | tf_op jit(solution)/shard_map/convert_element_type | solution.py:98
  44.6 1.2 shard_map.68
  45.8 1.2 shard_map.71
  47.0 2.4 %collective-permute-start.7 = (f32[128,1024]{1,0:T(8,128)S(1)}, f32[128,1024]{1,0:T(8,128)S(1)}, u32[]{:S(2)}, u32[]{:S(2)}) collective-permute-start(f32[128,1024]{1,0:T(8,128)S(1)} %get-tuple-element.42), channel_id=1, source_target_pairs={{0,96},{16,145},{2,98},{18,147},{4,100},{20,149},{6,102},{22,151},... | collective-permute-start | bytes 1572872 | tf_op jit(solution)/shard_map/ppermute | solution.py:63
  50.7 1.2 shard_map.69
  51.9 1.3 collective-permute-start.5
  53.2 2.4 %collective-permute-done.7 = f32[128,1024]{1,0:T(8,128)S(1)} collective-permute-done((f32[128,1024]{1,0:T(8,128)S(1)}, f32[128,1024]{1,0:T(8,128)S(1)}, u32[]{:S(2)}, u32[]{:S(2)}) %collective-permute-start.7) | collective-permute-done | bytes 524320 | tf_op jit(solution)/shard_map/ppermute | solution.py:63
  55.5 10.3 %collective-permute-done.6 = f32[128,1024]{1,0:T(8,128)S(1)} collective-permute-done((f32[128,1024]{1,0:T(8,128)S(1)}, f32[128,1024]{1,0:T(8,128)S(1)}, u32[]{:S(2)}, u32[]{:S(2)}) %collective-permute-start.6) | collective-permute-done | bytes 524320 | tf_op jit(solution)/shard_map/ppermute | solution.py:63
  67.0 7.6 %all-to-all-start.1 = ((f32[32,4,1024]{2,1,0:T(4,128)}), f32[32,4,1024]{2,1,0:T(4,128)S(1)}, u32[]{:S(2)}, u32[]{:S(2)}) async-start(f32[32,4,1024]{2,1,0:T(4,128)} %all_to_all.18), calls=%async_computation.1 | async-start | bytes 1048576 | tf_op jit(solution)/shard_map/all_to_all | solution.py:67
  74.5 2.5 %copy.16 = f32[256,1000]{1,0:T(8,128)} copy(f32[256,1000]{0,1:T(8,128)} %param.7) | data formatting | bytes 2048000 | tf_op args[2]
  77.1 1.8 %gather_fusion.1 = f32[4,1000]{1,0:T(4,128)S(1)} fusion(f32[256,1000]{1,0:T(8,128)} %copy.16, s32[1024]{0:T(1024)S(1)} %pad_clamp_fusion), kind=kCustom, calls=%fused_computation.1 | custom fusion | bytes 32016 | tf_op jit(solution)/shard_map/gather | solution.py:88
  78.9 11.0 %all-to-all-done.1 = f32[32,4,1024]{2,1,0:T(4,128)S(1)} async-done(((f32[32,4,1024]{2,1,0:T(4,128)}), f32[32,4,1024]{2,1,0:T(4,128)S(1)}, u32[]{:S(2)}, u32[]{:S(2)}) %all-to-all-start.1) | async-done | bytes 524320 | tf_op jit(solution)/shard_map/all_to_all | solution.py:67
  90.9 6.6 %all-to-all-start.2 = ((f32[32,4,1024]{2,1,0:T(4,128)}), f32[32,4,1024]{2,1,0:T(4,128)S(1)}, u32[]{:S(2)}, u32[]{:S(2)}) async-start(f32[32,4,1024]{2,1,0:T(4,128)} %broadcast_in_dim.22), calls=%async_computation.2 | async-start | bytes 1048576 | tf_op jit(solution)/shard_map/all_to_all | solution.py:67
  98.4 13.3 %all-to-all-done.2 = f32[32,4,1024]{2,1,0:T(4,128)S(1)} async-done(((f32[32,4,1024]{2,1,0:T(4,128)}), f32[32,4,1024]{2,1,0:T(4,128)S(1)}, u32[]{:S(2)}, u32[]{:S(2)}) %all-to-all-start.2) | async-done | bytes 524320 | tf_op jit(solution)/shard_map/all_to_all | solution.py:67
  112.1 1.4 collective-permute-start.10
  115.2 1.8 %fusion.3 = (bf16[512,256]{1,0:T(8,128)(2,1)}, bf16[512,256]{1,0:T(8,128)(2,1)S(1)}) fusion(bf16[512,512]{1,0:T(8,128)(2,1)} %constant_dynamic-update-slice_fusion.4), kind=kLoop, calls=%fused_computation.39 | loop fusion | bytes 1048576 | tf_op jit(solution)/shard_map/slice | solution.py:220
  116.9 3.4 %collective-permute-done.8.resid_1 = f32[128,1024]{1,0:T(8,128)S(1)} collective-permute-done((f32[128,1024]{1,0:T(8,128)S(1)}, f32[128,1024]{1,0:T(8,128)S(1)}, u32[]{:S(2)}, u32[]{:S(2)}) %collective-permute-start.8) | collective-permute-done | bytes 524320 | tf_op jit(solution)/shard_map/ppermute | solution.py:63
  120.3 1.6 %collective-permute-done.9.resid_2 = f32[128,1024]{1,0:T(8,128)S(1)} collective-permute-done((f32[128,1024]{1,0:T(8,128)S(1)}, f32[128,1024]{1,0:T(8,128)S(1)}, u32[]{:S(2)}, u32[]{:S(2)}) %collective-permute-start.9) | collective-permute-done | bytes 524320 | tf_op jit(solution)/shard_map/ppermute | solution.py:63
  121.9 5.6 %collective-permute-done.10.resid_3 = f32[128,1024]{1,0:T(8,128)S(1)} collective-permute-done((f32[128,1024]{1,0:T(8,128)S(1)}, f32[128,1024]{1,0:T(8,128)S(1)}, u32[]{:S(2)}, u32[]{:S(2)}) %collective-permute-start.10) | collective-permute-done | bytes 524320 | tf_op jit(solution)/shard_map/ppermute | solution.py:63
  127.5 2.2 %shard_map.72 = (f32[1000,256]{1,0:T(8,128)}, bf16[512,1024]{1,0:T(8,128)(2,1)S(1)}, bf16[512,1024]{1,0:T(8,128)(2,1)S(1)}) custom-call(f32[128,1024]{1,0:T(8,128)S(1)} %all_to_all.21.resid_0, f32[128,1024]{1,0:T(8,128)S(1)} %collective-permute-done.8.resid_1, f32[128,1024]{1,0:T(8,128)S(1)} %collective-permute-done.9.resid_2, ...), custom_call_target="tpu_custom_call" | custom-call | tf_op jit(solution)/shard_map/pallas_call | solution.py:137
  131.7 5.5 %collective-permute-start.11 = (f32[1000,256]{1,0:T(8,128)}, f32[1000,256]{1,0:T(8,128)}, u32[]{:S(2)}, u32[]{:S(2)}) collective-permute-start(f32[1000,256]{1,0:T(8,128)} %get-tuple-element.53), channel_id=1, source_target_pairs={{0,16},{16,0},{2,18},{18,2},{4,20},{20,4},{6,22},{22,6},{8,24},{24... | collective-permute-start | bytes 3072008 | tf_op jit(solution)/shard_map/ppermute | solution.py:63
  138.5 1.2 copy-done.4
  142.6 2.4 %fusion.2 = f32[256,1000]{0,1:T(8,128)} fusion(f32[256,1000]{0,1:T(8,128)S(1)} %copy-done.6, f32[1000,256]{1,0:T(8,128)S(1)} %shard_map.73, f32[1000,256]{1,0:T(8,128)} %collective-permute-done.11), kind=kLoop, calls=%fused_computation.13 | loop fusion | flops 768000 | bytes 4096000 | tf_op jit(solution)/shard_map/transpose | solution.py:222
  (62 shorter events, 16.7 us)
Async XLA Ops:
  0.6 1.2 copy-start
  0.6 15.8 %copy-start.7 = (f32[256,1024]{1,0:T(8,128)S(1)}, f32[256,1024]{1,0:T(8,128)}, u32[]{:S(2)}) copy-start(f32[256,1024]{1,0:T(8,128)} %param.8) | copy-start | bytes 3145732
  3.4 25.6 %all-to-all-start = ((f32[32,4,1024]{2,1,0:T(4,128)}), f32[32,4,1024]{2,1,0:T(4,128)S(1)}, u32[]{:S(2)}, u32[]{:S(2)}) async-start(f32[32,4,1024]{2,1,0:T(4,128)} %broadcast_in_dim.9), calls=%async_computation | async-start | bytes 1048576 | tf_op jit(solution)/shard_map/all_to_all | solution.py:67
  15.2 21.2 %collective-permute-start.4 = (f32[256,1000]{0,1:T(8,128)}, f32[256,1000]{0,1:T(8,128)}, u32[]{:S(2)}, u32[]{:S(2)}) collective-permute-start(f32[256,1000]{0,1:T(8,128)} %param.9), channel_id=1, source_target_pairs={{0,16},{16,0},{2,18},{18,2},{4,20},{20,4},{6,22},{22,6},{8,24},{24... | collective-permute-start | bytes 3072008 | tf_op jit(solution)/shard_map/ppermute | solution.py:63
  17.8 23.2 %collective-permute-start.3 = (f32[256,1024]{0,1:T(8,128)}, f32[256,1024]{0,1:T(8,128)}, u32[]{:S(2)}, u32[]{:S(2)}) collective-permute-start(f32[256,1024]{0,1:T(8,128)} %copy.13), channel_id=1, source_target_pairs={{0,16},{16,0},{2,18},{18,2},{4,20},{20,4},{6,22},{22,6},{8,24},{24... | collective-permute-start | bytes 3145736 | tf_op jit(solution)/shard_map/ppermute | solution.py:63
  29.1 16.7 %collective-permute-start = (f32[128,1024]{1,0:T(8,128)S(1)}, f32[128,1024]{1,0:T(8,128)S(1)}, u32[]{:S(2)}, u32[]{:S(2)}) collective-permute-start(f32[128,1024]{1,0:T(8,128)S(1)} %all_to_all.17.rows), channel_id=1, source_target_pairs={{0,64},{16,17},{2,66},{18,19},{4,68},{20,21},{6,70},{22,23},{8,72}... | collective-permute-start | bytes 1572872 | tf_op jit(solution)/shard_map/ppermute | solution.py:63
  32.5 13.4 %collective-permute-start.1 = (f32[128,1024]{1,0:T(8,128)S(1)}, f32[128,1024]{1,0:T(8,128)S(1)}, u32[]{:S(2)}, u32[]{:S(2)}) collective-permute-start(f32[128,1024]{1,0:T(8,128)S(1)} %all_to_all.17.rows), channel_id=1, source_target_pairs={{0,96},{16,145},{2,98},{18,147},{4,100},{20,149},{6,102},{22,151},... | collective-permute-start | bytes 1572872 | tf_op jit(solution)/shard_map/ppermute | solution.py:63
  33.1 12.7 %collective-permute-start.2 = (f32[128,1024]{1,0:T(8,128)S(1)}, f32[128,1024]{1,0:T(8,128)S(1)}, u32[]{:S(2)}, u32[]{:S(2)}) collective-permute-start(f32[128,1024]{1,0:T(8,128)S(1)} %all_to_all.17.rows), channel_id=1, source_target_pairs={{0,32},{16,144},{2,34},{18,146},{4,36},{20,148},{6,38},{22,150},{8... | collective-permute-start | bytes 1572872 | tf_op jit(solution)/shard_map/ppermute | solution.py:63
  47.0 8.5 %collective-permute-start.7 = (f32[128,1024]{1,0:T(8,128)S(1)}, f32[128,1024]{1,0:T(8,128)S(1)}, u32[]{:S(2)}, u32[]{:S(2)}) collective-permute-start(f32[128,1024]{1,0:T(8,128)S(1)} %get-tuple-element.42), channel_id=1, source_target_pairs={{0,96},{16,145},{2,98},{18,147},{4,100},{20,149},{6,102},{22,151},... | collective-permute-start | bytes 1572872 | tf_op jit(solution)/shard_map/ppermute | solution.py:63
  50.6 15.2 %collective-permute-start.6 = (f32[128,1024]{1,0:T(8,128)S(1)}, f32[128,1024]{1,0:T(8,128)S(1)}, u32[]{:S(2)}, u32[]{:S(2)}) collective-permute-start(f32[128,1024]{1,0:T(8,128)S(1)} %get-tuple-element.40), channel_id=1, source_target_pairs={{0,32},{16,144},{2,34},{18,146},{4,36},{20,148},{6,38},{22,150},{8... | collective-permute-start | bytes 1572872 | tf_op jit(solution)/shard_map/ppermute | solution.py:63
  51.9 14.0 %collective-permute-start.5 = (f32[128,1024]{1,0:T(8,128)S(1)}, f32[128,1024]{1,0:T(8,128)S(1)}, u32[]{:S(2)}, u32[]{:S(2)}) collective-permute-start(f32[128,1024]{1,0:T(8,128)S(1)} %get-tuple-element.38), channel_id=1, source_target_pairs={{0,64},{16,17},{2,66},{18,19},{4,68},{20,21},{6,70},{22,23},{8,72}... | collective-permute-start | bytes 1572872 | tf_op jit(solution)/shard_map/ppermute | solution.py:63
  67.0 23.0 %all-to-all-start.1 = ((f32[32,4,1024]{2,1,0:T(4,128)}), f32[32,4,1024]{2,1,0:T(4,128)S(1)}, u32[]{:S(2)}, u32[]{:S(2)}) async-start(f32[32,4,1024]{2,1,0:T(4,128)} %all_to_all.18), calls=%async_computation.1 | async-start | bytes 1048576 | tf_op jit(solution)/shard_map/all_to_all | solution.py:67
  90.9 20.8 %all-to-all-start.2 = ((f32[32,4,1024]{2,1,0:T(4,128)}), f32[32,4,1024]{2,1,0:T(4,128)S(1)}, u32[]{:S(2)}, u32[]{:S(2)}) async-start(f32[32,4,1024]{2,1,0:T(4,128)} %broadcast_in_dim.22), calls=%async_computation.2 | async-start | bytes 1048576 | tf_op jit(solution)/shard_map/all_to_all | solution.py:67
  97.6 0.8 copy-start.9
  98.4 13.5 %copy-start.8 = (bf16[512,512]{1,0:T(8,128)(2,1)}, bf16[512,512]{1,0:T(8,128)(2,1)S(1)}, u32[]{:S(2)}) copy-start(bf16[512,512]{1,0:T(8,128)(2,1)S(1)} %constant_dynamic-update-slice_fusion.5) | copy-start | bytes 1572868
  111.9 8.4 %collective-permute-start.8 = (f32[128,1024]{1,0:T(8,128)S(1)}, f32[128,1024]{1,0:T(8,128)S(1)}, u32[]{:S(2)}, u32[]{:S(2)}) collective-permute-start(f32[128,1024]{1,0:T(8,128)S(1)} %all_to_all.21.resid_0), channel_id=1, source_target_pairs={{0,96},{16,145},{2,98},{18,147},{4,100},{20,149},{6,102},{22,151},... | collective-permute-start | bytes 1572872 | tf_op jit(solution)/shard_map/ppermute | solution.py:63
  112.0 10.0 %collective-permute-start.9 = (f32[128,1024]{1,0:T(8,128)S(1)}, f32[128,1024]{1,0:T(8,128)S(1)}, u32[]{:S(2)}, u32[]{:S(2)}) collective-permute-start(f32[128,1024]{1,0:T(8,128)S(1)} %all_to_all.21.resid_0), channel_id=1, source_target_pairs={{0,64},{16,17},{2,66},{18,19},{4,68},{20,21},{6,70},{22,23},{8,72}... | collective-permute-start | bytes 1572872 | tf_op jit(solution)/shard_map/ppermute | solution.py:63
  112.1 15.4 %collective-permute-start.10 = (f32[128,1024]{1,0:T(8,128)S(1)}, f32[128,1024]{1,0:T(8,128)S(1)}, u32[]{:S(2)}, u32[]{:S(2)}) collective-permute-start(f32[128,1024]{1,0:T(8,128)S(1)} %all_to_all.21.resid_0), channel_id=1, source_target_pairs={{0,32},{16,144},{2,34},{18,146},{4,36},{20,148},{6,38},{22,150},{8... | collective-permute-start | bytes 1572872 | tf_op jit(solution)/shard_map/ppermute | solution.py:63
  129.7 1.0 copy-start.1
  130.7 1.0 copy-start.3
  131.7 10.9 %collective-permute-start.11 = (f32[1000,256]{1,0:T(8,128)}, f32[1000,256]{1,0:T(8,128)}, u32[]{:S(2)}, u32[]{:S(2)}) collective-permute-start(f32[1000,256]{1,0:T(8,128)} %get-tuple-element.53), channel_id=1, source_target_pairs={{0,16},{16,0},{2,18},{18,2},{4,20},{20,4},{6,22},{22,6},{8,24},{24... | collective-permute-start | bytes 3072008 | tf_op jit(solution)/shard_map/ppermute | solution.py:63
  137.3 1.2 copy-start.2
  137.6 4.3 %collective-permute-start.12 = (f32[32,1000]{1,0:T(8,128)S(1)}, f32[32,1000]{1,0:T(8,128)S(1)}, u32[]{:S(2)}, u32[]{:S(2)}) collective-permute-start(f32[32,1000]{1,0:T(8,128)S(1)} %bitcast.15), channel_id=1, source_target_pairs={{0,16},{16,0},{2,18},{18,2},{4,20},{20,4},{6,22},{22,6},{8,24},{24... | collective-permute-start | bytes 384008 | tf_op jit(solution)/shard_map/ppermute | solution.py:63
  138.5 1.2 copy-start.4
  139.8 0.9 copy-start.5
  140.7 1.9 %copy-start.6 = (f32[256,1000]{0,1:T(8,128)S(1)}, f32[256,1000]{0,1:T(8,128)}, u32[]{:S(2)}) copy-start(f32[256,1000]{0,1:T(8,128)} %param.9) | copy-start | bytes 3072004

commit v6 on v5

--- a/solution.py
+++ b/solution.py
@@ -47,14 +47,21 @@
     ]
 
 
+def ring_shift(offset):
+    return [
+        (
+            position(x, y, z, core),
+            position(x, y + offset, z, 0) if core == 0 else position(x + offset, y, z, 1),
+        )
+        for x, y, z, core in everywhere()
+    ]
+
+
 SWAP = [(position(x, y, z, core), position(x, y, z, 1 - core)) for x, y, z, core in everywhere()]
-SHEETS = [
-    [
-        position(i, k, z, 0) if core == 0 else position(k, i, z, 1)
-        for k in range(RING)
-        for z in range(LEVELS)
-    ]
-    for i in range(RING)
+COLUMNS = [
+    [position(x, y, z, core) for z in range(LEVELS)]
+    for x in range(RING)
+    for y in range(RING)
     for core in range(2)
 ]
 
@@ -78,10 +85,24 @@
     return exchange(array, groups).reshape((count, -1) + array.shape[1:]).sum(axis=0)
 
 
-def quarters(own):
-    received = {offset: permute(own, bulk_shift(-offset)) for offset in ORDER}
+def gathered(own, shift):
+    received = {offset: permute(own, shift(-offset)) for offset in ORDER}
     received[0] = own
     return received
+
+
+def quarters(column):
+    pieces = gathered(column, ring_shift)
+    quarter = jnp.concatenate([pieces[offset] for offset in range(RING)], axis=0)
+    return gathered(quarter, bulk_shift)
+
+
+def ring_sum(array):
+    pieces = jnp.split(array, RING, axis=0)
+    total = pieces[0]
+    for offset in ORDER:
+        total = total + permute(pieces[offset], ring_shift(offset))
+    return total
 
 
 def pick(array, index):
@@ -91,11 +112,6 @@
 def parts(array):
     high = array.astype(jnp.bfloat16)
     return high, (array - high.astype(jnp.float32)).astype(jnp.bfloat16)
-
-
-def rounded_parts(array):
-    high = lax.reduce_precision(array, 8, 7)
-    return high.astype(jnp.bfloat16), (array - high).astype(jnp.bfloat16)
 
 
 def product(left, right, contract):
@@ -105,6 +121,23 @@
         )
 
     return one(left[0], right[0]) + (one(left[0], right[1]) + one(left[1], right[0]))
+
+
+def prepare_kernel(
+    own_centers, other_centers, own_weights, other_weights, high, low, center_sq, value_high, value_low
+):
+    here = own_centers.shape[0]
+    outputs, lanes = own_weights.shape[0], value_high.shape[1]
+    for i, (centers, weights) in enumerate(
+        ((own_centers, own_weights), (other_centers, other_weights))
+    ):
+        place = pl.ds(i * here, here)
+        turned = centers[...].T
+        center_sq[:, place] = jnp.sum(turned * turned, axis=0, keepdims=True)
+        high[:, place], low[:, place] = parts(turned)
+        zeros = jnp.zeros((lanes - outputs, here), jnp.float32)
+        padded = jnp.concatenate([weights[...], zeros], axis=0)
+        value_high[place, :], value_low[place, :] = parts(padded.T)
 
 
 def quarter_kernel(
@@ -119,24 +152,20 @@
     value[...] = product(kernel, (weights_high[...], weights_low[...]), ((1,), (0,)))
 
 
-def first_delta_kernel(resid_0, resid_1, resid_2, resid_3, high, low, delta, out_high, out_low):
+def delta_kernel(resid_0, resid_1, resid_2, resid_3, high, low, delta, resid_high, resid_low):
     quarter = resid_0.shape[0]
     for i, resid in enumerate((resid_0, resid_1, resid_2, resid_3)):
         place = pl.ds(i * quarter, quarter)
-        out_high[place, :], out_low[place, :] = parts(resid[...])
-    found = product((high[...], low[...]), (out_high[...], out_low[...]), ((0,), (0,)))
-    delta[...] = found.T[: delta.shape[0]]
-
-
-def second_delta_kernel(resid_high, resid_low, high, low, delta):
+        resid_high[place, :], resid_low[place, :] = parts(resid[...])
     found = product((high[...], low[...]), (resid_high[...], resid_low[...]), ((0,), (0,)))
     delta[...] = found.T[: delta.shape[0]]
 
 
-def call(kernel, outs, *operands):
+def call(kernel, outs, *operands, scratch=()):
     return pl.pallas_call(
         kernel,
         out_shape=[jax.ShapeDtypeStruct(shape, dtype) for shape, dtype in outs],
+        scratch_shapes=[pltpu.VMEM(shape, dtype) for shape, dtype in scratch],
         compiler_params=pltpu.CompilerParams(vmem_limit_bytes=VMEM_BYTES),
     )(*operands)
 
@@ -160,17 +189,25 @@
     fill = ((0, 0), (0, lanes - outputs))
     targets = jnp.pad(pick(train_labels, index), fill)
 
-    pair_centers = jnp.concatenate([centers, permute(centers, SWAP)], axis=0)
-    pair_weights = jnp.pad(jnp.concatenate([weights, permute(weights, SWAP)], axis=0), fill)
-    held = lax.optimization_barrier(
-        (
-            *rounded_parts(pair_centers.T),
-            jnp.sum(pair_centers * pair_centers, axis=1)[None, :],
-            *rounded_parts(pair_weights),
-        )
+    column, centers, own_weights = lax.optimization_barrier(
+        (spread(rows, COLUMNS), centers, weights)
     )
     quarter = RING * LEVELS * own
     pair = 2 * here
+    held = call(
+        prepare_kernel,
+        (
+            ((features, pair), jnp.bfloat16),
+            ((features, pair), jnp.bfloat16),
+            ((1, pair), jnp.float32),
+            ((pair, lanes), jnp.bfloat16),
+            ((pair, lanes), jnp.bfloat16),
+        ),
+        centers,
+        permute(centers, SWAP),
+        own_weights.T,
+        permute(own_weights, SWAP).T,
+    )
 
     def quarter_of(part):
         return call(
@@ -184,7 +221,7 @@
             *held,
         )
 
-    rows_of = quarters(spread(rows, SHEETS))
+    rows_of = quarters(column)
     done = {0: quarter_of(rows_of[0])}
     value = done[0][0]
     later = [rows_of[offset] for offset in ORDER]
@@ -194,34 +231,26 @@
         value = value + permute(done[offset][0], bulk_shift(offset))
     high = jnp.concatenate([done[offset][1] for offset in range(RING)], axis=0)
     low = jnp.concatenate([done[offset][2] for offset in range(RING)], axis=0)
-    value = scatter_sum(value, SHEETS)
-    resid_of = quarters(spread(value * scale - targets, SHEETS))
+    value = scatter_sum(ring_sum(value), COLUMNS)
+    resid_of = quarters(spread(value * scale - targets, COLUMNS))
     resid_list = [resid_of[offset] for offset in range(RING)]
 
-    batch_rows = RING * quarter
-    first, resid_high, resid_low = call(
-        first_delta_kernel,
-        (
-            ((outputs, here), jnp.float32),
-            ((batch_rows, lanes), jnp.bfloat16),
-            ((batch_rows, lanes), jnp.bfloat16),
-        ),
-        *resid_list,
-        high[:, here:],
-        low[:, here:],
-    )
+    def delta_of(resid, low_end, high_end):
+        return call(
+            delta_kernel,
+            (((outputs, here), jnp.float32),),
+            *resid,
+            high[:, low_end:high_end],
+            low[:, low_end:high_end],
+            scratch=(((RING * quarter, lanes), jnp.bfloat16),) * 2,
+        )[0]
+
+    first = delta_of(resid_list, here, pair)
     received = permute(first, SWAP)
-    (second,) = call(
-        second_delta_kernel,
-        (((outputs, here), jnp.float32),),
-        resid_high,
-        resid_low,
-        high[:, :here],
-        low[:, :here],
-    )
+    *resid_list, first = lax.optimization_barrier((*resid_list, first))
+    second = delta_of(resid_list, 0, here)
     new_weights = (weights.T - step_size / batch * (second + received)).T
 
-    *resid_list, _ = lax.optimization_barrier((*resid_list, first))
     resid_all = jnp.concatenate(resid_list, axis=0)
     pieces = []
     for low in range(2):
@@ -229,7 +258,8 @@
             line = y_hi * 2 + low
             offset = jnp.where(core == 0, column - x, line - y) % RING
             slot = jnp.where(core == 0, line, column)
-            place = offset * quarter + (slot * LEVELS + z) * own
+            turn = (slot - jnp.where(core == 0, y, x)) % RING
+            place = offset * quarter + (turn * LEVELS + z) * own
             pieces.append(lax.dynamic_slice_in_dim(resid_all, place, own, 0))
     mine = jnp.concatenate(pieces, axis=0)[:, :outputs]
     theirs = permute(mine, SWAP)

time: 146 us -> 152 us (1.041)
  blocking collectives: 0 us -> 16.6 us
  other arithmetic: 9.85 us -> 4.2 us
  local copies, waits for them, and re-layouts: 24.4 us -> 20.2 us
    all_to_all x3 -> x2, waiting for transfers between devices: 35.5 us -> 13.7 us  [exchange(): lax.all_to_all(array, AXES, 0, 0, axis_index_groups=groups, tiled=True)]
    ppermute x13 -> x22, waiting for transfers between devices: 23.3 us -> 44.1 us  [permute(): return lax.ppermute(array, AXES, pairs)]
    all_to_all x3 -> x2, starting transfers between devices: 26 us -> 6.74 us  [exchange(): lax.all_to_all(array, AXES, 0, 0, axis_index_groups=groups, tiled=True)]
    ppermute x13 -> x22, starting transfers between devices: 16.9 us -> 35.3 us  [permute(): return lax.ppermute(array, AXES, pairs)]
    all_to_all x0 -> x1, blocking collectives: none -> 16.6 us  [exchange(): lax.all_to_all(array, AXES, 0, 0, axis_index_groups=groups, tiled=True)]
    unnamed x31 -> x29, local copies, waits for them, and re-layouts: 12.7 us -> 7.57 us
    convert_element_type x2 -> x0, other arithmetic: 3.83 us -> none  [rounded_parts(): return (high.astype(jnp.bfloat16), (array - high).astype(jnp.bfloat16))]
    concatenate x1, local copies, waits for them, and re-layouts: 0.11 us -> 3 us  [per_device(): mine = jnp.concatenate(pieces, axis=0)[:, :outputs]]
  transfers between devices with their start and end apart: 16 -> 24, of which waited for: 8 -> 16; matrix products, arithmetic and copies ran while one was open for 14% -> 10% of each run, Pallas kernels for 3% -> 4%
where the time goes in v6:
time: 152 us; the launch traced here: 151 us
  waiting for transfers between devices  57.7 us (38%)
  starting transfers between devices  42 us (28%)
  local copies, waits for them, and re-layouts  20.2 us (13%)
  blocking collectives  16.6 us (11%)
  Pallas kernels  9.04 us (6%)
  other arithmetic  4.2 us (3%)
    ppermute x22, waiting for transfers between devices, permute(): return lax.ppermute(array, AXES, pairs)  44.1 us
    ppermute x22, starting transfers between devices, permute(): return lax.ppermute(array, AXES, pairs)  35.3 us
    all_to_all x1, blocking collectives, exchange(): lax.all_to_all(array, AXES, 0, 0, axis_index_groups=groups, tiled=True)  16.6 us
    all_to_all x2, waiting for transfers between devices, exchange(): lax.all_to_all(array, AXES, 0, 0, axis_index_groups=groups, tiled=True)  13.7 us
    pallas_call x7, Pallas kernels, call(): pl.pallas_call(kernel, out_shape=[jax.ShapeDtypeStruct(shape, dtype) for...  9.04 us
    unnamed x29, local copies, waits for them, and re-layouts  7.57 us
    all_to_all x2, starting transfers between devices, exchange(): lax.all_to_all(array, AXES, 0, 0, axis_index_groups=groups, tiled=True)  6.74 us
  transfers between devices with their start and end apart: 24, of which 16 were waited for; matrix products, arithmetic and copies ran while one was open for 10% of the time, Pallas kernels for 4%

profile of v6, /device:TPU:1, one launch (start us, length us, event | category | flops | bytes accessed | tf_op | source)
XLA Modules:
  0.0 150.7 jit_solution(17189408666753915535)
XLA Ops:
  2.7 16.6 %all_to_all.27 = f32[8,4,1024]{2,1,0:T(4,128)S(1)} all-to-all(f32[8,4,1024]{2,1,0:T(4,128)S(1)} %broadcast_in_dim.7), channel_id=1, replica_groups={{0,2,4,6,8,10,12,14},{16,18,20,22,24,26,28,30},{128,130,132,134,136,138..., dimensions={0} | all-to-all | bytes 262144 | tf_op jit(solution)/shard_map/all_to_all | solution.py:74
  19.4 2.4 %collective-permute-start.6 = (f32[256,1024]{1,0:T(8,128)}, f32[256,1024]{1,0:T(8,128)S(1)}, u32[]{:S(2)}, u32[]{:S(2)}) collective-permute-start(f32[256,1024]{1,0:T(8,128)} %own_centers), channel_id=1, source_target_pairs={{0,16},{16,0},{2,18},{18,2},{4,20},{20,4},{6,22},{22,6},{8,24},{24... | collective-permute-start | bytes 3145736 | tf_op jit(solution)/shard_map/ppermute | solution.py:70
  21.8 2.5 %collective-permute-start = (f32[32,1024]{1,0:T(8,128)S(1)}, f32[32,1024]{1,0:T(8,128)S(1)}, u32[]{:S(2)}, u32[]{:S(2)}) collective-permute-start(f32[32,1024]{1,0:T(8,128)S(1)} %all_to_all.19), channel_id=1, source_target_pairs={{0,129},{16,112},{2,131},{18,114},{4,133},{20,116},{6,135},{22,118... | collective-permute-start | bytes 393224 | tf_op jit(solution)/shard_map/ppermute | solution.py:70
  25.5 2.1 %collective-permute-done = f32[32,1024]{1,0:T(8,128)S(1)} collective-permute-done((f32[32,1024]{1,0:T(8,128)S(1)}, f32[32,1024]{1,0:T(8,128)S(1)}, u32[]{:S(2)}, u32[]{:S(2)}) %collective-permute-start) | collective-permute-done | bytes 131104 | tf_op jit(solution)/shard_map/ppermute | solution.py:70
  27.7 2.3 %collective-permute-done.1 = f32[32,1024]{1,0:T(8,128)S(1)} collective-permute-done((f32[32,1024]{1,0:T(8,128)S(1)}, f32[32,1024]{1,0:T(8,128)S(1)}, u32[]{:S(2)}, u32[]{:S(2)}) %collective-permute-start.1) | collective-permute-done | bytes 131104 | tf_op jit(solution)/shard_map/ppermute | solution.py:70
  30.0 1.4 collective-permute-done.2
  31.4 2.7 %collective-permute-start.3 = (f32[128,1024]{1,0:T(8,128)S(1)}, f32[128,1024]{1,0:T(8,128)S(1)}, u32[]{:S(2)}, u32[]{:S(2)}) collective-permute-start(f32[128,1024]{1,0:T(8,128)S(1)} %constant_dynamic-update-slice_fusion.rows), channel_id=1, source_target_pairs={{0,64},{16,17},{2,66},{18,19},{4,68},{20,21},{6,70},{22,23},{8,72}... | collective-permute-start | bytes 1572872 | tf_op jit(solution)/shard_map/ppermute | solution.py:70
  36.8 1.2 shard_map.68
  39.2 2.1 %collective-permute-done.3.rows = f32[128,1024]{1,0:T(8,128)S(1)} collective-permute-done((f32[128,1024]{1,0:T(8,128)S(1)}, f32[128,1024]{1,0:T(8,128)S(1)}, u32[]{:S(2)}, u32[]{:S(2)}) %collective-permute-start.3) | collective-permute-done | bytes 524320 | tf_op jit(solution)/shard_map/ppermute | solution.py:70
  41.3 5.7 %collective-permute-done.4.rows = f32[128,1024]{1,0:T(8,128)S(1)} collective-permute-done((f32[128,1024]{1,0:T(8,128)S(1)}, f32[128,1024]{1,0:T(8,128)S(1)}, u32[]{:S(2)}, u32[]{:S(2)}) %collective-permute-start.4) | collective-permute-done | bytes 524320 | tf_op jit(solution)/shard_map/ppermute | solution.py:70
  48.1 2.4 %collective-permute-start.10 = (f32[128,1024]{1,0:T(8,128)S(1)}, f32[128,1024]{1,0:T(8,128)S(1)}, u32[]{:S(2)}, u32[]{:S(2)}) collective-permute-start(f32[128,1024]{1,0:T(8,128)S(1)} %get-tuple-element.45), channel_id=1, source_target_pairs={{0,96},{16,145},{2,98},{18,147},{4,100},{20,149},{6,102},{22,151},... | collective-permute-start | bytes 1572872 | tf_op jit(solution)/shard_map/ppermute | solution.py:70
  53.0 1.9 %collective-permute-start.8 = (f32[128,1024]{1,0:T(8,128)S(1)}, f32[128,1024]{1,0:T(8,128)S(1)}, u32[]{:S(2)}, u32[]{:S(2)}) collective-permute-start(f32[128,1024]{1,0:T(8,128)S(1)} %get-tuple-element.41), channel_id=1, source_target_pairs={{0,64},{16,17},{2,66},{18,19},{4,68},{20,21},{6,70},{22,23},{8,72}... | collective-permute-start | bytes 1572872 | tf_op jit(solution)/shard_map/ppermute | solution.py:70
  54.8 1.8 %collective-permute-done.10 = f32[128,1024]{1,0:T(8,128)S(1)} collective-permute-done((f32[128,1024]{1,0:T(8,128)S(1)}, f32[128,1024]{1,0:T(8,128)S(1)}, u32[]{:S(2)}, u32[]{:S(2)}) %collective-permute-start.10) | collective-permute-done | bytes 524320 | tf_op jit(solution)/shard_map/ppermute | solution.py:70
  56.7 10.3 %collective-permute-done.9 = f32[128,1024]{1,0:T(8,128)S(1)} collective-permute-done((f32[128,1024]{1,0:T(8,128)S(1)}, f32[128,1024]{1,0:T(8,128)S(1)}, u32[]{:S(2)}, u32[]{:S(2)}) %collective-permute-start.9) | collective-permute-done | bytes 524320 | tf_op jit(solution)/shard_map/ppermute | solution.py:70
  69.7 2.5 %copy.7 = f32[256,1000]{1,0:T(8,128)} copy(f32[256,1000]{0,1:T(8,128)} %param.7) | data formatting | bytes 2048000 | tf_op args[2]
  72.2 1.9 %gather_fusion.1 = f32[4,1000]{1,0:T(4,128)S(1)} fusion(f32[256,1000]{1,0:T(8,128)} %copy.7, s32[1024]{0:T(1024)} %copy-done.6), kind=kCustom, calls=%fused_computation.1 | custom fusion | bytes 32016 | tf_op jit(solution)/shard_map/gather | solution.py:109
  75.8 3.4 %all-to-all-start.1 = ((f32[8,4,1024]{2,1,0:T(4,128)}), f32[8,4,1024]{2,1,0:T(4,128)S(1)}, u32[]{:S(2)}, u32[]{:S(2)}) async-start(f32[8,4,1024]{2,1,0:T(4,128)} %all_to_all.20), calls=%async_computation.1 | async-start | bytes 262144 | tf_op jit(solution)/shard_map/all_to_all | solution.py:74
  80.5 6.5 %all-to-all-done.1 = f32[8,4,1024]{2,1,0:T(4,128)S(1)} async-done(((f32[8,4,1024]{2,1,0:T(4,128)}), f32[8,4,1024]{2,1,0:T(4,128)S(1)}, u32[]{:S(2)}, u32[]{:S(2)}) %all-to-all-start.1) | async-done | bytes 131104 | tf_op jit(solution)/shard_map/all_to_all | solution.py:74
  87.7 3.4 %all-to-all-start.2 = ((f32[8,4,1024]{2,1,0:T(4,128)}), f32[8,4,1024]{2,1,0:T(4,128)S(1)}, u32[]{:S(2)}, u32[]{:S(2)}) async-start(f32[8,4,1024]{2,1,0:T(4,128)} %broadcast_in_dim.8), calls=%async_computation.2 | async-start | bytes 262144 | tf_op jit(solution)/shard_map/all_to_all | solution.py:74
  91.8 7.2 %all-to-all-done.2 = f32[8,4,1024]{2,1,0:T(4,128)S(1)} async-done(((f32[8,4,1024]{2,1,0:T(4,128)}), f32[8,4,1024]{2,1,0:T(4,128)S(1)}, u32[]{:S(2)}, u32[]{:S(2)}) %all-to-all-start.2) | async-done | bytes 131104 | tf_op jit(solution)/shard_map/all_to_all | solution.py:74
  99.0 1.8 %collective-permute-start.14 = (f32[32,1024]{1,0:T(8,128)S(1)}, f32[32,1024]{1,0:T(8,128)S(1)}, u32[]{:S(2)}, u32[]{:S(2)}) collective-permute-start(f32[32,1024]{1,0:T(8,128)S(1)} %all_to_all.23), channel_id=1, source_target_pairs={{0,129},{16,112},{2,131},{18,114},{4,133},{20,116},{6,135},{22,118... | collective-permute-start | bytes 393224 | tf_op jit(solution)/shard_map/ppermute | solution.py:70
  100.9 2.1 %collective-permute-start.15 = (f32[32,1024]{1,0:T(8,128)S(1)}, f32[32,1024]{1,0:T(8,128)S(1)}, u32[]{:S(2)}, u32[]{:S(2)}) collective-permute-start(f32[32,1024]{1,0:T(8,128)S(1)} %all_to_all.23), channel_id=1, source_target_pairs={{0,1},{16,80},{2,3},{18,82},{4,5},{20,84},{6,7},{22,86},{8,9},{24,... | collective-permute-start | bytes 393224 | tf_op jit(solution)/shard_map/ppermute | solution.py:70
  103.8 2.5 %collective-permute-done.15 = f32[32,1024]{1,0:T(8,128)S(1)} collective-permute-done((f32[32,1024]{1,0:T(8,128)S(1)}, f32[32,1024]{1,0:T(8,128)S(1)}, u32[]{:S(2)}, u32[]{:S(2)}) %collective-permute-start.15) | collective-permute-done | bytes 131104 | tf_op jit(solution)/shard_map/ppermute | solution.py:70
  106.3 1.8 %collective-permute-done.16 = f32[32,1024]{1,0:T(8,128)S(1)} collective-permute-done((f32[32,1024]{1,0:T(8,128)S(1)}, f32[32,1024]{1,0:T(8,128)S(1)}, u32[]{:S(2)}, u32[]{:S(2)}) %collective-permute-start.16) | collective-permute-done | bytes 131104 | tf_op jit(solution)/shard_map/ppermute | solution.py:70
  111.4 1.8 %fusion.3 = (bf16[512,256]{1,0:T(8,128)(2,1)}, bf16[512,256]{1,0:T(8,128)(2,1)S(1)}) fusion(bf16[512,512]{1,0:T(8,128)(2,1)} %constant_dynamic-update-slice_fusion.12), kind=kLoop, calls=%fused_computation.40 | loop fusion | bytes 1048576 | tf_op jit(solution)/shard_map/slice | solution.py:244
  113.2 5.1 %collective-permute-done.17.resid_1 = f32[128,1024]{1,0:T(8,128)S(1)} collective-permute-done((f32[128,1024]{1,0:T(8,128)S(1)}, f32[128,1024]{1,0:T(8,128)S(1)}, u32[]{:S(2)}, u32[]{:S(2)}) %collective-permute-start.17) | collective-permute-done | bytes 524320 | tf_op jit(solution)/shard_map/ppermute | solution.py:70
  118.3 2.4 %collective-permute-done.18.resid_2 = f32[128,1024]{1,0:T(8,128)S(1)} collective-permute-done((f32[128,1024]{1,0:T(8,128)S(1)}, f32[128,1024]{1,0:T(8,128)S(1)}, u32[]{:S(2)}, u32[]{:S(2)}) %collective-permute-start.18) | collective-permute-done | bytes 524320 | tf_op jit(solution)/shard_map/ppermute | solution.py:70
  120.7 5.5 %collective-permute-done.19.resid_3 = f32[128,1024]{1,0:T(8,128)S(1)} collective-permute-done((f32[128,1024]{1,0:T(8,128)S(1)}, f32[128,1024]{1,0:T(8,128)S(1)}, u32[]{:S(2)}, u32[]{:S(2)}) %collective-permute-start.19) | collective-permute-done | bytes 524320 | tf_op jit(solution)/shard_map/ppermute | solution.py:70
  126.3 2.1 %shard_map.73 = f32[1000,256]{1,0:T(8,128)} custom-call(f32[128,1024]{1,0:T(8,128)S(1)} %constant_dynamic-update-slice_fusion.4.resid_0, f32[128,1024]{1,0:T(8,128)S(1)} %collective-permute-done.17.resid_1, f32[128,1024]{1,0:T(8,128)S(1)} %collective-permute-done.18.resid_2, f32[128,1024]{1,0:T(8,128)S(1)} %collective-permute-done.19.resid_3, ...), custom_call_target="tpu_custom_call" | custom-call | tf_op jit(solution)/shard_map/pallas_call | solution.py:165
  128.4 13.1 %collective-permute-start.20 = (f32[1000,256]{1,0:T(8,128)}, f32[1000,256]{1,0:T(8,128)}, u32[]{:S(2)}, u32[]{:S(2)}) collective-permute-start(f32[1000,256]{1,0:T(8,128)} %shard_map.73), channel_id=1, source_target_pairs={{0,16},{16,0},{2,18},{18,2},{4,20},{20,4},{6,22},{22,6},{8,24},{24... | collective-permute-start | bytes 3072008 | tf_op jit(solution)/shard_map/ppermute | solution.py:70
  142.3 3.0 %concatenate.29 = f32[32,1024]{1,0:T(8,128)S(1)} concatenate(f32[4,1024]{1,0:T(4,128)} %get-tuple-element.65, f32[4,1024]{1,0:T(4,128)} %get-tuple-element.64, f32[4,1024]{1,0:T(4,128)} %get-tuple-element.63, f32[4,1024]{1,0:T(4,128)} %get-tuple-element.62, f32[4,1024]{1,0:T(4,128)} %get-tuple-element.61, f32[4,1024]{1,0:T(4,128)} %get-tuple-element.60, ...), dimensions={0} | concatenate | bytes 262144 | tf_op jit(solution)/shard_map/concatenate | solution.py:264
  148.3 2.4 %fusion = f32[256,1000]{0,1:T(8,128)} fusion(f32[256,1000]{0,1:T(8,128)S(1)} %copy-done.2, f32[1000,256]{1,0:T(8,128)S(1)} %shard_map.74, f32[1000,256]{1,0:T(8,128)} %collective-permute-done.20), kind=kLoop, calls=%fused_computation.3 | loop fusion | flops 768000 | bytes 4096000 | tf_op jit(solution)/shard_map/transpose | solution.py:252
  (78 shorter events, 25.8 us)
Async XLA Ops:
  0.6 1.5 %copy-start = (f32[256,1024]{1,0:T(8,128)S(1)}, f32[256,1024]{1,0:T(8,128)}, u32[]{:S(2)}) copy-start(f32[256,1024]{1,0:T(8,128)} %param.6) | copy-start | bytes 3145732
  0.6 34.9 %copy-start.1 = (f32[256,1000]{0,1:T(8,128)S(1)}, f32[256,1000]{0,1:T(8,128)}, u32[]{:S(2)}) copy-start(f32[256,1000]{0,1:T(8,128)} %param.9) | copy-start | bytes 3072004
  1.6 0.6 copy-start.6
  19.4 16.2 %collective-permute-start.6 = (f32[256,1024]{1,0:T(8,128)}, f32[256,1024]{1,0:T(8,128)S(1)}, u32[]{:S(2)}, u32[]{:S(2)}) collective-permute-start(f32[256,1024]{1,0:T(8,128)} %own_centers), channel_id=1, source_target_pairs={{0,16},{16,0},{2,18},{18,2},{4,20},{20,4},{6,22},{22,6},{8,24},{24... | collective-permute-start | bytes 3145736 | tf_op jit(solution)/shard_map/ppermute | solution.py:70
  21.7 13.8 %collective-permute-start.7 = (f32[256,1000]{0,1:T(8,128)}, f32[256,1000]{0,1:T(8,128)S(1)}, u32[]{:S(2)}, u32[]{:S(2)}) collective-permute-start(f32[256,1000]{0,1:T(8,128)} %param.9), channel_id=1, source_target_pairs={{0,16},{16,0},{2,18},{18,2},{4,20},{20,4},{6,22},{22,6},{8,24},{24... | collective-permute-start | bytes 3072008 | tf_op jit(solution)/shard_map/ppermute | solution.py:70
  21.8 5.8 %collective-permute-start = (f32[32,1024]{1,0:T(8,128)S(1)}, f32[32,1024]{1,0:T(8,128)S(1)}, u32[]{:S(2)}, u32[]{:S(2)}) collective-permute-start(f32[32,1024]{1,0:T(8,128)S(1)} %all_to_all.19), channel_id=1, source_target_pairs={{0,129},{16,112},{2,131},{18,114},{4,133},{20,116},{6,135},{22,118... | collective-permute-start | bytes 393224 | tf_op jit(solution)/shard_map/ppermute | solution.py:70
  24.3 5.6 %collective-permute-start.1 = (f32[32,1024]{1,0:T(8,128)S(1)}, f32[32,1024]{1,0:T(8,128)S(1)}, u32[]{:S(2)}, u32[]{:S(2)}) collective-permute-start(f32[32,1024]{1,0:T(8,128)S(1)} %all_to_all.19), channel_id=1, source_target_pairs={{0,1},{16,80},{2,3},{18,82},{4,5},{20,84},{6,7},{22,86},{8,9},{24,... | collective-permute-start | bytes 393224 | tf_op jit(solution)/shard_map/ppermute | solution.py:70
  24.9 6.5 %collective-permute-start.2 = (f32[32,1024]{1,0:T(8,128)S(1)}, f32[32,1024]{1,0:T(8,128)S(1)}, u32[]{:S(2)}, u32[]{:S(2)}) collective-permute-start(f32[32,1024]{1,0:T(8,128)S(1)} %all_to_all.19), channel_id=1, source_target_pairs={{0,128},{16,48},{2,130},{18,50},{4,132},{20,52},{6,134},{22,54},{8... | collective-permute-start | bytes 393224 | tf_op jit(solution)/shard_map/ppermute | solution.py:70
  31.4 10.0 %collective-permute-start.3 = (f32[128,1024]{1,0:T(8,128)S(1)}, f32[128,1024]{1,0:T(8,128)S(1)}, u32[]{:S(2)}, u32[]{:S(2)}) collective-permute-start(f32[128,1024]{1,0:T(8,128)S(1)} %constant_dynamic-update-slice_fusion.rows), channel_id=1, source_target_pairs={{0,64},{16,17},{2,66},{18,19},{4,68},{20,21},{6,70},{22,23},{8,72}... | collective-permute-start | bytes 1572872 | tf_op jit(solution)/shard_map/ppermute | solution.py:70
  34.1 12.9 %collective-permute-start.4 = (f32[128,1024]{1,0:T(8,128)S(1)}, f32[128,1024]{1,0:T(8,128)S(1)}, u32[]{:S(2)}, u32[]{:S(2)}) collective-permute-start(f32[128,1024]{1,0:T(8,128)S(1)} %constant_dynamic-update-slice_fusion.rows), channel_id=1, source_target_pairs={{0,96},{16,145},{2,98},{18,147},{4,100},{20,149},{6,102},{22,151},... | collective-permute-start | bytes 1572872 | tf_op jit(solution)/shard_map/ppermute | solution.py:70
  34.8 12.1 %collective-permute-start.5 = (f32[128,1024]{1,0:T(8,128)S(1)}, f32[128,1024]{1,0:T(8,128)S(1)}, u32[]{:S(2)}, u32[]{:S(2)}) collective-permute-start(f32[128,1024]{1,0:T(8,128)S(1)} %constant_dynamic-update-slice_fusion.rows), channel_id=1, source_target_pairs={{0,32},{16,144},{2,34},{18,146},{4,36},{20,148},{6,38},{22,150},{8... | collective-permute-start | bytes 1572872 | tf_op jit(solution)/shard_map/ppermute | solution.py:70
  35.5 1.2 copy-start.4
  48.1 8.6 %collective-permute-start.10 = (f32[128,1024]{1,0:T(8,128)S(1)}, f32[128,1024]{1,0:T(8,128)S(1)}, u32[]{:S(2)}, u32[]{:S(2)}) collective-permute-start(f32[128,1024]{1,0:T(8,128)S(1)} %get-tuple-element.45), channel_id=1, source_target_pairs={{0,96},{16,145},{2,98},{18,147},{4,100},{20,149},{6,102},{22,151},... | collective-permute-start | bytes 1572872 | tf_op jit(solution)/shard_map/ppermute | solution.py:70
  51.7 15.2 %collective-permute-start.9 = (f32[128,1024]{1,0:T(8,128)S(1)}, f32[128,1024]{1,0:T(8,128)S(1)}, u32[]{:S(2)}, u32[]{:S(2)}) collective-permute-start(f32[128,1024]{1,0:T(8,128)S(1)} %get-tuple-element.43), channel_id=1, source_target_pairs={{0,32},{16,144},{2,34},{18,146},{4,36},{20,148},{6,38},{22,150},{8... | collective-permute-start | bytes 1572872 | tf_op jit(solution)/shard_map/ppermute | solution.py:70
  53.0 14.0 %collective-permute-start.8 = (f32[128,1024]{1,0:T(8,128)S(1)}, f32[128,1024]{1,0:T(8,128)S(1)}, u32[]{:S(2)}, u32[]{:S(2)}) collective-permute-start(f32[128,1024]{1,0:T(8,128)S(1)} %get-tuple-element.41), channel_id=1, source_target_pairs={{0,64},{16,17},{2,66},{18,19},{4,68},{20,21},{6,70},{22,23},{8,72}... | collective-permute-start | bytes 1572872 | tf_op jit(solution)/shard_map/ppermute | solution.py:70
  67.8 7.0 %collective-permute-start.13 = (f32[32,1024]{1,0:T(8,128)}, f32[32,1024]{1,0:T(8,128)S(1)}, u32[]{:S(2)}, u32[]{:S(2)}) collective-permute-start(f32[32,1024]{1,0:T(8,128)} %get-tuple-element.71), channel_id=1, source_target_pairs={{0,129},{16,112},{2,131},{18,114},{4,133},{20,116},{6,135},{22,118... | collective-permute-start | bytes 393224 | tf_op jit(solution)/shard_map/ppermute | solution.py:70
  68.4 6.6 %collective-permute-start.12 = (f32[32,1024]{1,0:T(8,128)}, f32[32,1024]{1,0:T(8,128)S(1)}, u32[]{:S(2)}, u32[]{:S(2)}) collective-permute-start(f32[32,1024]{1,0:T(8,128)} %get-tuple-element.72), channel_id=1, source_target_pairs={{0,128},{16,48},{2,130},{18,50},{4,132},{20,52},{6,134},{22,54},{8... | collective-permute-start | bytes 393224 | tf_op jit(solution)/shard_map/ppermute | solution.py:70
  69.3 5.8 %collective-permute-start.11 = (f32[32,1024]{1,0:T(8,128)}, f32[32,1024]{1,0:T(8,128)S(1)}, u32[]{:S(2)}, u32[]{:S(2)}) collective-permute-start(f32[32,1024]{1,0:T(8,128)} %get-tuple-element.70), channel_id=1, source_target_pairs={{0,1},{16,80},{2,3},{18,82},{4,5},{20,84},{6,7},{22,86},{8,9},{24,... | collective-permute-start | bytes 393224 | tf_op jit(solution)/shard_map/ppermute | solution.py:70
  75.8 11.2 %all-to-all-start.1 = ((f32[8,4,1024]{2,1,0:T(4,128)}), f32[8,4,1024]{2,1,0:T(4,128)S(1)}, u32[]{:S(2)}, u32[]{:S(2)}) async-start(f32[8,4,1024]{2,1,0:T(4,128)} %all_to_all.20), calls=%async_computation.1 | async-start | bytes 262144 | tf_op jit(solution)/shard_map/all_to_all | solution.py:74
  87.7 11.2 %all-to-all-start.2 = ((f32[8,4,1024]{2,1,0:T(4,128)}), f32[8,4,1024]{2,1,0:T(4,128)S(1)}, u32[]{:S(2)}, u32[]{:S(2)}) async-start(f32[8,4,1024]{2,1,0:T(4,128)} %broadcast_in_dim.8), calls=%async_computation.2 | async-start | bytes 262144 | tf_op jit(solution)/shard_map/all_to_all | solution.py:74
  99.0 4.7 %collective-permute-start.14 = (f32[32,1024]{1,0:T(8,128)S(1)}, f32[32,1024]{1,0:T(8,128)S(1)}, u32[]{:S(2)}, u32[]{:S(2)}) collective-permute-start(f32[32,1024]{1,0:T(8,128)S(1)} %all_to_all.23), channel_id=1, source_target_pairs={{0,129},{16,112},{2,131},{18,114},{4,133},{20,116},{6,135},{22,118... | collective-permute-start | bytes 393224 | tf_op jit(solution)/shard_map/ppermute | solution.py:70
  100.9 7.3 %copy-start.5 = (bf16[512,512]{1,0:T(8,128)(2,1)}, bf16[512,512]{1,0:T(8,128)(2,1)S(1)}, u32[]{:S(2)}) copy-start(bf16[512,512]{1,0:T(8,128)(2,1)S(1)} %constant_dynamic-update-slice_fusion.13) | copy-start | bytes 1572868
  100.9 5.4 %collective-permute-start.15 = (f32[32,1024]{1,0:T(8,128)S(1)}, f32[32,1024]{1,0:T(8,128)S(1)}, u32[]{:S(2)}, u32[]{:S(2)}) collective-permute-start(f32[32,1024]{1,0:T(8,128)S(1)} %all_to_all.23), channel_id=1, source_target_pairs={{0,1},{16,80},{2,3},{18,82},{4,5},{20,84},{6,7},{22,86},{8,9},{24,... | collective-permute-start | bytes 393224 | tf_op jit(solution)/shard_map/ppermute | solution.py:70
  103.0 5.1 %collective-permute-start.16 = (f32[32,1024]{1,0:T(8,128)S(1)}, f32[32,1024]{1,0:T(8,128)S(1)}, u32[]{:S(2)}, u32[]{:S(2)}) collective-permute-start(f32[32,1024]{1,0:T(8,128)S(1)} %all_to_all.23), channel_id=1, source_target_pairs={{0,128},{16,48},{2,130},{18,50},{4,132},{20,52},{6,134},{22,54},{8... | collective-permute-start | bytes 393224 | tf_op jit(solution)/shard_map/ppermute | solution.py:70
  108.1 10.2 %collective-permute-start.17 = (f32[128,1024]{1,0:T(8,128)S(1)}, f32[128,1024]{1,0:T(8,128)S(1)}, u32[]{:S(2)}, u32[]{:S(2)}) collective-permute-start(f32[128,1024]{1,0:T(8,128)S(1)} %constant_dynamic-update-slice_fusion.4.resid_0), channel_id=1, source_target_pairs={{0,96},{16,145},{2,98},{18,147},{4,100},{20,149},{6,102},{22,151},... | collective-permute-start | bytes 1572872 | tf_op jit(solution)/shard_map/ppermute | solution.py:70
  108.2 12.5 %collective-permute-start.18 = (f32[128,1024]{1,0:T(8,128)S(1)}, f32[128,1024]{1,0:T(8,128)S(1)}, u32[]{:S(2)}, u32[]{:S(2)}) collective-permute-start(f32[128,1024]{1,0:T(8,128)S(1)} %constant_dynamic-update-slice_fusion.4.resid_0), channel_id=1, source_target_pairs={{0,64},{16,17},{2,66},{18,19},{4,68},{20,21},{6,70},{22,23},{8,72}... | collective-permute-start | bytes 1572872 | tf_op jit(solution)/shard_map/ppermute | solution.py:70
  108.5 17.8 %collective-permute-start.19 = (f32[128,1024]{1,0:T(8,128)S(1)}, f32[128,1024]{1,0:T(8,128)S(1)}, u32[]{:S(2)}, u32[]{:S(2)}) collective-permute-start(f32[128,1024]{1,0:T(8,128)S(1)} %constant_dynamic-update-slice_fusion.4.resid_0), channel_id=1, source_target_pairs={{0,32},{16,144},{2,34},{18,146},{4,36},{20,148},{6,38},{22,150},{8... | collective-permute-start | bytes 1572872 | tf_op jit(solution)/shard_map/ppermute | solution.py:70
  128.4 19.9 %collective-permute-start.20 = (f32[1000,256]{1,0:T(8,128)}, f32[1000,256]{1,0:T(8,128)}, u32[]{:S(2)}, u32[]{:S(2)}) collective-permute-start(f32[1000,256]{1,0:T(8,128)} %shard_map.73), channel_id=1, source_target_pairs={{0,16},{16,0},{2,18},{18,2},{4,20},{20,4},{6,22},{22,6},{8,24},{24... | collective-permute-start | bytes 3072008 | tf_op jit(solution)/shard_map/ppermute | solution.py:70
  145.3 3.0 %copy-start.2 = (f32[256,1000]{0,1:T(8,128)S(1)}, f32[256,1000]{0,1:T(8,128)}, u32[]{:S(2)}) copy-start(f32[256,1000]{0,1:T(8,128)} %param.9) | copy-start | bytes 3072004
  145.3 2.3 %collective-permute-start.21 = (f32[32,1000]{1,0:T(8,128)S(1)}, f32[32,1000]{1,0:T(8,128)S(1)}, u32[]{:S(2)}, u32[]{:S(2)}) collective-permute-start(f32[32,1000]{1,0:T(8,128)S(1)} %bitcast.11), channel_id=1, source_target_pairs={{0,16},{16,0},{2,18},{18,2},{4,20},{20,4},{6,22},{22,6},{8,24},{24... | collective-permute-start | bytes 384008 | tf_op jit(solution)/shard_map/ppermute | solution.py:70
  145.4 1.0 copy-start.3

commit v7 on v6

--- a/solution.py
+++ b/solution.py
@@ -15,9 +15,9 @@
 RING = 4
 LEVELS = 8
 LANE = 128
-ORDER = (2, 1, 3)
-
-VMEM_BYTES = 24 * 1024 * 1024
+WAYS = (1, 2, 3)
+
+VMEM_BYTES = 16 * 1024 * 1024
 
 step_size = 1.0
 
@@ -37,31 +37,34 @@
     ]
 
 
-def bulk_shift(offset):
-    return [
-        (
-            position(x, y, z, core),
-            position(x + offset, y, z, 0) if core == 0 else position(x, y + offset, z, 1),
-        )
-        for x, y, z, core in everywhere()
+def beside(place, core):
+    return place + 1 if place % 2 == core else place - 1
+
+
+def neighbour(x, y, z, core, way):
+    if way == 1:
+        x = beside(x, core)
+    elif way == 2:
+        y = beside(y, core)
+    elif way == 3:
+        z = beside(z, core)
+    return position(x, y, z % LEVELS, core)
+
+
+def swap_pairs(way):
+    return [(position(*device), neighbour(*device, way)) for device in everywhere()]
+
+
+SWAP = [(position(x, y, z, core), position(x, y, z, 1 - core)) for x, y, z, core in everywhere()]
+CLASSES = [
+    [
+        position(2 * i + (low + z) % 2, 2 * k + (high + z) % 2, z, core)
+        for i in range(RING // 2)
+        for k in range(RING // 2)
+        for z in range(LEVELS)
     ]
-
-
-def ring_shift(offset):
-    return [
-        (
-            position(x, y, z, core),
-            position(x, y + offset, z, 0) if core == 0 else position(x + offset, y, z, 1),
-        )
-        for x, y, z, core in everywhere()
-    ]
-
-
-SWAP = [(position(x, y, z, core), position(x, y, z, 1 - core)) for x, y, z, core in everywhere()]
-COLUMNS = [
-    [position(x, y, z, core) for z in range(LEVELS)]
-    for x in range(RING)
-    for y in range(RING)
+    for low in range(2)
+    for high in range(2)
     for core in range(2)
 ]
 
@@ -85,24 +88,10 @@
     return exchange(array, groups).reshape((count, -1) + array.shape[1:]).sum(axis=0)
 
 
-def gathered(own, shift):
-    received = {offset: permute(own, shift(-offset)) for offset in ORDER}
+def quarters(own):
+    received = {way: permute(own, swap_pairs(way)) for way in WAYS}
     received[0] = own
     return received
-
-
-def quarters(column):
-    pieces = gathered(column, ring_shift)
-    quarter = jnp.concatenate([pieces[offset] for offset in range(RING)], axis=0)
-    return gathered(quarter, bulk_shift)
-
-
-def ring_sum(array):
-    pieces = jnp.split(array, RING, axis=0)
-    total = pieces[0]
-    for offset in ORDER:
-        total = total + permute(pieces[offset], ring_shift(offset))
-    return total
 
 
 def pick(array, index):
@@ -180,7 +169,6 @@
     scale = 1.0 / math.sqrt(here * devices)
     x, core, z = lax.axis_index("x"), lax.axis_index("core"), lax.axis_index("z")
     y_lo, y_hi = lax.axis_index("y_lo"), lax.axis_index("y_hi")
-    y = y_hi * 2 + y_lo
     own = block // (2 * RING * 2)
     start = (core * 2 * RING + y_lo * RING + x) * own
     index = lax.dynamic_slice_in_dim(batch_index, start, own, 0)
@@ -190,9 +178,9 @@
     targets = jnp.pad(pick(train_labels, index), fill)
 
     column, centers, own_weights = lax.optimization_barrier(
-        (spread(rows, COLUMNS), centers, weights)
-    )
-    quarter = RING * LEVELS * own
+        (spread(rows, CLASSES), centers, weights)
+    )
+    quarter = len(CLASSES[0]) * own
     pair = 2 * here
     held = call(
         prepare_kernel,
@@ -224,16 +212,16 @@
     rows_of = quarters(column)
     done = {0: quarter_of(rows_of[0])}
     value = done[0][0]
-    later = [rows_of[offset] for offset in ORDER]
+    later = [rows_of[way] for way in WAYS]
     *later, value = lax.optimization_barrier((*later, value))
-    for offset, part in zip(ORDER, later):
-        done[offset] = quarter_of(part)
-        value = value + permute(done[offset][0], bulk_shift(offset))
-    high = jnp.concatenate([done[offset][1] for offset in range(RING)], axis=0)
-    low = jnp.concatenate([done[offset][2] for offset in range(RING)], axis=0)
-    value = scatter_sum(ring_sum(value), COLUMNS)
-    resid_of = quarters(spread(value * scale - targets, COLUMNS))
-    resid_list = [resid_of[offset] for offset in range(RING)]
+    for way, part in zip(WAYS, later):
+        done[way] = quarter_of(part)
+        value = value + permute(done[way][0], swap_pairs(way))
+    high = jnp.concatenate([done[way][1] for way in range(4)], axis=0)
+    low = jnp.concatenate([done[way][2] for way in range(4)], axis=0)
+    value = scatter_sum(value, CLASSES)
+    resid_of = quarters(spread(value * scale - targets, CLASSES))
+    resid_list = [resid_of[way] for way in range(4)]
 
     def delta_of(resid, low_end, high_end):
         return call(
@@ -242,7 +230,7 @@
             *resid,
             high[:, low_end:high_end],
             low[:, low_end:high_end],
-            scratch=(((RING * quarter, lanes), jnp.bfloat16),) * 2,
+            scratch=(((4 * quarter, lanes), jnp.bfloat16),) * 2,
         )[0]
 
     first = delta_of(resid_list, here, pair)
@@ -255,12 +243,9 @@
     pieces = []
     for low in range(2):
         for column in range(RING):
-            line = y_hi * 2 + low
-            offset = jnp.where(core == 0, column - x, line - y) % RING
-            slot = jnp.where(core == 0, line, column)
-            turn = (slot - jnp.where(core == 0, y, x)) % RING
-            place = offset * quarter + (turn * LEVELS + z) * own
-            pieces.append(lax.dynamic_slice_in_dim(resid_all, place, own, 0))
+            way = (x + column) % 2 + 2 * ((y_lo + low) % 2)
+            slot = (column // 2 * (RING // 2) + y_hi) * LEVELS + z
+            pieces.append(lax.dynamic_slice_in_dim(resid_all, way * quarter + slot * own, own, 0))
     mine = jnp.concatenate(pieces, axis=0)[:, :outputs]
     theirs = permute(mine, SWAP)
     residual = jnp.where(

time: 152 us -> 140 us (0.921)
  waiting for transfers between devices: 57.7 us -> 41.9 us
  blocking collectives: 16.6 us -> 29.9 us
  starting transfers between devices: 42 us -> 34.3 us
  local copies, waits for them, and re-layouts: 20.2 us -> 18 us
    ppermute x22 -> x13, waiting for transfers between devices: 44.1 us -> 16.6 us  [permute(): return lax.ppermute(array, AXES, pairs)]
    ppermute x22 -> x13, starting transfers between devices: 35.3 us -> 21.2 us  [permute(): return lax.ppermute(array, AXES, pairs)]
    all_to_all x1, blocking collectives: 16.6 us -> 29.9 us  [exchange(): lax.all_to_all(array, AXES, 0, 0, axis_index_groups=groups, tiled=True)]
    all_to_all x2, waiting for transfers between devices: 13.7 us -> 25.3 us  [exchange(): lax.all_to_all(array, AXES, 0, 0, axis_index_groups=groups, tiled=True)]
    all_to_all x2, starting transfers between devices: 6.74 us -> 13.2 us  [exchange(): lax.all_to_all(array, AXES, 0, 0, axis_index_groups=groups, tiled=True)]
    unnamed x29 -> x23, local copies, waits for them, and re-layouts: 7.57 us -> 6.12 us
  transfers between devices with their start and end apart: 24 -> 15, of which waited for: 16 -> 10; matrix products, arithmetic and copies ran while one was open for 10% -> 10% of each run, Pallas kernels for 4% -> 4%
where the time goes in v7:
time: 140 us; the launch traced here: 139 us
  waiting for transfers between devices  41.9 us (30%)
  starting transfers between devices  34.3 us (24%)
  blocking collectives  29.9 us (21%)
  local copies, waits for them, and re-layouts  18 us (13%)
  Pallas kernels  9.02 us (6%)
  other arithmetic  5.23 us (4%)
    all_to_all x1, blocking collectives, exchange(): lax.all_to_all(array, AXES, 0, 0, axis_index_groups=groups, tiled=True)  29.9 us
    all_to_all x2, waiting for transfers between devices, exchange(): lax.all_to_all(array, AXES, 0, 0, axis_index_groups=groups, tiled=True)  25.3 us
    ppermute x13, starting transfers between devices, permute(): return lax.ppermute(array, AXES, pairs)  21.2 us
    ppermute x13, waiting for transfers between devices, permute(): return lax.ppermute(array, AXES, pairs)  16.6 us
    all_to_all x2, starting transfers between devices, exchange(): lax.all_to_all(array, AXES, 0, 0, axis_index_groups=groups, tiled=True)  13.2 us
    pallas_call x7, Pallas kernels, call(): pl.pallas_call(kernel, out_shape=[jax.ShapeDtypeStruct(shape, dtype) for...  9.02 us
    unnamed x23, local copies, waits for them, and re-layouts  6.12 us
    concatenate x1, local copies, waits for them, and re-layouts, per_device(): mine = jnp.concatenate(pieces, axis=0)[:, :outputs]  3 us
  transfers between devices with their start and end apart: 15, of which 10 were waited for; matrix products, arithmetic and copies ran while one was open for 10% of the time, Pallas kernels for 4%

profile of v7, /device:TPU:1, one launch (start us, length us, event | category | flops | bytes accessed | tf_op | source)
XLA Modules:
  0.0 139.2 jit_solution(10078549187989517693)
XLA Ops:
  2.6 29.9 %all_to_all.26 = f32[32,4,1024]{2,1,0:T(4,128)S(1)} all-to-all(f32[32,4,1024]{2,1,0:T(4,128)S(1)} %broadcast_in_dim.7), channel_id=1, replica_groups={{0,162,4,166,8,170,12,174,1,163,5,167,9,171,13,175,64,226,68,230,72,234..., dimensions={0} | all-to-all | bytes 1048576 | tf_op jit(solution)/shard_map/all_to_all | solution.py:77
  32.6 3.8 %collective-permute-start.3 = (f32[256,1024]{1,0:T(8,128)}, f32[256,1024]{1,0:T(8,128)S(1)}, u32[]{:S(2)}, u32[]{:S(2)}) collective-permute-start(f32[256,1024]{1,0:T(8,128)} %own_centers), channel_id=1, source_target_pairs={{0,16},{16,0},{2,18},{18,2},{4,20},{20,4},{6,22},{22,6},{8,24},{24... | collective-permute-start | bytes 3145736 | tf_op jit(solution)/shard_map/ppermute | solution.py:73
  36.5 1.7 %collective-permute-start = (f32[128,1024]{1,0:T(8,128)S(1)}, f32[128,1024]{1,0:T(8,128)S(1)}, u32[]{:S(2)}, u32[]{:S(2)}) collective-permute-start(f32[128,1024]{1,0:T(8,128)S(1)} %all_to_all.18.rows), channel_id=1, source_target_pairs={{0,32},{16,112},{2,34},{18,114},{4,36},{20,116},{6,38},{22,118},{8... | collective-permute-start | bytes 1572872 | tf_op jit(solution)/shard_map/ppermute | solution.py:73
  39.0 1.5 %collective-permute-start.2 = (f32[128,1024]{1,0:T(8,128)S(1)}, f32[128,1024]{1,0:T(8,128)S(1)}, u32[]{:S(2)}, u32[]{:S(2)}) collective-permute-start(f32[128,1024]{1,0:T(8,128)S(1)} %all_to_all.18.rows), channel_id=1, source_target_pairs={{0,2},{16,30},{2,0},{18,20},{4,6},{20,18},{6,4},{22,24},{8,10},{24... | collective-permute-start | bytes 1572872 | tf_op jit(solution)/shard_map/ppermute | solution.py:73
  40.5 1.2 copy-done.4
  41.7 1.2 shard_map.68
  43.0 1.1 shard_map.69
  44.1 1.6 %collective-permute-done.rows = f32[128,1024]{1,0:T(8,128)S(1)} collective-permute-done((f32[128,1024]{1,0:T(8,128)S(1)}, f32[128,1024]{1,0:T(8,128)S(1)}, u32[]{:S(2)}, u32[]{:S(2)}) %collective-permute-start) | collective-permute-done | bytes 524320 | tf_op jit(solution)/shard_map/ppermute | solution.py:73
  45.8 1.7 %collective-permute-done.1.rows = f32[128,1024]{1,0:T(8,128)S(1)} collective-permute-done((f32[128,1024]{1,0:T(8,128)S(1)}, f32[128,1024]{1,0:T(8,128)S(1)}, u32[]{:S(2)}, u32[]{:S(2)}) %collective-permute-start.1) | collective-permute-done | bytes 524320 | tf_op jit(solution)/shard_map/ppermute | solution.py:73
  48.3 1.1 shard_map.72
  49.4 1.6 %collective-permute-start.7 = (f32[128,1024]{1,0:T(8,128)S(1)}, f32[128,1024]{1,0:T(8,128)S(1)}, u32[]{:S(2)}, u32[]{:S(2)}) collective-permute-start(f32[128,1024]{1,0:T(8,128)S(1)} %get-tuple-element.45), channel_id=1, source_target_pairs={{0,2},{16,30},{2,0},{18,20},{4,6},{20,18},{6,4},{22,24},{8,10},{24... | collective-permute-start | bytes 1572872 | tf_op jit(solution)/shard_map/ppermute | solution.py:73
  51.0 1.1 shard_map.71
  52.8 1.1 shard_map.70
  54.0 2.3 %collective-permute-start.5 = (f32[128,1024]{1,0:T(8,128)S(1)}, f32[128,1024]{1,0:T(8,128)S(1)}, u32[]{:S(2)}, u32[]{:S(2)}) collective-permute-start(f32[128,1024]{1,0:T(8,128)S(1)} %get-tuple-element.41), channel_id=1, source_target_pairs={{0,32},{16,112},{2,34},{18,114},{4,36},{20,116},{6,38},{22,118},{8... | collective-permute-start | bytes 1572872 | tf_op jit(solution)/shard_map/ppermute | solution.py:73
  56.3 2.5 %collective-permute-done.7 = f32[128,1024]{1,0:T(8,128)S(1)} collective-permute-done((f32[128,1024]{1,0:T(8,128)S(1)}, f32[128,1024]{1,0:T(8,128)S(1)}, u32[]{:S(2)}, u32[]{:S(2)}) %collective-permute-start.7) | collective-permute-done | bytes 524320 | tf_op jit(solution)/shard_map/ppermute | solution.py:73
  58.7 2.7 %collective-permute-done.6 = f32[128,1024]{1,0:T(8,128)S(1)} collective-permute-done((f32[128,1024]{1,0:T(8,128)S(1)}, f32[128,1024]{1,0:T(8,128)S(1)}, u32[]{:S(2)}, u32[]{:S(2)}) %collective-permute-start.6) | collective-permute-done | bytes 524320 | tf_op jit(solution)/shard_map/ppermute | solution.py:73
  61.5 1.8 %collective-permute-done.5 = f32[128,1024]{1,0:T(8,128)S(1)} collective-permute-done((f32[128,1024]{1,0:T(8,128)S(1)}, f32[128,1024]{1,0:T(8,128)S(1)}, u32[]{:S(2)}, u32[]{:S(2)}) %collective-permute-start.5) | collective-permute-done | bytes 524320 | tf_op jit(solution)/shard_map/ppermute | solution.py:73
  64.4 6.2 %all-to-all-start.1 = ((f32[32,4,1024]{2,1,0:T(4,128)}), f32[32,4,1024]{2,1,0:T(4,128)S(1)}, u32[]{:S(2)}, u32[]{:S(2)}) async-start(f32[32,4,1024]{2,1,0:T(4,128)} %all_to_all.19), calls=%async_computation.1 | async-start | bytes 1048576 | tf_op jit(solution)/shard_map/all_to_all | solution.py:77
  70.6 2.5 %copy.7 = f32[256,1000]{1,0:T(8,128)} copy(f32[256,1000]{0,1:T(8,128)} %param.7) | data formatting | bytes 2048000 | tf_op args[2]
  73.2 1.8 %gather_fusion.1 = f32[4,1000]{1,0:T(4,128)S(1)} fusion(f32[256,1000]{1,0:T(8,128)} %copy.7, s32[1024]{0:T(1024)S(1)} %pad_clamp_fusion), kind=kCustom, calls=%fused_computation.1 | custom fusion | bytes 32016 | tf_op jit(solution)/shard_map/gather | solution.py:98
  75.0 12.6 %all-to-all-done.1 = f32[32,4,1024]{2,1,0:T(4,128)S(1)} async-done(((f32[32,4,1024]{2,1,0:T(4,128)}), f32[32,4,1024]{2,1,0:T(4,128)S(1)}, u32[]{:S(2)}, u32[]{:S(2)}) %all-to-all-start.1) | async-done | bytes 524320 | tf_op jit(solution)/shard_map/all_to_all | solution.py:77
  88.6 6.9 %all-to-all-start.2 = ((f32[32,4,1024]{2,1,0:T(4,128)}), f32[32,4,1024]{2,1,0:T(4,128)S(1)}, u32[]{:S(2)}, u32[]{:S(2)}) async-start(f32[32,4,1024]{2,1,0:T(4,128)} %broadcast_in_dim.8), calls=%async_computation.2 | async-start | bytes 1048576 | tf_op jit(solution)/shard_map/all_to_all | solution.py:77
  96.5 12.7 %all-to-all-done.2 = f32[32,4,1024]{2,1,0:T(4,128)S(1)} async-done(((f32[32,4,1024]{2,1,0:T(4,128)}), f32[32,4,1024]{2,1,0:T(4,128)S(1)}, u32[]{:S(2)}, u32[]{:S(2)}) %all-to-all-start.2) | async-done | bytes 524320 | tf_op jit(solution)/shard_map/all_to_all | solution.py:77
  109.4 7.8 %collective-permute-start.8 = (f32[128,1024]{1,0:T(8,128)S(1)}, f32[128,1024]{1,0:T(8,128)S(1)}, u32[]{:S(2)}, u32[]{:S(2)}) collective-permute-start(f32[128,1024]{1,0:T(8,128)S(1)} %all_to_all.22.resid_0), channel_id=1, source_target_pairs={{0,32},{16,112},{2,34},{18,114},{4,36},{20,116},{6,38},{22,118},{8... | collective-permute-start | bytes 1572872 | tf_op jit(solution)/shard_map/ppermute | solution.py:73
  119.2 1.8 %fusion.1 = (bf16[512,256]{1,0:T(8,128)(2,1)}, bf16[512,256]{1,0:T(8,128)(2,1)S(1)}) fusion(bf16[512,512]{1,0:T(8,128)(2,1)} %constant_dynamic-update-slice_fusion.4), kind=kLoop, calls=%fused_computation.29 | loop fusion | bytes 1048576 | tf_op jit(solution)/shard_map/slice | solution.py:232
  121.0 2.8 %collective-permute-done.8.resid_1 = f32[128,1024]{1,0:T(8,128)S(1)} collective-permute-done((f32[128,1024]{1,0:T(8,128)S(1)}, f32[128,1024]{1,0:T(8,128)S(1)}, u32[]{:S(2)}, u32[]{:S(2)}) %collective-permute-start.8) | collective-permute-done | bytes 524320 | tf_op jit(solution)/shard_map/ppermute | solution.py:73
  123.8 2.7 %collective-permute-done.9.resid_2 = f32[128,1024]{1,0:T(8,128)S(1)} collective-permute-done((f32[128,1024]{1,0:T(8,128)S(1)}, f32[128,1024]{1,0:T(8,128)S(1)}, u32[]{:S(2)}, u32[]{:S(2)}) %collective-permute-start.9) | collective-permute-done | bytes 524320 | tf_op jit(solution)/shard_map/ppermute | solution.py:73
  126.4 2.1 %shard_map.73 = f32[1000,256]{1,0:T(8,128)} custom-call(f32[128,1024]{1,0:T(8,128)S(1)} %all_to_all.22.resid_0, f32[128,1024]{1,0:T(8,128)S(1)} %collective-permute-done.8.resid_1, f32[128,1024]{1,0:T(8,128)S(1)} %collective-permute-done.9.resid_2, f32[128,1024]{1,0:T(8,128)S(1)} %collective-permute-done.10.resid_3, ...), custom_call_target="tpu_custom_call" | custom-call | tf_op jit(solution)/shard_map/pallas_call | solution.py:154
  129.8 3.0 %concatenate.21 = f32[32,1024]{1,0:T(8,128)S(1)} concatenate(f32[4,1024]{1,0:T(4,128)} %get-tuple-element.65, f32[4,1024]{1,0:T(4,128)} %get-tuple-element.64, f32[4,1024]{1,0:T(4,128)} %get-tuple-element.63, f32[4,1024]{1,0:T(4,128)} %get-tuple-element.62, f32[4,1024]{1,0:T(4,128)} %get-tuple-element.61, f32[4,1024]{1,0:T(4,128)} %get-tuple-element.60, ...), dimensions={0} | concatenate | bytes 262144 | tf_op jit(solution)/shard_map/concatenate | solution.py:249
  134.0 1.1 shard_map.74
  135.2 1.7 %maximum_select_fusion = f32[64,1000]{1,0:T(8,128)} fusion(f32[32,1000]{1,0:T(8,128)} %collective-permute-done.12, f32[32,1000]{1,0:T(8,128)S(1)} %bitcast.12, pred[]{:T(512)S(6)} %eq.20), kind=kLoop, calls=%fused_computation.5 | loop fusion | flops 192000 | bytes 512001 | tf_op jit(solution)/shard_map/jit(_where)/select_n | solution.py:251
  136.9 2.4 %fusion = f32[256,1000]{0,1:T(8,128)} fusion(f32[256,1000]{0,1:T(8,128)S(1)} %copy-done.2, f32[1000,256]{1,0:T(8,128)S(1)} %shard_map.74, f32[1000,256]{1,0:T(8,128)} %collective-permute-done.11), kind=kLoop, calls=%fused_computation.3 | loop fusion | flops 768000 | bytes 4096000 | tf_op jit(solution)/shard_map/transpose | solution.py:240
  (50 shorter events, 12.2 us)
Async XLA Ops:
  0.6 1.2 copy-start
  0.6 35.8 %copy-start.1 = (f32[256,1000]{0,1:T(8,128)S(1)}, f32[256,1000]{0,1:T(8,128)}, u32[]{:S(2)}) copy-start(f32[256,1000]{0,1:T(8,128)} %param.9) | copy-start | bytes 3072004
  32.6 7.9 %collective-permute-start.3 = (f32[256,1024]{1,0:T(8,128)}, f32[256,1024]{1,0:T(8,128)S(1)}, u32[]{:S(2)}, u32[]{:S(2)}) collective-permute-start(f32[256,1024]{1,0:T(8,128)} %own_centers), channel_id=1, source_target_pairs={{0,16},{16,0},{2,18},{18,2},{4,20},{20,4},{6,22},{22,6},{8,24},{24... | collective-permute-start | bytes 3145736 | tf_op jit(solution)/shard_map/ppermute | solution.py:73
  36.4 4.1 %collective-permute-start.4 = (f32[256,1000]{0,1:T(8,128)S(1)}, f32[256,1000]{0,1:T(8,128)S(1)}, u32[]{:S(2)}, u32[]{:S(2)}) collective-permute-start(f32[256,1000]{0,1:T(8,128)S(1)} %copy-done.1), channel_id=1, source_target_pairs={{0,16},{16,0},{2,18},{18,2},{4,20},{20,4},{6,22},{22,6},{8,24},{24... | collective-permute-start | bytes 3072008 | tf_op jit(solution)/shard_map/ppermute | solution.py:73
  36.5 9.2 %collective-permute-start = (f32[128,1024]{1,0:T(8,128)S(1)}, f32[128,1024]{1,0:T(8,128)S(1)}, u32[]{:S(2)}, u32[]{:S(2)}) collective-permute-start(f32[128,1024]{1,0:T(8,128)S(1)} %all_to_all.18.rows), channel_id=1, source_target_pairs={{0,32},{16,112},{2,34},{18,114},{4,36},{20,116},{6,38},{22,118},{8... | collective-permute-start | bytes 1572872 | tf_op jit(solution)/shard_map/ppermute | solution.py:73
  38.2 9.2 %collective-permute-start.1 = (f32[128,1024]{1,0:T(8,128)S(1)}, f32[128,1024]{1,0:T(8,128)S(1)}, u32[]{:S(2)}, u32[]{:S(2)}) collective-permute-start(f32[128,1024]{1,0:T(8,128)S(1)} %all_to_all.18.rows), channel_id=1, source_target_pairs={{0,128},{16,145},{2,130},{18,147},{4,132},{20,149},{6,134},{22,151... | collective-permute-start | bytes 1572872 | tf_op jit(solution)/shard_map/ppermute | solution.py:73
  39.0 9.2 %collective-permute-start.2 = (f32[128,1024]{1,0:T(8,128)S(1)}, f32[128,1024]{1,0:T(8,128)S(1)}, u32[]{:S(2)}, u32[]{:S(2)}) collective-permute-start(f32[128,1024]{1,0:T(8,128)S(1)} %all_to_all.18.rows), channel_id=1, source_target_pairs={{0,2},{16,30},{2,0},{18,20},{4,6},{20,18},{6,4},{22,24},{8,10},{24... | collective-permute-start | bytes 1572872 | tf_op jit(solution)/shard_map/ppermute | solution.py:73
  40.5 1.2 copy-start.4
  49.4 9.3 %collective-permute-start.7 = (f32[128,1024]{1,0:T(8,128)S(1)}, f32[128,1024]{1,0:T(8,128)S(1)}, u32[]{:S(2)}, u32[]{:S(2)}) collective-permute-start(f32[128,1024]{1,0:T(8,128)S(1)} %get-tuple-element.45), channel_id=1, source_target_pairs={{0,2},{16,30},{2,0},{18,20},{4,6},{20,18},{6,4},{22,24},{8,10},{24... | collective-permute-start | bytes 1572872 | tf_op jit(solution)/shard_map/ppermute | solution.py:73
  52.1 9.3 %collective-permute-start.6 = (f32[128,1024]{1,0:T(8,128)S(1)}, f32[128,1024]{1,0:T(8,128)S(1)}, u32[]{:S(2)}, u32[]{:S(2)}) collective-permute-start(f32[128,1024]{1,0:T(8,128)S(1)} %get-tuple-element.43), channel_id=1, source_target_pairs={{0,128},{16,145},{2,130},{18,147},{4,132},{20,149},{6,134},{22,151... | collective-permute-start | bytes 1572872 | tf_op jit(solution)/shard_map/ppermute | solution.py:73
  54.0 9.3 %collective-permute-start.5 = (f32[128,1024]{1,0:T(8,128)S(1)}, f32[128,1024]{1,0:T(8,128)S(1)}, u32[]{:S(2)}, u32[]{:S(2)}) collective-permute-start(f32[128,1024]{1,0:T(8,128)S(1)} %get-tuple-element.41), channel_id=1, source_target_pairs={{0,32},{16,112},{2,34},{18,114},{4,36},{20,116},{6,38},{22,118},{8... | collective-permute-start | bytes 1572872 | tf_op jit(solution)/shard_map/ppermute | solution.py:73
  64.4 23.2 %all-to-all-start.1 = ((f32[32,4,1024]{2,1,0:T(4,128)}), f32[32,4,1024]{2,1,0:T(4,128)S(1)}, u32[]{:S(2)}, u32[]{:S(2)}) async-start(f32[32,4,1024]{2,1,0:T(4,128)} %all_to_all.19), calls=%async_computation.1 | async-start | bytes 1048576 | tf_op jit(solution)/shard_map/all_to_all | solution.py:77
  88.6 20.6 %all-to-all-start.2 = ((f32[32,4,1024]{2,1,0:T(4,128)}), f32[32,4,1024]{2,1,0:T(4,128)S(1)}, u32[]{:S(2)}, u32[]{:S(2)}) async-start(f32[32,4,1024]{2,1,0:T(4,128)} %broadcast_in_dim.8), calls=%async_computation.2 | async-start | bytes 1048576 | tf_op jit(solution)/shard_map/all_to_all | solution.py:77
  95.6 0.8 copy-start.6
  96.5 12.9 %copy-start.5 = (bf16[512,512]{1,0:T(8,128)(2,1)}, bf16[512,512]{1,0:T(8,128)(2,1)S(1)}, u32[]{:S(2)}) copy-start(bf16[512,512]{1,0:T(8,128)(2,1)S(1)} %constant_dynamic-update-slice_fusion.5) | copy-start | bytes 1572868
  109.4 14.4 %collective-permute-start.8 = (f32[128,1024]{1,0:T(8,128)S(1)}, f32[128,1024]{1,0:T(8,128)S(1)}, u32[]{:S(2)}, u32[]{:S(2)}) collective-permute-start(f32[128,1024]{1,0:T(8,128)S(1)} %all_to_all.22.resid_0), channel_id=1, source_target_pairs={{0,32},{16,112},{2,34},{18,114},{4,36},{20,116},{6,38},{22,118},{8... | collective-permute-start | bytes 1572872 | tf_op jit(solution)/shard_map/ppermute | solution.py:73
  117.2 9.2 %collective-permute-start.9 = (f32[128,1024]{1,0:T(8,128)S(1)}, f32[128,1024]{1,0:T(8,128)S(1)}, u32[]{:S(2)}, u32[]{:S(2)}) collective-permute-start(f32[128,1024]{1,0:T(8,128)S(1)} %all_to_all.22.resid_0), channel_id=1, source_target_pairs={{0,128},{16,145},{2,130},{18,147},{4,132},{20,149},{6,134},{22,151... | collective-permute-start | bytes 1572872 | tf_op jit(solution)/shard_map/ppermute | solution.py:73
  117.2 9.2 %collective-permute-start.10 = (f32[128,1024]{1,0:T(8,128)S(1)}, f32[128,1024]{1,0:T(8,128)S(1)}, u32[]{:S(2)}, u32[]{:S(2)}) collective-permute-start(f32[128,1024]{1,0:T(8,128)S(1)} %all_to_all.22.resid_0), channel_id=1, source_target_pairs={{0,2},{16,30},{2,0},{18,20},{4,6},{20,18},{6,4},{22,24},{8,10},{24... | collective-permute-start | bytes 1572872 | tf_op jit(solution)/shard_map/ppermute | solution.py:73
  128.5 8.3 %collective-permute-start.11 = (f32[1000,256]{1,0:T(8,128)}, f32[1000,256]{1,0:T(8,128)}, u32[]{:S(2)}, u32[]{:S(2)}) collective-permute-start(f32[1000,256]{1,0:T(8,128)} %shard_map.73), channel_id=1, source_target_pairs={{0,16},{16,0},{2,18},{18,2},{4,20},{20,4},{6,22},{22,6},{8,24},{24... | collective-permute-start | bytes 3072008 | tf_op jit(solution)/shard_map/ppermute | solution.py:73
  132.8 2.4 %collective-permute-start.12 = (f32[32,1000]{1,0:T(8,128)S(1)}, f32[32,1000]{1,0:T(8,128)}, u32[]{:S(2)}, u32[]{:S(2)}) collective-permute-start(f32[32,1000]{1,0:T(8,128)S(1)} %bitcast.11), channel_id=1, source_target_pairs={{0,16},{16,0},{2,18},{18,2},{4,20},{20,4},{6,22},{22,6},{8,24},{24... | collective-permute-start | bytes 384008 | tf_op jit(solution)/shard_map/ppermute | solution.py:73
  133.0 3.9 %copy-start.2 = (f32[256,1000]{0,1:T(8,128)S(1)}, f32[256,1000]{0,1:T(8,128)}, u32[]{:S(2)}) copy-start(f32[256,1000]{0,1:T(8,128)} %param.9) | copy-start | bytes 3072004
  133.0 1.0 copy-start.3

commit v8 on v7

--- a/solution.py
+++ b/solution.py
@@ -37,34 +37,36 @@
     ]
 
 
-def beside(place, core):
-    return place + 1 if place % 2 == core else place - 1
-
-
-def neighbour(x, y, z, core, way):
+def beside(place, core, step):
+    return place + step if place // step % 2 == core else place - step
+
+
+def neighbour(x, y, z, core, step, way):
     if way == 1:
-        x = beside(x, core)
+        x = beside(x, core, step)
     elif way == 2:
-        y = beside(y, core)
+        y = beside(y, core, step)
     elif way == 3:
-        z = beside(z, core)
+        z = beside(z, core, step)
     return position(x, y, z % LEVELS, core)
 
 
-def swap_pairs(way):
-    return [(position(*device), neighbour(*device, way)) for device in everywhere()]
+def swap_pairs(step, way):
+    return [(position(*device), neighbour(*device, step, way)) for device in everywhere()]
 
 
 SWAP = [(position(x, y, z, core), position(x, y, z, 1 - core)) for x, y, z, core in everywhere()]
-CLASSES = [
+GROUPS = [
     [
-        position(2 * i + (low + z) % 2, 2 * k + (high + z) % 2, z, core)
-        for i in range(RING // 2)
-        for k in range(RING // 2)
+        position(
+            2 * (i ^ z // 2 % 2) + (low ^ z % 2), 2 * (k ^ z // 2 % 2) + (high ^ z % 2), z, core
+        )
         for z in range(LEVELS)
     ]
     for low in range(2)
     for high in range(2)
+    for i in range(2)
+    for k in range(2)
     for core in range(2)
 ]
 
@@ -88,10 +90,20 @@
     return exchange(array, groups).reshape((count, -1) + array.shape[1:]).sum(axis=0)
 
 
-def quarters(own):
-    received = {way: permute(own, swap_pairs(way)) for way in WAYS}
-    received[0] = own
-    return received
+def gathered(own, step):
+    return [own] + [permute(own, swap_pairs(step, way)) for way in WAYS]
+
+
+def quarters(column):
+    return gathered(jnp.concatenate(gathered(column, 2), axis=0), 1)
+
+
+def folded(array):
+    pieces = jnp.split(array, 4, axis=0)
+    total = pieces[0]
+    for way in WAYS:
+        total = total + permute(pieces[way], swap_pairs(2, way))
+    return total
 
 
 def pick(array, index):
@@ -150,9 +162,24 @@
     delta[...] = found.T[: delta.shape[0]]
 
 
-def call(kernel, outs, *operands, scratch=()):
+def first_delta_kernel(
+    source, target, resid_0, resid_1, resid_2, resid_3, high, low, delta, mine, resid_high, resid_low
+):
+    delta_kernel(
+        resid_0, resid_1, resid_2, resid_3, high, low, delta, resid_high, resid_low
+    )
+    for i, resid in enumerate((resid_0, resid_1, resid_2, resid_3)):
+        for j in range(2):
+            for row in range(mine.shape[0] // 8):
+                found = resid[pl.ds(source[i, j] + row, 1), :]
+                mine[pl.ds(target[i, j] + row, 1), :] = found[:, : mine.shape[1]]
+
+
+def call(kernel, outs, *operands, scratch=(), scalars=0):
     return pl.pallas_call(
         kernel,
+        in_specs=[pl.BlockSpec(memory_space=pltpu.SMEM)] * scalars
+        + [pl.BlockSpec(memory_space=pltpu.VMEM)] * (len(operands) - scalars),
         out_shape=[jax.ShapeDtypeStruct(shape, dtype) for shape, dtype in outs],
         scratch_shapes=[pltpu.VMEM(shape, dtype) for shape, dtype in scratch],
         compiler_params=pltpu.CompilerParams(vmem_limit_bytes=VMEM_BYTES),
@@ -169,6 +196,7 @@
     scale = 1.0 / math.sqrt(here * devices)
     x, core, z = lax.axis_index("x"), lax.axis_index("core"), lax.axis_index("z")
     y_lo, y_hi = lax.axis_index("y_lo"), lax.axis_index("y_hi")
+    y = y_hi * 2 + y_lo
     own = block // (2 * RING * 2)
     start = (core * 2 * RING + y_lo * RING + x) * own
     index = lax.dynamic_slice_in_dim(batch_index, start, own, 0)
@@ -178,9 +206,10 @@
     targets = jnp.pad(pick(train_labels, index), fill)
 
     column, centers, own_weights = lax.optimization_barrier(
-        (spread(rows, CLASSES), centers, weights)
-    )
-    quarter = len(CLASSES[0]) * own
+        (spread(rows, GROUPS), centers, weights)
+    )
+    column_rows = LEVELS * own
+    quarter = 4 * column_rows
     pair = 2 * here
     held = call(
         prepare_kernel,
@@ -209,44 +238,47 @@
             *held,
         )
 
-    rows_of = quarters(column)
-    done = {0: quarter_of(rows_of[0])}
+    first_rows, *later = quarters(column)
+    done = [quarter_of(first_rows)]
     value = done[0][0]
-    later = [rows_of[way] for way in WAYS]
     *later, value = lax.optimization_barrier((*later, value))
     for way, part in zip(WAYS, later):
-        done[way] = quarter_of(part)
-        value = value + permute(done[way][0], swap_pairs(way))
-    high = jnp.concatenate([done[way][1] for way in range(4)], axis=0)
-    low = jnp.concatenate([done[way][2] for way in range(4)], axis=0)
-    value = scatter_sum(value, CLASSES)
-    resid_of = quarters(spread(value * scale - targets, CLASSES))
-    resid_list = [resid_of[way] for way in range(4)]
-
-    def delta_of(resid, low_end, high_end):
-        return call(
-            delta_kernel,
-            (((outputs, here), jnp.float32),),
-            *resid,
-            high[:, low_end:high_end],
-            low[:, low_end:high_end],
-            scratch=(((4 * quarter, lanes), jnp.bfloat16),) * 2,
-        )[0]
-
-    first = delta_of(resid_list, here, pair)
+        done.append(quarter_of(part))
+        value = value + permute(done[way][0], swap_pairs(1, way))
+    high = jnp.concatenate([part[1] for part in done], axis=0)
+    low = jnp.concatenate([part[2] for part in done], axis=0)
+    value = scatter_sum(folded(value), GROUPS)
+    resid_list = quarters(spread(value * scale - targets, GROUPS))
+
+    way, half = jnp.arange(4)[:, None], jnp.arange(2)[None, :]
+    turn = z // 2 % 2
+    next_x = jnp.where(x % 2 == core, x + 1, x - 1) % RING
+    next_y = jnp.where(y % 2 == core, y + 1, y - 1) % RING
+    next_z = jnp.where(z % 2 == core, z + 1, z - 1) % LEVELS
+    held_turn = jnp.where(way == 3, next_z // 2 % 2, turn)
+    held_x = jnp.where(way == 1, next_x, x) // 2 ^ held_turn
+    held_y = jnp.where(way == 2, next_y, y) // 2 ^ held_turn
+    piece = (held_x ^ half ^ turn) + 2 * (held_y ^ y_hi ^ turn)
+    source = piece * column_rows + z * own
+    target = ((y_lo ^ way // 2) * RING + 2 * half + ((x ^ way) % 2)) * own + 0 * source
+    scratch = (((4 * quarter, lanes), jnp.bfloat16),) * 2
+    delta_out = ((outputs, here), jnp.float32)
+    first, mine = call(
+        first_delta_kernel,
+        (delta_out, ((block // 2, outputs), jnp.float32)),
+        source.astype(jnp.int32),
+        target.astype(jnp.int32),
+        *resid_list,
+        high[:, here:],
+        low[:, here:],
+        scratch=scratch,
+        scalars=2,
+    )
     received = permute(first, SWAP)
-    *resid_list, first = lax.optimization_barrier((*resid_list, first))
-    second = delta_of(resid_list, 0, here)
+    (second,) = call(
+        delta_kernel, (delta_out,), *resid_list, high[:, :here], low[:, :here], scratch=scratch
+    )
     new_weights = (weights.T - step_size / batch * (second + received)).T
-
-    resid_all = jnp.concatenate(resid_list, axis=0)
-    pieces = []
-    for low in range(2):
-        for column in range(RING):
-            way = (x + column) % 2 + 2 * ((y_lo + low) % 2)
-            slot = (column // 2 * (RING // 2) + y_hi) * LEVELS + z
-            pieces.append(lax.dynamic_slice_in_dim(resid_all, way * quarter + slot * own, own, 0))
-    mine = jnp.concatenate(pieces, axis=0)[:, :outputs]
     theirs = permute(mine, SWAP)
     residual = jnp.where(
         core == 0,

time: 140 us -> 150 us (1.071)
  blocking collectives: 29.9 us -> 23.3 us
  Pallas kernels: 9.02 us -> 15.5 us
  starting transfers between devices: 34.3 us -> 40.6 us
  waiting for transfers between devices: 41.9 us -> 44.4 us
    ppermute x13 -> x22, waiting for transfers between devices: 16.6 us -> 25.6 us  [permute(): return lax.ppermute(array, AXES, pairs)]
    ppermute x13 -> x22, starting transfers between devices: 21.2 us -> 28.9 us  [permute(): return lax.ppermute(array, AXES, pairs)]
    all_to_all x1, blocking collectives: 29.9 us -> 23.3 us  [exchange(): lax.all_to_all(array, AXES, 0, 0, axis_index_groups=groups, tiled=True)]
    pallas_call x7, Pallas kernels: 9.02 us -> 15.5 us  [call(): pl.pallas_call(kernel, in_specs=[pl.BlockSpec(memory_space=pltpu.SMEM)] *...]
    all_to_all x2, waiting for transfers between devices: 25.3 us -> 18.8 us  [exchange(): lax.all_to_all(array, AXES, 0, 0, axis_index_groups=groups, tiled=True)]
    unnamed x23 -> x36, local copies, waits for them, and re-layouts: 6.12 us -> 12.2 us
    concatenate x4, local copies, waits for them, and re-layouts: 3.72 us -> 1.35 us  [the longest x2 0.67 us: quarters(): return gathered(jnp.concatenate(gathered(column, 2), axis=0), 1)]
    slice x2, local copies, waits for them, and re-layouts: 2.83 us -> 0.77 us  [the longest x1 0.74 us: per_device(): low[:, here:]]
  transfers between devices with their start and end apart: 15 -> 24, of which waited for: 10 -> 16; matrix products, arithmetic and copies ran while one was open for 10% -> 9% of each run, Pallas kernels for 4% -> 7%
where the time goes in v8:
time: 150 us; the launch traced here: 149 us
  waiting for transfers between devices  44.4 us (30%)
  starting transfers between devices  40.6 us (27%)
  blocking collectives  23.3 us (16%)
  local copies, waits for them, and re-layouts  18.9 us (13%)
  Pallas kernels  15.5 us (10%)
  other arithmetic  5.57 us (4%)
    ppermute x22, starting transfers between devices, permute(): return lax.ppermute(array, AXES, pairs)  28.9 us
    ppermute x22, waiting for transfers between devices, permute(): return lax.ppermute(array, AXES, pairs)  25.6 us
    all_to_all x1, blocking collectives, exchange(): lax.all_to_all(array, AXES, 0, 0, axis_index_groups=groups, tiled=True)  23.3 us
    all_to_all x2, waiting for transfers between devices, exchange(): lax.all_to_all(array, AXES, 0, 0, axis_index_groups=groups, tiled=True)  18.8 us
    pallas_call x7, Pallas kernels, call(): pl.pallas_call(kernel, in_specs=[pl.BlockSpec(memory_space=pltpu.SMEM)] *...  15.5 us
    unnamed x36, local copies, waits for them, and re-layouts  12.2 us
    all_to_all x2, starting transfers between devices, exchange(): lax.all_to_all(array, AXES, 0, 0, axis_index_groups=groups, tiled=True)  11.7 us
  transfers between devices with their start and end apart: 24, of which 16 were waited for; matrix products, arithmetic and copies ran while one was open for 9% of the time, Pallas kernels for 7%

profile of v8, /device:TPU:1, one launch (start us, length us, event | category | flops | bytes accessed | tf_op | source)
XLA Modules:
  0.0 149.2 jit_solution(17526921006590910783)
XLA Ops:
  2.5 23.3 %all_to_all.27 = f32[8,4,1024]{2,1,0:T(4,128)S(1)} all-to-all(f32[8,4,1024]{2,1,0:T(4,128)S(1)} %broadcast_in_dim.39), channel_id=1, replica_groups={{0,162,69,231,8,170,77,239},{16,178,85,247,24,186,93,255},{1,163,68,230..., dimensions={0} | all-to-all | bytes 262144 | tf_op jit(solution)/shard_map/all_to_all | solution.py:79
  25.8 1.9 %collective-permute-start.6 = (f32[256,1024]{1,0:T(8,128)}, f32[256,1024]{1,0:T(8,128)}, u32[]{:S(2)}, u32[]{:S(2)}) collective-permute-start(f32[256,1024]{1,0:T(8,128)} %own_centers), channel_id=1, source_target_pairs={{0,16},{16,0},{2,18},{18,2},{4,20},{20,4},{6,22},{22,6},{8,24},{24... | collective-permute-start | bytes 3145736 | tf_op jit(solution)/shard_map/ppermute | solution.py:75
  28.4 2.0 %collective-permute-start.1 = (f32[32,1024]{1,0:T(8,128)S(1)}, f32[32,1024]{1,0:T(8,128)S(1)}, u32[]{:S(2)}, u32[]{:S(2)}) collective-permute-start(f32[32,1024]{1,0:T(8,128)S(1)} %all_to_all.19), channel_id=1, source_target_pairs={{0,1},{16,17},{2,3},{18,19},{4,5},{20,21},{6,7},{22,23},{8,9},{24,... | collective-permute-start | bytes 393224 | tf_op jit(solution)/shard_map/ppermute | solution.py:75
  31.1 1.5 %collective-permute-start.2 = (f32[32,1024]{1,0:T(8,128)S(1)}, f32[32,1024]{1,0:T(8,128)S(1)}, u32[]{:S(2)}, u32[]{:S(2)}) collective-permute-start(f32[32,1024]{1,0:T(8,128)S(1)} %all_to_all.19), channel_id=1, source_target_pairs={{0,4},{16,28},{2,6},{18,30},{4,0},{20,24},{6,2},{22,26},{8,12},{24... | collective-permute-start | bytes 393224 | tf_op jit(solution)/shard_map/ppermute | solution.py:75
  32.6 1.5 collective-permute-done
  35.4 1.7 %collective-permute-done.2 = f32[32,1024]{1,0:T(8,128)S(1)} collective-permute-done((f32[32,1024]{1,0:T(8,128)S(1)}, f32[32,1024]{1,0:T(8,128)S(1)}, u32[]{:S(2)}, u32[]{:S(2)}) %collective-permute-start.2) | collective-permute-done | bytes 131104 | tf_op jit(solution)/shard_map/ppermute | solution.py:75
  38.6 2.1 %collective-permute-start.4 = (f32[128,1024]{1,0:T(8,128)}, f32[128,1024]{1,0:T(8,128)}, u32[]{:S(2)}, u32[]{:S(2)}) collective-permute-start(f32[128,1024]{1,0:T(8,128)} %constant_dynamic-update-slice_fusion.rows), channel_id=1, source_target_pairs={{0,128},{16,145},{2,130},{18,147},{4,132},{20,149},{6,134},{22,151... | collective-permute-start | bytes 1572872 | tf_op jit(solution)/shard_map/ppermute | solution.py:75
  41.5 2.8 %shard_map.68 = (bf16[1024,512]{1,0:T(8,128)(2,1)S(1)}, bf16[1024,512]{1,0:T(8,128)(2,1)S(1)}, f32[1,512]{1,0:T(1,128)S(1)}, bf16[512,1024]{1,0:T(8,128)(2,1)S(1)}, bf16[512,1024]{1,0:T(8,128)(2,1)S(1)}) custom-call(f32[256,1024]{1,0:T(8,128)S(1)} %copy-done.7, f32[256,1024]{1,0:T(8,128)} %collective-permute-done.6.other_centers, f32[1000,256]{1,0:T(8,128)S(1)} %bitcast.8, ...), custom_call_target="tpu_custom_call" | custom-call | tf_op jit(solution)/shard_map/pallas_call | solution.py:179
  44.3 2.2 %shard_map.69 = (f32[128,1024]{1,0:T(8,128)S(1)}, bf16[128,512]{1,0:T(8,128)(2,1)S(1)}, bf16[128,512]{1,0:T(8,128)(2,1)S(1)}) custom-call(f32[128,1024]{1,0:T(8,128)} %constant_dynamic-update-slice_fusion.rows, bf16[1024,512]{1,0:T(8,128)(2,1)S(1)} %get-tuple-element.31.centers_high, bf16[1024,512]{1,0:T(8,128)(2,1)S(1)} %get-tuple-element.32.centers_low, ...), custom_call_target="tpu_custom_call" | custom-call | tf_op jit(solution)/shard_map/pallas_call | solution.py:179
  48.1 2.1 %collective-permute-done.5.rows = f32[128,1024]{1,0:T(8,128)} collective-permute-done((f32[128,1024]{1,0:T(8,128)}, f32[128,1024]{1,0:T(8,128)}, u32[]{:S(2)}, u32[]{:S(2)}) %collective-permute-start.5) | collective-permute-done | bytes 524320 | tf_op jit(solution)/shard_map/ppermute | solution.py:75
  50.3 2.2 %shard_map.72 = (f32[128,1024]{1,0:T(8,128)S(1)}, bf16[128,512]{1,0:T(8,128)(2,1)S(1)}, bf16[128,512]{1,0:T(8,128)(2,1)S(1)}) custom-call(f32[128,1024]{1,0:T(8,128)} %collective-permute-done.5.rows, bf16[1024,512]{1,0:T(8,128)(2,1)S(1)} %get-tuple-element.31.centers_high, bf16[1024,512]{1,0:T(8,128)(2,1)S(1)} %get-tuple-element.32.centers_low, ...), custom_call_target="tpu_custom_call" | custom-call | tf_op jit(solution)/shard_map/pallas_call | solution.py:179
  53.4 2.2 %shard_map.71 = (f32[128,1024]{1,0:T(8,128)S(1)}, bf16[128,512]{1,0:T(8,128)(2,1)S(1)}, bf16[128,512]{1,0:T(8,128)(2,1)S(1)}) custom-call(f32[128,1024]{1,0:T(8,128)} %collective-permute-done.4.rows, bf16[1024,512]{1,0:T(8,128)(2,1)S(1)} %get-tuple-element.31.centers_high, bf16[1024,512]{1,0:T(8,128)(2,1)S(1)} %get-tuple-element.32.centers_low, ...), custom_call_target="tpu_custom_call" | custom-call | tf_op jit(solution)/shard_map/pallas_call | solution.py:179
  55.6 2.4 %collective-permute-start.9 = (f32[128,1024]{1,0:T(8,128)S(1)}, f32[128,1024]{1,0:T(8,128)S(1)}, u32[]{:S(2)}, u32[]{:S(2)}) collective-permute-start(f32[128,1024]{1,0:T(8,128)S(1)} %get-tuple-element.41), channel_id=1, source_target_pairs={{0,128},{16,145},{2,130},{18,147},{4,132},{20,149},{6,134},{22,151... | collective-permute-start | bytes 1572872 | tf_op jit(solution)/shard_map/ppermute | solution.py:75
  58.0 2.2 %shard_map.70 = (f32[128,1024]{1,0:T(8,128)S(1)}, bf16[128,512]{1,0:T(8,128)(2,1)S(1)}, bf16[128,512]{1,0:T(8,128)(2,1)S(1)}) custom-call(f32[128,1024]{1,0:T(8,128)} %collective-permute-done.3.rows, bf16[1024,512]{1,0:T(8,128)(2,1)S(1)} %get-tuple-element.31.centers_high, bf16[1024,512]{1,0:T(8,128)(2,1)S(1)} %get-tuple-element.32.centers_low, ...), custom_call_target="tpu_custom_call" | custom-call | tf_op jit(solution)/shard_map/pallas_call | solution.py:179
  60.2 2.8 %collective-permute-start.8 = (f32[128,1024]{1,0:T(8,128)S(1)}, f32[128,1024]{1,0:T(8,128)S(1)}, u32[]{:S(2)}, u32[]{:S(2)}) collective-permute-start(f32[128,1024]{1,0:T(8,128)S(1)} %get-tuple-element.39), channel_id=1, source_target_pairs={{0,32},{16,112},{2,34},{18,114},{4,36},{20,116},{6,38},{22,118},{8... | collective-permute-start | bytes 1572872 | tf_op jit(solution)/shard_map/ppermute | solution.py:75
  63.1 1.8 %collective-permute-done.9 = f32[128,1024]{1,0:T(8,128)S(1)} collective-permute-done((f32[128,1024]{1,0:T(8,128)S(1)}, f32[128,1024]{1,0:T(8,128)S(1)}, u32[]{:S(2)}, u32[]{:S(2)}) %collective-permute-start.9) | collective-permute-done | bytes 524320 | tf_op jit(solution)/shard_map/ppermute | solution.py:75
  64.9 4.7 %collective-permute-done.8 = f32[128,1024]{1,0:T(8,128)S(1)} collective-permute-done((f32[128,1024]{1,0:T(8,128)S(1)}, f32[128,1024]{1,0:T(8,128)S(1)}, u32[]{:S(2)}, u32[]{:S(2)}) %collective-permute-start.8) | collective-permute-done | bytes 524320 | tf_op jit(solution)/shard_map/ppermute | solution.py:75
  71.6 2.6 %copy.7 = f32[256,1000]{1,0:T(8,128)} copy(f32[256,1000]{0,1:T(8,128)} %param.7) | data formatting | bytes 2048000 | tf_op args[2]
  74.1 1.8 %gather_fusion.1 = f32[4,1000]{1,0:T(4,128)S(1)} fusion(f32[256,1000]{1,0:T(8,128)} %copy.7, s32[1024]{0:T(1024)S(1)} %pad_clamp_fusion), kind=kCustom, calls=%fused_computation.1 | custom fusion | bytes 32016 | tf_op jit(solution)/shard_map/gather | solution.py:110
  80.1 7.6 %all-to-all-start.1 = ((f32[8,4,1024]{2,1,0:T(4,128)}), f32[8,4,1024]{2,1,0:T(4,128)S(1)}, u32[]{:S(2)}, u32[]{:S(2)}) async-start(f32[8,4,1024]{2,1,0:T(4,128)} %all_to_all.20), calls=%async_computation.1 | async-start | bytes 262144 | tf_op jit(solution)/shard_map/all_to_all | solution.py:79
  89.0 10.0 %all-to-all-done.1 = f32[8,4,1024]{2,1,0:T(4,128)S(1)} async-done(((f32[8,4,1024]{2,1,0:T(4,128)}), f32[8,4,1024]{2,1,0:T(4,128)S(1)}, u32[]{:S(2)}, u32[]{:S(2)}) %all-to-all-start.1) | async-done | bytes 131104 | tf_op jit(solution)/shard_map/all_to_all | solution.py:79
  99.8 4.1 %all-to-all-start.2 = ((f32[8,4,1024]{2,1,0:T(4,128)}), f32[8,4,1024]{2,1,0:T(4,128)S(1)}, u32[]{:S(2)}, u32[]{:S(2)}) async-start(f32[8,4,1024]{2,1,0:T(4,128)} %broadcast_in_dim.40), calls=%async_computation.2 | async-start | bytes 262144 | tf_op jit(solution)/shard_map/all_to_all | solution.py:79
  105.1 8.8 %all-to-all-done.2 = f32[8,4,1024]{2,1,0:T(4,128)S(1)} async-done(((f32[8,4,1024]{2,1,0:T(4,128)}), f32[8,4,1024]{2,1,0:T(4,128)S(1)}, u32[]{:S(2)}, u32[]{:S(2)}) %all-to-all-start.2) | async-done | bytes 131104 | tf_op jit(solution)/shard_map/all_to_all | solution.py:79
  115.5 2.9 %collective-permute-start.16 = (f32[32,1024]{1,0:T(8,128)S(1)}, f32[32,1024]{1,0:T(8,128)S(1)}, u32[]{:S(2)}, u32[]{:S(2)}) collective-permute-start(f32[32,1024]{1,0:T(8,128)S(1)} %all_to_all.23), channel_id=1, source_target_pairs={{0,4},{16,28},{2,6},{18,30},{4,0},{20,24},{6,2},{22,26},{8,12},{24... | collective-permute-start | bytes 393224 | tf_op jit(solution)/shard_map/ppermute | solution.py:75
  120.1 1.8 %collective-permute-done.16 = f32[32,1024]{1,0:T(8,128)S(1)} collective-permute-done((f32[32,1024]{1,0:T(8,128)S(1)}, f32[32,1024]{1,0:T(8,128)S(1)}, u32[]{:S(2)}, u32[]{:S(2)}) %collective-permute-start.16) | collective-permute-done | bytes 131104 | tf_op jit(solution)/shard_map/ppermute | solution.py:75
  121.8 2.6 %collective-permute-start.17 = (f32[128,1024]{1,0:T(8,128)S(1)}, f32[128,1024]{1,0:T(8,128)S(1)}, u32[]{:S(2)}, u32[]{:S(2)}) collective-permute-start(f32[128,1024]{1,0:T(8,128)S(1)} %constant_dynamic-update-slice_fusion.4.resid_0), channel_id=1, source_target_pairs={{0,32},{16,112},{2,34},{18,114},{4,36},{20,116},{6,38},{22,118},{8... | collective-permute-start | bytes 1572872 | tf_op jit(solution)/shard_map/ppermute | solution.py:75
  126.5 4.6 %collective-permute-done.17.resid_1 = f32[128,1024]{1,0:T(8,128)S(1)} collective-permute-done((f32[128,1024]{1,0:T(8,128)S(1)}, f32[128,1024]{1,0:T(8,128)S(1)}, u32[]{:S(2)}, u32[]{:S(2)}) %collective-permute-start.17) | collective-permute-done | bytes 524320 | tf_op jit(solution)/shard_map/ppermute | solution.py:75
  131.2 2.5 %collective-permute-done.18.resid_2 = f32[128,1024]{1,0:T(8,128)S(1)} collective-permute-done((f32[128,1024]{1,0:T(8,128)S(1)}, f32[128,1024]{1,0:T(8,128)S(1)}, u32[]{:S(2)}, u32[]{:S(2)}) %collective-permute-start.18) | collective-permute-done | bytes 524320 | tf_op jit(solution)/shard_map/ppermute | solution.py:75
  133.7 2.7 %shard_map.74 = (f32[1000,256]{1,0:T(8,128)}, f32[32,1000]{1,0:T(8,128)S(1)}) custom-call(s32[4,2]{1,0:T(4,128)S(1)} %multiply_add_fusion.source, s32[4,2]{1,0:T(4,128)S(1)} %add_multiply_fusion.target, f32[128,1024]{1,0:T(8,128)S(1)} %constant_dynamic-update-slice_fusion.4.resid_0, f32[128,1024]{1,0:T(8,128)S(1)} %collective-permute-done.17.resid_1, ...), custom_call_target="tpu_custom_call" | custom-call | tf_op jit(solution)/shard_map/pallas_call | solution.py:179
  136.4 4.3 %collective-permute-start.20 = (f32[1000,256]{1,0:T(8,128)}, f32[1000,256]{1,0:T(8,128)}, u32[]{:S(2)}, u32[]{:S(2)}) collective-permute-start(f32[1000,256]{1,0:T(8,128)} %get-tuple-element.52), channel_id=1, source_target_pairs={{0,16},{16,0},{2,18},{18,2},{4,20},{20,4},{6,22},{22,6},{8,24},{24... | collective-permute-start | bytes 3072008 | tf_op jit(solution)/shard_map/ppermute | solution.py:75
  145.1 1.7 %maximum_select_fusion = f32[64,1000]{1,0:T(8,128)} fusion(f32[32,1000]{1,0:T(8,128)} %collective-permute-done.21, f32[32,1000]{1,0:T(8,128)S(1)} %get-tuple-element.53, pred[]{:T(512)S(6)} %eq.56), kind=kLoop, calls=%fused_computation.5 | loop fusion | flops 192000 | bytes 512001 | tf_op jit(solution)/shard_map/jit(_where)/select_n | solution.py:283
  146.8 2.4 %fusion = f32[256,1000]{0,1:T(8,128)} fusion(f32[256,1000]{0,1:T(8,128)S(1)} %copy-done.1, f32[1000,256]{1,0:T(8,128)S(1)} %shard_map.73, f32[1000,256]{1,0:T(8,128)} %collective-permute-done.20), kind=kLoop, calls=%fused_computation.3 | loop fusion | flops 768000 | bytes 4096000 | tf_op jit(solution)/shard_map/transpose | solution.py:281
  (88 shorter events, 28.6 us)
Async XLA Ops:
  0.6 1.2 copy-start
  1.9 39.6 %copy-start.7 = (f32[256,1024]{1,0:T(8,128)S(1)}, f32[256,1024]{1,0:T(8,128)}, u32[]{:S(2)}) copy-start(f32[256,1024]{1,0:T(8,128)} %own_centers) | copy-start | bytes 3145732
  2.4 39.1 %copy-start.1 = (f32[256,1000]{0,1:T(8,128)S(1)}, f32[256,1000]{0,1:T(8,128)}, u32[]{:S(2)}) copy-start(f32[256,1000]{0,1:T(8,128)} %param.9) | copy-start | bytes 3072004
  25.8 15.7 %collective-permute-start.6 = (f32[256,1024]{1,0:T(8,128)}, f32[256,1024]{1,0:T(8,128)}, u32[]{:S(2)}, u32[]{:S(2)}) collective-permute-start(f32[256,1024]{1,0:T(8,128)} %own_centers), channel_id=1, source_target_pairs={{0,16},{16,0},{2,18},{18,2},{4,20},{20,4},{6,22},{22,6},{8,24},{24... | collective-permute-start | bytes 3145736 | tf_op jit(solution)/shard_map/ppermute | solution.py:75
  27.8 13.7 %collective-permute-start.7 = (f32[256,1000]{0,1:T(8,128)}, f32[256,1000]{0,1:T(8,128)}, u32[]{:S(2)}, u32[]{:S(2)}) collective-permute-start(f32[256,1000]{0,1:T(8,128)} %param.9), channel_id=1, source_target_pairs={{0,16},{16,0},{2,18},{18,2},{4,20},{20,4},{6,22},{22,6},{8,24},{24... | collective-permute-start | bytes 3072008 | tf_op jit(solution)/shard_map/ppermute | solution.py:75
  27.9 6.2 %collective-permute-start = (f32[32,1024]{1,0:T(8,128)S(1)}, f32[32,1024]{1,0:T(8,128)S(1)}, u32[]{:S(2)}, u32[]{:S(2)}) collective-permute-start(f32[32,1024]{1,0:T(8,128)S(1)} %all_to_all.19), channel_id=1, source_target_pairs={{0,64},{16,80},{2,66},{18,82},{4,68},{20,84},{6,70},{22,86},{8,72}... | collective-permute-start | bytes 393224 | tf_op jit(solution)/shard_map/ppermute | solution.py:75
  28.4 6.3 %collective-permute-start.1 = (f32[32,1024]{1,0:T(8,128)S(1)}, f32[32,1024]{1,0:T(8,128)S(1)}, u32[]{:S(2)}, u32[]{:S(2)}) collective-permute-start(f32[32,1024]{1,0:T(8,128)S(1)} %all_to_all.19), channel_id=1, source_target_pairs={{0,1},{16,17},{2,3},{18,19},{4,5},{20,21},{6,7},{22,23},{8,9},{24,... | collective-permute-start | bytes 393224 | tf_op jit(solution)/shard_map/ppermute | solution.py:75
  31.1 6.0 %collective-permute-start.2 = (f32[32,1024]{1,0:T(8,128)S(1)}, f32[32,1024]{1,0:T(8,128)S(1)}, u32[]{:S(2)}, u32[]{:S(2)}) collective-permute-start(f32[32,1024]{1,0:T(8,128)S(1)} %all_to_all.19), channel_id=1, source_target_pairs={{0,4},{16,28},{2,6},{18,30},{4,0},{20,24},{6,2},{22,26},{8,12},{24... | collective-permute-start | bytes 393224 | tf_op jit(solution)/shard_map/ppermute | solution.py:75
  37.7 9.6 %collective-permute-start.3 = (f32[128,1024]{1,0:T(8,128)}, f32[128,1024]{1,0:T(8,128)}, u32[]{:S(2)}, u32[]{:S(2)}) collective-permute-start(f32[128,1024]{1,0:T(8,128)} %constant_dynamic-update-slice_fusion.rows), channel_id=1, source_target_pairs={{0,32},{16,112},{2,34},{18,114},{4,36},{20,116},{6,38},{22,118},{8... | collective-permute-start | bytes 1572872 | tf_op jit(solution)/shard_map/ppermute | solution.py:75
  38.6 9.6 %collective-permute-start.4 = (f32[128,1024]{1,0:T(8,128)}, f32[128,1024]{1,0:T(8,128)}, u32[]{:S(2)}, u32[]{:S(2)}) collective-permute-start(f32[128,1024]{1,0:T(8,128)} %constant_dynamic-update-slice_fusion.rows), channel_id=1, source_target_pairs={{0,128},{16,145},{2,130},{18,147},{4,132},{20,149},{6,134},{22,151... | collective-permute-start | bytes 1572872 | tf_op jit(solution)/shard_map/ppermute | solution.py:75
  40.7 9.6 %collective-permute-start.5 = (f32[128,1024]{1,0:T(8,128)}, f32[128,1024]{1,0:T(8,128)}, u32[]{:S(2)}, u32[]{:S(2)}) collective-permute-start(f32[128,1024]{1,0:T(8,128)} %constant_dynamic-update-slice_fusion.rows), channel_id=1, source_target_pairs={{0,2},{16,30},{2,0},{18,20},{4,6},{20,18},{6,4},{22,24},{8,10},{24... | collective-permute-start | bytes 1572872 | tf_op jit(solution)/shard_map/ppermute | solution.py:75
  52.5 10.6 %collective-permute-start.10 = (f32[128,1024]{1,0:T(8,128)S(1)}, f32[128,1024]{1,0:T(8,128)S(1)}, u32[]{:S(2)}, u32[]{:S(2)}) collective-permute-start(f32[128,1024]{1,0:T(8,128)S(1)} %get-tuple-element.43), channel_id=1, source_target_pairs={{0,2},{16,30},{2,0},{18,20},{4,6},{20,18},{6,4},{22,24},{8,10},{24... | collective-permute-start | bytes 1572872 | tf_op jit(solution)/shard_map/ppermute | solution.py:75
  55.6 9.3 %collective-permute-start.9 = (f32[128,1024]{1,0:T(8,128)S(1)}, f32[128,1024]{1,0:T(8,128)S(1)}, u32[]{:S(2)}, u32[]{:S(2)}) collective-permute-start(f32[128,1024]{1,0:T(8,128)S(1)} %get-tuple-element.41), channel_id=1, source_target_pairs={{0,128},{16,145},{2,130},{18,147},{4,132},{20,149},{6,134},{22,151... | collective-permute-start | bytes 1572872 | tf_op jit(solution)/shard_map/ppermute | solution.py:75
  60.2 9.3 %collective-permute-start.8 = (f32[128,1024]{1,0:T(8,128)S(1)}, f32[128,1024]{1,0:T(8,128)S(1)}, u32[]{:S(2)}, u32[]{:S(2)}) collective-permute-start(f32[128,1024]{1,0:T(8,128)S(1)} %get-tuple-element.39), channel_id=1, source_target_pairs={{0,32},{16,112},{2,34},{18,114},{4,36},{20,116},{6,38},{22,118},{8... | collective-permute-start | bytes 1572872 | tf_op jit(solution)/shard_map/ppermute | solution.py:75
  69.7 1.8 %copy-start.8 = (f32[128,1024]{1,0:T(8,128)}, f32[128,1024]{1,0:T(8,128)S(1)}, u32[]{:S(2)}) copy-start(f32[128,1024]{1,0:T(8,128)S(1)} %add_add_fusion) | copy-start | bytes 1572868
  70.5 7.0 %collective-permute-start.13 = (f32[32,1024]{1,0:T(8,128)}, f32[32,1024]{1,0:T(8,128)S(1)}, u32[]{:S(2)}, u32[]{:S(2)}) collective-permute-start(f32[32,1024]{1,0:T(8,128)} %get-tuple-element.59), channel_id=1, source_target_pairs={{0,4},{16,28},{2,6},{18,30},{4,0},{20,24},{6,2},{22,26},{8,12},{24... | collective-permute-start | bytes 393224 | tf_op jit(solution)/shard_map/ppermute | solution.py:75
  71.5 6.9 %collective-permute-start.12 = (f32[32,1024]{1,0:T(8,128)}, f32[32,1024]{1,0:T(8,128)S(1)}, u32[]{:S(2)}, u32[]{:S(2)}) collective-permute-start(f32[32,1024]{1,0:T(8,128)} %get-tuple-element.60), channel_id=1, source_target_pairs={{0,1},{16,17},{2,3},{18,19},{4,5},{20,21},{6,7},{22,23},{8,9},{24,... | collective-permute-start | bytes 393224 | tf_op jit(solution)/shard_map/ppermute | solution.py:75
  71.5 6.9 %collective-permute-start.11 = (f32[32,1024]{1,0:T(8,128)S(1)}, f32[32,1024]{1,0:T(8,128)}, u32[]{:S(2)}, u32[]{:S(2)}) collective-permute-start(f32[32,1024]{1,0:T(8,128)S(1)} %get-tuple-element.58), channel_id=1, source_target_pairs={{0,64},{16,80},{2,66},{18,82},{4,68},{20,84},{6,70},{22,86},{8,72}... | collective-permute-start | bytes 393224 | tf_op jit(solution)/shard_map/ppermute | solution.py:75
  80.1 19.0 %all-to-all-start.1 = ((f32[8,4,1024]{2,1,0:T(4,128)}), f32[8,4,1024]{2,1,0:T(4,128)S(1)}, u32[]{:S(2)}, u32[]{:S(2)}) async-start(f32[8,4,1024]{2,1,0:T(4,128)} %all_to_all.20), calls=%async_computation.1 | async-start | bytes 262144 | tf_op jit(solution)/shard_map/all_to_all | solution.py:79
  99.8 14.2 %all-to-all-start.2 = ((f32[8,4,1024]{2,1,0:T(4,128)}), f32[8,4,1024]{2,1,0:T(4,128)S(1)}, u32[]{:S(2)}, u32[]{:S(2)}) async-start(f32[8,4,1024]{2,1,0:T(4,128)} %broadcast_in_dim.40), calls=%async_computation.2 | async-start | bytes 262144 | tf_op jit(solution)/shard_map/all_to_all | solution.py:79
  114.0 5.4 %collective-permute-start.14 = (f32[32,1024]{1,0:T(8,128)S(1)}, f32[32,1024]{1,0:T(8,128)S(1)}, u32[]{:S(2)}, u32[]{:S(2)}) collective-permute-start(f32[32,1024]{1,0:T(8,128)S(1)} %all_to_all.23), channel_id=1, source_target_pairs={{0,64},{16,80},{2,66},{18,82},{4,68},{20,84},{6,70},{22,86},{8,72}... | collective-permute-start | bytes 393224 | tf_op jit(solution)/shard_map/ppermute | solution.py:75
  114.7 11.0 %copy-start.9 = (bf16[512,512]{1,0:T(8,128)(2,1)S(1)}, bf16[512,512]{1,0:T(8,128)(2,1)}, u32[]{:S(2)}) copy-start(bf16[512,512]{1,0:T(8,128)(2,1)} %constant_dynamic-update-slice_fusion.13) | copy-start | bytes 1572868
  114.7 5.3 %collective-permute-start.15 = (f32[32,1024]{1,0:T(8,128)S(1)}, f32[32,1024]{1,0:T(8,128)S(1)}, u32[]{:S(2)}, u32[]{:S(2)}) collective-permute-start(f32[32,1024]{1,0:T(8,128)S(1)} %all_to_all.23), channel_id=1, source_target_pairs={{0,1},{16,17},{2,3},{18,19},{4,5},{20,21},{6,7},{22,23},{8,9},{24,... | collective-permute-start | bytes 393224 | tf_op jit(solution)/shard_map/ppermute | solution.py:75
  115.5 10.2 %copy-start.10 = (bf16[512,512]{1,0:T(8,128)(2,1)S(1)}, bf16[512,512]{1,0:T(8,128)(2,1)}, u32[]{:S(2)}) copy-start(bf16[512,512]{1,0:T(8,128)(2,1)} %constant_dynamic-update-slice_fusion.8) | copy-start | bytes 1572868
  115.5 6.3 %collective-permute-start.16 = (f32[32,1024]{1,0:T(8,128)S(1)}, f32[32,1024]{1,0:T(8,128)S(1)}, u32[]{:S(2)}, u32[]{:S(2)}) collective-permute-start(f32[32,1024]{1,0:T(8,128)S(1)} %all_to_all.23), channel_id=1, source_target_pairs={{0,4},{16,28},{2,6},{18,30},{4,0},{20,24},{6,2},{22,26},{8,12},{24... | collective-permute-start | bytes 393224 | tf_op jit(solution)/shard_map/ppermute | solution.py:75
  121.8 9.3 %collective-permute-start.17 = (f32[128,1024]{1,0:T(8,128)S(1)}, f32[128,1024]{1,0:T(8,128)S(1)}, u32[]{:S(2)}, u32[]{:S(2)}) collective-permute-start(f32[128,1024]{1,0:T(8,128)S(1)} %constant_dynamic-update-slice_fusion.4.resid_0), channel_id=1, source_target_pairs={{0,32},{16,112},{2,34},{18,114},{4,36},{20,116},{6,38},{22,118},{8... | collective-permute-start | bytes 1572872 | tf_op jit(solution)/shard_map/ppermute | solution.py:75
  124.4 9.2 %collective-permute-start.18 = (f32[128,1024]{1,0:T(8,128)S(1)}, f32[128,1024]{1,0:T(8,128)S(1)}, u32[]{:S(2)}, u32[]{:S(2)}) collective-permute-start(f32[128,1024]{1,0:T(8,128)S(1)} %constant_dynamic-update-slice_fusion.4.resid_0), channel_id=1, source_target_pairs={{0,128},{16,145},{2,130},{18,147},{4,132},{20,149},{6,134},{22,151... | collective-permute-start | bytes 1572872 | tf_op jit(solution)/shard_map/ppermute | solution.py:75
  124.5 9.2 %collective-permute-start.19 = (f32[128,1024]{1,0:T(8,128)S(1)}, f32[128,1024]{1,0:T(8,128)S(1)}, u32[]{:S(2)}, u32[]{:S(2)}) collective-permute-start(f32[128,1024]{1,0:T(8,128)S(1)} %constant_dynamic-update-slice_fusion.4.resid_0), channel_id=1, source_target_pairs={{0,2},{16,30},{2,0},{18,20},{4,6},{20,18},{6,4},{22,24},{8,10},{24... | collective-permute-start | bytes 1572872 | tf_op jit(solution)/shard_map/ppermute | solution.py:75
  133.7 2.8 %copy-start.2 = (f32[128,1024]{1,0:T(8,128)}, f32[128,1024]{1,0:T(8,128)S(1)}, u32[]{:S(2)}) copy-start(f32[128,1024]{1,0:T(8,128)S(1)} %collective-permute-done.18.resid_2) | copy-start | bytes 1572868
  133.7 2.8 %copy-start.4 = (f32[128,1024]{1,0:T(8,128)}, f32[128,1024]{1,0:T(8,128)S(1)}, u32[]{:S(2)}) copy-start(f32[128,1024]{1,0:T(8,128)S(1)} %collective-permute-done.19.resid_3) | copy-start | bytes 1572868
  136.4 10.4 %collective-permute-start.20 = (f32[1000,256]{1,0:T(8,128)}, f32[1000,256]{1,0:T(8,128)}, u32[]{:S(2)}, u32[]{:S(2)}) collective-permute-start(f32[1000,256]{1,0:T(8,128)} %get-tuple-element.52), channel_id=1, source_target_pairs={{0,16},{16,0},{2,18},{18,2},{4,20},{20,4},{6,22},{22,6},{8,24},{24... | collective-permute-start | bytes 3072008 | tf_op jit(solution)/shard_map/ppermute | solution.py:75
  140.8 4.3 %collective-permute-start.21 = (f32[32,1000]{1,0:T(8,128)S(1)}, f32[32,1000]{1,0:T(8,128)}, u32[]{:S(2)}, u32[]{:S(2)}) collective-permute-start(f32[32,1000]{1,0:T(8,128)S(1)} %get-tuple-element.53), channel_id=1, source_target_pairs={{0,16},{16,0},{2,18},{18,2},{4,20},{20,4},{6,22},{22,6},{8,24},{24... | collective-permute-start | bytes 384008 | tf_op jit(solution)/shard_map/ppermute | solution.py:75
  (4 other events, 3.8 us)

commit v9 on v7

--- a/solution.py
+++ b/solution.py
@@ -1,3 +1,4 @@
+import functools
 import math
 
 import jax
@@ -56,15 +57,23 @@
 
 
 SWAP = [(position(x, y, z, core), position(x, y, z, 1 - core)) for x, y, z, core in everywhere()]
-CLASSES = [
+PLANES = [
     [
-        position(2 * i + (low + z) % 2, 2 * k + (high + z) % 2, z, core)
-        for i in range(RING // 2)
-        for k in range(RING // 2)
-        for z in range(LEVELS)
+        position(2 * i + (low ^ odd), 2 * k + (high ^ odd), 2 * level + odd, core)
+        for i in range(2)
+        for k in range(2)
+        for odd in range(2)
     ]
     for low in range(2)
     for high in range(2)
+    for level in range(LEVELS // 2)
+    for core in range(2)
+]
+COLUMNS = [
+    [position(x, y, 2 * level + odd, core) for level in range(LEVELS // 2)]
+    for x in range(RING)
+    for y in range(RING)
+    for odd in range(2)
     for core in range(2)
 ]
 
@@ -89,9 +98,7 @@
 
 
 def quarters(own):
-    received = {way: permute(own, swap_pairs(way)) for way in WAYS}
-    received[0] = own
-    return received
+    return [own] + [permute(own, swap_pairs(way)) for way in WAYS]
 
 
 def pick(array, index):
@@ -141,18 +148,59 @@
     value[...] = product(kernel, (weights_high[...], weights_low[...]), ((1,), (0,)))
 
 
-def delta_kernel(resid_0, resid_1, resid_2, resid_3, high, low, delta, resid_high, resid_low):
+def delta_kernel(
+    source,
+    target,
+    resid_0,
+    resid_1,
+    resid_2,
+    resid_3,
+    high,
+    low,
+    other_delta,
+    own_delta,
+    mine,
+    resid_high,
+    resid_low,
+):
     quarter = resid_0.shape[0]
+    here = own_delta.shape[1]
     for i, resid in enumerate((resid_0, resid_1, resid_2, resid_3)):
         place = pl.ds(i * quarter, quarter)
         resid_high[place, :], resid_low[place, :] = parts(resid[...])
-    found = product((high[...], low[...]), (resid_high[...], resid_low[...]), ((0,), (0,)))
-    delta[...] = found.T[: delta.shape[0]]
-
-
-def call(kernel, outs, *operands, scratch=()):
+        for j in range(2):
+            for row in range(mine.shape[0] // 8):
+                found = resid[pl.ds(source[i, j] + row, 1), :]
+                mine[pl.ds(target[i, j] + row, 1), :] = found[:, : mine.shape[1]]
+    for start, delta in ((0, own_delta), (here, other_delta)):
+        place = pl.ds(start, here)
+        kernel = (high[:, place], low[:, place])
+        found = product(kernel, (resid_high[...], resid_low[...]), ((0,), (0,)))
+        delta[...] = found.T[: delta.shape[0]]
+
+
+def update_kernel(factor, weights, own_delta, other_delta, out):
+    out[...] = weights[...] - factor * (own_delta[...] + other_delta[...])
+
+
+def update(factor, *operands):
+    shape = operands[0].shape
+    spec = pl.BlockSpec((shape[0] // 5, shape[1]), lambda i: (i, 0))
+    return pl.pallas_call(
+        functools.partial(update_kernel, factor),
+        grid=(5,),
+        in_specs=[spec] * len(operands),
+        out_specs=spec,
+        out_shape=jax.ShapeDtypeStruct(shape, jnp.float32),
+        compiler_params=pltpu.CompilerParams(vmem_limit_bytes=VMEM_BYTES),
+    )(*operands)
+
+
+def call(kernel, outs, *operands, scratch=(), scalars=0):
     return pl.pallas_call(
         kernel,
+        in_specs=[pl.BlockSpec(memory_space=pltpu.SMEM)] * scalars
+        + [pl.BlockSpec(memory_space=pltpu.VMEM)] * (len(operands) - scalars),
         out_shape=[jax.ShapeDtypeStruct(shape, dtype) for shape, dtype in outs],
         scratch_shapes=[pltpu.VMEM(shape, dtype) for shape, dtype in scratch],
         compiler_params=pltpu.CompilerParams(vmem_limit_bytes=VMEM_BYTES),
@@ -178,9 +226,11 @@
     targets = jnp.pad(pick(train_labels, index), fill)
 
     column, centers, own_weights = lax.optimization_barrier(
-        (spread(rows, CLASSES), centers, weights)
-    )
-    quarter = len(CLASSES[0]) * own
+        (spread(spread(rows, COLUMNS), PLANES), centers, weights)
+    )
+    levels = LEVELS // 2
+    column_rows = levels * own
+    quarter = len(PLANES[0]) * column_rows
     pair = 2 * here
     held = call(
         prepare_kernel,
@@ -209,44 +259,38 @@
             *held,
         )
 
-    rows_of = quarters(column)
-    done = {0: quarter_of(rows_of[0])}
+    first_rows, *later = quarters(column)
+    done = [quarter_of(first_rows)]
     value = done[0][0]
-    later = [rows_of[way] for way in WAYS]
     *later, value = lax.optimization_barrier((*later, value))
     for way, part in zip(WAYS, later):
-        done[way] = quarter_of(part)
+        done.append(quarter_of(part))
         value = value + permute(done[way][0], swap_pairs(way))
-    high = jnp.concatenate([done[way][1] for way in range(4)], axis=0)
-    low = jnp.concatenate([done[way][2] for way in range(4)], axis=0)
-    value = scatter_sum(value, CLASSES)
-    resid_of = quarters(spread(value * scale - targets, CLASSES))
-    resid_list = [resid_of[way] for way in range(4)]
-
-    def delta_of(resid, low_end, high_end):
-        return call(
-            delta_kernel,
-            (((outputs, here), jnp.float32),),
-            *resid,
-            high[:, low_end:high_end],
-            low[:, low_end:high_end],
-            scratch=(((4 * quarter, lanes), jnp.bfloat16),) * 2,
-        )[0]
-
-    first = delta_of(resid_list, here, pair)
+    high = jnp.concatenate([part[1] for part in done], axis=0)
+    low = jnp.concatenate([part[2] for part in done], axis=0)
+    value = scatter_sum(value, PLANES) * scale
+    level = jnp.arange(levels)[:, None, None]
+    value = value - jnp.where(level == z // 2, targets[None], 0.0).reshape(value.shape)
+    partial_sums = spread(value, COLUMNS).reshape((levels,) + value.shape)
+    resid_list = quarters(spread(partial_sums.sum(axis=0), PLANES))
+
+    way, half = jnp.arange(4)[:, None], jnp.arange(2)[None, :]
+    source = (half * 4 + y_hi * 2 + z % 2) * column_rows + z // 2 * own + 0 * way
+    target = ((y_lo ^ way // 2) * RING + 2 * half + ((x ^ way) % 2)) * own
+    delta_out = ((outputs, here), jnp.float32)
+    first, second, mine = call(
+        delta_kernel,
+        (delta_out, delta_out, ((block // 2, outputs), jnp.float32)),
+        source.astype(jnp.int32),
+        target.astype(jnp.int32),
+        *resid_list,
+        high,
+        low,
+        scratch=(((4 * quarter, lanes), jnp.bfloat16),) * 2,
+        scalars=2,
+    )
     received = permute(first, SWAP)
-    *resid_list, first = lax.optimization_barrier((*resid_list, first))
-    second = delta_of(resid_list, 0, here)
-    new_weights = (weights.T - step_size / batch * (second + received)).T
-
-    resid_all = jnp.concatenate(resid_list, axis=0)
-    pieces = []
-    for low in range(2):
-        for column in range(RING):
-            way = (x + column) % 2 + 2 * ((y_lo + low) % 2)
-            slot = (column // 2 * (RING // 2) + y_hi) * LEVELS + z
-            pieces.append(lax.dynamic_slice_in_dim(resid_all, way * quarter + slot * own, own, 0))
-    mine = jnp.concatenate(pieces, axis=0)[:, :outputs]
+    new_weights = update(step_size / batch, weights.T, second, received).T
     theirs = permute(mine, SWAP)
     residual = jnp.where(
         core == 0,

time: 140 us -> 135 us (0.964)
  starting transfers between devices: 34.3 us -> 18.6 us
  blocking collectives: 29.9 us -> 44.9 us
  local copies, waits for them, and re-layouts: 18 us -> 11.5 us
  Pallas kernels: 9.02 us -> 11.6 us
    all_to_all x1 -> x3, blocking collectives: 29.9 us -> 44.9 us  [exchange(): lax.all_to_all(array, AXES, 0, 0, axis_index_groups=groups, tiled=True)]
    ppermute x13, starting transfers between devices: 21.2 us -> 10.9 us  [permute(): return lax.ppermute(array, AXES, pairs)]
    ppermute x13, waiting for transfers between devices: 16.6 us -> 26.1 us  [permute(): return lax.ppermute(array, AXES, pairs)]
    all_to_all x2, waiting for transfers between devices: 25.3 us -> 16.6 us  [exchange(): lax.all_to_all(array, AXES, 0, 0, axis_index_groups=groups, tiled=True)]
    all_to_all x2, starting transfers between devices: 13.2 us -> 7.75 us  [exchange(): lax.all_to_all(array, AXES, 0, 0, axis_index_groups=groups, tiled=True)]
    concatenate x4 -> x0, local copies, waits for them, and re-layouts: 3.72 us -> none  [the longest x1 3 us: per_device(): mine = jnp.concatenate(pieces, axis=0)[:, :outputs]]
    slice x2 -> x0, local copies, waits for them, and re-layouts: 2.83 us -> none  [the longest x1 1.77 us: delta_of(): low[:, low_end:high_end]]
    pallas_call x7, Pallas kernels: 9.02 us -> 11.6 us  [the longest x6 9.42 us: call(): pl.pallas_call(kernel, in_specs=[pl.BlockSpec(memory_space=pltpu.SMEM)] *...]
  transfers between devices with their start and end apart: 15 -> 15, of which waited for: 10 -> 11; matrix products, arithmetic and copies ran while one was open for 10% -> 6% of each run, Pallas kernels for 4% -> 2%
where the time goes in v9:
time: 135 us
  blocking collectives  44.9 us (33%)
  waiting for transfers between devices  42.7 us (32%)
  starting transfers between devices  18.6 us (14%)
  Pallas kernels  11.6 us (9%)
  local copies, waits for them, and re-layouts  11.5 us (9%)
  other arithmetic  4.46 us (3%)
    all_to_all x3, blocking collectives, exchange(): lax.all_to_all(array, AXES, 0, 0, axis_index_groups=groups, tiled=True)  44.9 us
    ppermute x13, waiting for transfers between devices, permute(): return lax.ppermute(array, AXES, pairs)  26.1 us
    all_to_all x2, waiting for transfers between devices, exchange(): lax.all_to_all(array, AXES, 0, 0, axis_index_groups=groups, tiled=True)  16.6 us
    ppermute x13, starting transfers between devices, permute(): return lax.ppermute(array, AXES, pairs)  10.9 us
    pallas_call x6, Pallas kernels, call(): pl.pallas_call(kernel, in_specs=[pl.BlockSpec(memory_space=pltpu.SMEM)] *...  9.42 us
    all_to_all x2, starting transfers between devices, exchange(): lax.all_to_all(array, AXES, 0, 0, axis_index_groups=groups, tiled=True)  7.75 us
    unnamed x15, local copies, waits for them, and re-layouts  5.93 us
  transfers between devices with their start and end apart: 15, of which 11 were waited for; matrix products, arithmetic and copies ran while one was open for 6% of the time, Pallas kernels for 2%

profile of v9, /device:TPU:1, one launch (start us, length us, event | category | flops | bytes accessed | tf_op | source)
XLA Modules:
  0.0 134.6 jit_solution(15946905088702543093)
XLA Ops:
  2.5 16.0 %all_to_all.38 = f32[4,4,1024]{2,1,0:T(4,128)S(1)} all-to-all(f32[4,4,1024]{2,1,0:T(4,128)S(1)} %broadcast_in_dim.61), channel_id=1, replica_groups={{0,4,8,12},{16,20,24,28},{2,6,10,14},{18,22,26,30},{128,132,136,140},{1..., dimensions={0} | all-to-all | bytes 131072 | tf_op jit(solution)/shard_map/all_to_all | solution.py:86
  18.5 16.5 %all_to_all.39 = f32[8,16,1024]{2,1,0:T(8,128)S(1)} all-to-all(f32[8,16,1024]{2,1,0:T(8,128)S(1)} %broadcast_in_dim.63), channel_id=1, replica_groups={{0,162,1,163,64,226,65,227},{16,178,17,179,80,242,81,243},{4,166,5,167,..., dimensions={0} | all-to-all | bytes 1048576 | tf_op jit(solution)/shard_map/all_to_all | solution.py:86
  35.0 3.2 %collective-permute-start.3 = (f32[256,1024]{1,0:T(8,128)S(1)}, f32[256,1024]{1,0:T(8,128)S(1)}, u32[]{:S(2)}, u32[]{:S(2)}) collective-permute-start(f32[256,1024]{1,0:T(8,128)S(1)} %copy-done.2), channel_id=1, source_target_pairs={{0,16},{16,0},{2,18},{18,2},{4,20},{20,4},{6,22},{22,6},{8,24},{24... | collective-permute-start | bytes 3145736 | tf_op jit(solution)/shard_map/ppermute | solution.py:82
  39.2 2.8 %collective-permute-done.4 = f32[256,1000]{0,1:T(8,128)S(1)} collective-permute-done((f32[256,1000]{0,1:T(8,128)S(1)}, f32[256,1000]{0,1:T(8,128)S(1)}, u32[]{:S(2)}, u32[]{:S(2)}) %collective-permute-start.4) | collective-permute-done | bytes 1024032 | tf_op jit(solution)/shard_map/ppermute | solution.py:82
  41.9 1.2 shard_map.68
  43.2 1.1 shard_map.69
  44.3 3.2 %collective-permute-done.rows = f32[128,1024]{1,0:T(8,128)S(1)} collective-permute-done((f32[128,1024]{1,0:T(8,128)S(1)}, f32[128,1024]{1,0:T(8,128)S(1)}, u32[]{:S(2)}, u32[]{:S(2)}) %collective-permute-start) | collective-permute-done | bytes 524320 | tf_op jit(solution)/shard_map/ppermute | solution.py:82
  48.0 1.1 shard_map.70
  49.1 1.1 shard_map.71
  50.3 1.1 shard_map.72
  51.4 2.4 %collective-permute-start.5 = (f32[128,1024]{1,0:T(8,128)S(1)}, f32[128,1024]{1,0:T(8,128)S(1)}, u32[]{:S(2)}, u32[]{:S(2)}) collective-permute-start(f32[128,1024]{1,0:T(8,128)S(1)} %get-tuple-element.40), channel_id=1, source_target_pairs={{0,32},{16,112},{2,34},{18,114},{4,36},{20,116},{6,38},{22,118},{8... | collective-permute-start | bytes 1572872 | tf_op jit(solution)/shard_map/ppermute | solution.py:82
  53.9 2.6 %collective-permute-start.6 = (f32[128,1024]{1,0:T(8,128)S(1)}, f32[128,1024]{1,0:T(8,128)S(1)}, u32[]{:S(2)}, u32[]{:S(2)}) collective-permute-start(f32[128,1024]{1,0:T(8,128)S(1)} %get-tuple-element.42), channel_id=1, source_target_pairs={{0,128},{16,145},{2,130},{18,147},{4,132},{20,149},{6,134},{22,151... | collective-permute-start | bytes 1572872 | tf_op jit(solution)/shard_map/ppermute | solution.py:82
  56.4 4.3 %collective-permute-done.5 = f32[128,1024]{1,0:T(8,128)S(1)} collective-permute-done((f32[128,1024]{1,0:T(8,128)S(1)}, f32[128,1024]{1,0:T(8,128)S(1)}, u32[]{:S(2)}, u32[]{:S(2)}) %collective-permute-start.5) | collective-permute-done | bytes 524320 | tf_op jit(solution)/shard_map/ppermute | solution.py:82
  60.8 2.3 %collective-permute-done.6 = f32[128,1024]{1,0:T(8,128)S(1)} collective-permute-done((f32[128,1024]{1,0:T(8,128)S(1)}, f32[128,1024]{1,0:T(8,128)S(1)}, u32[]{:S(2)}, u32[]{:S(2)}) %collective-permute-start.6) | collective-permute-done | bytes 524320 | tf_op jit(solution)/shard_map/ppermute | solution.py:82
  63.1 2.6 %collective-permute-done.7 = f32[128,1024]{1,0:T(8,128)S(1)} collective-permute-done((f32[128,1024]{1,0:T(8,128)S(1)}, f32[128,1024]{1,0:T(8,128)S(1)}, u32[]{:S(2)}, u32[]{:S(2)}) %collective-permute-start.7) | collective-permute-done | bytes 524320 | tf_op jit(solution)/shard_map/ppermute | solution.py:82
  66.6 3.5 %all-to-all-start.2 = ((f32[8,16,1024]{2,1,0:T(8,128)}), f32[8,16,1024]{2,1,0:T(8,128)S(1)}, u32[]{:S(2)}, u32[]{:S(2)}) async-start(f32[8,16,1024]{2,1,0:T(8,128)} %bitcast.4), calls=%async_computation.2 | async-start | bytes 1048576 | tf_op jit(solution)/shard_map/all_to_all | solution.py:86
  70.3 2.6 %copy.8 = f32[256,1000]{1,0:T(8,128)} copy(f32[256,1000]{0,1:T(8,128)} %param.7) | data formatting | bytes 2048000 | tf_op args[2]
  72.9 1.8 %gather_fusion.1 = f32[4,1000]{1,0:T(4,128)S(1)} fusion(f32[256,1000]{1,0:T(8,128)} %copy.8, s32[1024]{0:T(1024)S(1)} %pad_clamp_fusion), kind=kCustom, calls=%fused_computation.1 | custom fusion | bytes 32016 | tf_op jit(solution)/shard_map/gather | solution.py:105
  75.3 1.5 %broadcast_in_dim.68 = f32[16,1024]{1,0:T(8,128)} reshape(f32[4,4,1024]{2,1,0:T(4,128)} %broadcast_in_dim.67) | data formatting | bytes 131072 | tf_op jit(solution)/shard_map/jit(_where)/broadcast_in_dim | solution.py:273
  76.8 5.2 %all-to-all-done.2 = f32[8,16,1024]{2,1,0:T(8,128)S(1)} async-done(((f32[8,16,1024]{2,1,0:T(8,128)}), f32[8,16,1024]{2,1,0:T(8,128)S(1)}, u32[]{:S(2)}, u32[]{:S(2)}) %all-to-all-start.2) | async-done | bytes 524320 | tf_op jit(solution)/shard_map/all_to_all | solution.py:86
  82.6 0.9 select_subtract_fusion
  83.6 12.4 %all_to_all.40 = f32[4,16,1024]{2,1,0:T(8,128)S(1)} all-to-all(f32[4,16,1024]{2,1,0:T(8,128)S(1)} %broadcast_in_dim.70), channel_id=1, replica_groups={{0,4,8,12},{16,20,24,28},{2,6,10,14},{18,22,26,30},{128,132,136,140},{1..., dimensions={0} | all-to-all | bytes 524288 | tf_op jit(solution)/shard_map/all_to_all | solution.py:86
  96.9 4.3 %all-to-all-start.4 = ((f32[8,16,1024]{2,1,0:T(8,128)}), f32[8,16,1024]{2,1,0:T(8,128)S(1)}, u32[]{:S(2)}, u32[]{:S(2)}) async-start(f32[8,16,1024]{2,1,0:T(8,128)} %broadcast_in_dim.71), calls=%async_computation.4 | async-start | bytes 1048576 | tf_op jit(solution)/shard_map/all_to_all | solution.py:86
  101.1 11.4 %all-to-all-done.4 = f32[8,16,1024]{2,1,0:T(8,128)S(1)} async-done(((f32[8,16,1024]{2,1,0:T(8,128)}), f32[8,16,1024]{2,1,0:T(8,128)S(1)}, u32[]{:S(2)}, u32[]{:S(2)}) %all-to-all-start.4) | async-done | bytes 524320 | tf_op jit(solution)/shard_map/all_to_all | solution.py:86
  112.7 1.0 pad_maximum_fusion
  113.7 8.1 %collective-permute-done.10.resid_3 = f32[128,1024]{1,0:T(8,128)S(1)} collective-permute-done((f32[128,1024]{1,0:T(8,128)S(1)}, f32[128,1024]{1,0:T(8,128)S(1)}, u32[]{:S(2)}, u32[]{:S(2)}) %collective-permute-start.10) | collective-permute-done | bytes 524320 | tf_op jit(solution)/shard_map/ppermute | solution.py:82
  121.8 3.6 %shard_map.73 = (f32[1000,256]{1,0:T(8,128)}, f32[1000,256]{1,0:T(8,128)S(1)}, f32[32,1000]{1,0:T(8,128)S(1)}) custom-call(s32[4,2]{1,0:T(4,128)S(1)} %add.112.source, s32[4,2]{1,0:T(4,128)S(1)} %add_multiply_fusion.target, f32[128,1024]{1,0:T(8,128)S(1)} %bitcast.16, f32[128,1024]{1,0:T(8,128)S(1)} %collective-permute-done.8.resid_1, ...), custom_call_target="tpu_custom_call" | custom-call | tf_op jit(solution)/shard_map/pallas_call | solution.py:200
  125.4 1.0 copy-done.3
  126.4 1.7 %collective-permute-start.11 = (f32[1000,256]{1,0:T(8,128)}, f32[1000,256]{1,0:T(8,128)S(1)}, u32[]{:S(2)}, u32[]{:S(2)}) collective-permute-start(f32[1000,256]{1,0:T(8,128)} %get-tuple-element.54), channel_id=1, source_target_pairs={{0,16},{16,0},{2,18},{18,2},{4,20},{20,4},{6,22},{22,6},{8,24},{24... | collective-permute-start | bytes 3072008 | tf_op jit(solution)/shard_map/ppermute | solution.py:82
  128.2 2.3 %collective-permute-done.12 = f32[32,1000]{1,0:T(8,128)S(1)} collective-permute-done((f32[32,1000]{1,0:T(8,128)S(1)}, f32[32,1000]{1,0:T(8,128)S(1)}, u32[]{:S(2)}, u32[]{:S(2)}) %collective-permute-start.12) | collective-permute-done | bytes 128032 | tf_op jit(solution)/shard_map/ppermute | solution.py:82
  131.2 1.2 copy-done.4
  132.4 2.2 %shard_map.74 = f32[1000,256]{1,0:T(8,128)} custom-call(f32[1000,256]{1,0:T(8,128)S(1)} %bitcast.8, f32[1000,256]{1,0:T(8,128)S(1)} %copy-done.4, f32[1000,256]{1,0:T(8,128)S(1)} %collective-permute-done.11.other_delta), custom_call_target="tpu_custom_call" | custom-call | tf_op jit(solution)/shard_map/pallas_call | solution.py:189
  (49 shorter events, 7.4 us)
Async XLA Ops:
  0.6 1.2 copy-start
  0.7 0.7 copy-start.6
  1.9 33.2 %copy-start.2 = (f32[256,1024]{1,0:T(8,128)S(1)}, f32[256,1024]{1,0:T(8,128)}, u32[]{:S(2)}) copy-start(f32[256,1024]{1,0:T(8,128)} %own_centers) | copy-start | bytes 3145732
  2.4 35.7 %copy-start.1 = (f32[256,1000]{0,1:T(8,128)S(1)}, f32[256,1000]{0,1:T(8,128)}, u32[]{:S(2)}) copy-start(f32[256,1000]{0,1:T(8,128)} %param.9) | copy-start | bytes 3072004
  35.0 6.9 %collective-permute-start.3 = (f32[256,1024]{1,0:T(8,128)S(1)}, f32[256,1024]{1,0:T(8,128)S(1)}, u32[]{:S(2)}, u32[]{:S(2)}) collective-permute-start(f32[256,1024]{1,0:T(8,128)S(1)} %copy-done.2), channel_id=1, source_target_pairs={{0,16},{16,0},{2,18},{18,2},{4,20},{20,4},{6,22},{22,6},{8,24},{24... | collective-permute-start | bytes 3145736 | tf_op jit(solution)/shard_map/ppermute | solution.py:82
  38.2 3.7 %collective-permute-start.4 = (f32[256,1000]{0,1:T(8,128)S(1)}, f32[256,1000]{0,1:T(8,128)S(1)}, u32[]{:S(2)}, u32[]{:S(2)}) collective-permute-start(f32[256,1000]{0,1:T(8,128)S(1)} %copy-done.1), channel_id=1, source_target_pairs={{0,16},{16,0},{2,18},{18,2},{4,20},{20,4},{6,22},{22,6},{8,24},{24... | collective-permute-start | bytes 3072008 | tf_op jit(solution)/shard_map/ppermute | solution.py:82
  38.3 9.2 %collective-permute-start = (f32[128,1024]{1,0:T(8,128)S(1)}, f32[128,1024]{1,0:T(8,128)S(1)}, u32[]{:S(2)}, u32[]{:S(2)}) collective-permute-start(f32[128,1024]{1,0:T(8,128)S(1)} %bitcast.9), channel_id=1, source_target_pairs={{0,32},{16,112},{2,34},{18,114},{4,36},{20,116},{6,38},{22,118},{8... | collective-permute-start | bytes 1572872 | tf_op jit(solution)/shard_map/ppermute | solution.py:82
  38.6 9.2 %collective-permute-start.1 = (f32[128,1024]{1,0:T(8,128)S(1)}, f32[128,1024]{1,0:T(8,128)S(1)}, u32[]{:S(2)}, u32[]{:S(2)}) collective-permute-start(f32[128,1024]{1,0:T(8,128)S(1)} %bitcast.10), channel_id=1, source_target_pairs={{0,128},{16,145},{2,130},{18,147},{4,132},{20,149},{6,134},{22,151... | collective-permute-start | bytes 1572872 | tf_op jit(solution)/shard_map/ppermute | solution.py:82
  38.7 9.2 %collective-permute-start.2 = (f32[128,1024]{1,0:T(8,128)S(1)}, f32[128,1024]{1,0:T(8,128)S(1)}, u32[]{:S(2)}, u32[]{:S(2)}) collective-permute-start(f32[128,1024]{1,0:T(8,128)S(1)} %bitcast.11), channel_id=1, source_target_pairs={{0,2},{16,30},{2,0},{18,20},{4,6},{20,18},{6,4},{22,24},{8,10},{24... | collective-permute-start | bytes 1572872 | tf_op jit(solution)/shard_map/ppermute | solution.py:82
  51.4 15.2 %copy-start.5 = (bf16[128,512]{1,0:T(8,128)(2,1)}, bf16[128,512]{1,0:T(8,128)(2,1)S(1)}, u32[]{:S(2)}) copy-start(bf16[128,512]{1,0:T(8,128)(2,1)S(1)} %get-tuple-element.52) | copy-start | bytes 393220
  51.4 9.3 %collective-permute-start.5 = (f32[128,1024]{1,0:T(8,128)S(1)}, f32[128,1024]{1,0:T(8,128)S(1)}, u32[]{:S(2)}, u32[]{:S(2)}) collective-permute-start(f32[128,1024]{1,0:T(8,128)S(1)} %get-tuple-element.40), channel_id=1, source_target_pairs={{0,32},{16,112},{2,34},{18,114},{4,36},{20,116},{6,38},{22,118},{8... | collective-permute-start | bytes 1572872 | tf_op jit(solution)/shard_map/ppermute | solution.py:82
  53.9 9.2 %collective-permute-start.6 = (f32[128,1024]{1,0:T(8,128)S(1)}, f32[128,1024]{1,0:T(8,128)S(1)}, u32[]{:S(2)}, u32[]{:S(2)}) collective-permute-start(f32[128,1024]{1,0:T(8,128)S(1)} %get-tuple-element.42), channel_id=1, source_target_pairs={{0,128},{16,145},{2,130},{18,147},{4,132},{20,149},{6,134},{22,151... | collective-permute-start | bytes 1572872 | tf_op jit(solution)/shard_map/ppermute | solution.py:82
  56.4 9.2 %collective-permute-start.7 = (f32[128,1024]{1,0:T(8,128)S(1)}, f32[128,1024]{1,0:T(8,128)S(1)}, u32[]{:S(2)}, u32[]{:S(2)}) collective-permute-start(f32[128,1024]{1,0:T(8,128)S(1)} %get-tuple-element.44), channel_id=1, source_target_pairs={{0,2},{16,30},{2,0},{18,20},{4,6},{20,18},{6,4},{22,24},{8,10},{24... | collective-permute-start | bytes 1572872 | tf_op jit(solution)/shard_map/ppermute | solution.py:82
  66.6 15.4 %all-to-all-start.2 = ((f32[8,16,1024]{2,1,0:T(8,128)}), f32[8,16,1024]{2,1,0:T(8,128)S(1)}, u32[]{:S(2)}, u32[]{:S(2)}) async-start(f32[8,16,1024]{2,1,0:T(8,128)} %bitcast.4), calls=%async_computation.2 | async-start | bytes 1048576 | tf_op jit(solution)/shard_map/all_to_all | solution.py:86
  96.9 15.7 %all-to-all-start.4 = ((f32[8,16,1024]{2,1,0:T(8,128)}), f32[8,16,1024]{2,1,0:T(8,128)S(1)}, u32[]{:S(2)}, u32[]{:S(2)}) async-start(f32[8,16,1024]{2,1,0:T(8,128)} %broadcast_in_dim.71), calls=%async_computation.4 | async-start | bytes 1048576 | tf_op jit(solution)/shard_map/all_to_all | solution.py:86
  112.6 9.2 %collective-permute-start.10 = (f32[128,1024]{1,0:T(8,128)S(1)}, f32[128,1024]{1,0:T(8,128)S(1)}, u32[]{:S(2)}, u32[]{:S(2)}) collective-permute-start(f32[128,1024]{1,0:T(8,128)S(1)} %bitcast.13), channel_id=1, source_target_pairs={{0,2},{16,30},{2,0},{18,20},{4,6},{20,18},{6,4},{22,24},{8,10},{24... | collective-permute-start | bytes 1572872 | tf_op jit(solution)/shard_map/ppermute | solution.py:82
  112.6 9.2 %collective-permute-start.8 = (f32[128,1024]{1,0:T(8,128)S(1)}, f32[128,1024]{1,0:T(8,128)S(1)}, u32[]{:S(2)}, u32[]{:S(2)}) collective-permute-start(f32[128,1024]{1,0:T(8,128)S(1)} %bitcast.14), channel_id=1, source_target_pairs={{0,32},{16,112},{2,34},{18,114},{4,36},{20,116},{6,38},{22,118},{8... | collective-permute-start | bytes 1572872 | tf_op jit(solution)/shard_map/ppermute | solution.py:82
  112.6 9.2 %collective-permute-start.9 = (f32[128,1024]{1,0:T(8,128)S(1)}, f32[128,1024]{1,0:T(8,128)S(1)}, u32[]{:S(2)}, u32[]{:S(2)}) collective-permute-start(f32[128,1024]{1,0:T(8,128)S(1)} %bitcast.15), channel_id=1, source_target_pairs={{0,128},{16,145},{2,130},{18,147},{4,132},{20,149},{6,134},{22,151... | collective-permute-start | bytes 1572872 | tf_op jit(solution)/shard_map/ppermute | solution.py:82
  125.4 1.0 copy-start.3
  126.4 4.8 %collective-permute-start.11 = (f32[1000,256]{1,0:T(8,128)}, f32[1000,256]{1,0:T(8,128)S(1)}, u32[]{:S(2)}, u32[]{:S(2)}) collective-permute-start(f32[1000,256]{1,0:T(8,128)} %get-tuple-element.54), channel_id=1, source_target_pairs={{0,16},{16,0},{2,18},{18,2},{4,20},{20,4},{6,22},{22,6},{8,24},{24... | collective-permute-start | bytes 3072008 | tf_op jit(solution)/shard_map/ppermute | solution.py:82
  128.2 2.3 %collective-permute-start.12 = (f32[32,1000]{1,0:T(8,128)S(1)}, f32[32,1000]{1,0:T(8,128)S(1)}, u32[]{:S(2)}, u32[]{:S(2)}) collective-permute-start(f32[32,1000]{1,0:T(8,128)S(1)} %get-tuple-element.55), channel_id=1, source_target_pairs={{0,16},{16,0},{2,18},{18,2},{4,20},{20,4},{6,22},{22,6},{8,24},{24... | collective-permute-start | bytes 384008 | tf_op jit(solution)/shard_map/ppermute | solution.py:82
  131.2 1.2 copy-start.4

commit v10 on v9

--- a/solution.py
+++ b/solution.py
@@ -69,13 +69,25 @@
     for level in range(LEVELS // 2)
     for core in range(2)
 ]
-COLUMNS = [
-    [position(x, y, 2 * level + odd, core) for level in range(LEVELS // 2)]
-    for x in range(RING)
-    for y in range(RING)
-    for odd in range(2)
+CLASSES = [
+    [
+        position(2 * i + (low ^ odd), 2 * k + (high ^ odd), 2 * level + odd, core)
+        for i in range(2)
+        for k in range(2)
+        for odd in range(2)
+        for level in range(LEVELS // 2)
+    ]
+    for low in range(2)
+    for high in range(2)
     for core in range(2)
 ]
+
+
+def along_z(step):
+    return [
+        (position(x, y, z, core), position(x, y, (z + step) % LEVELS, core))
+        for x, y, z, core in everywhere()
+    ]
 
 
 def permute(array, pairs):
@@ -90,11 +102,6 @@
     count = len(groups[0])
     copies = jnp.broadcast_to(array[None], (count,) + array.shape)
     return exchange(copies.reshape((-1,) + array.shape[1:]), groups)
-
-
-def scatter_sum(array, groups):
-    count = len(groups[0])
-    return exchange(array, groups).reshape((count, -1) + array.shape[1:]).sum(axis=0)
 
 
 def quarters(own):
@@ -148,39 +155,55 @@
     value[...] = product(kernel, (weights_high[...], weights_low[...]), ((1,), (0,)))
 
 
-def delta_kernel(
-    source,
-    target,
-    resid_0,
-    resid_1,
-    resid_2,
-    resid_3,
-    high,
-    low,
-    other_delta,
-    own_delta,
-    mine,
-    resid_high,
-    resid_low,
-):
-    quarter = resid_0.shape[0]
-    here = own_delta.shape[1]
-    for i, resid in enumerate((resid_0, resid_1, resid_2, resid_3)):
-        place = pl.ds(i * quarter, quarter)
-        resid_high[place, :], resid_low[place, :] = parts(resid[...])
-        for j in range(2):
-            for row in range(mine.shape[0] // 8):
-                found = resid[pl.ds(source[i, j] + row, 1), :]
-                mine[pl.ds(target[i, j] + row, 1), :] = found[:, : mine.shape[1]]
-    for start, delta in ((0, own_delta), (here, other_delta)):
-        place = pl.ds(start, here)
-        kernel = (high[:, place], low[:, place])
-        found = product(kernel, (resid_high[...], resid_low[...]), ((0,), (0,)))
-        delta[...] = found.T[: delta.shape[0]]
-
-
-def update_kernel(factor, weights, own_delta, other_delta, out):
-    out[...] = weights[...] - factor * (own_delta[...] + other_delta[...])
+def targets_kernel(own, index, place, labels, out, turned):
+    rows, outputs = index.shape[0], labels.shape[0]
+    width = labels.shape[1]
+    zeros = jnp.zeros((out.shape[1] - outputs, width), jnp.float32)
+    turned[...] = jnp.concatenate([labels[...], zeros], axis=0).T
+    out[...] = jnp.zeros_like(out)
+    start = place[3] // 2 * own
+    for row in range(rows):
+        out[pl.ds(start + row, 1), :] = turned[pl.ds(index[row], 1), :]
+
+
+def plane_kernel(scale, sums, targets, out):
+    total = sums[0]
+    for i in range(1, sums.shape[0]):
+        total = total + sums[i]
+    out[...] = total * scale - targets[...]
+
+
+def delta_kernel(factor, place, *refs):
+    resid_refs, high_refs, low_refs = refs[:4], refs[4:8], refs[8:12]
+    weights, other_delta, new_weights, mine, resid_high, resid_low, high, low = refs[12:]
+    quarter = resid_refs[0].shape[0]
+    outputs, here = weights.shape
+    own = mine.shape[0] // 8
+    x, y_lo, y_hi, z = place[0], place[1], place[2], place[3]
+    for way in range(4):
+        resid = resid_refs[way]
+        rows = pl.ds(way * quarter, quarter)
+        resid_high[rows, :], resid_low[rows, :] = parts(resid[...])
+        high[rows, :], low[rows, :] = high_refs[way][...], low_refs[way][...]
+        for half in range(2):
+            source = (half * 4 + y_hi * 2 + z % 2) * (quarter // 8) + z // 2 * own
+            target = ((y_lo + way // 2) % 2 * RING + 2 * half + (x + way) % 2) * own
+            for row in range(own):
+                mine[pl.ds(target + row, 1), :] = resid[pl.ds(source + row, 1), :][:, :outputs]
+
+    def delta_of(start):
+        columns = pl.ds(start, here)
+        found = product(
+            (high[:, columns], low[:, columns]), (resid_high[...], resid_low[...]), ((0,), (0,))
+        )
+        return found.T[:outputs]
+
+    other_delta[...] = delta_of(here)
+    new_weights[...] = weights[...] - factor * delta_of(0)
+
+
+def update_kernel(factor, weights, delta, out):
+    out[...] = weights[...] - factor * delta[...]
 
 
 def update(factor, *operands):
@@ -196,7 +219,7 @@
     )(*operands)
 
 
-def call(kernel, outs, *operands, scratch=(), scalars=0):
+def call(kernel, outs, *operands, scratch=(), scalars=0, products=0):
     return pl.pallas_call(
         kernel,
         in_specs=[pl.BlockSpec(memory_space=pltpu.SMEM)] * scalars
@@ -204,6 +227,9 @@
         out_shape=[jax.ShapeDtypeStruct(shape, dtype) for shape, dtype in outs],
         scratch_shapes=[pltpu.VMEM(shape, dtype) for shape, dtype in scratch],
         compiler_params=pltpu.CompilerParams(vmem_limit_bytes=VMEM_BYTES),
+        cost_estimate=pl.CostEstimate(
+            flops=2 * products, bytes_accessed=VMEM_BYTES // 8, transcendentals=0
+        ),
     )(*operands)
 
 
@@ -222,15 +248,14 @@
     index = lax.dynamic_slice_in_dim(batch_index, start, own, 0)
     rows = pick(train_features, index)
     lanes = -(-outputs // LANE) * LANE
-    fill = ((0, 0), (0, lanes - outputs))
-    targets = jnp.pad(pick(train_labels, index), fill)
-
-    column, centers, own_weights = lax.optimization_barrier(
-        (spread(spread(rows, COLUMNS), PLANES), centers, weights)
-    )
-    levels = LEVELS // 2
-    column_rows = levels * own
-    quarter = len(PLANES[0]) * column_rows
+    place = jnp.stack([x, y_lo, y_hi, z]).astype(jnp.int32)
+    rows, place = lax.optimization_barrier((rows, place))
+
+    column, centers, own_weights, train_labels = lax.optimization_barrier(
+        (spread(rows, CLASSES), centers, weights, train_labels)
+    )
+    column_rows = LEVELS // 2 * own
+    quarter = len(CLASSES[0]) * own
     pair = 2 * here
     held = call(
         prepare_kernel,
@@ -257,40 +282,47 @@
             ),
             part,
             *held,
+            products=3 * quarter * pair * (features + lanes),
         )
 
     first_rows, *later = quarters(column)
     done = [quarter_of(first_rows)]
     value = done[0][0]
-    *later, value = lax.optimization_barrier((*later, value))
+    (targets,) = call(
+        functools.partial(targets_kernel, own),
+        (((column_rows, lanes), jnp.float32),),
+        index,
+        place,
+        train_labels.T,
+        scratch=(((train_labels.shape[0], lanes), jnp.float32),),
+        scalars=2,
+    )
+    *later, value, targets = lax.optimization_barrier((*later, value, targets))
     for way, part in zip(WAYS, later):
         done.append(quarter_of(part))
         value = value + permute(done[way][0], swap_pairs(way))
-    high = jnp.concatenate([part[1] for part in done], axis=0)
-    low = jnp.concatenate([part[2] for part in done], axis=0)
-    value = scatter_sum(value, PLANES) * scale
-    level = jnp.arange(levels)[:, None, None]
-    value = value - jnp.where(level == z // 2, targets[None], 0.0).reshape(value.shape)
-    partial_sums = spread(value, COLUMNS).reshape((levels,) + value.shape)
-    resid_list = quarters(spread(partial_sums.sum(axis=0), PLANES))
-
-    way, half = jnp.arange(4)[:, None], jnp.arange(2)[None, :]
-    source = (half * 4 + y_hi * 2 + z % 2) * column_rows + z // 2 * own + 0 * way
-    target = ((y_lo ^ way // 2) * RING + 2 * half + ((x ^ way) % 2)) * own
+    sums = exchange(value, PLANES).reshape(len(PLANES[0]), column_rows, lanes)
+    (value,) = call(
+        functools.partial(plane_kernel, scale), (((column_rows, lanes), jnp.float32),), sums, targets
+    )
+    opposite, up, down = (permute(value, along_z(step)) for step in (4, 2, -2))
+    resid_list = quarters(spread((value + opposite) + (up + down), PLANES))
+
+    factor = step_size / batch
     delta_out = ((outputs, here), jnp.float32)
-    first, second, mine = call(
-        delta_kernel,
+    first, partly, mine = call(
+        functools.partial(delta_kernel, factor),
         (delta_out, delta_out, ((block // 2, outputs), jnp.float32)),
-        source.astype(jnp.int32),
-        target.astype(jnp.int32),
+        place,
         *resid_list,
-        high,
-        low,
-        scratch=(((4 * quarter, lanes), jnp.bfloat16),) * 2,
-        scalars=2,
-    )
-    received = permute(first, SWAP)
-    new_weights = update(step_size / batch, weights.T, second, received).T
+        *(part[1] for part in done),
+        *(part[2] for part in done),
+        weights.T,
+        scratch=(((4 * quarter, lanes), jnp.bfloat16),) * 2 + (((4 * quarter, pair), jnp.bfloat16),) * 2,
+        scalars=1,
+        products=3 * 4 * quarter * pair * lanes,
+    )
+    new_weights = update(factor, partly, permute(first, SWAP)).T
     theirs = permute(mine, SWAP)
     residual = jnp.where(
         core == 0,

time: 135 us -> 128 us (0.948)
  waiting for transfers between devices: 42.7 us -> 24.9 us
  blocking collectives: 44.9 us -> 60.4 us
  local copies, waits for them, and re-layouts: 11.5 us -> 3.56 us
  starting transfers between devices: 18.6 us -> 24.3 us
  other arithmetic: 4.46 us -> 1.06 us
    all_to_all x2 -> x0, waiting for transfers between devices: 16.6 us -> none  [exchange(): lax.all_to_all(array, AXES, 0, 0, axis_index_groups=groups, tiled=True)]
    all_to_all x3, blocking collectives: 44.9 us -> 60.4 us  [exchange(): lax.all_to_all(array, AXES, 0, 0, axis_index_groups=groups, tiled=True)]
    ppermute x13 -> x16, starting transfers between devices: 10.9 us -> 24.3 us  [permute(): return lax.ppermute(array, AXES, pairs)]
    all_to_all x2 -> x0, starting transfers between devices: 7.75 us -> none  [exchange(): lax.all_to_all(array, AXES, 0, 0, axis_index_groups=groups, tiled=True)]
    unnamed x15 -> x10, local copies, waits for them, and re-layouts: 5.93 us -> 2.67 us
    broadcast_in_dim x4 -> x0, local copies, waits for them, and re-layouts: 2.29 us -> none  [per_device(): jnp.where(level == z // 2, targets[None], 0.0).reshape(value.shape)]
    gather x2 -> x1, local copies, waits for them, and re-layouts: 2.36 us -> 0.56 us  [pick(): return array.at[index].get(mode='promise_in_bounds')]
    ppermute x13 -> x16, waiting for transfers between devices: 26.1 us -> 24.9 us  [permute(): return lax.ppermute(array, AXES, pairs)]
  transfers between devices with their start and end apart: 15 -> 16, of which waited for: 11 -> 11; matrix products, arithmetic and copies ran while one was open for 6% -> 1% of each run, Pallas kernels for 2% -> 4%
where the time goes in v10:
time: 128 us; the launch traced here: 127 us
  blocking collectives  60.4 us (47%)
  waiting for transfers between devices  24.9 us (19%)
  starting transfers between devices  24.3 us (19%)
  Pallas kernels  12.2 us (10%)
  local copies, waits for them, and re-layouts  3.56 us (3%)
    all_to_all x3, blocking collectives, exchange(): lax.all_to_all(array, AXES, 0, 0, axis_index_groups=groups, tiled=True)  60.4 us
    ppermute x16, waiting for transfers between devices, permute(): return lax.ppermute(array, AXES, pairs)  24.9 us
    ppermute x16, starting transfers between devices, permute(): return lax.ppermute(array, AXES, pairs)  24.3 us
    pallas_call x8, Pallas kernels, call(): pl.pallas_call(kernel, in_specs=[pl.BlockSpec(memory_space=pltpu.SMEM)] *...  10 us
    unnamed x10, local copies, waits for them, and re-layouts  2.67 us
  transfers between devices with their start and end apart: 16, of which 11 were waited for; matrix products, arithmetic and copies ran while one was open for 1% of the time, Pallas kernels for 4%

profile of v10, /device:TPU:1, one launch (start us, length us, event | category | flops | bytes accessed | tf_op | source)
XLA Modules:
  0.0 127.2 jit_solution(1008408720994270349)
XLA Ops:
  0.7 0.7 copy-done.4
  2.7 32.0 %all_to_all.26 = f32[32,4,1024]{2,1,0:T(4,128)S(1)} all-to-all(f32[32,4,1024]{2,1,0:T(4,128)S(1)} %broadcast_in_dim.7), channel_id=1, replica_groups={{0,4,8,12,162,166,170,174,1,5,9,13,163,167,171,175,64,68,72,76,226,230,..., dimensions={0} | all-to-all | bytes 1048576 | tf_op jit(solution)/shard_map/all_to_all | solution.py:98
  34.8 1.6 %collective-permute-start.3 = (f32[256,1024]{1,0:T(8,128)S(1)}, f32[256,1024]{1,0:T(8,128)S(1)}, u32[]{:S(2)}, u32[]{:S(2)}) collective-permute-start(f32[256,1024]{1,0:T(8,128)S(1)} %copy-done.1), channel_id=1, source_target_pairs={{0,16},{16,0},{2,18},{18,2},{4,20},{20,4},{6,22},{22,6},{8,24},{24... | collective-permute-start | bytes 3145736 | tf_op jit(solution)/shard_map/ppermute | solution.py:94
  36.5 1.5 %collective-permute-start = (f32[128,1024]{1,0:T(8,128)S(1)}, f32[128,1024]{1,0:T(8,128)S(1)}, u32[]{:S(2)}, u32[]{:S(2)}) collective-permute-start(f32[128,1024]{1,0:T(8,128)S(1)} %all_to_all.18.rows), channel_id=1, source_target_pairs={{0,32},{16,112},{2,34},{18,114},{4,36},{20,116},{6,38},{22,118},{8... | collective-permute-start | bytes 1572872 | tf_op jit(solution)/shard_map/ppermute | solution.py:94
  38.3 3.6 %collective-permute-start.2 = (f32[128,1024]{1,0:T(8,128)S(1)}, f32[128,1024]{1,0:T(8,128)S(1)}, u32[]{:S(2)}, u32[]{:S(2)}) collective-permute-start(f32[128,1024]{1,0:T(8,128)S(1)} %all_to_all.18.rows), channel_id=1, source_target_pairs={{0,2},{16,30},{2,0},{18,20},{4,6},{20,18},{6,4},{22,24},{8,10},{24... | collective-permute-start | bytes 1572872 | tf_op jit(solution)/shard_map/ppermute | solution.py:94
  41.9 1.2 copy-done.2
  43.1 0.9 shard_map.70.targets
  44.3 1.2 shard_map.68
  45.6 1.1 shard_map.69
  47.2 1.3 collective-permute-done.2.rows
  48.5 1.2 shard_map.71
  49.7 1.8 %collective-permute-start.5 = (f32[128,1024]{1,0:T(8,128)S(1)}, f32[128,1024]{1,0:T(8,128)S(1)}, u32[]{:S(2)}, u32[]{:S(2)}) collective-permute-start(f32[128,1024]{1,0:T(8,128)S(1)} %get-tuple-element.47), channel_id=1, source_target_pairs={{0,32},{16,112},{2,34},{18,114},{4,36},{20,116},{6,38},{22,118},{8... | collective-permute-start | bytes 1572872 | tf_op jit(solution)/shard_map/ppermute | solution.py:94
  51.5 1.2 shard_map.72
  52.6 1.0 collective-permute-start.6
  53.7 1.2 shard_map.73
  54.8 2.5 %collective-permute-start.7 = (f32[128,1024]{1,0:T(8,128)S(1)}, f32[128,1024]{1,0:T(8,128)S(1)}, u32[]{:S(2)}, u32[]{:S(2)}) collective-permute-start(f32[128,1024]{1,0:T(8,128)S(1)} %get-tuple-element.51), channel_id=1, source_target_pairs={{0,2},{16,30},{2,0},{18,20},{4,6},{20,18},{6,4},{22,24},{8,10},{24... | collective-permute-start | bytes 1572872 | tf_op jit(solution)/shard_map/ppermute | solution.py:94
  57.3 1.7 %collective-permute-done.5 = f32[128,1024]{1,0:T(8,128)S(1)} collective-permute-done((f32[128,1024]{1,0:T(8,128)S(1)}, f32[128,1024]{1,0:T(8,128)S(1)}, u32[]{:S(2)}, u32[]{:S(2)}) %collective-permute-start.5) | collective-permute-done | bytes 524320 | tf_op jit(solution)/shard_map/ppermute | solution.py:94
  59.0 3.0 %collective-permute-done.6 = f32[128,1024]{1,0:T(8,128)S(1)} collective-permute-done((f32[128,1024]{1,0:T(8,128)S(1)}, f32[128,1024]{1,0:T(8,128)S(1)}, u32[]{:S(2)}, u32[]{:S(2)}) %collective-permute-start.6) | collective-permute-done | bytes 524320 | tf_op jit(solution)/shard_map/ppermute | solution.py:94
  62.0 2.2 %collective-permute-done.7 = f32[128,1024]{1,0:T(8,128)S(1)} collective-permute-done((f32[128,1024]{1,0:T(8,128)S(1)}, f32[128,1024]{1,0:T(8,128)S(1)}, u32[]{:S(2)}, u32[]{:S(2)}) %collective-permute-start.7) | collective-permute-done | bytes 524320 | tf_op jit(solution)/shard_map/ppermute | solution.py:94
  64.3 14.9 %all_to_all.27.sums = f32[8,16,1024]{2,1,0:T(8,128)S(1)} all-to-all(f32[8,16,1024]{2,1,0:T(8,128)S(1)} %bitcast.19), channel_id=1, replica_groups={{0,162,1,163,64,226,65,227},{16,178,17,179,80,242,81,243},{4,166,5,167,..., dimensions={0} | all-to-all | bytes 1048576 | tf_op jit(solution)/shard_map/all_to_all | solution.py:98
  79.2 4.5 %collective-permute-start.10 = (f32[16,1024]{1,0:T(8,128)S(1)}, f32[16,1024]{1,0:T(8,128)S(1)}, u32[]{:S(2)}, u32[]{:S(2)}) collective-permute-start(f32[16,1024]{1,0:T(8,128)S(1)} %shard_map.74), channel_id=1, source_target_pairs={{0,12},{16,28},{2,14},{18,30},{4,0},{20,16},{6,2},{22,18},{8,4},{2... | collective-permute-start | bytes 196616 | tf_op jit(solution)/shard_map/ppermute | solution.py:94
  83.7 2.4 %collective-permute-start.8 = (f32[16,1024]{1,0:T(8,128)S(1)}, f32[16,1024]{1,0:T(8,128)S(1)}, u32[]{:S(2)}, u32[]{:S(2)}) collective-permute-start(f32[16,1024]{1,0:T(8,128)S(1)} %shard_map.74), channel_id=1, source_target_pairs={{0,8},{16,24},{2,10},{18,26},{4,12},{20,28},{6,14},{22,30},{8,0},{... | collective-permute-start | bytes 196616 | tf_op jit(solution)/shard_map/ppermute | solution.py:94
  86.2 2.5 %collective-permute-done.10 = f32[16,1024]{1,0:T(8,128)S(1)} collective-permute-done((f32[16,1024]{1,0:T(8,128)S(1)}, f32[16,1024]{1,0:T(8,128)S(1)}, u32[]{:S(2)}, u32[]{:S(2)}) %collective-permute-start.10) | collective-permute-done | bytes 65568 | tf_op jit(solution)/shard_map/ppermute | solution.py:94
  88.6 4.9 %collective-permute-done.8 = f32[16,1024]{1,0:T(8,128)S(1)} collective-permute-done((f32[16,1024]{1,0:T(8,128)S(1)}, f32[16,1024]{1,0:T(8,128)S(1)}, u32[]{:S(2)}, u32[]{:S(2)}) %collective-permute-start.8) | collective-permute-done | bytes 65568 | tf_op jit(solution)/shard_map/ppermute | solution.py:94
  93.6 13.6 %all_to_all.28 = f32[8,16,1024]{2,1,0:T(8,128)S(1)} all-to-all(f32[8,16,1024]{2,1,0:T(8,128)S(1)} %broadcast_in_dim.8), channel_id=1, replica_groups={{0,162,1,163,64,226,65,227},{16,178,17,179,80,242,81,243},{4,166,5,167,..., dimensions={0} | all-to-all | bytes 1048576 | tf_op jit(solution)/shard_map/all_to_all | solution.py:98
  107.5 3.0 %collective-permute-start.13 = (f32[128,1024]{1,0:T(8,128)S(1)}, f32[128,1024]{1,0:T(8,128)S(1)}, u32[]{:S(2)}, u32[]{:S(2)}) collective-permute-start(f32[128,1024]{1,0:T(8,128)S(1)} %bitcast.17), channel_id=1, source_target_pairs={{0,2},{16,30},{2,0},{18,20},{4,6},{20,18},{6,4},{22,24},{8,10},{24... | collective-permute-start | bytes 1572872 | tf_op jit(solution)/shard_map/ppermute | solution.py:94
  110.5 5.9 %collective-permute-done.11.refs_1_ = f32[128,1024]{1,0:T(8,128)S(1)} collective-permute-done((f32[128,1024]{1,0:T(8,128)S(1)}, f32[128,1024]{1,0:T(8,128)S(1)}, u32[]{:S(2)}, u32[]{:S(2)}) %collective-permute-start.11) | collective-permute-done | bytes 524320 | tf_op jit(solution)/shard_map/ppermute | solution.py:94
  117.1 3.2 %shard_map.75 = (f32[1000,256]{1,0:T(8,128)}, f32[1000,256]{1,0:T(8,128)S(1)}, f32[32,1000]{1,0:T(8,128)S(1)}) custom-call(s32[4]{0:T(128)S(1)} %pad_add_fusion.place, f32[128,1024]{1,0:T(8,128)S(1)} %bitcast.18, f32[128,1024]{1,0:T(8,128)S(1)} %collective-permute-done.11.refs_1_, f32[128,1024]{1,0:T(8,128)S(1)} %collective-permute-done.12.refs_2_, ...), custom_call_target="tpu_custom_call" | custom-call | flops 1610612736 | bytes 2097152 | tf_op jit(solution)/shard_map/pallas_call | solution.py:223
  120.3 1.7 %collective-permute-start.14 = (f32[1000,256]{1,0:T(8,128)}, f32[1000,256]{1,0:T(8,128)S(1)}, u32[]{:S(2)}, u32[]{:S(2)}) collective-permute-start(f32[1000,256]{1,0:T(8,128)} %get-tuple-element.62), channel_id=1, source_target_pairs={{0,16},{16,0},{2,18},{18,2},{4,20},{20,4},{6,22},{22,6},{8,24},{24... | collective-permute-start | bytes 3072008 | tf_op jit(solution)/shard_map/ppermute | solution.py:94
  122.1 2.3 %collective-permute-done.15 = f32[32,1000]{1,0:T(8,128)S(1)} collective-permute-done((f32[32,1000]{1,0:T(8,128)S(1)}, f32[32,1000]{1,0:T(8,128)S(1)}, u32[]{:S(2)}, u32[]{:S(2)}) %collective-permute-start.15) | collective-permute-done | bytes 128032 | tf_op jit(solution)/shard_map/ppermute | solution.py:94
  124.4 0.7 maximum_select_fusion
  125.1 2.1 %shard_map.76 = f32[1000,256]{1,0:T(8,128)} custom-call(f32[1000,256]{1,0:T(8,128)S(1)} %get-tuple-element.61.weights, f32[1000,256]{1,0:T(8,128)S(1)} %collective-permute-done.14.delta), custom_call_target="tpu_custom_call" | custom-call | tf_op jit(solution)/shard_map/pallas_call | solution.py:212
  (32 shorter events, 3.8 us)
Async XLA Ops:
  0.6 1.2 copy-start
  0.7 0.7 copy-start.4
  2.6 32.2 %copy-start.1 = (f32[256,1024]{1,0:T(8,128)S(1)}, f32[256,1024]{1,0:T(8,128)}, u32[]{:S(2)}) copy-start(f32[256,1024]{1,0:T(8,128)} %own_centers) | copy-start | bytes 3145732
  34.8 9.2 %collective-permute-start.3 = (f32[256,1024]{1,0:T(8,128)S(1)}, f32[256,1024]{1,0:T(8,128)S(1)}, u32[]{:S(2)}, u32[]{:S(2)}) collective-permute-start(f32[256,1024]{1,0:T(8,128)S(1)} %copy-done.1), channel_id=1, source_target_pairs={{0,16},{16,0},{2,18},{18,2},{4,20},{20,4},{6,22},{22,6},{8,24},{24... | collective-permute-start | bytes 3145736 | tf_op jit(solution)/shard_map/ppermute | solution.py:94
  36.4 7.6 %collective-permute-start.4 = (f32[256,1000]{0,1:T(8,128)}, f32[256,1000]{0,1:T(8,128)S(1)}, u32[]{:S(2)}, u32[]{:S(2)}) collective-permute-start(f32[256,1000]{0,1:T(8,128)} %param.9), channel_id=1, source_target_pairs={{0,16},{16,0},{2,18},{18,2},{4,20},{20,4},{6,22},{22,6},{8,24},{24... | collective-permute-start | bytes 3072008 | tf_op jit(solution)/shard_map/ppermute | solution.py:94
  36.5 10.2 %collective-permute-start = (f32[128,1024]{1,0:T(8,128)S(1)}, f32[128,1024]{1,0:T(8,128)S(1)}, u32[]{:S(2)}, u32[]{:S(2)}) collective-permute-start(f32[128,1024]{1,0:T(8,128)S(1)} %all_to_all.18.rows), channel_id=1, source_target_pairs={{0,32},{16,112},{2,34},{18,114},{4,36},{20,116},{6,38},{22,118},{8... | collective-permute-start | bytes 1572872 | tf_op jit(solution)/shard_map/ppermute | solution.py:94
  38.0 9.2 %collective-permute-start.1 = (f32[128,1024]{1,0:T(8,128)S(1)}, f32[128,1024]{1,0:T(8,128)S(1)}, u32[]{:S(2)}, u32[]{:S(2)}) collective-permute-start(f32[128,1024]{1,0:T(8,128)S(1)} %all_to_all.18.rows), channel_id=1, source_target_pairs={{0,128},{16,145},{2,130},{18,147},{4,132},{20,149},{6,134},{22,151... | collective-permute-start | bytes 1572872 | tf_op jit(solution)/shard_map/ppermute | solution.py:94
  38.3 10.2 %collective-permute-start.2 = (f32[128,1024]{1,0:T(8,128)S(1)}, f32[128,1024]{1,0:T(8,128)S(1)}, u32[]{:S(2)}, u32[]{:S(2)}) collective-permute-start(f32[128,1024]{1,0:T(8,128)S(1)} %all_to_all.18.rows), channel_id=1, source_target_pairs={{0,2},{16,30},{2,0},{18,20},{4,6},{20,18},{6,4},{22,24},{8,10},{24... | collective-permute-start | bytes 1572872 | tf_op jit(solution)/shard_map/ppermute | solution.py:94
  41.9 1.2 copy-start.2
  43.1 1.2 copy-start.3
  49.7 9.3 %collective-permute-start.5 = (f32[128,1024]{1,0:T(8,128)S(1)}, f32[128,1024]{1,0:T(8,128)S(1)}, u32[]{:S(2)}, u32[]{:S(2)}) collective-permute-start(f32[128,1024]{1,0:T(8,128)S(1)} %get-tuple-element.47), channel_id=1, source_target_pairs={{0,32},{16,112},{2,34},{18,114},{4,36},{20,116},{6,38},{22,118},{8... | collective-permute-start | bytes 1572872 | tf_op jit(solution)/shard_map/ppermute | solution.py:94
  52.6 9.3 %collective-permute-start.6 = (f32[128,1024]{1,0:T(8,128)S(1)}, f32[128,1024]{1,0:T(8,128)S(1)}, u32[]{:S(2)}, u32[]{:S(2)}) collective-permute-start(f32[128,1024]{1,0:T(8,128)S(1)} %get-tuple-element.49), channel_id=1, source_target_pairs={{0,128},{16,145},{2,130},{18,147},{4,132},{20,149},{6,134},{22,151... | collective-permute-start | bytes 1572872 | tf_op jit(solution)/shard_map/ppermute | solution.py:94
  54.8 9.3 %collective-permute-start.7 = (f32[128,1024]{1,0:T(8,128)S(1)}, f32[128,1024]{1,0:T(8,128)S(1)}, u32[]{:S(2)}, u32[]{:S(2)}) collective-permute-start(f32[128,1024]{1,0:T(8,128)S(1)} %get-tuple-element.51), channel_id=1, source_target_pairs={{0,2},{16,30},{2,0},{18,20},{4,6},{20,18},{6,4},{22,24},{8,10},{24... | collective-permute-start | bytes 1572872 | tf_op jit(solution)/shard_map/ppermute | solution.py:94
  79.2 9.4 %collective-permute-start.10 = (f32[16,1024]{1,0:T(8,128)S(1)}, f32[16,1024]{1,0:T(8,128)S(1)}, u32[]{:S(2)}, u32[]{:S(2)}) collective-permute-start(f32[16,1024]{1,0:T(8,128)S(1)} %shard_map.74), channel_id=1, source_target_pairs={{0,12},{16,28},{2,14},{18,30},{4,0},{20,16},{6,2},{22,18},{8,4},{2... | collective-permute-start | bytes 196616 | tf_op jit(solution)/shard_map/ppermute | solution.py:94
  83.7 9.8 %collective-permute-start.8 = (f32[16,1024]{1,0:T(8,128)S(1)}, f32[16,1024]{1,0:T(8,128)S(1)}, u32[]{:S(2)}, u32[]{:S(2)}) collective-permute-start(f32[16,1024]{1,0:T(8,128)S(1)} %shard_map.74), channel_id=1, source_target_pairs={{0,8},{16,24},{2,10},{18,26},{4,12},{20,28},{6,14},{22,30},{8,0},{... | collective-permute-start | bytes 196616 | tf_op jit(solution)/shard_map/ppermute | solution.py:94
  86.1 7.4 %collective-permute-start.9 = (f32[16,1024]{1,0:T(8,128)S(1)}, f32[16,1024]{1,0:T(8,128)S(1)}, u32[]{:S(2)}, u32[]{:S(2)}) collective-permute-start(f32[16,1024]{1,0:T(8,128)S(1)} %shard_map.74), channel_id=1, source_target_pairs={{0,4},{16,20},{2,6},{18,22},{4,8},{20,24},{6,10},{22,26},{8,12},{2... | collective-permute-start | bytes 196616 | tf_op jit(solution)/shard_map/ppermute | solution.py:94
  107.2 9.2 %collective-permute-start.11 = (f32[128,1024]{1,0:T(8,128)S(1)}, f32[128,1024]{1,0:T(8,128)S(1)}, u32[]{:S(2)}, u32[]{:S(2)}) collective-permute-start(f32[128,1024]{1,0:T(8,128)S(1)} %bitcast.15), channel_id=1, source_target_pairs={{0,32},{16,112},{2,34},{18,114},{4,36},{20,116},{6,38},{22,118},{8... | collective-permute-start | bytes 1572872 | tf_op jit(solution)/shard_map/ppermute | solution.py:94
  107.5 9.2 %collective-permute-start.12 = (f32[128,1024]{1,0:T(8,128)S(1)}, f32[128,1024]{1,0:T(8,128)S(1)}, u32[]{:S(2)}, u32[]{:S(2)}) collective-permute-start(f32[128,1024]{1,0:T(8,128)S(1)} %bitcast.16), channel_id=1, source_target_pairs={{0,128},{16,145},{2,130},{18,147},{4,132},{20,149},{6,134},{22,151... | collective-permute-start | bytes 1572872 | tf_op jit(solution)/shard_map/ppermute | solution.py:94
  107.5 9.6 %collective-permute-start.13 = (f32[128,1024]{1,0:T(8,128)S(1)}, f32[128,1024]{1,0:T(8,128)S(1)}, u32[]{:S(2)}, u32[]{:S(2)}) collective-permute-start(f32[128,1024]{1,0:T(8,128)S(1)} %bitcast.17), channel_id=1, source_target_pairs={{0,2},{16,30},{2,0},{18,20},{4,6},{20,18},{6,4},{22,24},{8,10},{24... | collective-permute-start | bytes 1572872 | tf_op jit(solution)/shard_map/ppermute | solution.py:94
  120.3 4.8 %collective-permute-start.14 = (f32[1000,256]{1,0:T(8,128)}, f32[1000,256]{1,0:T(8,128)S(1)}, u32[]{:S(2)}, u32[]{:S(2)}) collective-permute-start(f32[1000,256]{1,0:T(8,128)} %get-tuple-element.62), channel_id=1, source_target_pairs={{0,16},{16,0},{2,18},{18,2},{4,20},{20,4},{6,22},{22,6},{8,24},{24... | collective-permute-start | bytes 3072008 | tf_op jit(solution)/shard_map/ppermute | solution.py:94
  122.1 2.3 %collective-permute-start.15 = (f32[32,1000]{1,0:T(8,128)S(1)}, f32[32,1000]{1,0:T(8,128)S(1)}, u32[]{:S(2)}, u32[]{:S(2)}) collective-permute-start(f32[32,1000]{1,0:T(8,128)S(1)} %get-tuple-element.63), channel_id=1, source_target_pairs={{0,16},{16,0},{2,18},{18,2},{4,20},{20,4},{6,22},{22,6},{8,24},{24... | collective-permute-start | bytes 384008 | tf_op jit(solution)/shard_map/ppermute | solution.py:94

commit v11 on v10

--- a/solution.py
+++ b/solution.py
@@ -69,16 +69,14 @@
     for level in range(LEVELS // 2)
     for core in range(2)
 ]
-CLASSES = [
+LINES = [
     [
-        position(2 * i + (low ^ odd), 2 * k + (high ^ odd), 2 * level + odd, core)
-        for i in range(2)
-        for k in range(2)
-        for odd in range(2)
-        for level in range(LEVELS // 2)
+        position(x, first if high == 0 else RING - 1 - first, z, core)
+        for high in range(2)
+        for z in range(LEVELS)
     ]
-    for low in range(2)
-    for high in range(2)
+    for x in range(RING)
+    for first in range(2)
     for core in range(2)
 ]
 
@@ -155,6 +153,17 @@
     value[...] = product(kernel, (weights_high[...], weights_low[...]), ((1,), (0,)))
 
 
+def order_kernel(own, found, out):
+    levels = LEVELS // 2
+    for i in range(2):
+        for k in range(2):
+            for odd in range(2):
+                for level in range(levels):
+                    source = (((k * levels + level) * 2 + odd) * 2 + i) * own
+                    target = (((i * 2 + k) * 2 + odd) * levels + level) * own
+                    out[target : target + own, :] = found[source : source + own, :]
+
+
 def targets_kernel(own, index, place, labels, out, turned):
     rows, outputs = index.shape[0], labels.shape[0]
     width = labels.shape[1]
@@ -173,50 +182,35 @@
     out[...] = total * scale - targets[...]
 
 
-def delta_kernel(factor, place, *refs):
+def delta_kernel(start, place, *refs):
     resid_refs, high_refs, low_refs = refs[:4], refs[4:8], refs[8:12]
-    weights, other_delta, new_weights, mine, resid_high, resid_low, high, low = refs[12:]
+    delta, *mine, resid_high, resid_low, high, low = refs[12:]
     quarter = resid_refs[0].shape[0]
-    outputs, here = weights.shape
-    own = mine.shape[0] // 8
+    outputs, here = delta.shape
+    columns = pl.ds(start, here)
     x, y_lo, y_hi, z = place[0], place[1], place[2], place[3]
     for way in range(4):
         resid = resid_refs[way]
         rows = pl.ds(way * quarter, quarter)
         resid_high[rows, :], resid_low[rows, :] = parts(resid[...])
-        high[rows, :], low[rows, :] = high_refs[way][...], low_refs[way][...]
-        for half in range(2):
-            source = (half * 4 + y_hi * 2 + z % 2) * (quarter // 8) + z // 2 * own
-            target = ((y_lo + way // 2) % 2 * RING + 2 * half + (x + way) % 2) * own
-            for row in range(own):
-                mine[pl.ds(target + row, 1), :] = resid[pl.ds(source + row, 1), :][:, :outputs]
-
-    def delta_of(start):
-        columns = pl.ds(start, here)
-        found = product(
-            (high[:, columns], low[:, columns]), (resid_high[...], resid_low[...]), ((0,), (0,))
-        )
-        return found.T[:outputs]
-
-    other_delta[...] = delta_of(here)
-    new_weights[...] = weights[...] - factor * delta_of(0)
-
-
-def update_kernel(factor, weights, delta, out):
-    out[...] = weights[...] - factor * delta[...]
-
-
-def update(factor, *operands):
-    shape = operands[0].shape
-    spec = pl.BlockSpec((shape[0] // 5, shape[1]), lambda i: (i, 0))
-    return pl.pallas_call(
-        functools.partial(update_kernel, factor),
-        grid=(5,),
-        in_specs=[spec] * len(operands),
-        out_specs=spec,
-        out_shape=jax.ShapeDtypeStruct(shape, jnp.float32),
-        compiler_params=pltpu.CompilerParams(vmem_limit_bytes=VMEM_BYTES),
-    )(*operands)
+        high[rows, :], low[rows, :] = high_refs[way][:, columns], low_refs[way][:, columns]
+        for out in mine:
+            own = out.shape[0] // 8
+            for half in range(2):
+                source = (half * 4 + y_hi * 2 + z % 2) * (quarter // 8) + z // 2 * own
+                target = ((y_lo + way // 2) % 2 * RING + 2 * half + (x + way) % 2) * own
+                for row in range(own):
+                    out[pl.ds(target + row, 1), :] = resid[pl.ds(source + row, 1), :][:, :outputs]
+    found = product((high[...], low[...]), (resid_high[...], resid_low[...]), ((0,), (0,)))
+    delta[...] = found.T[:outputs]
+
+
+def update_kernel(factor, place, weights, own_delta, other_delta, mine, theirs, out, residual):
+    rows = mine.shape[0]
+    core = place[4]
+    residual[pl.ds(pl.multiple_of(core * rows, 8), rows), :] = mine[...]
+    residual[pl.ds(pl.multiple_of((1 - core) * rows, 8), rows), :] = theirs[...]
+    out[...] = weights[...] - factor * (own_delta[...] + other_delta[...])
 
 
 def call(kernel, outs, *operands, scratch=(), scalars=0, products=0):
@@ -246,16 +240,29 @@
     own = block // (2 * RING * 2)
     start = (core * 2 * RING + y_lo * RING + x) * own
     index = lax.dynamic_slice_in_dim(batch_index, start, own, 0)
-    rows = pick(train_features, index)
     lanes = -(-outputs // LANE) * LANE
-    place = jnp.stack([x, y_lo, y_hi, z]).astype(jnp.int32)
+    half_block = block // 2
+    order = jnp.arange(half_block)
+    high, odd, far, row = order // (4 * own), order // (2 * own) % 2, order // own % 2, order % own
+    turn = odd ^ z % 2
+    wanted = ((y_lo ^ y_hi ^ high ^ turn) * RING + 2 * far + (x % 2 ^ turn)) * own + row
+    match = (core * half_block + wanted)[:, None] == jnp.arange(block)[None, :]
+    wanted_index = jnp.sum(jnp.where(match, batch_index[None, :], 0), axis=1)
+    rows = pick(train_features, wanted_index)
+    place = jnp.stack([x, y_lo, y_hi, z, core]).astype(jnp.int32)
     rows, place = lax.optimization_barrier((rows, place))
-
-    column, centers, own_weights, train_labels = lax.optimization_barrier(
-        (spread(rows, CLASSES), centers, weights, train_labels)
+    sent = jnp.broadcast_to(
+        rows.reshape(2, 1, 2, 2 * own, features), (2, LEVELS // 2, 2, 2 * own, features)
+    )
+    found = exchange(sent.reshape(-1, features), LINES)
+    found, centers, own_weights, train_labels = lax.optimization_barrier(
+        (found, centers, weights, train_labels)
+    )
+    (column,) = call(
+        functools.partial(order_kernel, own), ((found.shape, jnp.float32),), found
     )
     column_rows = LEVELS // 2 * own
-    quarter = len(CLASSES[0]) * own
+    quarter = found.shape[0]
     pair = 2 * here
     held = call(
         prepare_kernel,
@@ -297,10 +304,13 @@
         scratch=(((train_labels.shape[0], lanes), jnp.float32),),
         scalars=2,
     )
-    *later, value, targets = lax.optimization_barrier((*later, value, targets))
+    sums = []
     for way, part in zip(WAYS, later):
+        part, value, targets = lax.optimization_barrier((part, value, targets))
         done.append(quarter_of(part))
-        value = value + permute(done[way][0], swap_pairs(way))
+        sums.append(permute(done[way][0], swap_pairs(way)))
+    for found in sums:
+        value = value + found
     sums = exchange(value, PLANES).reshape(len(PLANES[0]), column_rows, lanes)
     (value,) = call(
         functools.partial(plane_kernel, scale), (((column_rows, lanes), jnp.float32),), sums, targets
@@ -308,28 +318,36 @@
     opposite, up, down = (permute(value, along_z(step)) for step in (4, 2, -2))
     resid_list = quarters(spread((value + opposite) + (up + down), PLANES))
 
-    factor = step_size / batch
-    delta_out = ((outputs, here), jnp.float32)
-    first, partly, mine = call(
-        functools.partial(delta_kernel, factor),
-        (delta_out, delta_out, ((block // 2, outputs), jnp.float32)),
+    def delta_of(start, *outs):
+        return call(
+            functools.partial(delta_kernel, start),
+            (((outputs, here), jnp.float32), *outs),
+            place,
+            *resid_list,
+            *(part[1] for part in done),
+            *(part[2] for part in done),
+            scratch=(((4 * quarter, lanes), jnp.bfloat16),) * 2
+            + (((4 * quarter, here), jnp.bfloat16),) * 2,
+            scalars=1,
+            products=3 * 4 * quarter * here * lanes,
+        )
+
+    first, mine = delta_of(here, ((half_block, outputs), jnp.float32))
+    received, theirs = permute(first, SWAP), permute(mine, SWAP)
+    *resid_list, first = lax.optimization_barrier((*resid_list, first))
+    (second,) = delta_of(0)
+    new_weights, residual = call(
+        functools.partial(update_kernel, step_size / batch),
+        (((outputs, here), jnp.float32), ((block, outputs), jnp.float32)),
         place,
-        *resid_list,
-        *(part[1] for part in done),
-        *(part[2] for part in done),
         weights.T,
-        scratch=(((4 * quarter, lanes), jnp.bfloat16),) * 2 + (((4 * quarter, pair), jnp.bfloat16),) * 2,
+        second,
+        received,
+        mine,
+        theirs,
         scalars=1,
-        products=3 * 4 * quarter * pair * lanes,
-    )
-    new_weights = update(factor, partly, permute(first, SWAP)).T
-    theirs = permute(mine, SWAP)
-    residual = jnp.where(
-        core == 0,
-        jnp.concatenate([mine, theirs], axis=0),
-        jnp.concatenate([theirs, mine], axis=0),
-    )
-    return (new_weights, residual)
+    )
+    return (new_weights.T, residual)
 
 
 def solution(mesh):

time: 128 us -> 122 us (0.953)
  starting transfers between devices: 24.3 us -> 18.4 us
  Pallas kernels: 12.2 us -> 16.2 us
  blocking collectives: 60.4 us -> 57.1 us
    pallas_call x8 -> x11, Pallas kernels: 10 us -> 16.2 us  [call(): pl.pallas_call(kernel, in_specs=[pl.BlockSpec(memory_space=pltpu.SMEM)] *...]
    ppermute x16, starting transfers between devices: 24.3 us -> 18.4 us  [permute(): return lax.ppermute(array, AXES, pairs)]
    all_to_all x3, blocking collectives: 60.4 us -> 57.1 us  [exchange(): lax.all_to_all(array, AXES, 0, 0, axis_index_groups=groups, tiled=True)]
    pallas_call x1 -> x0, Pallas kernels: 2.13 us -> none  [update(): pl.pallas_call(functools.partial(update_kernel, factor), grid=(5,), in_sp...]
    unnamed x10 -> x8, local copies, waits for them, and re-layouts: 2.67 us -> 2.21 us
  transfers between devices with their start and end apart: 16 -> 16, of which waited for: 11 -> 8; matrix products, arithmetic and copies ran while one was open for 1% -> 0% of each run, Pallas kernels for 4% -> 10%
where the time goes in v11:
time: 122 us; the launch traced here: 121 us
  blocking collectives  57.1 us (47%)
  waiting for transfers between devices  25.3 us (21%)
  starting transfers between devices  18.4 us (15%)
  Pallas kernels  16.2 us (13%)
  local copies, waits for them, and re-layouts  3.07 us (3%)
    all_to_all x3, blocking collectives, exchange(): lax.all_to_all(array, AXES, 0, 0, axis_index_groups=groups, tiled=True)  57.1 us
    ppermute x16, waiting for transfers between devices, permute(): return lax.ppermute(array, AXES, pairs)  25.3 us
    ppermute x16, starting transfers between devices, permute(): return lax.ppermute(array, AXES, pairs)  18.4 us
    pallas_call x11, Pallas kernels, call(): pl.pallas_call(kernel, in_specs=[pl.BlockSpec(memory_space=pltpu.SMEM)] *...  16.2 us
  transfers between devices with their start and end apart: 16, of which 8 were waited for; matrix products, arithmetic and copies ran while one was open for 0% of the time, Pallas kernels for 10%

profile of v11, /device:TPU:1, one launch (start us, length us, event | category | flops | bytes accessed | tf_op | source)
XLA Modules:
  0.0 121.3 jit_solution(6356347074149828777)
XLA Ops:
  0.7 0.7 copy-done.3
  1.9 0.6 gather_fusion
  2.6 26.5 %all_to_all.29 = f32[16,8,1024]{2,1,0:T(8,128)S(1)} all-to-all(f32[16,8,1024]{2,1,0:T(8,128)S(1)} %bitcast.29), channel_id=1, replica_groups={{0,2,4,6,8,10,12,14,129,131,133,135,137,139,141,143},{16,18,20,22,24,26..., dimensions={0} | all-to-all | bytes 1048576 | tf_op jit(solution)/shard_map/all_to_all | solution.py:96
  29.1 2.9 %collective-permute-start.3 = (f32[256,1024]{1,0:T(8,128)}, f32[256,1024]{1,0:T(8,128)}, u32[]{:S(2)}, u32[]{:S(2)}) collective-permute-start(f32[256,1024]{1,0:T(8,128)} %own_centers), channel_id=1, source_target_pairs={{0,16},{16,0},{2,18},{18,2},{4,20},{20,4},{6,22},{22,6},{8,24},{24... | collective-permute-start | bytes 3145736 | tf_op jit(solution)/shard_map/ppermute | solution.py:92
  32.1 2.6 %collective-permute-start.2 = (f32[128,1024]{1,0:T(8,128)S(1)}, f32[128,1024]{1,0:T(8,128)}, u32[]{:S(2)}, u32[]{:S(2)}) collective-permute-start(f32[128,1024]{1,0:T(8,128)S(1)} %shard_map.68.rows), channel_id=1, source_target_pairs={{0,32},{16,112},{2,34},{18,114},{4,36},{20,116},{6,38},{22,118},{8... | collective-permute-start | bytes 1572872 | tf_op jit(solution)/shard_map/ppermute | solution.py:92
  34.7 0.4 collective-permute-start.1
  35.1 2.4 %collective-permute-start = (f32[128,1024]{1,0:T(8,128)S(1)}, f32[128,1024]{1,0:T(8,128)S(1)}, u32[]{:S(2)}, u32[]{:S(2)}) collective-permute-start(f32[128,1024]{1,0:T(8,128)S(1)} %shard_map.68.rows), channel_id=1, source_target_pairs={{0,2},{16,30},{2,0},{18,20},{4,6},{20,18},{6,4},{22,24},{8,10},{24... | collective-permute-start | bytes 1572872 | tf_op jit(solution)/shard_map/ppermute | solution.py:92
  37.6 1.2 %copy-done.2 = f32[256,1000]{0,1:T(8,128)S(1)} copy-done((f32[256,1000]{0,1:T(8,128)S(1)}, f32[256,1000]{0,1:T(8,128)}, u32[]{:S(2)}) %copy-start.2) | copy-done | bytes 1024024
  38.8 0.9 shard_map.71.targets
  39.7 3.1 %shard_map.69 = (bf16[1024,512]{1,0:T(8,128)(2,1)S(1)}, bf16[1024,512]{1,0:T(8,128)(2,1)S(1)}, f32[1,512]{1,0:T(1,128)S(1)}, bf16[512,1024]{1,0:T(8,128)(2,1)S(1)}, bf16[512,1024]{1,0:T(8,128)(2,1)S(1)}) custom-call(f32[256,1024]{1,0:T(8,128)} %own_centers, f32[256,1024]{1,0:T(8,128)} %collective-permute-done.3.other_centers, f32[1000,256]{1,0:T(8,128)S(1)} %bitcast.24, ...), custom_call_target="tpu_custom_call" | custom-call | bytes 2097152 | tf_op jit(solution)/shard_map/pallas_call | solution.py:217
  42.8 1.2 shard_map.70
  44.0 2.2 %shard_map.72 = (f32[128,1024]{1,0:T(8,128)S(1)}, bf16[128,512]{1,0:T(8,128)(2,1)S(1)}, bf16[128,512]{1,0:T(8,128)(2,1)S(1)}) custom-call(f32[128,1024]{1,0:T(8,128)} %collective-permute-done.2.rows, bf16[1024,512]{1,0:T(8,128)(2,1)S(1)} %get-tuple-element.47.centers_high, bf16[1024,512]{1,0:T(8,128)(2,1)S(1)} %get-tuple-element.48.centers_low, ...), custom_call_target="tpu_custom_call" | custom-call | flops 805306368 | bytes 2097152 | tf_op jit(solution)/shard_map/pallas_call | solution.py:217
  46.5 2.2 %shard_map.73 = (f32[128,1024]{1,0:T(8,128)S(1)}, bf16[128,512]{1,0:T(8,128)(2,1)S(1)}, bf16[128,512]{1,0:T(8,128)(2,1)S(1)}) custom-call(f32[128,1024]{1,0:T(8,128)} %collective-permute-done.1.rows, bf16[1024,512]{1,0:T(8,128)(2,1)S(1)} %get-tuple-element.47.centers_high, bf16[1024,512]{1,0:T(8,128)(2,1)S(1)} %get-tuple-element.48.centers_low, ...), custom_call_target="tpu_custom_call" | custom-call | flops 805306368 | bytes 2097152 | tf_op jit(solution)/shard_map/pallas_call | solution.py:217
  48.7 2.3 %collective-permute-start.6 = (f32[128,1024]{1,0:T(8,128)S(1)}, f32[128,1024]{1,0:T(8,128)S(1)}, u32[]{:S(2)}, u32[]{:S(2)}) collective-permute-start(f32[128,1024]{1,0:T(8,128)S(1)} %get-tuple-element.62), channel_id=1, source_target_pairs={{0,128},{16,145},{2,130},{18,147},{4,132},{20,149},{6,134},{22,151... | collective-permute-start | bytes 1572872 | tf_op jit(solution)/shard_map/ppermute | solution.py:92
  51.0 1.2 shard_map.74
  52.2 0.5 collective-permute-start.7
  52.7 2.8 %collective-permute-done.5 = f32[128,1024]{1,0:T(8,128)S(1)} collective-permute-done((f32[128,1024]{1,0:T(8,128)S(1)}, f32[128,1024]{1,0:T(8,128)S(1)}, u32[]{:S(2)}, u32[]{:S(2)}) %collective-permute-start.5) | collective-permute-done | bytes 524320 | tf_op jit(solution)/shard_map/ppermute | solution.py:92
  55.5 2.5 %collective-permute-done.6 = f32[128,1024]{1,0:T(8,128)S(1)} collective-permute-done((f32[128,1024]{1,0:T(8,128)S(1)}, f32[128,1024]{1,0:T(8,128)S(1)}, u32[]{:S(2)}, u32[]{:S(2)}) %collective-permute-start.6) | collective-permute-done | bytes 524320 | tf_op jit(solution)/shard_map/ppermute | solution.py:92
  58.0 3.5 %collective-permute-done.7 = f32[128,1024]{1,0:T(8,128)S(1)} collective-permute-done((f32[128,1024]{1,0:T(8,128)S(1)}, f32[128,1024]{1,0:T(8,128)S(1)}, u32[]{:S(2)}, u32[]{:S(2)}) %collective-permute-start.7) | collective-permute-done | bytes 524320 | tf_op jit(solution)/shard_map/ppermute | solution.py:92
  61.7 14.9 %all_to_all.30.sums = f32[8,16,1024]{2,1,0:T(8,128)S(1)} all-to-all(f32[8,16,1024]{2,1,0:T(8,128)S(1)} %bitcast.28), channel_id=1, replica_groups={{0,162,1,163,64,226,65,227},{16,178,17,179,80,242,81,243},{4,166,5,167,..., dimensions={0} | all-to-all | bytes 1048576 | tf_op jit(solution)/shard_map/all_to_all | solution.py:96
  76.7 1.9 %collective-permute-start.10 = (f32[16,1024]{1,0:T(8,128)S(1)}, f32[16,1024]{1,0:T(8,128)S(1)}, u32[]{:S(2)}, u32[]{:S(2)}) collective-permute-start(f32[16,1024]{1,0:T(8,128)S(1)} %shard_map.75), channel_id=1, source_target_pairs={{0,12},{16,28},{2,14},{18,30},{4,0},{20,16},{6,2},{22,18},{8,4},{2... | collective-permute-start | bytes 196616 | tf_op jit(solution)/shard_map/ppermute | solution.py:92
  78.6 3.2 %collective-permute-start.8 = (f32[16,1024]{1,0:T(8,128)S(1)}, f32[16,1024]{1,0:T(8,128)S(1)}, u32[]{:S(2)}, u32[]{:S(2)}) collective-permute-start(f32[16,1024]{1,0:T(8,128)S(1)} %shard_map.75), channel_id=1, source_target_pairs={{0,8},{16,24},{2,10},{18,26},{4,12},{20,28},{6,14},{22,30},{8,0},{... | collective-permute-start | bytes 196616 | tf_op jit(solution)/shard_map/ppermute | solution.py:92
  81.9 0.8 collective-permute-done.10
  82.7 4.6 %collective-permute-done.8 = f32[16,1024]{1,0:T(8,128)S(1)} collective-permute-done((f32[16,1024]{1,0:T(8,128)S(1)}, f32[16,1024]{1,0:T(8,128)S(1)}, u32[]{:S(2)}, u32[]{:S(2)}) %collective-permute-start.8) | collective-permute-done | bytes 65568 | tf_op jit(solution)/shard_map/ppermute | solution.py:92
  87.3 1.3 %collective-permute-done.9 = f32[16,1024]{1,0:T(8,128)S(1)} collective-permute-done((f32[16,1024]{1,0:T(8,128)S(1)}, f32[16,1024]{1,0:T(8,128)S(1)}, u32[]{:S(2)}, u32[]{:S(2)}) %collective-permute-start.9) | collective-permute-done | bytes 65568 | tf_op jit(solution)/shard_map/ppermute | solution.py:92
  88.6 15.8 %all_to_all.31 = f32[8,16,1024]{2,1,0:T(8,128)S(1)} all-to-all(f32[8,16,1024]{2,1,0:T(8,128)S(1)} %broadcast_in_dim.33), channel_id=1, replica_groups={{0,162,1,163,64,226,65,227},{16,178,17,179,80,242,81,243},{4,166,5,167,..., dimensions={0} | all-to-all | bytes 1048576 | tf_op jit(solution)/shard_map/all_to_all | solution.py:96
  104.4 9.2 %collective-permute-done.11.refs_1_ = f32[128,1024]{1,0:T(8,128)S(1)} collective-permute-done((f32[128,1024]{1,0:T(8,128)S(1)}, f32[128,1024]{1,0:T(8,128)S(1)}, u32[]{:S(2)}, u32[]{:S(2)}) %collective-permute-start.11) | collective-permute-done | bytes 524320 | tf_op jit(solution)/shard_map/ppermute | solution.py:92
  113.6 1.8 %shard_map.76 = (f32[1000,256]{1,0:T(8,128)S(1)}, f32[32,1000]{1,0:T(8,128)S(1)}) custom-call(s32[5]{0:T(128)S(1)} %stack.23.place, f32[128,1024]{1,0:T(8,128)S(1)} %bitcast.22, f32[128,1024]{1,0:T(8,128)S(1)} %collective-permute-done.11.refs_1_, f32[128,1024]{1,0:T(8,128)S(1)} %collective-permute-done.12.refs_2_, ...), custom_call_target="tpu_custom_call" | custom-call | flops 805306368 | bytes 2097152 | tf_op jit(solution)/shard_map/pallas_call | solution.py:217
  115.4 1.7 %collective-permute-start.14 = (f32[1000,256]{1,0:T(8,128)S(1)}, f32[1000,256]{1,0:T(8,128)S(1)}, u32[]{:S(2)}, u32[]{:S(2)}) collective-permute-start(f32[1000,256]{1,0:T(8,128)S(1)} %get-tuple-element.74), channel_id=1, source_target_pairs={{0,16},{16,0},{2,18},{18,2},{4,20},{20,4},{6,22},{22,6},{8,24},{24... | collective-permute-start | bytes 3072008 | tf_op jit(solution)/shard_map/ppermute | solution.py:92
  117.2 1.8 %shard_map.77.own_delta = f32[1000,256]{1,0:T(8,128)S(1)} custom-call(s32[5]{0:T(128)S(1)} %stack.23.place, f32[128,1024]{1,0:T(8,128)S(1)} %bitcast.23, f32[128,1024]{1,0:T(8,128)S(1)} %collective-permute-done.11.refs_1_, f32[128,1024]{1,0:T(8,128)S(1)} %collective-permute-done.12.refs_2_, f32[128,1024]{1,0:T(8,128)S(1)} %collective-permute-done.13.refs_3_, ...), custom_call_target="tpu_custom_call" | custom-call | flops 805306368 | bytes 2097152 | tf_op jit(solution)/shard_map/pallas_call | solution.py:217
  119.0 0.6 collective-permute-done.15.theirs
  119.6 1.7 %shard_map.78 = (f32[1000,256]{1,0:T(8,128)}, f32[64,1000]{1,0:T(8,128)}) custom-call(s32[5]{0:T(128)S(1)} %stack.23.place, f32[1000,256]{1,0:T(8,128)S(1)} %bitcast.25, f32[1000,256]{1,0:T(8,128)S(1)} %shard_map.77.own_delta, f32[1000,256]{1,0:T(8,128)S(1)} %collective-permute-done.14.other_delta, f32[32,1000]{1,0:T(8,128)S(1)} %get-tuple-element.79.mine, ...), custom_call_target="tpu_custom_call" | custom-call | bytes 2097152 | tf_op jit(solution)/shard_map/pallas_call | solution.py:217
  (33 shorter events, 1.5 us)
Async XLA Ops:
  0.6 1.2 %copy-start = (f32[256,1024]{1,0:T(8,128)S(1)}, f32[256,1024]{1,0:T(8,128)}, u32[]{:S(2)}) copy-start(f32[256,1024]{1,0:T(8,128)} %param.6) | copy-start | bytes 3145732
  0.7 0.7 copy-start.3
  2.5 29.5 %copy-start.1 = (f32[256,1000]{0,1:T(8,128)S(1)}, f32[256,1000]{0,1:T(8,128)}, u32[]{:S(2)}) copy-start(f32[256,1000]{0,1:T(8,128)} %param.9) | copy-start | bytes 3072004
  29.1 10.6 %collective-permute-start.3 = (f32[256,1024]{1,0:T(8,128)}, f32[256,1024]{1,0:T(8,128)}, u32[]{:S(2)}, u32[]{:S(2)}) collective-permute-start(f32[256,1024]{1,0:T(8,128)} %own_centers), channel_id=1, source_target_pairs={{0,16},{16,0},{2,18},{18,2},{4,20},{20,4},{6,22},{22,6},{8,24},{24... | collective-permute-start | bytes 3145736 | tf_op jit(solution)/shard_map/ppermute | solution.py:92
  32.0 7.7 %collective-permute-start.4 = (f32[256,1000]{0,1:T(8,128)S(1)}, f32[256,1000]{0,1:T(8,128)}, u32[]{:S(2)}, u32[]{:S(2)}) collective-permute-start(f32[256,1000]{0,1:T(8,128)S(1)} %copy-done.1), channel_id=1, source_target_pairs={{0,16},{16,0},{2,18},{18,2},{4,20},{20,4},{6,22},{22,6},{8,24},{24... | collective-permute-start | bytes 3072008 | tf_op jit(solution)/shard_map/ppermute | solution.py:92
  32.1 11.9 %collective-permute-start.2 = (f32[128,1024]{1,0:T(8,128)S(1)}, f32[128,1024]{1,0:T(8,128)}, u32[]{:S(2)}, u32[]{:S(2)}) collective-permute-start(f32[128,1024]{1,0:T(8,128)S(1)} %shard_map.68.rows), channel_id=1, source_target_pairs={{0,32},{16,112},{2,34},{18,114},{4,36},{20,116},{6,38},{22,118},{8... | collective-permute-start | bytes 1572872 | tf_op jit(solution)/shard_map/ppermute | solution.py:92
  34.7 11.8 %collective-permute-start.1 = (f32[128,1024]{1,0:T(8,128)S(1)}, f32[128,1024]{1,0:T(8,128)}, u32[]{:S(2)}, u32[]{:S(2)}) collective-permute-start(f32[128,1024]{1,0:T(8,128)S(1)} %shard_map.68.rows), channel_id=1, source_target_pairs={{0,128},{16,145},{2,130},{18,147},{4,132},{20,149},{6,134},{22,151... | collective-permute-start | bytes 1572872 | tf_op jit(solution)/shard_map/ppermute | solution.py:92
  35.1 15.9 %collective-permute-start = (f32[128,1024]{1,0:T(8,128)S(1)}, f32[128,1024]{1,0:T(8,128)S(1)}, u32[]{:S(2)}, u32[]{:S(2)}) collective-permute-start(f32[128,1024]{1,0:T(8,128)S(1)} %shard_map.68.rows), channel_id=1, source_target_pairs={{0,2},{16,30},{2,0},{18,20},{4,6},{20,18},{6,4},{22,24},{8,10},{24... | collective-permute-start | bytes 1572872 | tf_op jit(solution)/shard_map/ppermute | solution.py:92
  37.6 1.2 %copy-start.2 = (f32[256,1000]{0,1:T(8,128)S(1)}, f32[256,1000]{0,1:T(8,128)}, u32[]{:S(2)}) copy-start(f32[256,1000]{0,1:T(8,128)} %param.7) | copy-start | bytes 3072004
  46.2 9.3 %collective-permute-start.5 = (f32[128,1024]{1,0:T(8,128)S(1)}, f32[128,1024]{1,0:T(8,128)S(1)}, u32[]{:S(2)}, u32[]{:S(2)}) collective-permute-start(f32[128,1024]{1,0:T(8,128)S(1)} %get-tuple-element.60), channel_id=1, source_target_pairs={{0,32},{16,112},{2,34},{18,114},{4,36},{20,116},{6,38},{22,118},{8... | collective-permute-start | bytes 1572872 | tf_op jit(solution)/shard_map/ppermute | solution.py:92
  48.7 9.3 %collective-permute-start.6 = (f32[128,1024]{1,0:T(8,128)S(1)}, f32[128,1024]{1,0:T(8,128)S(1)}, u32[]{:S(2)}, u32[]{:S(2)}) collective-permute-start(f32[128,1024]{1,0:T(8,128)S(1)} %get-tuple-element.62), channel_id=1, source_target_pairs={{0,128},{16,145},{2,130},{18,147},{4,132},{20,149},{6,134},{22,151... | collective-permute-start | bytes 1572872 | tf_op jit(solution)/shard_map/ppermute | solution.py:92
  52.2 9.3 %collective-permute-start.7 = (f32[128,1024]{1,0:T(8,128)S(1)}, f32[128,1024]{1,0:T(8,128)S(1)}, u32[]{:S(2)}, u32[]{:S(2)}) collective-permute-start(f32[128,1024]{1,0:T(8,128)S(1)} %get-tuple-element.64), channel_id=1, source_target_pairs={{0,2},{16,30},{2,0},{18,20},{4,6},{20,18},{6,4},{22,24},{8,10},{24... | collective-permute-start | bytes 1572872 | tf_op jit(solution)/shard_map/ppermute | solution.py:92
  76.7 6.0 %collective-permute-start.10 = (f32[16,1024]{1,0:T(8,128)S(1)}, f32[16,1024]{1,0:T(8,128)S(1)}, u32[]{:S(2)}, u32[]{:S(2)}) collective-permute-start(f32[16,1024]{1,0:T(8,128)S(1)} %shard_map.75), channel_id=1, source_target_pairs={{0,12},{16,28},{2,14},{18,30},{4,0},{20,16},{6,2},{22,18},{8,4},{2... | collective-permute-start | bytes 196616 | tf_op jit(solution)/shard_map/ppermute | solution.py:92
  78.6 8.6 %collective-permute-start.8 = (f32[16,1024]{1,0:T(8,128)S(1)}, f32[16,1024]{1,0:T(8,128)S(1)}, u32[]{:S(2)}, u32[]{:S(2)}) collective-permute-start(f32[16,1024]{1,0:T(8,128)S(1)} %shard_map.75), channel_id=1, source_target_pairs={{0,8},{16,24},{2,10},{18,26},{4,12},{20,28},{6,14},{22,30},{8,0},{... | collective-permute-start | bytes 196616 | tf_op jit(solution)/shard_map/ppermute | solution.py:92
  81.9 6.7 %collective-permute-start.9 = (f32[16,1024]{1,0:T(8,128)S(1)}, f32[16,1024]{1,0:T(8,128)S(1)}, u32[]{:S(2)}, u32[]{:S(2)}) collective-permute-start(f32[16,1024]{1,0:T(8,128)S(1)} %shard_map.75), channel_id=1, source_target_pairs={{0,4},{16,20},{2,6},{18,22},{4,8},{20,24},{6,10},{22,26},{8,12},{2... | collective-permute-start | bytes 196616 | tf_op jit(solution)/shard_map/ppermute | solution.py:92
  104.4 9.2 %collective-permute-start.11 = (f32[128,1024]{1,0:T(8,128)S(1)}, f32[128,1024]{1,0:T(8,128)S(1)}, u32[]{:S(2)}, u32[]{:S(2)}) collective-permute-start(f32[128,1024]{1,0:T(8,128)S(1)} %bitcast.19), channel_id=1, source_target_pairs={{0,32},{16,112},{2,34},{18,114},{4,36},{20,116},{6,38},{22,118},{8... | collective-permute-start | bytes 1572872 | tf_op jit(solution)/shard_map/ppermute | solution.py:92
  104.4 9.2 %collective-permute-start.12 = (f32[128,1024]{1,0:T(8,128)S(1)}, f32[128,1024]{1,0:T(8,128)S(1)}, u32[]{:S(2)}, u32[]{:S(2)}) collective-permute-start(f32[128,1024]{1,0:T(8,128)S(1)} %bitcast.20), channel_id=1, source_target_pairs={{0,128},{16,145},{2,130},{18,147},{4,132},{20,149},{6,134},{22,151... | collective-permute-start | bytes 1572872 | tf_op jit(solution)/shard_map/ppermute | solution.py:92
  104.4 9.2 %collective-permute-start.13 = (f32[128,1024]{1,0:T(8,128)S(1)}, f32[128,1024]{1,0:T(8,128)S(1)}, u32[]{:S(2)}, u32[]{:S(2)}) collective-permute-start(f32[128,1024]{1,0:T(8,128)S(1)} %bitcast.21), channel_id=1, source_target_pairs={{0,2},{16,30},{2,0},{18,20},{4,6},{20,18},{6,4},{22,24},{8,10},{24... | collective-permute-start | bytes 1572872 | tf_op jit(solution)/shard_map/ppermute | solution.py:92
  115.4 4.1 %collective-permute-start.14 = (f32[1000,256]{1,0:T(8,128)S(1)}, f32[1000,256]{1,0:T(8,128)S(1)}, u32[]{:S(2)}, u32[]{:S(2)}) collective-permute-start(f32[1000,256]{1,0:T(8,128)S(1)} %get-tuple-element.74), channel_id=1, source_target_pairs={{0,16},{16,0},{2,18},{18,2},{4,20},{20,4},{6,22},{22,6},{8,24},{24... | collective-permute-start | bytes 3072008 | tf_op jit(solution)/shard_map/ppermute | solution.py:92
  117.1 2.4 %collective-permute-start.15 = (f32[32,1000]{1,0:T(8,128)S(1)}, f32[32,1000]{1,0:T(8,128)S(1)}, u32[]{:S(2)}, u32[]{:S(2)}) collective-permute-start(f32[32,1000]{1,0:T(8,128)S(1)} %get-tuple-element.79.mine), channel_id=1, source_target_pairs={{0,16},{16,0},{2,18},{18,2},{4,20},{20,4},{6,22},{22,6},{8,24},{24... | collective-permute-start | bytes 384008 | tf_op jit(solution)/shard_map/ppermute | solution.py:92

commit v12 on v11

--- a/solution.py
+++ b/solution.py
@@ -125,20 +125,42 @@
 
 
 def prepare_kernel(
-    own_centers, other_centers, own_weights, other_weights, high, low, center_sq, value_high, value_low
+    own,
+    index,
+    place,
+    own_centers,
+    other_centers,
+    own_weights,
+    other_weights,
+    labels,
+    high,
+    low,
+    center_sq,
+    value_high,
+    value_low,
+    targets,
+    turned_labels,
 ):
     here = own_centers.shape[0]
     outputs, lanes = own_weights.shape[0], value_high.shape[1]
+
+    def padded(array):
+        zeros = jnp.zeros((lanes - outputs, array.shape[1]), jnp.float32)
+        return jnp.concatenate([array, zeros], axis=0).T
+
     for i, (centers, weights) in enumerate(
         ((own_centers, own_weights), (other_centers, other_weights))
     ):
-        place = pl.ds(i * here, here)
+        columns = pl.ds(i * here, here)
         turned = centers[...].T
-        center_sq[:, place] = jnp.sum(turned * turned, axis=0, keepdims=True)
-        high[:, place], low[:, place] = parts(turned)
-        zeros = jnp.zeros((lanes - outputs, here), jnp.float32)
-        padded = jnp.concatenate([weights[...], zeros], axis=0)
-        value_high[place, :], value_low[place, :] = parts(padded.T)
+        center_sq[:, columns] = jnp.sum(turned * turned, axis=0, keepdims=True)
+        high[:, columns], low[:, columns] = parts(turned)
+        value_high[columns, :], value_low[columns, :] = parts(padded(weights[...]))
+    turned_labels[...] = padded(labels[...])
+    targets[...] = jnp.zeros_like(targets)
+    start = place[3] // 2 * own
+    for row in range(own):
+        targets[pl.ds(start + row, 1), :] = turned_labels[pl.ds(index[row], 1), :]
 
 
 def quarter_kernel(
@@ -162,17 +184,6 @@
                     source = (((k * levels + level) * 2 + odd) * 2 + i) * own
                     target = (((i * 2 + k) * 2 + odd) * levels + level) * own
                     out[target : target + own, :] = found[source : source + own, :]
-
-
-def targets_kernel(own, index, place, labels, out, turned):
-    rows, outputs = index.shape[0], labels.shape[0]
-    width = labels.shape[1]
-    zeros = jnp.zeros((out.shape[1] - outputs, width), jnp.float32)
-    turned[...] = jnp.concatenate([labels[...], zeros], axis=0).T
-    out[...] = jnp.zeros_like(out)
-    start = place[3] // 2 * own
-    for row in range(rows):
-        out[pl.ds(start + row, 1), :] = turned[pl.ds(index[row], 1), :]
 
 
 def plane_kernel(scale, sums, targets, out):
@@ -250,7 +261,7 @@
     wanted_index = jnp.sum(jnp.where(match, batch_index[None, :], 0), axis=1)
     rows = pick(train_features, wanted_index)
     place = jnp.stack([x, y_lo, y_hi, z, core]).astype(jnp.int32)
-    rows, place = lax.optimization_barrier((rows, place))
+    rows, place, index = lax.optimization_barrier((rows, place, index))
     sent = jnp.broadcast_to(
         rows.reshape(2, 1, 2, 2 * own, features), (2, LEVELS // 2, 2, 2 * own, features)
     )
@@ -264,19 +275,25 @@
     column_rows = LEVELS // 2 * own
     quarter = found.shape[0]
     pair = 2 * here
-    held = call(
-        prepare_kernel,
+    *held, targets = call(
+        functools.partial(prepare_kernel, own),
         (
             ((features, pair), jnp.bfloat16),
             ((features, pair), jnp.bfloat16),
             ((1, pair), jnp.float32),
             ((pair, lanes), jnp.bfloat16),
             ((pair, lanes), jnp.bfloat16),
+            ((column_rows, lanes), jnp.float32),
         ),
+        index,
+        place,
         centers,
         permute(centers, SWAP),
         own_weights.T,
         permute(own_weights, SWAP).T,
+        train_labels.T,
+        scratch=(((train_labels.shape[0], lanes), jnp.float32),),
+        scalars=2,
     )
 
     def quarter_of(part):
@@ -295,18 +312,9 @@
     first_rows, *later = quarters(column)
     done = [quarter_of(first_rows)]
     value = done[0][0]
-    (targets,) = call(
-        functools.partial(targets_kernel, own),
-        (((column_rows, lanes), jnp.float32),),
-        index,
-        place,
-        train_labels.T,
-        scratch=(((train_labels.shape[0], lanes), jnp.float32),),
-        scalars=2,
-    )
     sums = []
     for way, part in zip(WAYS, later):
-        part, value, targets = lax.optimization_barrier((part, value, targets))
+        part, value = lax.optimization_barrier((part, value))
         done.append(quarter_of(part))
         sums.append(permute(done[way][0], swap_pairs(way)))
     for found in sums:

time: 122 us -> 117 us (0.959)
  starting transfers between devices: 18.4 us -> 29 us
  waiting for transfers between devices: 25.3 us -> 20.2 us
  blocking collectives: 57.1 us -> 52.9 us
  Pallas kernels: 16.2 us -> 12.1 us
  local copies, waits for them, and re-layouts: 3.07 us -> 1.78 us
    ppermute x16, starting transfers between devices: 18.4 us -> 29 us  [permute(): return lax.ppermute(array, AXES, pairs)]
    ppermute x16, waiting for transfers between devices: 25.3 us -> 20.2 us  [permute(): return lax.ppermute(array, AXES, pairs)]
    all_to_all x3, blocking collectives: 57.1 us -> 52.9 us  [exchange(): lax.all_to_all(array, AXES, 0, 0, axis_index_groups=groups, tiled=True)]
    pallas_call x11 -> x10, Pallas kernels: 16.2 us -> 12.1 us  [call(): pl.pallas_call(kernel, in_specs=[pl.BlockSpec(memory_space=pltpu.SMEM)] *...]
    unnamed x8 -> x10, local copies, waits for them, and re-layouts: 2.21 us -> 0.92 us
  transfers between devices with their start and end apart: 16 -> 16, of which waited for: 8 -> 9; matrix products, arithmetic and copies ran while one was open for 0% -> 0% of each run, Pallas kernels for 10% -> 7%
where the time goes in v12:
time: 117 us
  blocking collectives  52.9 us (45%)
  starting transfers between devices  29 us (25%)
  waiting for transfers between devices  20.2 us (17%)
  Pallas kernels  12.1 us (10%)
  local copies, waits for them, and re-layouts  1.78 us (2%)
    all_to_all x3, blocking collectives, exchange(): lax.all_to_all(array, AXES, 0, 0, axis_index_groups=groups, tiled=True)  52.9 us
    ppermute x16, starting transfers between devices, permute(): return lax.ppermute(array, AXES, pairs)  29 us
    ppermute x16, waiting for transfers between devices, permute(): return lax.ppermute(array, AXES, pairs)  20.2 us
    pallas_call x10, Pallas kernels, call(): pl.pallas_call(kernel, in_specs=[pl.BlockSpec(memory_space=pltpu.SMEM)] *...  12.1 us
  transfers between devices with their start and end apart: 16, of which 9 were waited for; matrix products, arithmetic and copies ran while one was open for 0% of the time, Pallas kernels for 7%

profile of v12, /device:TPU:1, one launch (start us, length us, event | category | flops | bytes accessed | tf_op | source)
XLA Modules:
  0.0 117.1 jit_solution(3966811359885109168)
XLA Ops:
  0.7 0.7 copy-done.4
  1.9 0.6 gather_fusion
  2.7 26.5 %all_to_all.29 = f32[16,8,1024]{2,1,0:T(8,128)S(1)} all-to-all(f32[16,8,1024]{2,1,0:T(8,128)S(1)} %bitcast.30), channel_id=1, replica_groups={{0,2,4,6,8,10,12,14,129,131,133,135,137,139,141,143},{16,18,20,22,24,26..., dimensions={0} | all-to-all | bytes 1048576 | tf_op jit(solution)/shard_map/all_to_all | solution.py:96
  29.1 2.9 %collective-permute-start.3 = (f32[256,1024]{1,0:T(8,128)S(1)}, f32[256,1024]{1,0:T(8,128)S(1)}, u32[]{:S(2)}, u32[]{:S(2)}) collective-permute-start(f32[256,1024]{1,0:T(8,128)S(1)} %copy-done.2), channel_id=1, source_target_pairs={{0,16},{16,0},{2,18},{18,2},{4,20},{20,4},{6,22},{22,6},{8,24},{24... | collective-permute-start | bytes 3145736 | tf_op jit(solution)/shard_map/ppermute | solution.py:92
  32.2 2.6 %collective-permute-start.2 = (f32[128,1024]{1,0:T(8,128)S(1)}, f32[128,1024]{1,0:T(8,128)S(1)}, u32[]{:S(2)}, u32[]{:S(2)}) collective-permute-start(f32[128,1024]{1,0:T(8,128)S(1)} %shard_map.68.rows), channel_id=1, source_target_pairs={{0,32},{16,112},{2,34},{18,114},{4,36},{20,116},{6,38},{22,118},{8... | collective-permute-start | bytes 1572872 | tf_op jit(solution)/shard_map/ppermute | solution.py:92
  35.2 2.4 %collective-permute-start = (f32[128,1024]{1,0:T(8,128)S(1)}, f32[128,1024]{1,0:T(8,128)S(1)}, u32[]{:S(2)}, u32[]{:S(2)}) collective-permute-start(f32[128,1024]{1,0:T(8,128)S(1)} %shard_map.68.rows), channel_id=1, source_target_pairs={{0,2},{16,30},{2,0},{18,20},{4,6},{20,18},{6,4},{22,24},{8,10},{24... | collective-permute-start | bytes 1572872 | tf_op jit(solution)/shard_map/ppermute | solution.py:92
  37.6 2.1 %shard_map.69 = (bf16[1024,512]{1,0:T(8,128)(2,1)S(1)}, bf16[1024,512]{1,0:T(8,128)(2,1)S(1)}, f32[1,512]{1,0:T(1,128)S(1)}, bf16[512,1024]{1,0:T(8,128)(2,1)S(1...) custom-call(s32[4]{0:T(128)S(1)} %dynamic_slice.3.index, s32[5]{0:T(128)S(1)} %stack.23.place, ...), custom_call_target="tpu_custom_call" | custom-call | bytes 2097152 | tf_op jit(solution)/shard_map/pallas_call | solution.py:228
  39.7 1.1 shard_map.70
  40.8 0.7 collective-permute-done.2.rows
  41.6 1.2 shard_map.71
  42.7 2.6 %collective-permute-start.5 = (f32[128,1024]{1,0:T(8,128)S(1)}, f32[128,1024]{1,0:T(8,128)S(1)}, u32[]{:S(2)}, u32[]{:S(2)}) collective-permute-start(f32[128,1024]{1,0:T(8,128)S(1)} %get-tuple-element.58), channel_id=1, source_target_pairs={{0,32},{16,112},{2,34},{18,114},{4,36},{20,116},{6,38},{22,118},{8... | collective-permute-start | bytes 1572872 | tf_op jit(solution)/shard_map/ppermute | solution.py:92
  45.3 1.1 shard_map.72
  46.4 0.5 collective-permute-start.6
  47.0 1.2 %shard_map.73 = (f32[128,1024]{1,0:T(8,128)S(1)}, bf16[128,512]{1,0:T(8,128)(2,1)S(1)}, bf16[128,512]{1,0:T(8,128)(2,1)S(1)}) custom-call(f32[128,1024]{1,0:T(8,128)S(1)} %collective-permute-done.rows, bf16[1024,512]{1,0:T(8,128)(2,1)S(1)} %get-tuple-element.48.centers_high, bf16[1024,512]{1,0:T(8,128)(2,1)S(1)} %get-tuple-element.49.centers_low, ...), custom_call_target="tpu_custom_call" | custom-call | flops 805306368 | bytes 2097152 | tf_op jit(solution)/shard_map/pallas_call | solution.py:228
  48.1 2.5 %collective-permute-start.7 = (f32[128,1024]{1,0:T(8,128)S(1)}, f32[128,1024]{1,0:T(8,128)S(1)}, u32[]{:S(2)}, u32[]{:S(2)}) collective-permute-start(f32[128,1024]{1,0:T(8,128)S(1)} %get-tuple-element.62), channel_id=1, source_target_pairs={{0,2},{16,30},{2,0},{18,20},{4,6},{20,18},{6,4},{22,24},{8,10},{24... | collective-permute-start | bytes 1572872 | tf_op jit(solution)/shard_map/ppermute | solution.py:92
  50.6 1.4 %collective-permute-done.5 = f32[128,1024]{1,0:T(8,128)S(1)} collective-permute-done((f32[128,1024]{1,0:T(8,128)S(1)}, f32[128,1024]{1,0:T(8,128)S(1)}, u32[]{:S(2)}, u32[]{:S(2)}) %collective-permute-start.5) | collective-permute-done | bytes 524320 | tf_op jit(solution)/shard_map/ppermute | solution.py:92
  52.0 3.7 %collective-permute-done.6 = f32[128,1024]{1,0:T(8,128)S(1)} collective-permute-done((f32[128,1024]{1,0:T(8,128)S(1)}, f32[128,1024]{1,0:T(8,128)S(1)}, u32[]{:S(2)}, u32[]{:S(2)}) %collective-permute-start.6) | collective-permute-done | bytes 524320 | tf_op jit(solution)/shard_map/ppermute | solution.py:92
  55.8 1.7 %collective-permute-done.7 = f32[128,1024]{1,0:T(8,128)S(1)} collective-permute-done((f32[128,1024]{1,0:T(8,128)S(1)}, f32[128,1024]{1,0:T(8,128)S(1)}, u32[]{:S(2)}, u32[]{:S(2)}) %collective-permute-start.7) | collective-permute-done | bytes 524320 | tf_op jit(solution)/shard_map/ppermute | solution.py:92
  57.7 13.6 %all_to_all.30.sums = f32[8,16,1024]{2,1,0:T(8,128)S(1)} all-to-all(f32[8,16,1024]{2,1,0:T(8,128)S(1)} %bitcast.29), channel_id=1, replica_groups={{0,162,1,163,64,226,65,227},{16,178,17,179,80,242,81,243},{4,166,5,167,..., dimensions={0} | all-to-all | bytes 1048576 | tf_op jit(solution)/shard_map/all_to_all | solution.py:96
  71.3 4.6 %collective-permute-start.10 = (f32[16,1024]{1,0:T(8,128)S(1)}, f32[16,1024]{1,0:T(8,128)S(1)}, u32[]{:S(2)}, u32[]{:S(2)}) collective-permute-start(f32[16,1024]{1,0:T(8,128)S(1)} %shard_map.74), channel_id=1, source_target_pairs={{0,12},{16,28},{2,14},{18,30},{4,0},{20,16},{6,2},{22,18},{8,4},{2... | collective-permute-start | bytes 196616 | tf_op jit(solution)/shard_map/ppermute | solution.py:92
  76.4 1.7 %collective-permute-start.9 = (f32[16,1024]{1,0:T(8,128)S(1)}, f32[16,1024]{1,0:T(8,128)S(1)}, u32[]{:S(2)}, u32[]{:S(2)}) collective-permute-start(f32[16,1024]{1,0:T(8,128)S(1)} %shard_map.74), channel_id=1, source_target_pairs={{0,4},{16,20},{2,6},{18,22},{4,8},{20,24},{6,10},{22,26},{8,12},{2... | collective-permute-start | bytes 196616 | tf_op jit(solution)/shard_map/ppermute | solution.py:92
  78.1 5.5 %collective-permute-done.8 = f32[16,1024]{1,0:T(8,128)S(1)} collective-permute-done((f32[16,1024]{1,0:T(8,128)S(1)}, f32[16,1024]{1,0:T(8,128)S(1)}, u32[]{:S(2)}, u32[]{:S(2)}) %collective-permute-start.8) | collective-permute-done | bytes 65568 | tf_op jit(solution)/shard_map/ppermute | solution.py:92
  83.6 12.8 %all_to_all.31 = f32[8,16,1024]{2,1,0:T(8,128)S(1)} all-to-all(f32[8,16,1024]{2,1,0:T(8,128)S(1)} %broadcast_in_dim.33), channel_id=1, replica_groups={{0,162,1,163,64,226,65,227},{16,178,17,179,80,242,81,243},{4,166,5,167,..., dimensions={0} | all-to-all | bytes 1048576 | tf_op jit(solution)/shard_map/all_to_all | solution.py:96
  96.4 3.8 %collective-permute-start.11 = (f32[128,1024]{1,0:T(8,128)S(1)}, f32[128,1024]{1,0:T(8,128)S(1)}, u32[]{:S(2)}, u32[]{:S(2)}) collective-permute-start(f32[128,1024]{1,0:T(8,128)S(1)} %bitcast.19), channel_id=1, source_target_pairs={{0,32},{16,112},{2,34},{18,114},{4,36},{20,116},{6,38},{22,118},{8... | collective-permute-start | bytes 1572872 | tf_op jit(solution)/shard_map/ppermute | solution.py:92
  100.3 3.2 %collective-permute-start.13 = (f32[128,1024]{1,0:T(8,128)S(1)}, f32[128,1024]{1,0:T(8,128)S(1)}, u32[]{:S(2)}, u32[]{:S(2)}) collective-permute-start(f32[128,1024]{1,0:T(8,128)S(1)} %bitcast.21), channel_id=1, source_target_pairs={{0,2},{16,30},{2,0},{18,20},{4,6},{20,18},{6,4},{22,24},{8,10},{24... | collective-permute-start | bytes 1572872 | tf_op jit(solution)/shard_map/ppermute | solution.py:92
  103.4 3.4 %collective-permute-done.11.refs_1_ = f32[128,1024]{1,0:T(8,128)S(1)} collective-permute-done((f32[128,1024]{1,0:T(8,128)S(1)}, f32[128,1024]{1,0:T(8,128)S(1)}, u32[]{:S(2)}, u32[]{:S(2)}) %collective-permute-start.11) | collective-permute-done | bytes 524320 | tf_op jit(solution)/shard_map/ppermute | solution.py:92
  106.8 2.7 %collective-permute-done.12.refs_2_ = f32[128,1024]{1,0:T(8,128)S(1)} collective-permute-done((f32[128,1024]{1,0:T(8,128)S(1)}, f32[128,1024]{1,0:T(8,128)S(1)}, u32[]{:S(2)}, u32[]{:S(2)}) %collective-permute-start.12) | collective-permute-done | bytes 524320 | tf_op jit(solution)/shard_map/ppermute | solution.py:92
  110.0 1.8 %shard_map.75 = (f32[1000,256]{1,0:T(8,128)S(1)}, f32[32,1000]{1,0:T(8,128)S(1)}) custom-call(s32[5]{0:T(128)S(1)} %stack.23.place, f32[128,1024]{1,0:T(8,128)S(1)} %bitcast.22, f32[128,1024]{1,0:T(8,128)S(1)} %collective-permute-done.11.refs_1_, f32[128,1024]{1,0:T(8,128)S(1)} %collective-permute-done.12.refs_2_, ...), custom_call_target="tpu_custom_call" | custom-call | flops 805306368 | bytes 2097152 | tf_op jit(solution)/shard_map/pallas_call | solution.py:228
  111.8 1.2 collective-permute-start.14
  113.0 1.8 %shard_map.76.own_delta = f32[1000,256]{1,0:T(8,128)S(1)} custom-call(s32[5]{0:T(128)S(1)} %stack.23.place, f32[128,1024]{1,0:T(8,128)S(1)} %bitcast.23, f32[128,1024]{1,0:T(8,128)S(1)} %collective-permute-done.11.refs_1_, f32[128,1024]{1,0:T(8,128)S(1)} %collective-permute-done.12.refs_2_, f32[128,1024]{1,0:T(8,128)S(1)} %collective-permute-done.13.refs_3_, ...), custom_call_target="tpu_custom_call" | custom-call | flops 805306368 | bytes 2097152 | tf_op jit(solution)/shard_map/pallas_call | solution.py:228
  114.8 0.6 collective-permute-done.15.theirs
  115.4 1.7 %shard_map.77 = (f32[1000,256]{1,0:T(8,128)}, f32[64,1000]{1,0:T(8,128)}) custom-call(s32[5]{0:T(128)S(1)} %stack.23.place, f32[1000,256]{1,0:T(8,128)S(1)} %bitcast.25, f32[1000,256]{1,0:T(8,128)S(1)} %shard_map.76.own_delta, f32[1000,256]{1,0:T(8,128)S(1)} %collective-permute-done.14.other_delta, f32[32,1000]{1,0:T(8,128)S(1)} %get-tuple-element.77.mine, ...), custom_call_target="tpu_custom_call" | custom-call | bytes 2097152 | tf_op jit(solution)/shard_map/pallas_call | solution.py:228
  (34 shorter events, 2.6 us)
Async XLA Ops:
  0.6 1.2 %copy-start = (f32[256,1024]{1,0:T(8,128)S(1)}, f32[256,1024]{1,0:T(8,128)}, u32[]{:S(2)}) copy-start(f32[256,1024]{1,0:T(8,128)} %param.6) | copy-start | bytes 3145732
  0.7 0.7 copy-start.4
  1.9 27.2 %copy-start.2 = (f32[256,1024]{1,0:T(8,128)S(1)}, f32[256,1024]{1,0:T(8,128)}, u32[]{:S(2)}) copy-start(f32[256,1024]{1,0:T(8,128)} %own_centers) | copy-start | bytes 3145732
  2.5 29.5 %copy-start.1 = (f32[256,1000]{0,1:T(8,128)S(1)}, f32[256,1000]{0,1:T(8,128)}, u32[]{:S(2)}) copy-start(f32[256,1000]{0,1:T(8,128)} %param.9) | copy-start | bytes 3072004
  2.6 35.0 %copy-start.3 = (f32[256,1000]{0,1:T(8,128)S(1)}, f32[256,1000]{0,1:T(8,128)}, u32[]{:S(2)}) copy-start(f32[256,1000]{0,1:T(8,128)} %param.7) | copy-start | bytes 3072004
  29.1 8.5 %collective-permute-start.3 = (f32[256,1024]{1,0:T(8,128)S(1)}, f32[256,1024]{1,0:T(8,128)S(1)}, u32[]{:S(2)}, u32[]{:S(2)}) collective-permute-start(f32[256,1024]{1,0:T(8,128)S(1)} %copy-done.2), channel_id=1, source_target_pairs={{0,16},{16,0},{2,18},{18,2},{4,20},{20,4},{6,22},{22,6},{8,24},{24... | collective-permute-start | bytes 3145736 | tf_op jit(solution)/shard_map/ppermute | solution.py:92
  32.0 5.6 %collective-permute-start.4 = (f32[256,1000]{0,1:T(8,128)S(1)}, f32[256,1000]{0,1:T(8,128)S(1)}, u32[]{:S(2)}, u32[]{:S(2)}) collective-permute-start(f32[256,1000]{0,1:T(8,128)S(1)} %copy-done.1), channel_id=1, source_target_pairs={{0,16},{16,0},{2,18},{18,2},{4,20},{20,4},{6,22},{22,6},{8,24},{24... | collective-permute-start | bytes 3072008 | tf_op jit(solution)/shard_map/ppermute | solution.py:92
  32.2 9.3 %collective-permute-start.2 = (f32[128,1024]{1,0:T(8,128)S(1)}, f32[128,1024]{1,0:T(8,128)S(1)}, u32[]{:S(2)}, u32[]{:S(2)}) collective-permute-start(f32[128,1024]{1,0:T(8,128)S(1)} %shard_map.68.rows), channel_id=1, source_target_pairs={{0,32},{16,112},{2,34},{18,114},{4,36},{20,116},{6,38},{22,118},{8... | collective-permute-start | bytes 1572872 | tf_op jit(solution)/shard_map/ppermute | solution.py:92
  34.8 10.5 %collective-permute-start.1 = (f32[128,1024]{1,0:T(8,128)S(1)}, f32[128,1024]{1,0:T(8,128)S(1)}, u32[]{:S(2)}, u32[]{:S(2)}) collective-permute-start(f32[128,1024]{1,0:T(8,128)S(1)} %shard_map.68.rows), channel_id=1, source_target_pairs={{0,128},{16,145},{2,130},{18,147},{4,132},{20,149},{6,134},{22,151... | collective-permute-start | bytes 1572872 | tf_op jit(solution)/shard_map/ppermute | solution.py:92
  35.2 11.7 %collective-permute-start = (f32[128,1024]{1,0:T(8,128)S(1)}, f32[128,1024]{1,0:T(8,128)S(1)}, u32[]{:S(2)}, u32[]{:S(2)}) collective-permute-start(f32[128,1024]{1,0:T(8,128)S(1)} %shard_map.68.rows), channel_id=1, source_target_pairs={{0,2},{16,30},{2,0},{18,20},{4,6},{20,18},{6,4},{22,24},{8,10},{24... | collective-permute-start | bytes 1572872 | tf_op jit(solution)/shard_map/ppermute | solution.py:92
  42.7 9.3 %collective-permute-start.5 = (f32[128,1024]{1,0:T(8,128)S(1)}, f32[128,1024]{1,0:T(8,128)S(1)}, u32[]{:S(2)}, u32[]{:S(2)}) collective-permute-start(f32[128,1024]{1,0:T(8,128)S(1)} %get-tuple-element.58), channel_id=1, source_target_pairs={{0,32},{16,112},{2,34},{18,114},{4,36},{20,116},{6,38},{22,118},{8... | collective-permute-start | bytes 1572872 | tf_op jit(solution)/shard_map/ppermute | solution.py:92
  46.4 9.3 %collective-permute-start.6 = (f32[128,1024]{1,0:T(8,128)S(1)}, f32[128,1024]{1,0:T(8,128)S(1)}, u32[]{:S(2)}, u32[]{:S(2)}) collective-permute-start(f32[128,1024]{1,0:T(8,128)S(1)} %get-tuple-element.60), channel_id=1, source_target_pairs={{0,128},{16,145},{2,130},{18,147},{4,132},{20,149},{6,134},{22,151... | collective-permute-start | bytes 1572872 | tf_op jit(solution)/shard_map/ppermute | solution.py:92
  48.1 9.3 %collective-permute-start.7 = (f32[128,1024]{1,0:T(8,128)S(1)}, f32[128,1024]{1,0:T(8,128)S(1)}, u32[]{:S(2)}, u32[]{:S(2)}) collective-permute-start(f32[128,1024]{1,0:T(8,128)S(1)} %get-tuple-element.62), channel_id=1, source_target_pairs={{0,2},{16,30},{2,0},{18,20},{4,6},{20,18},{6,4},{22,24},{8,10},{24... | collective-permute-start | bytes 1572872 | tf_op jit(solution)/shard_map/ppermute | solution.py:92
  71.3 6.8 %collective-permute-start.10 = (f32[16,1024]{1,0:T(8,128)S(1)}, f32[16,1024]{1,0:T(8,128)S(1)}, u32[]{:S(2)}, u32[]{:S(2)}) collective-permute-start(f32[16,1024]{1,0:T(8,128)S(1)} %shard_map.74), channel_id=1, source_target_pairs={{0,12},{16,28},{2,14},{18,30},{4,0},{20,16},{6,2},{22,18},{8,4},{2... | collective-permute-start | bytes 196616 | tf_op jit(solution)/shard_map/ppermute | solution.py:92
  75.9 7.6 %collective-permute-start.8 = (f32[16,1024]{1,0:T(8,128)S(1)}, f32[16,1024]{1,0:T(8,128)S(1)}, u32[]{:S(2)}, u32[]{:S(2)}) collective-permute-start(f32[16,1024]{1,0:T(8,128)S(1)} %shard_map.74), channel_id=1, source_target_pairs={{0,8},{16,24},{2,10},{18,26},{4,12},{20,28},{6,14},{22,30},{8,0},{... | collective-permute-start | bytes 196616 | tf_op jit(solution)/shard_map/ppermute | solution.py:92
  76.4 7.2 %collective-permute-start.9 = (f32[16,1024]{1,0:T(8,128)S(1)}, f32[16,1024]{1,0:T(8,128)S(1)}, u32[]{:S(2)}, u32[]{:S(2)}) collective-permute-start(f32[16,1024]{1,0:T(8,128)S(1)} %shard_map.74), channel_id=1, source_target_pairs={{0,4},{16,20},{2,6},{18,22},{4,8},{20,24},{6,10},{22,26},{8,12},{2... | collective-permute-start | bytes 196616 | tf_op jit(solution)/shard_map/ppermute | solution.py:92
  96.4 10.4 %collective-permute-start.11 = (f32[128,1024]{1,0:T(8,128)S(1)}, f32[128,1024]{1,0:T(8,128)S(1)}, u32[]{:S(2)}, u32[]{:S(2)}) collective-permute-start(f32[128,1024]{1,0:T(8,128)S(1)} %bitcast.19), channel_id=1, source_target_pairs={{0,32},{16,112},{2,34},{18,114},{4,36},{20,116},{6,38},{22,118},{8... | collective-permute-start | bytes 1572872 | tf_op jit(solution)/shard_map/ppermute | solution.py:92
  100.3 9.2 %collective-permute-start.12 = (f32[128,1024]{1,0:T(8,128)S(1)}, f32[128,1024]{1,0:T(8,128)S(1)}, u32[]{:S(2)}, u32[]{:S(2)}) collective-permute-start(f32[128,1024]{1,0:T(8,128)S(1)} %bitcast.20), channel_id=1, source_target_pairs={{0,128},{16,145},{2,130},{18,147},{4,132},{20,149},{6,134},{22,151... | collective-permute-start | bytes 1572872 | tf_op jit(solution)/shard_map/ppermute | solution.py:92
  100.3 9.7 %collective-permute-start.13 = (f32[128,1024]{1,0:T(8,128)S(1)}, f32[128,1024]{1,0:T(8,128)S(1)}, u32[]{:S(2)}, u32[]{:S(2)}) collective-permute-start(f32[128,1024]{1,0:T(8,128)S(1)} %bitcast.21), channel_id=1, source_target_pairs={{0,2},{16,30},{2,0},{18,20},{4,6},{20,18},{6,4},{22,24},{8,10},{24... | collective-permute-start | bytes 1572872 | tf_op jit(solution)/shard_map/ppermute | solution.py:92
  111.8 3.6 %collective-permute-start.14 = (f32[1000,256]{1,0:T(8,128)S(1)}, f32[1000,256]{1,0:T(8,128)S(1)}, u32[]{:S(2)}, u32[]{:S(2)}) collective-permute-start(f32[1000,256]{1,0:T(8,128)S(1)} %get-tuple-element.72), channel_id=1, source_target_pairs={{0,16},{16,0},{2,18},{18,2},{4,20},{20,4},{6,22},{22,6},{8,24},{24... | collective-permute-start | bytes 3072008 | tf_op jit(solution)/shard_map/ppermute | solution.py:92
  112.9 2.4 %collective-permute-start.15 = (f32[32,1000]{1,0:T(8,128)S(1)}, f32[32,1000]{1,0:T(8,128)S(1)}, u32[]{:S(2)}, u32[]{:S(2)}) collective-permute-start(f32[32,1000]{1,0:T(8,128)S(1)} %get-tuple-element.77.mine), channel_id=1, source_target_pairs={{0,16},{16,0},{2,18},{18,2},{4,20},{20,4},{6,22},{22,6},{8,24},{24... | collective-permute-start | bytes 384008 | tf_op jit(solution)/shard_map/ppermute | solution.py:92

commit v13 on v12

--- a/solution.py
+++ b/solution.py
@@ -163,16 +163,21 @@
         targets[pl.ds(start + row, 1), :] = turned_labels[pl.ds(index[row], 1), :]
 
 
-def quarter_kernel(
-    rows, centers_high, centers_low, center_sq, weights_high, weights_low, value, high, low
-):
-    features = rows.shape[1]
-    part = rows[...]
+def quarters_kernel(count, *refs):
+    rows, refs = refs[:count], refs[count:]
+    centers_high, centers_low, center_sq, weights_high, weights_low = refs[:5]
+    values, highs, lows = (refs[5 + i * count : 5 + (i + 1) * count] for i in range(3))
+    quarter, features = rows[0].shape
+    part = jnp.concatenate([ref[...] for ref in rows], axis=0)
     row_sq = jnp.sum(part * part, axis=1, keepdims=True)
     inner = product(parts(part), (centers_high[...], centers_low[...]), ((1,), (0,)))
     kernel = parts(jnp.exp((2.0 * features - row_sq - center_sq[...] + 2.0 * inner) / 128.0))
-    high[...], low[...] = kernel
-    value[...] = product(kernel, (weights_high[...], weights_low[...]), ((1,), (0,)))
+    value = product(kernel, (weights_high[...], weights_low[...]), ((1,), (0,)))
+    for i in range(count):
+        place = slice(i * quarter, (i + 1) * quarter)
+        values[i][...] = value[place]
+        highs[i][...] = kernel[0][place]
+        lows[i][...] = kernel[1][place]
 
 
 def order_kernel(own, found, out):
@@ -261,13 +266,18 @@
     wanted_index = jnp.sum(jnp.where(match, batch_index[None, :], 0), axis=1)
     rows = pick(train_features, wanted_index)
     place = jnp.stack([x, y_lo, y_hi, z, core]).astype(jnp.int32)
-    rows, place, index = lax.optimization_barrier((rows, place, index))
+    rows, place, index, own_centers, own_weights = lax.optimization_barrier(
+        (rows, place, index, centers, weights)
+    )
+    other_centers, other_weights = permute(own_centers, SWAP), permute(own_weights, SWAP)
     sent = jnp.broadcast_to(
         rows.reshape(2, 1, 2, 2 * own, features), (2, LEVELS // 2, 2, 2 * own, features)
     )
     found = exchange(sent.reshape(-1, features), LINES)
-    found, centers, own_weights, train_labels = lax.optimization_barrier(
-        (found, centers, weights, train_labels)
+    found, own_centers, own_weights, other_centers, other_weights, train_labels = (
+        lax.optimization_barrier(
+            (found, own_centers, own_weights, other_centers, other_weights, train_labels)
+        )
     )
     (column,) = call(
         functools.partial(order_kernel, own), ((found.shape, jnp.float32),), found
@@ -287,36 +297,33 @@
         ),
         index,
         place,
-        centers,
-        permute(centers, SWAP),
+        own_centers,
+        other_centers,
         own_weights.T,
-        permute(own_weights, SWAP).T,
+        other_weights.T,
         train_labels.T,
         scratch=(((train_labels.shape[0], lanes), jnp.float32),),
         scalars=2,
     )
 
-    def quarter_of(part):
-        return call(
-            quarter_kernel,
-            (
-                ((quarter, lanes), jnp.float32),
-                ((quarter, pair), jnp.bfloat16),
-                ((quarter, pair), jnp.bfloat16),
-            ),
-            part,
+    def quarters_of(*rows):
+        count = len(rows)
+        found = call(
+            functools.partial(quarters_kernel, count),
+            (((quarter, lanes), jnp.float32),) * count
+            + (((quarter, pair), jnp.bfloat16),) * 2 * count,
+            *rows,
             *held,
-            products=3 * quarter * pair * (features + lanes),
+            products=3 * count * quarter * pair * (features + lanes),
         )
+        return list(zip(found[:count], found[count : 2 * count], found[2 * count :]))
 
     first_rows, *later = quarters(column)
-    done = [quarter_of(first_rows)]
+    done = quarters_of(first_rows)
     value = done[0][0]
-    sums = []
-    for way, part in zip(WAYS, later):
-        part, value = lax.optimization_barrier((part, value))
-        done.append(quarter_of(part))
-        sums.append(permute(done[way][0], swap_pairs(way)))
+    *later, value = lax.optimization_barrier((*later, value))
+    done += quarters_of(*later)
+    sums = [permute(done[way][0], swap_pairs(way)) for way in WAYS]
     for found in sums:
         value = value + found
     sums = exchange(value, PLANES).reshape(len(PLANES[0]), column_rows, lanes)

time: 117 us -> 117 us (level)
  waiting for transfers between devices: 20.2 us -> 26.8 us
  blocking collectives: 52.9 us -> 47.9 us
  starting transfers between devices: 29 us -> 26.9 us
    ppermute x16, waiting for transfers between devices: 20.2 us -> 26.8 us  [permute(): return lax.ppermute(array, AXES, pairs)]
    all_to_all x3, blocking collectives: 52.9 us -> 47.9 us  [exchange(): lax.all_to_all(array, AXES, 0, 0, axis_index_groups=groups, tiled=True)]
    ppermute x16, starting transfers between devices: 29 us -> 26.9 us  [permute(): return lax.ppermute(array, AXES, pairs)]
    pallas_call x10 -> x8, Pallas kernels: 12.1 us -> 11.4 us  [call(): pl.pallas_call(kernel, in_specs=[pl.BlockSpec(memory_space=pltpu.SMEM)] *...]
  transfers between devices with their start and end apart: 16 -> 16, of which waited for: 9 -> 10; matrix products, arithmetic and copies ran while one was open for 0% -> 0% of each run, Pallas kernels for 7% -> 4%
where the time goes in v13:
time: 117 us
  blocking collectives  47.9 us (41%)
  starting transfers between devices  26.9 us (23%)
  waiting for transfers between devices  26.8 us (23%)
  Pallas kernels  11.4 us (10%)
  local copies, waits for them, and re-layouts  1.69 us (1%)
    all_to_all x3, blocking collectives, exchange(): lax.all_to_all(array, AXES, 0, 0, axis_index_groups=groups, tiled=True)  47.9 us
    ppermute x16, starting transfers between devices, permute(): return lax.ppermute(array, AXES, pairs)  26.9 us
    ppermute x16, waiting for transfers between devices, permute(): return lax.ppermute(array, AXES, pairs)  26.8 us
    pallas_call x8, Pallas kernels, call(): pl.pallas_call(kernel, in_specs=[pl.BlockSpec(memory_space=pltpu.SMEM)] *...  11.4 us
  transfers between devices with their start and end apart: 16, of which 10 were waited for; matrix products, arithmetic and copies ran while one was open for 0% of the time, Pallas kernels for 4%

profile of v13, /device:TPU:1, one launch (start us, length us, event | category | flops | bytes accessed | tf_op | source)
XLA Modules:
  0.0 116.5 jit_solution(6773934131399494217)
XLA Ops:
  0.7 0.9 dynamic_slice.3.index
  1.6 0.8 select_reduce_fusion
  2.4 0.6 gather_fusion
  3.1 3.3 %collective-permute-start = (f32[256,1024]{1,0:T(8,128)}, f32[256,1024]{1,0:T(8,128)S(1)}, u32[]{:S(2)}, u32[]{:S(2)}) collective-permute-start(f32[256,1024]{1,0:T(8,128)} %own_centers), channel_id=1, source_target_pairs={{0,16},{16,0},{2,18},{18,2},{4,20},{20,4},{6,22},{22,6},{8,24},{24... | collective-permute-start | bytes 3145736 | tf_op jit(solution)/shard_map/ppermute | solution.py:92
  6.6 23.4 %all_to_all.29 = f32[16,8,1024]{2,1,0:T(8,128)S(1)} all-to-all(f32[16,8,1024]{2,1,0:T(8,128)S(1)} %bitcast.30), channel_id=1, replica_groups={{0,2,4,6,8,10,12,14,129,131,133,135,137,139,141,143},{16,18,20,22,24,26..., dimensions={0} | all-to-all | bytes 1048576 | tf_op jit(solution)/shard_map/all_to_all | solution.py:96
  30.1 2.2 %collective-permute-start.4 = (f32[128,1024]{1,0:T(8,128)S(1)}, f32[128,1024]{1,0:T(8,128)S(1)}, u32[]{:S(2)}, u32[]{:S(2)}) collective-permute-start(f32[128,1024]{1,0:T(8,128)S(1)} %shard_map.68.refs_0_), channel_id=1, source_target_pairs={{0,2},{16,30},{2,0},{18,20},{4,6},{20,18},{6,4},{22,24},{8,10},{24... | collective-permute-start | bytes 1572872 | tf_op jit(solution)/shard_map/ppermute | solution.py:92
  32.3 1.8 %collective-permute-start.3 = (f32[128,1024]{1,0:T(8,128)S(1)}, f32[128,1024]{1,0:T(8,128)S(1)}, u32[]{:S(2)}, u32[]{:S(2)}) collective-permute-start(f32[128,1024]{1,0:T(8,128)S(1)} %shard_map.68.refs_0_), channel_id=1, source_target_pairs={{0,128},{16,145},{2,130},{18,147},{4,132},{20,149},{6,134},{22,151... | collective-permute-start | bytes 1572872 | tf_op jit(solution)/shard_map/ppermute | solution.py:92
  34.1 2.5 %collective-permute-start.2 = (f32[128,1024]{1,0:T(8,128)S(1)}, f32[128,1024]{1,0:T(8,128)S(1)}, u32[]{:S(2)}, u32[]{:S(2)}) collective-permute-start(f32[128,1024]{1,0:T(8,128)S(1)} %shard_map.68.refs_0_), channel_id=1, source_target_pairs={{0,32},{16,112},{2,34},{18,114},{4,36},{20,116},{6,38},{22,118},{8... | collective-permute-start | bytes 1572872 | tf_op jit(solution)/shard_map/ppermute | solution.py:92
  36.6 2.0 %shard_map.69 = (bf16[1024,512]{1,0:T(8,128)(2,1)S(1)}, bf16[1024,512]{1,0:T(8,128)(2,1)S(1)}, f32[1,512]{1,0:T(1,128)S(1)}, bf16[512,1024]{1,0:T(8,128)(2,1)S(1...) custom-call(s32[4]{0:T(128)S(1)} %dynamic_slice.3.index, s32[5]{0:T(128)S(1)} %stack.23.place, ...), custom_call_target="tpu_custom_call" | custom-call | bytes 2097152 | tf_op jit(solution)/shard_map/pallas_call | solution.py:233
  38.6 1.2 shard_map.70
  39.8 1.8 %collective-permute-done.3.refs_1_ = f32[128,1024]{1,0:T(8,128)S(1)} collective-permute-done((f32[128,1024]{1,0:T(8,128)S(1)}, f32[128,1024]{1,0:T(8,128)S(1)}, u32[]{:S(2)}, u32[]{:S(2)}) %collective-permute-start.3) | collective-permute-done | bytes 524320 | tf_op jit(solution)/shard_map/ppermute | solution.py:92
  41.6 1.8 %collective-permute-done.2.refs_0_ = f32[128,1024]{1,0:T(8,128)S(1)} collective-permute-done((f32[128,1024]{1,0:T(8,128)S(1)}, f32[128,1024]{1,0:T(8,128)S(1)}, u32[]{:S(2)}, u32[]{:S(2)}) %collective-permute-start.2) | collective-permute-done | bytes 524320 | tf_op jit(solution)/shard_map/ppermute | solution.py:92
  43.3 2.8 %shard_map.71 = (f32[128,1024]{1,0:T(8,128)S(1)}, f32[128,1024]{1,0:T(8,128)S(1)}, f32[128,1024]{1,0:T(8,128)S(1)}, bf16[128,512]{1,0:T(8,128)(2,1)S(1)}, bf16[1...) custom-call(f32[128,1024]{1,0:T(8,128)S(1)} %collective-permute-done, ...), custom_call_target="tpu_custom_call" | custom-call | flops 2415919104 | bytes 2097152 | tf_op jit(solution)/shard_map/pallas_call | solution.py:233
  46.2 2.6 %collective-permute-start.5 = (f32[128,1024]{1,0:T(8,128)S(1)}, f32[128,1024]{1,0:T(8,128)S(1)}, u32[]{:S(2)}, u32[]{:S(2)}) collective-permute-start(f32[128,1024]{1,0:T(8,128)S(1)} %get-tuple-element.64), channel_id=1, source_target_pairs={{0,32},{16,112},{2,34},{18,114},{4,36},{20,116},{6,38},{22,118},{8... | collective-permute-start | bytes 1572872 | tf_op jit(solution)/shard_map/ppermute | solution.py:92
  48.7 0.9 collective-permute-start.6
  50.2 5.3 %collective-permute-done.5 = f32[128,1024]{1,0:T(8,128)S(1)} collective-permute-done((f32[128,1024]{1,0:T(8,128)S(1)}, f32[128,1024]{1,0:T(8,128)S(1)}, u32[]{:S(2)}, u32[]{:S(2)}) %collective-permute-start.5) | collective-permute-done | bytes 524320 | tf_op jit(solution)/shard_map/ppermute | solution.py:92
  55.5 2.5 %collective-permute-done.6 = f32[128,1024]{1,0:T(8,128)S(1)} collective-permute-done((f32[128,1024]{1,0:T(8,128)S(1)}, f32[128,1024]{1,0:T(8,128)S(1)}, u32[]{:S(2)}, u32[]{:S(2)}) %collective-permute-start.6) | collective-permute-done | bytes 524320 | tf_op jit(solution)/shard_map/ppermute | solution.py:92
  58.0 0.9 collective-permute-done.7
  59.1 12.3 %all_to_all.30.sums = f32[8,16,1024]{2,1,0:T(8,128)S(1)} all-to-all(f32[8,16,1024]{2,1,0:T(8,128)S(1)} %bitcast.29), channel_id=1, replica_groups={{0,162,1,163,64,226,65,227},{16,178,17,179,80,242,81,243},{4,166,5,167,..., dimensions={0} | all-to-all | bytes 1048576 | tf_op jit(solution)/shard_map/all_to_all | solution.py:96
  71.4 1.3 %collective-permute-start.10 = (f32[16,1024]{1,0:T(8,128)S(1)}, f32[16,1024]{1,0:T(8,128)S(1)}, u32[]{:S(2)}, u32[]{:S(2)}) collective-permute-start(f32[16,1024]{1,0:T(8,128)S(1)} %shard_map.72), channel_id=1, source_target_pairs={{0,12},{16,28},{2,14},{18,30},{4,0},{20,16},{6,2},{22,18},{8,4},{2... | collective-permute-start | bytes 196616 | tf_op jit(solution)/shard_map/ppermute | solution.py:92
  72.7 2.8 %collective-permute-start.9 = (f32[16,1024]{1,0:T(8,128)S(1)}, f32[16,1024]{1,0:T(8,128)S(1)}, u32[]{:S(2)}, u32[]{:S(2)}) collective-permute-start(f32[16,1024]{1,0:T(8,128)S(1)} %shard_map.72), channel_id=1, source_target_pairs={{0,4},{16,20},{2,6},{18,22},{4,8},{20,24},{6,10},{22,26},{8,12},{2... | collective-permute-start | bytes 196616 | tf_op jit(solution)/shard_map/ppermute | solution.py:92
  75.5 3.2 %collective-permute-start.8 = (f32[16,1024]{1,0:T(8,128)S(1)}, f32[16,1024]{1,0:T(8,128)S(1)}, u32[]{:S(2)}, u32[]{:S(2)}) collective-permute-start(f32[16,1024]{1,0:T(8,128)S(1)} %shard_map.72), channel_id=1, source_target_pairs={{0,8},{16,24},{2,10},{18,26},{4,12},{20,28},{6,14},{22,30},{8,0},{... | collective-permute-start | bytes 196616 | tf_op jit(solution)/shard_map/ppermute | solution.py:92
  78.7 5.0 %collective-permute-done.8 = f32[16,1024]{1,0:T(8,128)S(1)} collective-permute-done((f32[16,1024]{1,0:T(8,128)S(1)}, f32[16,1024]{1,0:T(8,128)S(1)}, u32[]{:S(2)}, u32[]{:S(2)}) %collective-permute-start.8) | collective-permute-done | bytes 65568 | tf_op jit(solution)/shard_map/ppermute | solution.py:92
  83.8 12.2 %all_to_all.31 = f32[8,16,1024]{2,1,0:T(8,128)S(1)} all-to-all(f32[8,16,1024]{2,1,0:T(8,128)S(1)} %broadcast_in_dim.33), channel_id=1, replica_groups={{0,162,1,163,64,226,65,227},{16,178,17,179,80,242,81,243},{4,166,5,167,..., dimensions={0} | all-to-all | bytes 1048576 | tf_op jit(solution)/shard_map/all_to_all | solution.py:96
  96.0 1.8 %collective-permute-start.13 = (f32[128,1024]{1,0:T(8,128)S(1)}, f32[128,1024]{1,0:T(8,128)S(1)}, u32[]{:S(2)}, u32[]{:S(2)}) collective-permute-start(f32[128,1024]{1,0:T(8,128)S(1)} %bitcast.19), channel_id=1, source_target_pairs={{0,2},{16,30},{2,0},{18,20},{4,6},{20,18},{6,4},{22,24},{8,10},{24... | collective-permute-start | bytes 1572872 | tf_op jit(solution)/shard_map/ppermute | solution.py:92
  98.6 6.6 %collective-permute-done.13.refs_3_ = f32[128,1024]{1,0:T(8,128)S(1)} collective-permute-done((f32[128,1024]{1,0:T(8,128)S(1)}, f32[128,1024]{1,0:T(8,128)S(1)}, u32[]{:S(2)}, u32[]{:S(2)}) %collective-permute-start.13) | collective-permute-done | bytes 524320 | tf_op jit(solution)/shard_map/ppermute | solution.py:92
  105.3 1.8 %collective-permute-done.12.refs_2_ = f32[128,1024]{1,0:T(8,128)S(1)} collective-permute-done((f32[128,1024]{1,0:T(8,128)S(1)}, f32[128,1024]{1,0:T(8,128)S(1)}, u32[]{:S(2)}, u32[]{:S(2)}) %collective-permute-start.12) | collective-permute-done | bytes 524320 | tf_op jit(solution)/shard_map/ppermute | solution.py:92
  107.5 1.8 %shard_map.73 = (f32[1000,256]{1,0:T(8,128)S(1)}, f32[32,1000]{1,0:T(8,128)S(1)}) custom-call(s32[5]{0:T(128)S(1)} %stack.23.place, f32[128,1024]{1,0:T(8,128)S(1)} %bitcast.22, f32[128,1024]{1,0:T(8,128)S(1)} %collective-permute-done.11.refs_1_, f32[128,1024]{1,0:T(8,128)S(1)} %collective-permute-done.12.refs_2_, ...), custom_call_target="tpu_custom_call" | custom-call | flops 805306368 | bytes 2097152 | tf_op jit(solution)/shard_map/pallas_call | solution.py:233
  109.3 3.1 %collective-permute-start.14 = (f32[1000,256]{1,0:T(8,128)S(1)}, f32[1000,256]{1,0:T(8,128)S(1)}, u32[]{:S(2)}, u32[]{:S(2)}) collective-permute-start(f32[1000,256]{1,0:T(8,128)S(1)} %get-tuple-element.76), channel_id=1, source_target_pairs={{0,16},{16,0},{2,18},{18,2},{4,20},{20,4},{6,22},{22,6},{8,24},{24... | collective-permute-start | bytes 3072008 | tf_op jit(solution)/shard_map/ppermute | solution.py:92
  112.4 1.7 %shard_map.74.own_delta = f32[1000,256]{1,0:T(8,128)S(1)} custom-call(s32[5]{0:T(128)S(1)} %stack.23.place, f32[128,1024]{1,0:T(8,128)S(1)} %bitcast.23, f32[128,1024]{1,0:T(8,128)S(1)} %collective-permute-done.11.refs_1_, f32[128,1024]{1,0:T(8,128)S(1)} %collective-permute-done.12.refs_2_, f32[128,1024]{1,0:T(8,128)S(1)} %collective-permute-done.13.refs_3_, ...), custom_call_target="tpu_custom_call" | custom-call | flops 805306368 | bytes 2097152 | tf_op jit(solution)/shard_map/pallas_call | solution.py:233
  114.2 0.6 collective-permute-done.15.theirs
  114.8 1.7 %shard_map.75 = (f32[1000,256]{1,0:T(8,128)}, f32[64,1000]{1,0:T(8,128)}) custom-call(s32[5]{0:T(128)S(1)} %stack.23.place, f32[1000,256]{1,0:T(8,128)S(1)} %bitcast.25, f32[1000,256]{1,0:T(8,128)S(1)} %shard_map.74.own_delta, f32[1000,256]{1,0:T(8,128)S(1)} %collective-permute-done.14.other_delta, f32[32,1000]{1,0:T(8,128)S(1)} %get-tuple-element.81.mine, ...), custom_call_target="tpu_custom_call" | custom-call | bytes 2097152 | tf_op jit(solution)/shard_map/pallas_call | solution.py:233
  (30 shorter events, 2.7 us)
Async XLA Ops:
  0.6 1.8 %copy-start = (f32[256,1024]{1,0:T(8,128)S(1)}, f32[256,1024]{1,0:T(8,128)}, u32[]{:S(2)}) copy-start(f32[256,1024]{1,0:T(8,128)} %param.6) | copy-start | bytes 3145732
  0.6 5.8 %copy-start.1 = (f32[256,1000]{0,1:T(8,128)S(1)}, f32[256,1000]{0,1:T(8,128)}, u32[]{:S(2)}) copy-start(f32[256,1000]{0,1:T(8,128)} %param.9) | copy-start | bytes 3072004
  3.1 26.9 %collective-permute-start = (f32[256,1024]{1,0:T(8,128)}, f32[256,1024]{1,0:T(8,128)S(1)}, u32[]{:S(2)}, u32[]{:S(2)}) collective-permute-start(f32[256,1024]{1,0:T(8,128)} %own_centers), channel_id=1, source_target_pairs={{0,16},{16,0},{2,18},{18,2},{4,20},{20,4},{6,22},{22,6},{8,24},{24... | collective-permute-start | bytes 3145736 | tf_op jit(solution)/shard_map/ppermute | solution.py:92
  6.4 23.6 %collective-permute-start.1 = (f32[256,1000]{0,1:T(8,128)S(1)}, f32[256,1000]{0,1:T(8,128)S(1)}, u32[]{:S(2)}, u32[]{:S(2)}) collective-permute-start(f32[256,1000]{0,1:T(8,128)S(1)} %copy-done.1), channel_id=1, source_target_pairs={{0,16},{16,0},{2,18},{18,2},{4,20},{20,4},{6,22},{22,6},{8,24},{24... | collective-permute-start | bytes 3072008 | tf_op jit(solution)/shard_map/ppermute | solution.py:92
  6.6 30.0 %copy-start.2 = (f32[256,1024]{1,0:T(8,128)S(1)}, f32[256,1024]{1,0:T(8,128)}, u32[]{:S(2)}) copy-start(f32[256,1024]{1,0:T(8,128)} %own_centers) | copy-start | bytes 3145732
  6.6 30.0 %copy-start.3 = (f32[256,1000]{0,1:T(8,128)S(1)}, f32[256,1000]{0,1:T(8,128)}, u32[]{:S(2)}) copy-start(f32[256,1000]{0,1:T(8,128)} %param.7) | copy-start | bytes 3072004
  30.1 9.6 %collective-permute-start.4 = (f32[128,1024]{1,0:T(8,128)S(1)}, f32[128,1024]{1,0:T(8,128)S(1)}, u32[]{:S(2)}, u32[]{:S(2)}) collective-permute-start(f32[128,1024]{1,0:T(8,128)S(1)} %shard_map.68.refs_0_), channel_id=1, source_target_pairs={{0,2},{16,30},{2,0},{18,20},{4,6},{20,18},{6,4},{22,24},{8,10},{24... | collective-permute-start | bytes 1572872 | tf_op jit(solution)/shard_map/ppermute | solution.py:92
  32.3 9.2 %collective-permute-start.3 = (f32[128,1024]{1,0:T(8,128)S(1)}, f32[128,1024]{1,0:T(8,128)S(1)}, u32[]{:S(2)}, u32[]{:S(2)}) collective-permute-start(f32[128,1024]{1,0:T(8,128)S(1)} %shard_map.68.refs_0_), channel_id=1, source_target_pairs={{0,128},{16,145},{2,130},{18,147},{4,132},{20,149},{6,134},{22,151... | collective-permute-start | bytes 1572872 | tf_op jit(solution)/shard_map/ppermute | solution.py:92
  34.1 9.2 %collective-permute-start.2 = (f32[128,1024]{1,0:T(8,128)S(1)}, f32[128,1024]{1,0:T(8,128)S(1)}, u32[]{:S(2)}, u32[]{:S(2)}) collective-permute-start(f32[128,1024]{1,0:T(8,128)S(1)} %shard_map.68.refs_0_), channel_id=1, source_target_pairs={{0,32},{16,112},{2,34},{18,114},{4,36},{20,116},{6,38},{22,118},{8... | collective-permute-start | bytes 1572872 | tf_op jit(solution)/shard_map/ppermute | solution.py:92
  46.2 9.3 %collective-permute-start.5 = (f32[128,1024]{1,0:T(8,128)S(1)}, f32[128,1024]{1,0:T(8,128)S(1)}, u32[]{:S(2)}, u32[]{:S(2)}) collective-permute-start(f32[128,1024]{1,0:T(8,128)S(1)} %get-tuple-element.64), channel_id=1, source_target_pairs={{0,32},{16,112},{2,34},{18,114},{4,36},{20,116},{6,38},{22,118},{8... | collective-permute-start | bytes 1572872 | tf_op jit(solution)/shard_map/ppermute | solution.py:92
  48.7 9.2 %collective-permute-start.6 = (f32[128,1024]{1,0:T(8,128)S(1)}, f32[128,1024]{1,0:T(8,128)S(1)}, u32[]{:S(2)}, u32[]{:S(2)}) collective-permute-start(f32[128,1024]{1,0:T(8,128)S(1)} %get-tuple-element.65), channel_id=1, source_target_pairs={{0,128},{16,145},{2,130},{18,147},{4,132},{20,149},{6,134},{22,151... | collective-permute-start | bytes 1572872 | tf_op jit(solution)/shard_map/ppermute | solution.py:92
  49.7 9.2 %collective-permute-start.7 = (f32[128,1024]{1,0:T(8,128)S(1)}, f32[128,1024]{1,0:T(8,128)S(1)}, u32[]{:S(2)}, u32[]{:S(2)}) collective-permute-start(f32[128,1024]{1,0:T(8,128)S(1)} %get-tuple-element.66), channel_id=1, source_target_pairs={{0,2},{16,30},{2,0},{18,20},{4,6},{20,18},{6,4},{22,24},{8,10},{24... | collective-permute-start | bytes 1572872 | tf_op jit(solution)/shard_map/ppermute | solution.py:92
  71.4 7.3 %collective-permute-start.10 = (f32[16,1024]{1,0:T(8,128)S(1)}, f32[16,1024]{1,0:T(8,128)S(1)}, u32[]{:S(2)}, u32[]{:S(2)}) collective-permute-start(f32[16,1024]{1,0:T(8,128)S(1)} %shard_map.72), channel_id=1, source_target_pairs={{0,12},{16,28},{2,14},{18,30},{4,0},{20,16},{6,2},{22,18},{8,4},{2... | collective-permute-start | bytes 196616 | tf_op jit(solution)/shard_map/ppermute | solution.py:92
  72.7 6.0 %collective-permute-start.9 = (f32[16,1024]{1,0:T(8,128)S(1)}, f32[16,1024]{1,0:T(8,128)S(1)}, u32[]{:S(2)}, u32[]{:S(2)}) collective-permute-start(f32[16,1024]{1,0:T(8,128)S(1)} %shard_map.72), channel_id=1, source_target_pairs={{0,4},{16,20},{2,6},{18,22},{4,8},{20,24},{6,10},{22,26},{8,12},{2... | collective-permute-start | bytes 196616 | tf_op jit(solution)/shard_map/ppermute | solution.py:92
  75.5 8.2 %collective-permute-start.8 = (f32[16,1024]{1,0:T(8,128)S(1)}, f32[16,1024]{1,0:T(8,128)S(1)}, u32[]{:S(2)}, u32[]{:S(2)}) collective-permute-start(f32[16,1024]{1,0:T(8,128)S(1)} %shard_map.72), channel_id=1, source_target_pairs={{0,8},{16,24},{2,10},{18,26},{4,12},{20,28},{6,14},{22,30},{8,0},{... | collective-permute-start | bytes 196616 | tf_op jit(solution)/shard_map/ppermute | solution.py:92
  96.0 9.2 %collective-permute-start.13 = (f32[128,1024]{1,0:T(8,128)S(1)}, f32[128,1024]{1,0:T(8,128)S(1)}, u32[]{:S(2)}, u32[]{:S(2)}) collective-permute-start(f32[128,1024]{1,0:T(8,128)S(1)} %bitcast.19), channel_id=1, source_target_pairs={{0,2},{16,30},{2,0},{18,20},{4,6},{20,18},{6,4},{22,24},{8,10},{24... | collective-permute-start | bytes 1572872 | tf_op jit(solution)/shard_map/ppermute | solution.py:92
  97.8 9.2 %collective-permute-start.12 = (f32[128,1024]{1,0:T(8,128)S(1)}, f32[128,1024]{1,0:T(8,128)S(1)}, u32[]{:S(2)}, u32[]{:S(2)}) collective-permute-start(f32[128,1024]{1,0:T(8,128)S(1)} %bitcast.20), channel_id=1, source_target_pairs={{0,128},{16,145},{2,130},{18,147},{4,132},{20,149},{6,134},{22,151... | collective-permute-start | bytes 1572872 | tf_op jit(solution)/shard_map/ppermute | solution.py:92
  98.3 9.2 %collective-permute-start.11 = (f32[128,1024]{1,0:T(8,128)S(1)}, f32[128,1024]{1,0:T(8,128)S(1)}, u32[]{:S(2)}, u32[]{:S(2)}) collective-permute-start(f32[128,1024]{1,0:T(8,128)S(1)} %bitcast.21), channel_id=1, source_target_pairs={{0,32},{16,112},{2,34},{18,114},{4,36},{20,116},{6,38},{22,118},{8... | collective-permute-start | bytes 1572872 | tf_op jit(solution)/shard_map/ppermute | solution.py:92
  109.3 5.5 %collective-permute-start.14 = (f32[1000,256]{1,0:T(8,128)S(1)}, f32[1000,256]{1,0:T(8,128)S(1)}, u32[]{:S(2)}, u32[]{:S(2)}) collective-permute-start(f32[1000,256]{1,0:T(8,128)S(1)} %get-tuple-element.76), channel_id=1, source_target_pairs={{0,16},{16,0},{2,18},{18,2},{4,20},{20,4},{6,22},{22,6},{8,24},{24... | collective-permute-start | bytes 3072008 | tf_op jit(solution)/shard_map/ppermute | solution.py:92
  112.3 2.4 %collective-permute-start.15 = (f32[32,1000]{1,0:T(8,128)S(1)}, f32[32,1000]{1,0:T(8,128)S(1)}, u32[]{:S(2)}, u32[]{:S(2)}) collective-permute-start(f32[32,1000]{1,0:T(8,128)S(1)} %get-tuple-element.81.mine), channel_id=1, source_target_pairs={{0,16},{16,0},{2,18},{18,2},{4,20},{20,4},{6,22},{22,6},{8,24},{24... | collective-permute-start | bytes 384008 | tf_op jit(solution)/shard_map/ppermute | solution.py:92

commit v14 on v12

--- a/solution.py
+++ b/solution.py
@@ -261,13 +261,18 @@
     wanted_index = jnp.sum(jnp.where(match, batch_index[None, :], 0), axis=1)
     rows = pick(train_features, wanted_index)
     place = jnp.stack([x, y_lo, y_hi, z, core]).astype(jnp.int32)
-    rows, place, index = lax.optimization_barrier((rows, place, index))
+    rows, place, index, own_centers, own_weights = lax.optimization_barrier(
+        (rows, place, index, centers, weights)
+    )
+    other_centers, other_weights = permute(own_centers, SWAP), permute(own_weights, SWAP)
     sent = jnp.broadcast_to(
         rows.reshape(2, 1, 2, 2 * own, features), (2, LEVELS // 2, 2, 2 * own, features)
     )
     found = exchange(sent.reshape(-1, features), LINES)
-    found, centers, own_weights, train_labels = lax.optimization_barrier(
-        (found, centers, weights, train_labels)
+    found, own_centers, own_weights, other_centers, other_weights, train_labels = (
+        lax.optimization_barrier(
+            (found, own_centers, own_weights, other_centers, other_weights, train_labels)
+        )
     )
     (column,) = call(
         functools.partial(order_kernel, own), ((found.shape, jnp.float32),), found
@@ -287,10 +292,10 @@
         ),
         index,
         place,
-        centers,
-        permute(centers, SWAP),
+        own_centers,
+        other_centers,
         own_weights.T,
-        permute(own_weights, SWAP).T,
+        other_weights.T,
         train_labels.T,
         scratch=(((train_labels.shape[0], lanes), jnp.float32),),
         scalars=2,

time: 117 us -> 116 us (level)
  blocking collectives: 52.9 us -> 49.1 us
  starting transfers between devices: 29 us -> 30.5 us
    all_to_all x3, blocking collectives: 52.9 us -> 49.1 us  [exchange(): lax.all_to_all(array, AXES, 0, 0, axis_index_groups=groups, tiled=True)]
    ppermute x16, starting transfers between devices: 29 us -> 30.5 us  [permute(): return lax.ppermute(array, AXES, pairs)]
where the time goes in v14:
time: 116 us
  blocking collectives  49.1 us (42%)
  starting transfers between devices  30.5 us (26%)
  waiting for transfers between devices  20.8 us (18%)
  Pallas kernels  12.1 us (10%)
  local copies, waits for them, and re-layouts  1.55 us (1%)
  other arithmetic  1.19 us (1%)
    all_to_all x3, blocking collectives, exchange(): lax.all_to_all(array, AXES, 0, 0, axis_index_groups=groups, tiled=True)  49.1 us
    ppermute x16, starting transfers between devices, permute(): return lax.ppermute(array, AXES, pairs)  30.5 us
    ppermute x16, waiting for transfers between devices, permute(): return lax.ppermute(array, AXES, pairs)  20.8 us
    pallas_call x10, Pallas kernels, call(): pl.pallas_call(kernel, in_specs=[pl.BlockSpec(memory_space=pltpu.SMEM)] *...  12.1 us
  transfers between devices with their start and end apart: 16, of which 9 were waited for; matrix products, arithmetic and copies ran while one was open for 0% of the time, Pallas kernels for 7%

profile of v14, /device:TPU:1, one launch (start us, length us, event | category | flops | bytes accessed | tf_op | source)
XLA Modules:
  0.0 116.1 jit_solution(17398800949613018641)
XLA Ops:
  0.7 1.0 select_reduce_fusion
  1.7 0.7 dynamic_slice.3.index
  3.1 3.3 %collective-permute-start = (f32[256,1024]{1,0:T(8,128)}, f32[256,1024]{1,0:T(8,128)S(1)}, u32[]{:S(2)}, u32[]{:S(2)}) collective-permute-start(f32[256,1024]{1,0:T(8,128)} %own_centers), channel_id=1, source_target_pairs={{0,16},{16,0},{2,18},{18,2},{4,20},{20,4},{6,22},{22,6},{8,24},{24... | collective-permute-start | bytes 3145736 | tf_op jit(solution)/shard_map/ppermute | solution.py:92
  6.6 23.4 %all_to_all.29 = f32[16,8,1024]{2,1,0:T(8,128)S(1)} all-to-all(f32[16,8,1024]{2,1,0:T(8,128)S(1)} %bitcast.30), channel_id=1, replica_groups={{0,2,4,6,8,10,12,14,129,131,133,135,137,139,141,143},{16,18,20,22,24,26..., dimensions={0} | all-to-all | bytes 1048576 | tf_op jit(solution)/shard_map/all_to_all | solution.py:96
  30.1 2.6 %collective-permute-start.4 = (f32[128,1024]{1,0:T(8,128)S(1)}, f32[128,1024]{1,0:T(8,128)S(1)}, u32[]{:S(2)}, u32[]{:S(2)}) collective-permute-start(f32[128,1024]{1,0:T(8,128)S(1)} %shard_map.68.rows), channel_id=1, source_target_pairs={{0,32},{16,112},{2,34},{18,114},{4,36},{20,116},{6,38},{22,118},{8... | collective-permute-start | bytes 1572872 | tf_op jit(solution)/shard_map/ppermute | solution.py:92
  33.3 3.2 %collective-permute-start.2 = (f32[128,1024]{1,0:T(8,128)S(1)}, f32[128,1024]{1,0:T(8,128)S(1)}, u32[]{:S(2)}, u32[]{:S(2)}) collective-permute-start(f32[128,1024]{1,0:T(8,128)S(1)} %shard_map.68.rows), channel_id=1, source_target_pairs={{0,2},{16,30},{2,0},{18,20},{4,6},{20,18},{6,4},{22,24},{8,10},{24... | collective-permute-start | bytes 1572872 | tf_op jit(solution)/shard_map/ppermute | solution.py:92
  36.6 2.1 %shard_map.69 = (bf16[1024,512]{1,0:T(8,128)(2,1)S(1)}, bf16[1024,512]{1,0:T(8,128)(2,1)S(1)}, f32[1,512]{1,0:T(1,128)S(1)}, bf16[512,1024]{1,0:T(8,128)(2,1)S(1...) custom-call(s32[4]{0:T(128)S(1)} %dynamic_slice.3.index, s32[5]{0:T(128)S(1)} %stack.23.place, ...), custom_call_target="tpu_custom_call" | custom-call | bytes 2097152 | tf_op jit(solution)/shard_map/pallas_call | solution.py:228
  38.7 1.1 shard_map.70
  39.8 1.1 shard_map.71
  41.0 2.2 %collective-permute-start.5 = (f32[128,1024]{1,0:T(8,128)S(1)}, f32[128,1024]{1,0:T(8,128)S(1)}, u32[]{:S(2)}, u32[]{:S(2)}) collective-permute-start(f32[128,1024]{1,0:T(8,128)S(1)} %get-tuple-element.66), channel_id=1, source_target_pairs={{0,32},{16,112},{2,34},{18,114},{4,36},{20,116},{6,38},{22,118},{8... | collective-permute-start | bytes 1572872 | tf_op jit(solution)/shard_map/ppermute | solution.py:92
  43.2 1.1 shard_map.72
  44.3 0.7 collective-permute-start.6
  45.1 1.2 %shard_map.73 = (f32[128,1024]{1,0:T(8,128)S(1)}, bf16[128,512]{1,0:T(8,128)(2,1)S(1)}, bf16[128,512]{1,0:T(8,128)(2,1)S(1)}) custom-call(f32[128,1024]{1,0:T(8,128)S(1)} %collective-permute-done.2.rows, bf16[1024,512]{1,0:T(8,128)(2,1)S(1)} %get-tuple-element.56.centers_high, bf16[1024,512]{1,0:T(8,128)(2,1)S(1)} %get-tuple-element.57.centers_low, ...), custom_call_target="tpu_custom_call" | custom-call | flops 805306368 | bytes 2097152 | tf_op jit(solution)/shard_map/pallas_call | solution.py:228
  46.3 3.3 %collective-permute-start.7 = (f32[128,1024]{1,0:T(8,128)S(1)}, f32[128,1024]{1,0:T(8,128)S(1)}, u32[]{:S(2)}, u32[]{:S(2)}) collective-permute-start(f32[128,1024]{1,0:T(8,128)S(1)} %get-tuple-element.70), channel_id=1, source_target_pairs={{0,2},{16,30},{2,0},{18,20},{4,6},{20,18},{6,4},{22,24},{8,10},{24... | collective-permute-start | bytes 1572872 | tf_op jit(solution)/shard_map/ppermute | solution.py:92
  49.6 0.7 collective-permute-done.5
  50.3 3.3 %collective-permute-done.6 = f32[128,1024]{1,0:T(8,128)S(1)} collective-permute-done((f32[128,1024]{1,0:T(8,128)S(1)}, f32[128,1024]{1,0:T(8,128)S(1)}, u32[]{:S(2)}, u32[]{:S(2)}) %collective-permute-start.6) | collective-permute-done | bytes 524320 | tf_op jit(solution)/shard_map/ppermute | solution.py:92
  53.6 2.5 %collective-permute-done.7 = f32[128,1024]{1,0:T(8,128)S(1)} collective-permute-done((f32[128,1024]{1,0:T(8,128)S(1)}, f32[128,1024]{1,0:T(8,128)S(1)}, u32[]{:S(2)}, u32[]{:S(2)}) %collective-permute-start.7) | collective-permute-done | bytes 524320 | tf_op jit(solution)/shard_map/ppermute | solution.py:92
  56.3 12.7 %all_to_all.30.sums = f32[8,16,1024]{2,1,0:T(8,128)S(1)} all-to-all(f32[8,16,1024]{2,1,0:T(8,128)S(1)} %bitcast.29), channel_id=1, replica_groups={{0,162,1,163,64,226,65,227},{16,178,17,179,80,242,81,243},{4,166,5,167,..., dimensions={0} | all-to-all | bytes 1048576 | tf_op jit(solution)/shard_map/all_to_all | solution.py:96
  69.1 2.8 %collective-permute-start.10 = (f32[16,1024]{1,0:T(8,128)S(1)}, f32[16,1024]{1,0:T(8,128)S(1)}, u32[]{:S(2)}, u32[]{:S(2)}) collective-permute-start(f32[16,1024]{1,0:T(8,128)S(1)} %shard_map.74), channel_id=1, source_target_pairs={{0,12},{16,28},{2,14},{18,30},{4,0},{20,16},{6,2},{22,18},{8,4},{2... | collective-permute-start | bytes 196616 | tf_op jit(solution)/shard_map/ppermute | solution.py:92
  71.9 3.0 %collective-permute-start.8 = (f32[16,1024]{1,0:T(8,128)S(1)}, f32[16,1024]{1,0:T(8,128)S(1)}, u32[]{:S(2)}, u32[]{:S(2)}) collective-permute-start(f32[16,1024]{1,0:T(8,128)S(1)} %shard_map.74), channel_id=1, source_target_pairs={{0,8},{16,24},{2,10},{18,26},{4,12},{20,28},{6,14},{22,30},{8,0},{... | collective-permute-start | bytes 196616 | tf_op jit(solution)/shard_map/ppermute | solution.py:92
  74.9 1.2 %collective-permute-start.9 = (f32[16,1024]{1,0:T(8,128)S(1)}, f32[16,1024]{1,0:T(8,128)S(1)}, u32[]{:S(2)}, u32[]{:S(2)}) collective-permute-start(f32[16,1024]{1,0:T(8,128)S(1)} %shard_map.74), channel_id=1, source_target_pairs={{0,4},{16,20},{2,6},{18,22},{4,8},{20,24},{6,10},{22,26},{8,12},{2... | collective-permute-start | bytes 196616 | tf_op jit(solution)/shard_map/ppermute | solution.py:92
  76.1 2.9 %collective-permute-done.8 = f32[16,1024]{1,0:T(8,128)S(1)} collective-permute-done((f32[16,1024]{1,0:T(8,128)S(1)}, f32[16,1024]{1,0:T(8,128)S(1)}, u32[]{:S(2)}, u32[]{:S(2)}) %collective-permute-start.8) | collective-permute-done | bytes 65568 | tf_op jit(solution)/shard_map/ppermute | solution.py:92
  79.0 1.6 %collective-permute-done.9 = f32[16,1024]{1,0:T(8,128)S(1)} collective-permute-done((f32[16,1024]{1,0:T(8,128)S(1)}, f32[16,1024]{1,0:T(8,128)S(1)}, u32[]{:S(2)}, u32[]{:S(2)}) %collective-permute-start.9) | collective-permute-done | bytes 65568 | tf_op jit(solution)/shard_map/ppermute | solution.py:92
  80.6 12.9 %all_to_all.31 = f32[8,16,1024]{2,1,0:T(8,128)S(1)} all-to-all(f32[8,16,1024]{2,1,0:T(8,128)S(1)} %broadcast_in_dim.33), channel_id=1, replica_groups={{0,162,1,163,64,226,65,227},{16,178,17,179,80,242,81,243},{4,166,5,167,..., dimensions={0} | all-to-all | bytes 1048576 | tf_op jit(solution)/shard_map/all_to_all | solution.py:96
  93.6 2.6 %collective-permute-start.12 = (f32[128,1024]{1,0:T(8,128)S(1)}, f32[128,1024]{1,0:T(8,128)S(1)}, u32[]{:S(2)}, u32[]{:S(2)}) collective-permute-start(f32[128,1024]{1,0:T(8,128)S(1)} %bitcast.20), channel_id=1, source_target_pairs={{0,128},{16,145},{2,130},{18,147},{4,132},{20,149},{6,134},{22,151... | collective-permute-start | bytes 1572872 | tf_op jit(solution)/shard_map/ppermute | solution.py:92
  96.1 6.8 %collective-permute-done.11.refs_1_ = f32[128,1024]{1,0:T(8,128)S(1)} collective-permute-done((f32[128,1024]{1,0:T(8,128)S(1)}, f32[128,1024]{1,0:T(8,128)S(1)}, u32[]{:S(2)}, u32[]{:S(2)}) %collective-permute-start.11) | collective-permute-done | bytes 524320 | tf_op jit(solution)/shard_map/ppermute | solution.py:92
  102.9 1.3 %collective-permute-done.12.refs_2_ = f32[128,1024]{1,0:T(8,128)S(1)} collective-permute-done((f32[128,1024]{1,0:T(8,128)S(1)}, f32[128,1024]{1,0:T(8,128)S(1)}, u32[]{:S(2)}, u32[]{:S(2)}) %collective-permute-start.12) | collective-permute-done | bytes 524320 | tf_op jit(solution)/shard_map/ppermute | solution.py:92
  104.2 1.2 %collective-permute-done.13.refs_3_ = f32[128,1024]{1,0:T(8,128)S(1)} collective-permute-done((f32[128,1024]{1,0:T(8,128)S(1)}, f32[128,1024]{1,0:T(8,128)S(1)}, u32[]{:S(2)}, u32[]{:S(2)}) %collective-permute-start.13) | collective-permute-done | bytes 524320 | tf_op jit(solution)/shard_map/ppermute | solution.py:92
  105.4 1.8 %shard_map.75 = (f32[1000,256]{1,0:T(8,128)S(1)}, f32[32,1000]{1,0:T(8,128)S(1)}) custom-call(s32[5]{0:T(128)S(1)} %stack.23.place, f32[128,1024]{1,0:T(8,128)S(1)} %bitcast.22, f32[128,1024]{1,0:T(8,128)S(1)} %collective-permute-done.11.refs_1_, f32[128,1024]{1,0:T(8,128)S(1)} %collective-permute-done.12.refs_2_, ...), custom_call_target="tpu_custom_call" | custom-call | flops 805306368 | bytes 2097152 | tf_op jit(solution)/shard_map/pallas_call | solution.py:228
  107.2 4.8 %collective-permute-start.14 = (f32[1000,256]{1,0:T(8,128)S(1)}, f32[1000,256]{1,0:T(8,128)S(1)}, u32[]{:S(2)}, u32[]{:S(2)}) collective-permute-start(f32[1000,256]{1,0:T(8,128)S(1)} %get-tuple-element.80), channel_id=1, source_target_pairs={{0,16},{16,0},{2,18},{18,2},{4,20},{20,4},{6,22},{22,6},{8,24},{24... | collective-permute-start | bytes 3072008 | tf_op jit(solution)/shard_map/ppermute | solution.py:92
  112.0 1.8 %shard_map.76.own_delta = f32[1000,256]{1,0:T(8,128)S(1)} custom-call(s32[5]{0:T(128)S(1)} %stack.23.place, f32[128,1024]{1,0:T(8,128)S(1)} %bitcast.23, f32[128,1024]{1,0:T(8,128)S(1)} %collective-permute-done.11.refs_1_, f32[128,1024]{1,0:T(8,128)S(1)} %collective-permute-done.12.refs_2_, f32[128,1024]{1,0:T(8,128)S(1)} %collective-permute-done.13.refs_3_, ...), custom_call_target="tpu_custom_call" | custom-call | flops 805306368 | bytes 2097152 | tf_op jit(solution)/shard_map/pallas_call | solution.py:228
  114.4 1.7 %shard_map.77 = (f32[1000,256]{1,0:T(8,128)}, f32[64,1000]{1,0:T(8,128)}) custom-call(s32[5]{0:T(128)S(1)} %stack.23.place, f32[1000,256]{1,0:T(8,128)S(1)} %bitcast.25, f32[1000,256]{1,0:T(8,128)S(1)} %shard_map.76.own_delta, f32[1000,256]{1,0:T(8,128)S(1)} %collective-permute-done.14.other_delta, f32[32,1000]{1,0:T(8,128)S(1)} %get-tuple-element.85.mine, ...), custom_call_target="tpu_custom_call" | custom-call | bytes 2097152 | tf_op jit(solution)/shard_map/pallas_call | solution.py:228
  (32 shorter events, 2.6 us)
Async XLA Ops:
  0.6 1.8 %copy-start = (f32[256,1024]{1,0:T(8,128)S(1)}, f32[256,1024]{1,0:T(8,128)}, u32[]{:S(2)}) copy-start(f32[256,1024]{1,0:T(8,128)} %param.6) | copy-start | bytes 3145732
  0.6 5.8 %copy-start.1 = (f32[256,1000]{0,1:T(8,128)S(1)}, f32[256,1000]{0,1:T(8,128)}, u32[]{:S(2)}) copy-start(f32[256,1000]{0,1:T(8,128)} %param.9) | copy-start | bytes 3072004
  3.1 26.9 %collective-permute-start = (f32[256,1024]{1,0:T(8,128)}, f32[256,1024]{1,0:T(8,128)S(1)}, u32[]{:S(2)}, u32[]{:S(2)}) collective-permute-start(f32[256,1024]{1,0:T(8,128)} %own_centers), channel_id=1, source_target_pairs={{0,16},{16,0},{2,18},{18,2},{4,20},{20,4},{6,22},{22,6},{8,24},{24... | collective-permute-start | bytes 3145736 | tf_op jit(solution)/shard_map/ppermute | solution.py:92
  6.4 23.6 %collective-permute-start.1 = (f32[256,1000]{0,1:T(8,128)S(1)}, f32[256,1000]{0,1:T(8,128)S(1)}, u32[]{:S(2)}, u32[]{:S(2)}) collective-permute-start(f32[256,1000]{0,1:T(8,128)S(1)} %copy-done.1), channel_id=1, source_target_pairs={{0,16},{16,0},{2,18},{18,2},{4,20},{20,4},{6,22},{22,6},{8,24},{24... | collective-permute-start | bytes 3072008 | tf_op jit(solution)/shard_map/ppermute | solution.py:92
  6.6 30.0 %copy-start.2 = (f32[256,1024]{1,0:T(8,128)S(1)}, f32[256,1024]{1,0:T(8,128)}, u32[]{:S(2)}) copy-start(f32[256,1024]{1,0:T(8,128)} %own_centers) | copy-start | bytes 3145732
  6.6 30.0 %copy-start.3 = (f32[256,1000]{0,1:T(8,128)S(1)}, f32[256,1000]{0,1:T(8,128)}, u32[]{:S(2)}) copy-start(f32[256,1000]{0,1:T(8,128)} %param.7) | copy-start | bytes 3072004
  30.1 9.7 %collective-permute-start.4 = (f32[128,1024]{1,0:T(8,128)S(1)}, f32[128,1024]{1,0:T(8,128)S(1)}, u32[]{:S(2)}, u32[]{:S(2)}) collective-permute-start(f32[128,1024]{1,0:T(8,128)S(1)} %shard_map.68.rows), channel_id=1, source_target_pairs={{0,32},{16,112},{2,34},{18,114},{4,36},{20,116},{6,38},{22,118},{8... | collective-permute-start | bytes 1572872 | tf_op jit(solution)/shard_map/ppermute | solution.py:92
  32.7 10.5 %collective-permute-start.3 = (f32[128,1024]{1,0:T(8,128)S(1)}, f32[128,1024]{1,0:T(8,128)S(1)}, u32[]{:S(2)}, u32[]{:S(2)}) collective-permute-start(f32[128,1024]{1,0:T(8,128)S(1)} %shard_map.68.rows), channel_id=1, source_target_pairs={{0,128},{16,145},{2,130},{18,147},{4,132},{20,149},{6,134},{22,151... | collective-permute-start | bytes 1572872 | tf_op jit(solution)/shard_map/ppermute | solution.py:92
  33.3 11.7 %collective-permute-start.2 = (f32[128,1024]{1,0:T(8,128)S(1)}, f32[128,1024]{1,0:T(8,128)S(1)}, u32[]{:S(2)}, u32[]{:S(2)}) collective-permute-start(f32[128,1024]{1,0:T(8,128)S(1)} %shard_map.68.rows), channel_id=1, source_target_pairs={{0,2},{16,30},{2,0},{18,20},{4,6},{20,18},{6,4},{22,24},{8,10},{24... | collective-permute-start | bytes 1572872 | tf_op jit(solution)/shard_map/ppermute | solution.py:92
  41.0 9.3 %collective-permute-start.5 = (f32[128,1024]{1,0:T(8,128)S(1)}, f32[128,1024]{1,0:T(8,128)S(1)}, u32[]{:S(2)}, u32[]{:S(2)}) collective-permute-start(f32[128,1024]{1,0:T(8,128)S(1)} %get-tuple-element.66), channel_id=1, source_target_pairs={{0,32},{16,112},{2,34},{18,114},{4,36},{20,116},{6,38},{22,118},{8... | collective-permute-start | bytes 1572872 | tf_op jit(solution)/shard_map/ppermute | solution.py:92
  44.3 9.3 %collective-permute-start.6 = (f32[128,1024]{1,0:T(8,128)S(1)}, f32[128,1024]{1,0:T(8,128)S(1)}, u32[]{:S(2)}, u32[]{:S(2)}) collective-permute-start(f32[128,1024]{1,0:T(8,128)S(1)} %get-tuple-element.68), channel_id=1, source_target_pairs={{0,128},{16,145},{2,130},{18,147},{4,132},{20,149},{6,134},{22,151... | collective-permute-start | bytes 1572872 | tf_op jit(solution)/shard_map/ppermute | solution.py:92
  46.3 9.9 %collective-permute-start.7 = (f32[128,1024]{1,0:T(8,128)S(1)}, f32[128,1024]{1,0:T(8,128)S(1)}, u32[]{:S(2)}, u32[]{:S(2)}) collective-permute-start(f32[128,1024]{1,0:T(8,128)S(1)} %get-tuple-element.70), channel_id=1, source_target_pairs={{0,2},{16,30},{2,0},{18,20},{4,6},{20,18},{6,4},{22,24},{8,10},{24... | collective-permute-start | bytes 1572872 | tf_op jit(solution)/shard_map/ppermute | solution.py:92
  69.1 7.0 %collective-permute-start.10 = (f32[16,1024]{1,0:T(8,128)S(1)}, f32[16,1024]{1,0:T(8,128)S(1)}, u32[]{:S(2)}, u32[]{:S(2)}) collective-permute-start(f32[16,1024]{1,0:T(8,128)S(1)} %shard_map.74), channel_id=1, source_target_pairs={{0,12},{16,28},{2,14},{18,30},{4,0},{20,16},{6,2},{22,18},{8,4},{2... | collective-permute-start | bytes 196616 | tf_op jit(solution)/shard_map/ppermute | solution.py:92
  71.9 7.1 %collective-permute-start.8 = (f32[16,1024]{1,0:T(8,128)S(1)}, f32[16,1024]{1,0:T(8,128)S(1)}, u32[]{:S(2)}, u32[]{:S(2)}) collective-permute-start(f32[16,1024]{1,0:T(8,128)S(1)} %shard_map.74), channel_id=1, source_target_pairs={{0,8},{16,24},{2,10},{18,26},{4,12},{20,28},{6,14},{22,30},{8,0},{... | collective-permute-start | bytes 196616 | tf_op jit(solution)/shard_map/ppermute | solution.py:92
  74.9 5.7 %collective-permute-start.9 = (f32[16,1024]{1,0:T(8,128)S(1)}, f32[16,1024]{1,0:T(8,128)S(1)}, u32[]{:S(2)}, u32[]{:S(2)}) collective-permute-start(f32[16,1024]{1,0:T(8,128)S(1)} %shard_map.74), channel_id=1, source_target_pairs={{0,4},{16,20},{2,6},{18,22},{4,8},{20,24},{6,10},{22,26},{8,12},{2... | collective-permute-start | bytes 196616 | tf_op jit(solution)/shard_map/ppermute | solution.py:92
  93.6 9.4 %collective-permute-start.11 = (f32[128,1024]{1,0:T(8,128)S(1)}, f32[128,1024]{1,0:T(8,128)S(1)}, u32[]{:S(2)}, u32[]{:S(2)}) collective-permute-start(f32[128,1024]{1,0:T(8,128)S(1)} %bitcast.19), channel_id=1, source_target_pairs={{0,32},{16,112},{2,34},{18,114},{4,36},{20,116},{6,38},{22,118},{8... | collective-permute-start | bytes 1572872 | tf_op jit(solution)/shard_map/ppermute | solution.py:92
  93.6 10.7 %collective-permute-start.12 = (f32[128,1024]{1,0:T(8,128)S(1)}, f32[128,1024]{1,0:T(8,128)S(1)}, u32[]{:S(2)}, u32[]{:S(2)}) collective-permute-start(f32[128,1024]{1,0:T(8,128)S(1)} %bitcast.20), channel_id=1, source_target_pairs={{0,128},{16,145},{2,130},{18,147},{4,132},{20,149},{6,134},{22,151... | collective-permute-start | bytes 1572872 | tf_op jit(solution)/shard_map/ppermute | solution.py:92
  96.1 9.2 %collective-permute-start.13 = (f32[128,1024]{1,0:T(8,128)S(1)}, f32[128,1024]{1,0:T(8,128)S(1)}, u32[]{:S(2)}, u32[]{:S(2)}) collective-permute-start(f32[128,1024]{1,0:T(8,128)S(1)} %bitcast.21), channel_id=1, source_target_pairs={{0,2},{16,30},{2,0},{18,20},{4,6},{20,18},{6,4},{22,24},{8,10},{24... | collective-permute-start | bytes 1572872 | tf_op jit(solution)/shard_map/ppermute | solution.py:92
  107.2 7.2 %collective-permute-start.14 = (f32[1000,256]{1,0:T(8,128)S(1)}, f32[1000,256]{1,0:T(8,128)S(1)}, u32[]{:S(2)}, u32[]{:S(2)}) collective-permute-start(f32[1000,256]{1,0:T(8,128)S(1)} %get-tuple-element.80), channel_id=1, source_target_pairs={{0,16},{16,0},{2,18},{18,2},{4,20},{20,4},{6,22},{22,6},{8,24},{24... | collective-permute-start | bytes 3072008 | tf_op jit(solution)/shard_map/ppermute | solution.py:92
  111.9 2.4 %collective-permute-start.15 = (f32[32,1000]{1,0:T(8,128)S(1)}, f32[32,1000]{1,0:T(8,128)S(1)}, u32[]{:S(2)}, u32[]{:S(2)}) collective-permute-start(f32[32,1000]{1,0:T(8,128)S(1)} %get-tuple-element.85.mine), channel_id=1, source_target_pairs={{0,16},{16,0},{2,18},{18,2},{4,20},{20,4},{6,22},{22,6},{8,24},{24... | collective-permute-start | bytes 384008 | tf_op jit(solution)/shard_map/ppermute | solution.py:92

commit v15 on v14

--- a/solution.py
+++ b/solution.py
@@ -169,10 +169,19 @@
     features = rows.shape[1]
     part = rows[...]
     row_sq = jnp.sum(part * part, axis=1, keepdims=True)
-    inner = product(parts(part), (centers_high[...], centers_low[...]), ((1,), (0,)))
+    inner = stacked_product(parts(part), (centers_high[...], centers_low[...]))
     kernel = parts(jnp.exp((2.0 * features - row_sq - center_sq[...] + 2.0 * inner) / 128.0))
     high[...], low[...] = kernel
-    value[...] = product(kernel, (weights_high[...], weights_low[...]), ((1,), (0,)))
+    value[...] = stacked_product(kernel, (weights_high[...], weights_low[...]))
+
+
+def stacked_product(left, right):
+    def one(a, b):
+        return jnp.dot(a, b, preferred_element_type=jnp.float32)
+
+    rows = left[0].shape[0]
+    both = one(jnp.concatenate(left, axis=0), right[0])
+    return both[:rows] + (one(left[0], right[1]) + both[rows:])
 
 
 def order_kernel(own, found, out):

time: 116 us -> 116 us (level)
  no operation moved by 1% of the time
where the time goes in v15:
time: 116 us
  blocking collectives  49 us (42%)
  starting transfers between devices  30.6 us (26%)
  waiting for transfers between devices  20.8 us (18%)
  Pallas kernels  12 us (10%)
  local copies, waits for them, and re-layouts  1.55 us (1%)
  other arithmetic  1.19 us (1%)
    all_to_all x3, blocking collectives, exchange(): lax.all_to_all(array, AXES, 0, 0, axis_index_groups=groups, tiled=True)  49 us
    ppermute x16, starting transfers between devices, permute(): return lax.ppermute(array, AXES, pairs)  30.6 us
    ppermute x16, waiting for transfers between devices, permute(): return lax.ppermute(array, AXES, pairs)  20.8 us
    pallas_call x10, Pallas kernels, call(): pl.pallas_call(kernel, in_specs=[pl.BlockSpec(memory_space=pltpu.SMEM)] *...  12 us
  transfers between devices with their start and end apart: 16, of which 9 were waited for; matrix products, arithmetic and copies ran while one was open for 0% of the time, Pallas kernels for 7%

profile of v15, /device:TPU:1, one launch (start us, length us, event | category | flops | bytes accessed | tf_op | source)
XLA Modules:
  0.0 116.0 jit_solution(5640941276161808772)
XLA Ops:
  0.7 1.0 select_reduce_fusion
  1.7 0.7 dynamic_slice.3.index
  3.1 3.3 %collective-permute-start = (f32[256,1024]{1,0:T(8,128)}, f32[256,1024]{1,0:T(8,128)S(1)}, u32[]{:S(2)}, u32[]{:S(2)}) collective-permute-start(f32[256,1024]{1,0:T(8,128)} %own_centers), channel_id=1, source_target_pairs={{0,16},{16,0},{2,18},{18,2},{4,20},{20,4},{6,22},{22,6},{8,24},{24... | collective-permute-start | bytes 3145736 | tf_op jit(solution)/shard_map/ppermute | solution.py:92
  6.6 23.4 %all_to_all.29 = f32[16,8,1024]{2,1,0:T(8,128)S(1)} all-to-all(f32[16,8,1024]{2,1,0:T(8,128)S(1)} %bitcast.30), channel_id=1, replica_groups={{0,2,4,6,8,10,12,14,129,131,133,135,137,139,141,143},{16,18,20,22,24,26..., dimensions={0} | all-to-all | bytes 1048576 | tf_op jit(solution)/shard_map/all_to_all | solution.py:96
  30.1 2.6 %collective-permute-start.4 = (f32[128,1024]{1,0:T(8,128)S(1)}, f32[128,1024]{1,0:T(8,128)S(1)}, u32[]{:S(2)}, u32[]{:S(2)}) collective-permute-start(f32[128,1024]{1,0:T(8,128)S(1)} %shard_map.68.rows), channel_id=1, source_target_pairs={{0,32},{16,112},{2,34},{18,114},{4,36},{20,116},{6,38},{22,118},{8... | collective-permute-start | bytes 1572872 | tf_op jit(solution)/shard_map/ppermute | solution.py:92
  33.3 3.2 %collective-permute-start.2 = (f32[128,1024]{1,0:T(8,128)S(1)}, f32[128,1024]{1,0:T(8,128)S(1)}, u32[]{:S(2)}, u32[]{:S(2)}) collective-permute-start(f32[128,1024]{1,0:T(8,128)S(1)} %shard_map.68.rows), channel_id=1, source_target_pairs={{0,2},{16,30},{2,0},{18,20},{4,6},{20,18},{6,4},{22,24},{8,10},{24... | collective-permute-start | bytes 1572872 | tf_op jit(solution)/shard_map/ppermute | solution.py:92
  36.6 2.1 %shard_map.69 = (bf16[1024,512]{1,0:T(8,128)(2,1)S(1)}, bf16[1024,512]{1,0:T(8,128)(2,1)S(1)}, f32[1,512]{1,0:T(1,128)S(1)}, bf16[512,1024]{1,0:T(8,128)(2,1)S(1...) custom-call(s32[4]{0:T(128)S(1)} %dynamic_slice.3.index, s32[5]{0:T(128)S(1)} %stack.23.place, ...), custom_call_target="tpu_custom_call" | custom-call | bytes 2097152 | tf_op jit(solution)/shard_map/pallas_call | solution.py:237
  38.7 1.1 shard_map.70
  39.8 1.1 shard_map.71
  40.9 2.2 %collective-permute-start.5 = (f32[128,1024]{1,0:T(8,128)S(1)}, f32[128,1024]{1,0:T(8,128)S(1)}, u32[]{:S(2)}, u32[]{:S(2)}) collective-permute-start(f32[128,1024]{1,0:T(8,128)S(1)} %get-tuple-element.66), channel_id=1, source_target_pairs={{0,32},{16,112},{2,34},{18,114},{4,36},{20,116},{6,38},{22,118},{8... | collective-permute-start | bytes 1572872 | tf_op jit(solution)/shard_map/ppermute | solution.py:92
  43.1 1.1 shard_map.72
  44.3 0.7 collective-permute-start.6
  45.0 1.2 shard_map.73
  46.2 3.3 %collective-permute-start.7 = (f32[128,1024]{1,0:T(8,128)S(1)}, f32[128,1024]{1,0:T(8,128)S(1)}, u32[]{:S(2)}, u32[]{:S(2)}) collective-permute-start(f32[128,1024]{1,0:T(8,128)S(1)} %get-tuple-element.70), channel_id=1, source_target_pairs={{0,2},{16,30},{2,0},{18,20},{4,6},{20,18},{6,4},{22,24},{8,10},{24... | collective-permute-start | bytes 1572872 | tf_op jit(solution)/shard_map/ppermute | solution.py:92
  49.5 0.8 collective-permute-done.5
  50.3 3.3 %collective-permute-done.6 = f32[128,1024]{1,0:T(8,128)S(1)} collective-permute-done((f32[128,1024]{1,0:T(8,128)S(1)}, f32[128,1024]{1,0:T(8,128)S(1)}, u32[]{:S(2)}, u32[]{:S(2)}) %collective-permute-start.6) | collective-permute-done | bytes 524320 | tf_op jit(solution)/shard_map/ppermute | solution.py:92
  53.6 2.5 %collective-permute-done.7 = f32[128,1024]{1,0:T(8,128)S(1)} collective-permute-done((f32[128,1024]{1,0:T(8,128)S(1)}, f32[128,1024]{1,0:T(8,128)S(1)}, u32[]{:S(2)}, u32[]{:S(2)}) %collective-permute-start.7) | collective-permute-done | bytes 524320 | tf_op jit(solution)/shard_map/ppermute | solution.py:92
  56.3 12.7 %all_to_all.30.sums = f32[8,16,1024]{2,1,0:T(8,128)S(1)} all-to-all(f32[8,16,1024]{2,1,0:T(8,128)S(1)} %bitcast.29), channel_id=1, replica_groups={{0,162,1,163,64,226,65,227},{16,178,17,179,80,242,81,243},{4,166,5,167,..., dimensions={0} | all-to-all | bytes 1048576 | tf_op jit(solution)/shard_map/all_to_all | solution.py:96
  69.0 2.8 %collective-permute-start.10 = (f32[16,1024]{1,0:T(8,128)S(1)}, f32[16,1024]{1,0:T(8,128)S(1)}, u32[]{:S(2)}, u32[]{:S(2)}) collective-permute-start(f32[16,1024]{1,0:T(8,128)S(1)} %shard_map.74), channel_id=1, source_target_pairs={{0,12},{16,28},{2,14},{18,30},{4,0},{20,16},{6,2},{22,18},{8,4},{2... | collective-permute-start | bytes 196616 | tf_op jit(solution)/shard_map/ppermute | solution.py:92
  71.8 3.0 %collective-permute-start.8 = (f32[16,1024]{1,0:T(8,128)S(1)}, f32[16,1024]{1,0:T(8,128)S(1)}, u32[]{:S(2)}, u32[]{:S(2)}) collective-permute-start(f32[16,1024]{1,0:T(8,128)S(1)} %shard_map.74), channel_id=1, source_target_pairs={{0,8},{16,24},{2,10},{18,26},{4,12},{20,28},{6,14},{22,30},{8,0},{... | collective-permute-start | bytes 196616 | tf_op jit(solution)/shard_map/ppermute | solution.py:92
  74.8 1.2 %collective-permute-start.9 = (f32[16,1024]{1,0:T(8,128)S(1)}, f32[16,1024]{1,0:T(8,128)S(1)}, u32[]{:S(2)}, u32[]{:S(2)}) collective-permute-start(f32[16,1024]{1,0:T(8,128)S(1)} %shard_map.74), channel_id=1, source_target_pairs={{0,4},{16,20},{2,6},{18,22},{4,8},{20,24},{6,10},{22,26},{8,12},{2... | collective-permute-start | bytes 196616 | tf_op jit(solution)/shard_map/ppermute | solution.py:92
  76.0 2.9 %collective-permute-done.8 = f32[16,1024]{1,0:T(8,128)S(1)} collective-permute-done((f32[16,1024]{1,0:T(8,128)S(1)}, f32[16,1024]{1,0:T(8,128)S(1)}, u32[]{:S(2)}, u32[]{:S(2)}) %collective-permute-start.8) | collective-permute-done | bytes 65568 | tf_op jit(solution)/shard_map/ppermute | solution.py:92
  78.9 1.6 %collective-permute-done.9 = f32[16,1024]{1,0:T(8,128)S(1)} collective-permute-done((f32[16,1024]{1,0:T(8,128)S(1)}, f32[16,1024]{1,0:T(8,128)S(1)}, u32[]{:S(2)}, u32[]{:S(2)}) %collective-permute-start.9) | collective-permute-done | bytes 65568 | tf_op jit(solution)/shard_map/ppermute | solution.py:92
  80.5 12.9 %all_to_all.31 = f32[8,16,1024]{2,1,0:T(8,128)S(1)} all-to-all(f32[8,16,1024]{2,1,0:T(8,128)S(1)} %broadcast_in_dim.33), channel_id=1, replica_groups={{0,162,1,163,64,226,65,227},{16,178,17,179,80,242,81,243},{4,166,5,167,..., dimensions={0} | all-to-all | bytes 1048576 | tf_op jit(solution)/shard_map/all_to_all | solution.py:96
  93.5 2.7 %collective-permute-start.12 = (f32[128,1024]{1,0:T(8,128)S(1)}, f32[128,1024]{1,0:T(8,128)S(1)}, u32[]{:S(2)}, u32[]{:S(2)}) collective-permute-start(f32[128,1024]{1,0:T(8,128)S(1)} %bitcast.20), channel_id=1, source_target_pairs={{0,128},{16,145},{2,130},{18,147},{4,132},{20,149},{6,134},{22,151... | collective-permute-start | bytes 1572872 | tf_op jit(solution)/shard_map/ppermute | solution.py:92
  96.2 6.7 %collective-permute-done.11.refs_1_ = f32[128,1024]{1,0:T(8,128)S(1)} collective-permute-done((f32[128,1024]{1,0:T(8,128)S(1)}, f32[128,1024]{1,0:T(8,128)S(1)}, u32[]{:S(2)}, u32[]{:S(2)}) %collective-permute-start.11) | collective-permute-done | bytes 524320 | tf_op jit(solution)/shard_map/ppermute | solution.py:92
  102.9 1.3 %collective-permute-done.12.refs_2_ = f32[128,1024]{1,0:T(8,128)S(1)} collective-permute-done((f32[128,1024]{1,0:T(8,128)S(1)}, f32[128,1024]{1,0:T(8,128)S(1)}, u32[]{:S(2)}, u32[]{:S(2)}) %collective-permute-start.12) | collective-permute-done | bytes 524320 | tf_op jit(solution)/shard_map/ppermute | solution.py:92
  104.2 1.2 %collective-permute-done.13.refs_3_ = f32[128,1024]{1,0:T(8,128)S(1)} collective-permute-done((f32[128,1024]{1,0:T(8,128)S(1)}, f32[128,1024]{1,0:T(8,128)S(1)}, u32[]{:S(2)}, u32[]{:S(2)}) %collective-permute-start.13) | collective-permute-done | bytes 524320 | tf_op jit(solution)/shard_map/ppermute | solution.py:92
  105.4 1.8 %shard_map.75 = (f32[1000,256]{1,0:T(8,128)S(1)}, f32[32,1000]{1,0:T(8,128)S(1)}) custom-call(s32[5]{0:T(128)S(1)} %stack.23.place, f32[128,1024]{1,0:T(8,128)S(1)} %bitcast.22, f32[128,1024]{1,0:T(8,128)S(1)} %collective-permute-done.11.refs_1_, f32[128,1024]{1,0:T(8,128)S(1)} %collective-permute-done.12.refs_2_, ...), custom_call_target="tpu_custom_call" | custom-call | flops 805306368 | bytes 2097152 | tf_op jit(solution)/shard_map/pallas_call | solution.py:237
  107.2 4.6 %collective-permute-start.14 = (f32[1000,256]{1,0:T(8,128)S(1)}, f32[1000,256]{1,0:T(8,128)S(1)}, u32[]{:S(2)}, u32[]{:S(2)}) collective-permute-start(f32[1000,256]{1,0:T(8,128)S(1)} %get-tuple-element.80), channel_id=1, source_target_pairs={{0,16},{16,0},{2,18},{18,2},{4,20},{20,4},{6,22},{22,6},{8,24},{24... | collective-permute-start | bytes 3072008 | tf_op jit(solution)/shard_map/ppermute | solution.py:92
  112.0 1.8 %shard_map.76.own_delta = f32[1000,256]{1,0:T(8,128)S(1)} custom-call(s32[5]{0:T(128)S(1)} %stack.23.place, f32[128,1024]{1,0:T(8,128)S(1)} %bitcast.23, f32[128,1024]{1,0:T(8,128)S(1)} %collective-permute-done.11.refs_1_, f32[128,1024]{1,0:T(8,128)S(1)} %collective-permute-done.12.refs_2_, f32[128,1024]{1,0:T(8,128)S(1)} %collective-permute-done.13.refs_3_, ...), custom_call_target="tpu_custom_call" | custom-call | flops 805306368 | bytes 2097152 | tf_op jit(solution)/shard_map/pallas_call | solution.py:237
  114.3 1.7 %shard_map.77 = (f32[1000,256]{1,0:T(8,128)}, f32[64,1000]{1,0:T(8,128)}) custom-call(s32[5]{0:T(128)S(1)} %stack.23.place, f32[1000,256]{1,0:T(8,128)S(1)} %bitcast.25, f32[1000,256]{1,0:T(8,128)S(1)} %shard_map.76.own_delta, f32[1000,256]{1,0:T(8,128)S(1)} %collective-permute-done.14.other_delta, f32[32,1000]{1,0:T(8,128)S(1)} %get-tuple-element.85.mine, ...), custom_call_target="tpu_custom_call" | custom-call | bytes 2097152 | tf_op jit(solution)/shard_map/pallas_call | solution.py:237
  (32 shorter events, 2.6 us)
Async XLA Ops:
  0.6 1.8 %copy-start = (f32[256,1024]{1,0:T(8,128)S(1)}, f32[256,1024]{1,0:T(8,128)}, u32[]{:S(2)}) copy-start(f32[256,1024]{1,0:T(8,128)} %param.6) | copy-start | bytes 3145732
  0.6 5.8 %copy-start.1 = (f32[256,1000]{0,1:T(8,128)S(1)}, f32[256,1000]{0,1:T(8,128)}, u32[]{:S(2)}) copy-start(f32[256,1000]{0,1:T(8,128)} %param.9) | copy-start | bytes 3072004
  3.1 26.9 %collective-permute-start = (f32[256,1024]{1,0:T(8,128)}, f32[256,1024]{1,0:T(8,128)S(1)}, u32[]{:S(2)}, u32[]{:S(2)}) collective-permute-start(f32[256,1024]{1,0:T(8,128)} %own_centers), channel_id=1, source_target_pairs={{0,16},{16,0},{2,18},{18,2},{4,20},{20,4},{6,22},{22,6},{8,24},{24... | collective-permute-start | bytes 3145736 | tf_op jit(solution)/shard_map/ppermute | solution.py:92
  6.4 23.6 %collective-permute-start.1 = (f32[256,1000]{0,1:T(8,128)S(1)}, f32[256,1000]{0,1:T(8,128)S(1)}, u32[]{:S(2)}, u32[]{:S(2)}) collective-permute-start(f32[256,1000]{0,1:T(8,128)S(1)} %copy-done.1), channel_id=1, source_target_pairs={{0,16},{16,0},{2,18},{18,2},{4,20},{20,4},{6,22},{22,6},{8,24},{24... | collective-permute-start | bytes 3072008 | tf_op jit(solution)/shard_map/ppermute | solution.py:92
  6.6 30.0 %copy-start.2 = (f32[256,1024]{1,0:T(8,128)S(1)}, f32[256,1024]{1,0:T(8,128)}, u32[]{:S(2)}) copy-start(f32[256,1024]{1,0:T(8,128)} %own_centers) | copy-start | bytes 3145732
  6.6 30.0 %copy-start.3 = (f32[256,1000]{0,1:T(8,128)S(1)}, f32[256,1000]{0,1:T(8,128)}, u32[]{:S(2)}) copy-start(f32[256,1000]{0,1:T(8,128)} %param.7) | copy-start | bytes 3072004
  30.1 9.7 %collective-permute-start.4 = (f32[128,1024]{1,0:T(8,128)S(1)}, f32[128,1024]{1,0:T(8,128)S(1)}, u32[]{:S(2)}, u32[]{:S(2)}) collective-permute-start(f32[128,1024]{1,0:T(8,128)S(1)} %shard_map.68.rows), channel_id=1, source_target_pairs={{0,32},{16,112},{2,34},{18,114},{4,36},{20,116},{6,38},{22,118},{8... | collective-permute-start | bytes 1572872 | tf_op jit(solution)/shard_map/ppermute | solution.py:92
  32.7 10.5 %collective-permute-start.3 = (f32[128,1024]{1,0:T(8,128)S(1)}, f32[128,1024]{1,0:T(8,128)S(1)}, u32[]{:S(2)}, u32[]{:S(2)}) collective-permute-start(f32[128,1024]{1,0:T(8,128)S(1)} %shard_map.68.rows), channel_id=1, source_target_pairs={{0,128},{16,145},{2,130},{18,147},{4,132},{20,149},{6,134},{22,151... | collective-permute-start | bytes 1572872 | tf_op jit(solution)/shard_map/ppermute | solution.py:92
  33.3 11.7 %collective-permute-start.2 = (f32[128,1024]{1,0:T(8,128)S(1)}, f32[128,1024]{1,0:T(8,128)S(1)}, u32[]{:S(2)}, u32[]{:S(2)}) collective-permute-start(f32[128,1024]{1,0:T(8,128)S(1)} %shard_map.68.rows), channel_id=1, source_target_pairs={{0,2},{16,30},{2,0},{18,20},{4,6},{20,18},{6,4},{22,24},{8,10},{24... | collective-permute-start | bytes 1572872 | tf_op jit(solution)/shard_map/ppermute | solution.py:92
  40.9 9.3 %collective-permute-start.5 = (f32[128,1024]{1,0:T(8,128)S(1)}, f32[128,1024]{1,0:T(8,128)S(1)}, u32[]{:S(2)}, u32[]{:S(2)}) collective-permute-start(f32[128,1024]{1,0:T(8,128)S(1)} %get-tuple-element.66), channel_id=1, source_target_pairs={{0,32},{16,112},{2,34},{18,114},{4,36},{20,116},{6,38},{22,118},{8... | collective-permute-start | bytes 1572872 | tf_op jit(solution)/shard_map/ppermute | solution.py:92
  44.3 9.3 %collective-permute-start.6 = (f32[128,1024]{1,0:T(8,128)S(1)}, f32[128,1024]{1,0:T(8,128)S(1)}, u32[]{:S(2)}, u32[]{:S(2)}) collective-permute-start(f32[128,1024]{1,0:T(8,128)S(1)} %get-tuple-element.68), channel_id=1, source_target_pairs={{0,128},{16,145},{2,130},{18,147},{4,132},{20,149},{6,134},{22,151... | collective-permute-start | bytes 1572872 | tf_op jit(solution)/shard_map/ppermute | solution.py:92
  46.2 9.9 %collective-permute-start.7 = (f32[128,1024]{1,0:T(8,128)S(1)}, f32[128,1024]{1,0:T(8,128)S(1)}, u32[]{:S(2)}, u32[]{:S(2)}) collective-permute-start(f32[128,1024]{1,0:T(8,128)S(1)} %get-tuple-element.70), channel_id=1, source_target_pairs={{0,2},{16,30},{2,0},{18,20},{4,6},{20,18},{6,4},{22,24},{8,10},{24... | collective-permute-start | bytes 1572872 | tf_op jit(solution)/shard_map/ppermute | solution.py:92
  69.0 7.0 %collective-permute-start.10 = (f32[16,1024]{1,0:T(8,128)S(1)}, f32[16,1024]{1,0:T(8,128)S(1)}, u32[]{:S(2)}, u32[]{:S(2)}) collective-permute-start(f32[16,1024]{1,0:T(8,128)S(1)} %shard_map.74), channel_id=1, source_target_pairs={{0,12},{16,28},{2,14},{18,30},{4,0},{20,16},{6,2},{22,18},{8,4},{2... | collective-permute-start | bytes 196616 | tf_op jit(solution)/shard_map/ppermute | solution.py:92
  71.8 7.1 %collective-permute-start.8 = (f32[16,1024]{1,0:T(8,128)S(1)}, f32[16,1024]{1,0:T(8,128)S(1)}, u32[]{:S(2)}, u32[]{:S(2)}) collective-permute-start(f32[16,1024]{1,0:T(8,128)S(1)} %shard_map.74), channel_id=1, source_target_pairs={{0,8},{16,24},{2,10},{18,26},{4,12},{20,28},{6,14},{22,30},{8,0},{... | collective-permute-start | bytes 196616 | tf_op jit(solution)/shard_map/ppermute | solution.py:92
  74.8 5.7 %collective-permute-start.9 = (f32[16,1024]{1,0:T(8,128)S(1)}, f32[16,1024]{1,0:T(8,128)S(1)}, u32[]{:S(2)}, u32[]{:S(2)}) collective-permute-start(f32[16,1024]{1,0:T(8,128)S(1)} %shard_map.74), channel_id=1, source_target_pairs={{0,4},{16,20},{2,6},{18,22},{4,8},{20,24},{6,10},{22,26},{8,12},{2... | collective-permute-start | bytes 196616 | tf_op jit(solution)/shard_map/ppermute | solution.py:92
  93.4 9.4 %collective-permute-start.11 = (f32[128,1024]{1,0:T(8,128)S(1)}, f32[128,1024]{1,0:T(8,128)S(1)}, u32[]{:S(2)}, u32[]{:S(2)}) collective-permute-start(f32[128,1024]{1,0:T(8,128)S(1)} %bitcast.19), channel_id=1, source_target_pairs={{0,32},{16,112},{2,34},{18,114},{4,36},{20,116},{6,38},{22,118},{8... | collective-permute-start | bytes 1572872 | tf_op jit(solution)/shard_map/ppermute | solution.py:92
  93.5 10.8 %collective-permute-start.12 = (f32[128,1024]{1,0:T(8,128)S(1)}, f32[128,1024]{1,0:T(8,128)S(1)}, u32[]{:S(2)}, u32[]{:S(2)}) collective-permute-start(f32[128,1024]{1,0:T(8,128)S(1)} %bitcast.20), channel_id=1, source_target_pairs={{0,128},{16,145},{2,130},{18,147},{4,132},{20,149},{6,134},{22,151... | collective-permute-start | bytes 1572872 | tf_op jit(solution)/shard_map/ppermute | solution.py:92
  96.2 9.2 %collective-permute-start.13 = (f32[128,1024]{1,0:T(8,128)S(1)}, f32[128,1024]{1,0:T(8,128)S(1)}, u32[]{:S(2)}, u32[]{:S(2)}) collective-permute-start(f32[128,1024]{1,0:T(8,128)S(1)} %bitcast.21), channel_id=1, source_target_pairs={{0,2},{16,30},{2,0},{18,20},{4,6},{20,18},{6,4},{22,24},{8,10},{24... | collective-permute-start | bytes 1572872 | tf_op jit(solution)/shard_map/ppermute | solution.py:92
  107.2 7.1 %collective-permute-start.14 = (f32[1000,256]{1,0:T(8,128)S(1)}, f32[1000,256]{1,0:T(8,128)S(1)}, u32[]{:S(2)}, u32[]{:S(2)}) collective-permute-start(f32[1000,256]{1,0:T(8,128)S(1)} %get-tuple-element.80), channel_id=1, source_target_pairs={{0,16},{16,0},{2,18},{18,2},{4,20},{20,4},{6,22},{22,6},{8,24},{24... | collective-permute-start | bytes 3072008 | tf_op jit(solution)/shard_map/ppermute | solution.py:92
  111.9 2.4 %collective-permute-start.15 = (f32[32,1000]{1,0:T(8,128)S(1)}, f32[32,1000]{1,0:T(8,128)S(1)}, u32[]{:S(2)}, u32[]{:S(2)}) collective-permute-start(f32[32,1000]{1,0:T(8,128)S(1)} %get-tuple-element.85.mine), channel_id=1, source_target_pairs={{0,16},{16,0},{2,18},{18,2},{4,20},{20,4},{6,22},{22,6},{8,24},{24... | collective-permute-start | bytes 384008 | tf_op jit(solution)/shard_map/ppermute | solution.py:92

commit v16 on v15

--- a/solution.py
+++ b/solution.py
@@ -226,11 +226,37 @@
 
 
 def update_kernel(factor, place, weights, own_delta, other_delta, mine, theirs, out, residual):
-    rows = mine.shape[0]
-    core = place[4]
-    residual[pl.ds(pl.multiple_of(core * rows, 8), rows), :] = mine[...]
-    residual[pl.ds(pl.multiple_of((1 - core) * rows, 8), rows), :] = theirs[...]
-    out[...] = weights[...] - factor * (own_delta[...] + other_delta[...])
+    step = pl.program_id(0)
+
+    @pl.when(step == 0)
+    def _():
+        rows = mine.shape[0]
+        core = place[4]
+        residual[pl.ds(pl.multiple_of(core * rows, 8), rows), :] = mine[...]
+        residual[pl.ds(pl.multiple_of((1 - core) * rows, 8), rows), :] = theirs[...]
+
+    rows = pl.ds(pl.multiple_of(step * out.shape[0], 8), out.shape[0])
+    out[...] = weights[rows, :] - factor * (own_delta[rows, :] + other_delta[rows, :])
+
+
+def update(factor, steps, place, weights, own_delta, other_delta, mine, theirs):
+    outputs, here = weights.shape
+    block = 2 * mine.shape[0]
+    return pl.pallas_call(
+        functools.partial(update_kernel, factor),
+        grid=(steps,),
+        in_specs=[pl.BlockSpec(memory_space=pltpu.SMEM)]
+        + [pl.BlockSpec(memory_space=pltpu.VMEM)] * 5,
+        out_specs=[
+            pl.BlockSpec((outputs // steps, here), lambda i: (i, 0)),
+            pl.BlockSpec((block, outputs), lambda i: (0, 0)),
+        ],
+        out_shape=[
+            jax.ShapeDtypeStruct((outputs, here), jnp.float32),
+            jax.ShapeDtypeStruct((block, outputs), jnp.float32),
+        ],
+        compiler_params=pltpu.CompilerParams(vmem_limit_bytes=VMEM_BYTES),
+    )(place, weights, own_delta, other_delta, mine, theirs)
 
 
 def call(kernel, outs, *operands, scratch=(), scalars=0, products=0):
@@ -358,16 +384,8 @@
     received, theirs = permute(first, SWAP), permute(mine, SWAP)
     *resid_list, first = lax.optimization_barrier((*resid_list, first))
     (second,) = delta_of(0)
-    new_weights, residual = call(
-        functools.partial(update_kernel, step_size / batch),
-        (((outputs, here), jnp.float32), ((block, outputs), jnp.float32)),
-        place,
-        weights.T,
-        second,
-        received,
-        mine,
-        theirs,
-        scalars=1,
+    new_weights, residual = update(
+        step_size / batch, 5, place, weights.T, second, received, mine, theirs
     )
     return (new_weights.T, residual)
 

time: 116 us -> 117 us (level)
    pallas_call x0 -> x1, Pallas kernels: none -> 2.84 us  [update(): pl.pallas_call(functools.partial(update_kernel, factor), grid=(steps,), i...]
    pallas_call x10 -> x9, Pallas kernels: 12 us -> 10.3 us  [call(): pl.pallas_call(kernel, in_specs=[pl.BlockSpec(memory_space=pltpu.SMEM)] *...]
where the time goes in v16:
time: 117 us
  blocking collectives  49 us (42%)
  starting transfers between devices  30.6 us (26%)
  waiting for transfers between devices  20.8 us (18%)
  Pallas kernels  13.1 us (11%)
  local copies, waits for them, and re-layouts  1.55 us (1%)
  other arithmetic  1.19 us (1%)
    all_to_all x3, blocking collectives, exchange(): lax.all_to_all(array, AXES, 0, 0, axis_index_groups=groups, tiled=True)  49 us
    ppermute x16, starting transfers between devices, permute(): return lax.ppermute(array, AXES, pairs)  30.6 us
    ppermute x16, waiting for transfers between devices, permute(): return lax.ppermute(array, AXES, pairs)  20.8 us
    pallas_call x9, Pallas kernels, call(): pl.pallas_call(kernel, in_specs=[pl.BlockSpec(memory_space=pltpu.SMEM)] *...  10.3 us
    pallas_call x1, Pallas kernels, update(): pl.pallas_call(functools.partial(update_kernel, factor), grid=(steps,), i...  2.84 us
  transfers between devices with their start and end apart: 16, of which 9 were waited for; matrix products, arithmetic and copies ran while one was open for 0% of the time, Pallas kernels for 7%

profile of v16, /device:TPU:1, one launch (start us, length us, event | category | flops | bytes accessed | tf_op | source)
XLA Modules:
  0.0 117.1 jit_solution(11768165988093599404)
XLA Ops:
  0.7 1.0 select_reduce_fusion
  1.7 0.7 dynamic_slice.3.index
  3.1 3.3 %collective-permute-start = (f32[256,1024]{1,0:T(8,128)}, f32[256,1024]{1,0:T(8,128)S(1)}, u32[]{:S(2)}, u32[]{:S(2)}) collective-permute-start(f32[256,1024]{1,0:T(8,128)} %own_centers), channel_id=1, source_target_pairs={{0,16},{16,0},{2,18},{18,2},{4,20},{20,4},{6,22},{22,6},{8,24},{24... | collective-permute-start | bytes 3145736 | tf_op jit(solution)/shard_map/ppermute | solution.py:92
  6.6 23.4 %all_to_all.29 = f32[16,8,1024]{2,1,0:T(8,128)S(1)} all-to-all(f32[16,8,1024]{2,1,0:T(8,128)S(1)} %bitcast.30), channel_id=1, replica_groups={{0,2,4,6,8,10,12,14,129,131,133,135,137,139,141,143},{16,18,20,22,24,26..., dimensions={0} | all-to-all | bytes 1048576 | tf_op jit(solution)/shard_map/all_to_all | solution.py:96
  30.1 2.6 %collective-permute-start.4 = (f32[128,1024]{1,0:T(8,128)S(1)}, f32[128,1024]{1,0:T(8,128)S(1)}, u32[]{:S(2)}, u32[]{:S(2)}) collective-permute-start(f32[128,1024]{1,0:T(8,128)S(1)} %shard_map.68.rows), channel_id=1, source_target_pairs={{0,32},{16,112},{2,34},{18,114},{4,36},{20,116},{6,38},{22,118},{8... | collective-permute-start | bytes 1572872 | tf_op jit(solution)/shard_map/ppermute | solution.py:92
  33.3 3.2 %collective-permute-start.2 = (f32[128,1024]{1,0:T(8,128)S(1)}, f32[128,1024]{1,0:T(8,128)S(1)}, u32[]{:S(2)}, u32[]{:S(2)}) collective-permute-start(f32[128,1024]{1,0:T(8,128)S(1)} %shard_map.68.rows), channel_id=1, source_target_pairs={{0,2},{16,30},{2,0},{18,20},{4,6},{20,18},{6,4},{22,24},{8,10},{24... | collective-permute-start | bytes 1572872 | tf_op jit(solution)/shard_map/ppermute | solution.py:92
  36.6 2.1 %shard_map.69 = (bf16[1024,512]{1,0:T(8,128)(2,1)S(1)}, bf16[1024,512]{1,0:T(8,128)(2,1)S(1)}, f32[1,512]{1,0:T(1,128)S(1)}, bf16[512,1024]{1,0:T(8,128)(2,1)S(1...) custom-call(s32[4]{0:T(128)S(1)} %dynamic_slice.3.index, s32[5]{0:T(128)S(1)} %stack.23.place, ...), custom_call_target="tpu_custom_call" | custom-call | bytes 2097152 | tf_op jit(solution)/shard_map/pallas_call | solution.py:263
  38.7 1.1 shard_map.70
  39.8 1.1 shard_map.71
  40.9 2.2 %collective-permute-start.5 = (f32[128,1024]{1,0:T(8,128)S(1)}, f32[128,1024]{1,0:T(8,128)S(1)}, u32[]{:S(2)}, u32[]{:S(2)}) collective-permute-start(f32[128,1024]{1,0:T(8,128)S(1)} %get-tuple-element.66), channel_id=1, source_target_pairs={{0,32},{16,112},{2,34},{18,114},{4,36},{20,116},{6,38},{22,118},{8... | collective-permute-start | bytes 1572872 | tf_op jit(solution)/shard_map/ppermute | solution.py:92
  43.1 1.1 shard_map.72
  44.3 0.7 collective-permute-start.6
  45.0 1.2 shard_map.73
  46.2 3.3 %collective-permute-start.7 = (f32[128,1024]{1,0:T(8,128)S(1)}, f32[128,1024]{1,0:T(8,128)S(1)}, u32[]{:S(2)}, u32[]{:S(2)}) collective-permute-start(f32[128,1024]{1,0:T(8,128)S(1)} %get-tuple-element.70), channel_id=1, source_target_pairs={{0,2},{16,30},{2,0},{18,20},{4,6},{20,18},{6,4},{22,24},{8,10},{24... | collective-permute-start | bytes 1572872 | tf_op jit(solution)/shard_map/ppermute | solution.py:92
  49.5 0.8 collective-permute-done.5
  50.3 3.3 %collective-permute-done.6 = f32[128,1024]{1,0:T(8,128)S(1)} collective-permute-done((f32[128,1024]{1,0:T(8,128)S(1)}, f32[128,1024]{1,0:T(8,128)S(1)}, u32[]{:S(2)}, u32[]{:S(2)}) %collective-permute-start.6) | collective-permute-done | bytes 524320 | tf_op jit(solution)/shard_map/ppermute | solution.py:92
  53.6 2.5 %collective-permute-done.7 = f32[128,1024]{1,0:T(8,128)S(1)} collective-permute-done((f32[128,1024]{1,0:T(8,128)S(1)}, f32[128,1024]{1,0:T(8,128)S(1)}, u32[]{:S(2)}, u32[]{:S(2)}) %collective-permute-start.7) | collective-permute-done | bytes 524320 | tf_op jit(solution)/shard_map/ppermute | solution.py:92
  56.3 12.7 %all_to_all.30.sums = f32[8,16,1024]{2,1,0:T(8,128)S(1)} all-to-all(f32[8,16,1024]{2,1,0:T(8,128)S(1)} %bitcast.29), channel_id=1, replica_groups={{0,162,1,163,64,226,65,227},{16,178,17,179,80,242,81,243},{4,166,5,167,..., dimensions={0} | all-to-all | bytes 1048576 | tf_op jit(solution)/shard_map/all_to_all | solution.py:96
  69.0 2.8 %collective-permute-start.10 = (f32[16,1024]{1,0:T(8,128)S(1)}, f32[16,1024]{1,0:T(8,128)S(1)}, u32[]{:S(2)}, u32[]{:S(2)}) collective-permute-start(f32[16,1024]{1,0:T(8,128)S(1)} %shard_map.74), channel_id=1, source_target_pairs={{0,12},{16,28},{2,14},{18,30},{4,0},{20,16},{6,2},{22,18},{8,4},{2... | collective-permute-start | bytes 196616 | tf_op jit(solution)/shard_map/ppermute | solution.py:92
  71.8 3.0 %collective-permute-start.8 = (f32[16,1024]{1,0:T(8,128)S(1)}, f32[16,1024]{1,0:T(8,128)S(1)}, u32[]{:S(2)}, u32[]{:S(2)}) collective-permute-start(f32[16,1024]{1,0:T(8,128)S(1)} %shard_map.74), channel_id=1, source_target_pairs={{0,8},{16,24},{2,10},{18,26},{4,12},{20,28},{6,14},{22,30},{8,0},{... | collective-permute-start | bytes 196616 | tf_op jit(solution)/shard_map/ppermute | solution.py:92
  74.8 1.2 %collective-permute-start.9 = (f32[16,1024]{1,0:T(8,128)S(1)}, f32[16,1024]{1,0:T(8,128)S(1)}, u32[]{:S(2)}, u32[]{:S(2)}) collective-permute-start(f32[16,1024]{1,0:T(8,128)S(1)} %shard_map.74), channel_id=1, source_target_pairs={{0,4},{16,20},{2,6},{18,22},{4,8},{20,24},{6,10},{22,26},{8,12},{2... | collective-permute-start | bytes 196616 | tf_op jit(solution)/shard_map/ppermute | solution.py:92
  76.0 2.9 %collective-permute-done.8 = f32[16,1024]{1,0:T(8,128)S(1)} collective-permute-done((f32[16,1024]{1,0:T(8,128)S(1)}, f32[16,1024]{1,0:T(8,128)S(1)}, u32[]{:S(2)}, u32[]{:S(2)}) %collective-permute-start.8) | collective-permute-done | bytes 65568 | tf_op jit(solution)/shard_map/ppermute | solution.py:92
  78.9 1.6 %collective-permute-done.9 = f32[16,1024]{1,0:T(8,128)S(1)} collective-permute-done((f32[16,1024]{1,0:T(8,128)S(1)}, f32[16,1024]{1,0:T(8,128)S(1)}, u32[]{:S(2)}, u32[]{:S(2)}) %collective-permute-start.9) | collective-permute-done | bytes 65568 | tf_op jit(solution)/shard_map/ppermute | solution.py:92
  80.5 12.9 %all_to_all.31 = f32[8,16,1024]{2,1,0:T(8,128)S(1)} all-to-all(f32[8,16,1024]{2,1,0:T(8,128)S(1)} %broadcast_in_dim.33), channel_id=1, replica_groups={{0,162,1,163,64,226,65,227},{16,178,17,179,80,242,81,243},{4,166,5,167,..., dimensions={0} | all-to-all | bytes 1048576 | tf_op jit(solution)/shard_map/all_to_all | solution.py:96
  93.5 2.7 %collective-permute-start.12 = (f32[128,1024]{1,0:T(8,128)S(1)}, f32[128,1024]{1,0:T(8,128)S(1)}, u32[]{:S(2)}, u32[]{:S(2)}) collective-permute-start(f32[128,1024]{1,0:T(8,128)S(1)} %bitcast.20), channel_id=1, source_target_pairs={{0,128},{16,145},{2,130},{18,147},{4,132},{20,149},{6,134},{22,151... | collective-permute-start | bytes 1572872 | tf_op jit(solution)/shard_map/ppermute | solution.py:92
  96.2 6.7 %collective-permute-done.11.refs_1_ = f32[128,1024]{1,0:T(8,128)S(1)} collective-permute-done((f32[128,1024]{1,0:T(8,128)S(1)}, f32[128,1024]{1,0:T(8,128)S(1)}, u32[]{:S(2)}, u32[]{:S(2)}) %collective-permute-start.11) | collective-permute-done | bytes 524320 | tf_op jit(solution)/shard_map/ppermute | solution.py:92
  102.9 1.3 %collective-permute-done.12.refs_2_ = f32[128,1024]{1,0:T(8,128)S(1)} collective-permute-done((f32[128,1024]{1,0:T(8,128)S(1)}, f32[128,1024]{1,0:T(8,128)S(1)}, u32[]{:S(2)}, u32[]{:S(2)}) %collective-permute-start.12) | collective-permute-done | bytes 524320 | tf_op jit(solution)/shard_map/ppermute | solution.py:92
  104.2 1.2 %collective-permute-done.13.refs_3_ = f32[128,1024]{1,0:T(8,128)S(1)} collective-permute-done((f32[128,1024]{1,0:T(8,128)S(1)}, f32[128,1024]{1,0:T(8,128)S(1)}, u32[]{:S(2)}, u32[]{:S(2)}) %collective-permute-start.13) | collective-permute-done | bytes 524320 | tf_op jit(solution)/shard_map/ppermute | solution.py:92
  105.4 1.8 %shard_map.75 = (f32[1000,256]{1,0:T(8,128)S(1)}, f32[32,1000]{1,0:T(8,128)S(1)}) custom-call(s32[5]{0:T(128)S(1)} %stack.23.place, f32[128,1024]{1,0:T(8,128)S(1)} %bitcast.22, f32[128,1024]{1,0:T(8,128)S(1)} %collective-permute-done.11.refs_1_, f32[128,1024]{1,0:T(8,128)S(1)} %collective-permute-done.12.refs_2_, ...), custom_call_target="tpu_custom_call" | custom-call | flops 805306368 | bytes 2097152 | tf_op jit(solution)/shard_map/pallas_call | solution.py:263
  107.2 4.6 %collective-permute-start.14 = (f32[1000,256]{1,0:T(8,128)S(1)}, f32[1000,256]{1,0:T(8,128)S(1)}, u32[]{:S(2)}, u32[]{:S(2)}) collective-permute-start(f32[1000,256]{1,0:T(8,128)S(1)} %get-tuple-element.80), channel_id=1, source_target_pairs={{0,16},{16,0},{2,18},{18,2},{4,20},{20,4},{6,22},{22,6},{8,24},{24... | collective-permute-start | bytes 3072008 | tf_op jit(solution)/shard_map/ppermute | solution.py:92
  112.0 1.8 %shard_map.76.own_delta = f32[1000,256]{1,0:T(8,128)S(1)} custom-call(s32[5]{0:T(128)S(1)} %stack.23.place, f32[128,1024]{1,0:T(8,128)S(1)} %bitcast.23, f32[128,1024]{1,0:T(8,128)S(1)} %collective-permute-done.11.refs_1_, f32[128,1024]{1,0:T(8,128)S(1)} %collective-permute-done.12.refs_2_, f32[128,1024]{1,0:T(8,128)S(1)} %collective-permute-done.13.refs_3_, ...), custom_call_target="tpu_custom_call" | custom-call | flops 805306368 | bytes 2097152 | tf_op jit(solution)/shard_map/pallas_call | solution.py:263
  114.3 2.8 %shard_map.77 = (f32[1000,256]{1,0:T(8,128)}, f32[64,1000]{1,0:T(8,128)}) custom-call(s32[5]{0:T(128)S(1)} %stack.23.place, f32[1000,256]{1,0:T(8,128)S(1)} %bitcast.25, f32[1000,256]{1,0:T(8,128)S(1)} %shard_map.76.own_delta, f32[1000,256]{1,0:T(8,128)S(1)} %collective-permute-done.14.other_delta, f32[32,1000]{1,0:T(8,128)S(1)} %get-tuple-element.85.mine, ...), custom_call_target="tpu_custom_call" | custom-call | tf_op jit(solution)/shard_map/pallas_call | solution.py:245
  (32 shorter events, 2.6 us)
Async XLA Ops:
  0.6 1.8 %copy-start = (f32[256,1024]{1,0:T(8,128)S(1)}, f32[256,1024]{1,0:T(8,128)}, u32[]{:S(2)}) copy-start(f32[256,1024]{1,0:T(8,128)} %param.6) | copy-start | bytes 3145732
  0.6 5.8 %copy-start.1 = (f32[256,1000]{0,1:T(8,128)S(1)}, f32[256,1000]{0,1:T(8,128)}, u32[]{:S(2)}) copy-start(f32[256,1000]{0,1:T(8,128)} %param.9) | copy-start | bytes 3072004
  3.1 26.9 %collective-permute-start = (f32[256,1024]{1,0:T(8,128)}, f32[256,1024]{1,0:T(8,128)S(1)}, u32[]{:S(2)}, u32[]{:S(2)}) collective-permute-start(f32[256,1024]{1,0:T(8,128)} %own_centers), channel_id=1, source_target_pairs={{0,16},{16,0},{2,18},{18,2},{4,20},{20,4},{6,22},{22,6},{8,24},{24... | collective-permute-start | bytes 3145736 | tf_op jit(solution)/shard_map/ppermute | solution.py:92
  6.4 23.6 %collective-permute-start.1 = (f32[256,1000]{0,1:T(8,128)S(1)}, f32[256,1000]{0,1:T(8,128)S(1)}, u32[]{:S(2)}, u32[]{:S(2)}) collective-permute-start(f32[256,1000]{0,1:T(8,128)S(1)} %copy-done.1), channel_id=1, source_target_pairs={{0,16},{16,0},{2,18},{18,2},{4,20},{20,4},{6,22},{22,6},{8,24},{24... | collective-permute-start | bytes 3072008 | tf_op jit(solution)/shard_map/ppermute | solution.py:92
  6.6 30.0 %copy-start.2 = (f32[256,1024]{1,0:T(8,128)S(1)}, f32[256,1024]{1,0:T(8,128)}, u32[]{:S(2)}) copy-start(f32[256,1024]{1,0:T(8,128)} %own_centers) | copy-start | bytes 3145732
  6.6 30.0 %copy-start.3 = (f32[256,1000]{0,1:T(8,128)S(1)}, f32[256,1000]{0,1:T(8,128)}, u32[]{:S(2)}) copy-start(f32[256,1000]{0,1:T(8,128)} %param.7) | copy-start | bytes 3072004
  30.1 9.7 %collective-permute-start.4 = (f32[128,1024]{1,0:T(8,128)S(1)}, f32[128,1024]{1,0:T(8,128)S(1)}, u32[]{:S(2)}, u32[]{:S(2)}) collective-permute-start(f32[128,1024]{1,0:T(8,128)S(1)} %shard_map.68.rows), channel_id=1, source_target_pairs={{0,32},{16,112},{2,34},{18,114},{4,36},{20,116},{6,38},{22,118},{8... | collective-permute-start | bytes 1572872 | tf_op jit(solution)/shard_map/ppermute | solution.py:92
  32.7 10.5 %collective-permute-start.3 = (f32[128,1024]{1,0:T(8,128)S(1)}, f32[128,1024]{1,0:T(8,128)S(1)}, u32[]{:S(2)}, u32[]{:S(2)}) collective-permute-start(f32[128,1024]{1,0:T(8,128)S(1)} %shard_map.68.rows), channel_id=1, source_target_pairs={{0,128},{16,145},{2,130},{18,147},{4,132},{20,149},{6,134},{22,151... | collective-permute-start | bytes 1572872 | tf_op jit(solution)/shard_map/ppermute | solution.py:92
  33.3 11.7 %collective-permute-start.2 = (f32[128,1024]{1,0:T(8,128)S(1)}, f32[128,1024]{1,0:T(8,128)S(1)}, u32[]{:S(2)}, u32[]{:S(2)}) collective-permute-start(f32[128,1024]{1,0:T(8,128)S(1)} %shard_map.68.rows), channel_id=1, source_target_pairs={{0,2},{16,30},{2,0},{18,20},{4,6},{20,18},{6,4},{22,24},{8,10},{24... | collective-permute-start | bytes 1572872 | tf_op jit(solution)/shard_map/ppermute | solution.py:92
  40.9 9.3 %collective-permute-start.5 = (f32[128,1024]{1,0:T(8,128)S(1)}, f32[128,1024]{1,0:T(8,128)S(1)}, u32[]{:S(2)}, u32[]{:S(2)}) collective-permute-start(f32[128,1024]{1,0:T(8,128)S(1)} %get-tuple-element.66), channel_id=1, source_target_pairs={{0,32},{16,112},{2,34},{18,114},{4,36},{20,116},{6,38},{22,118},{8... | collective-permute-start | bytes 1572872 | tf_op jit(solution)/shard_map/ppermute | solution.py:92
  44.3 9.3 %collective-permute-start.6 = (f32[128,1024]{1,0:T(8,128)S(1)}, f32[128,1024]{1,0:T(8,128)S(1)}, u32[]{:S(2)}, u32[]{:S(2)}) collective-permute-start(f32[128,1024]{1,0:T(8,128)S(1)} %get-tuple-element.68), channel_id=1, source_target_pairs={{0,128},{16,145},{2,130},{18,147},{4,132},{20,149},{6,134},{22,151... | collective-permute-start | bytes 1572872 | tf_op jit(solution)/shard_map/ppermute | solution.py:92
  46.2 9.9 %collective-permute-start.7 = (f32[128,1024]{1,0:T(8,128)S(1)}, f32[128,1024]{1,0:T(8,128)S(1)}, u32[]{:S(2)}, u32[]{:S(2)}) collective-permute-start(f32[128,1024]{1,0:T(8,128)S(1)} %get-tuple-element.70), channel_id=1, source_target_pairs={{0,2},{16,30},{2,0},{18,20},{4,6},{20,18},{6,4},{22,24},{8,10},{24... | collective-permute-start | bytes 1572872 | tf_op jit(solution)/shard_map/ppermute | solution.py:92
  69.0 7.0 %collective-permute-start.10 = (f32[16,1024]{1,0:T(8,128)S(1)}, f32[16,1024]{1,0:T(8,128)S(1)}, u32[]{:S(2)}, u32[]{:S(2)}) collective-permute-start(f32[16,1024]{1,0:T(8,128)S(1)} %shard_map.74), channel_id=1, source_target_pairs={{0,12},{16,28},{2,14},{18,30},{4,0},{20,16},{6,2},{22,18},{8,4},{2... | collective-permute-start | bytes 196616 | tf_op jit(solution)/shard_map/ppermute | solution.py:92
  71.8 7.1 %collective-permute-start.8 = (f32[16,1024]{1,0:T(8,128)S(1)}, f32[16,1024]{1,0:T(8,128)S(1)}, u32[]{:S(2)}, u32[]{:S(2)}) collective-permute-start(f32[16,1024]{1,0:T(8,128)S(1)} %shard_map.74), channel_id=1, source_target_pairs={{0,8},{16,24},{2,10},{18,26},{4,12},{20,28},{6,14},{22,30},{8,0},{... | collective-permute-start | bytes 196616 | tf_op jit(solution)/shard_map/ppermute | solution.py:92
  74.8 5.7 %collective-permute-start.9 = (f32[16,1024]{1,0:T(8,128)S(1)}, f32[16,1024]{1,0:T(8,128)S(1)}, u32[]{:S(2)}, u32[]{:S(2)}) collective-permute-start(f32[16,1024]{1,0:T(8,128)S(1)} %shard_map.74), channel_id=1, source_target_pairs={{0,4},{16,20},{2,6},{18,22},{4,8},{20,24},{6,10},{22,26},{8,12},{2... | collective-permute-start | bytes 196616 | tf_op jit(solution)/shard_map/ppermute | solution.py:92
  93.4 9.4 %collective-permute-start.11 = (f32[128,1024]{1,0:T(8,128)S(1)}, f32[128,1024]{1,0:T(8,128)S(1)}, u32[]{:S(2)}, u32[]{:S(2)}) collective-permute-start(f32[128,1024]{1,0:T(8,128)S(1)} %bitcast.19), channel_id=1, source_target_pairs={{0,32},{16,112},{2,34},{18,114},{4,36},{20,116},{6,38},{22,118},{8... | collective-permute-start | bytes 1572872 | tf_op jit(solution)/shard_map/ppermute | solution.py:92
  93.5 10.8 %collective-permute-start.12 = (f32[128,1024]{1,0:T(8,128)S(1)}, f32[128,1024]{1,0:T(8,128)S(1)}, u32[]{:S(2)}, u32[]{:S(2)}) collective-permute-start(f32[128,1024]{1,0:T(8,128)S(1)} %bitcast.20), channel_id=1, source_target_pairs={{0,128},{16,145},{2,130},{18,147},{4,132},{20,149},{6,134},{22,151... | collective-permute-start | bytes 1572872 | tf_op jit(solution)/shard_map/ppermute | solution.py:92
  96.2 9.2 %collective-permute-start.13 = (f32[128,1024]{1,0:T(8,128)S(1)}, f32[128,1024]{1,0:T(8,128)S(1)}, u32[]{:S(2)}, u32[]{:S(2)}) collective-permute-start(f32[128,1024]{1,0:T(8,128)S(1)} %bitcast.21), channel_id=1, source_target_pairs={{0,2},{16,30},{2,0},{18,20},{4,6},{20,18},{6,4},{22,24},{8,10},{24... | collective-permute-start | bytes 1572872 | tf_op jit(solution)/shard_map/ppermute | solution.py:92
  107.2 7.1 %collective-permute-start.14 = (f32[1000,256]{1,0:T(8,128)S(1)}, f32[1000,256]{1,0:T(8,128)S(1)}, u32[]{:S(2)}, u32[]{:S(2)}) collective-permute-start(f32[1000,256]{1,0:T(8,128)S(1)} %get-tuple-element.80), channel_id=1, source_target_pairs={{0,16},{16,0},{2,18},{18,2},{4,20},{20,4},{6,22},{22,6},{8,24},{24... | collective-permute-start | bytes 3072008 | tf_op jit(solution)/shard_map/ppermute | solution.py:92
  111.9 2.4 %collective-permute-start.15 = (f32[32,1000]{1,0:T(8,128)S(1)}, f32[32,1000]{1,0:T(8,128)S(1)}, u32[]{:S(2)}, u32[]{:S(2)}) collective-permute-start(f32[32,1000]{1,0:T(8,128)S(1)} %get-tuple-element.85.mine), channel_id=1, source_target_pairs={{0,16},{16,0},{2,18},{18,2},{4,20},{20,4},{6,22},{22,6},{8,24},{24... | collective-permute-start | bytes 384008 | tf_op jit(solution)/shard_map/ppermute | solution.py:92

commit v17 on v15

--- a/solution.py
+++ b/solution.py
@@ -202,9 +202,10 @@
     out[...] = total * scale - targets[...]
 
 
-def delta_kernel(start, place, *refs):
+def delta_kernel(start, factor, place, *refs):
     resid_refs, high_refs, low_refs = refs[:4], refs[4:8], refs[8:12]
-    delta, *mine, resid_high, resid_low, high, low = refs[12:]
+    weights, refs = (refs[12:13], refs[13:]) if factor else ((), refs[12:])
+    delta, *mine, resid_high, resid_low, high, low = refs
     quarter = resid_refs[0].shape[0]
     outputs, here = delta.shape
     columns = pl.ds(start, here)
@@ -222,15 +223,15 @@
                 for row in range(own):
                     out[pl.ds(target + row, 1), :] = resid[pl.ds(source + row, 1), :][:, :outputs]
     found = product((high[...], low[...]), (resid_high[...], resid_low[...]), ((0,), (0,)))
-    delta[...] = found.T[:outputs]
-
-
-def update_kernel(factor, place, weights, own_delta, other_delta, mine, theirs, out, residual):
+    delta[...] = weights[0][...] - factor * found.T[:outputs] if weights else found.T[:outputs]
+
+
+def update_kernel(factor, place, partly, other_delta, mine, theirs, out, residual):
     rows = mine.shape[0]
     core = place[4]
     residual[pl.ds(pl.multiple_of(core * rows, 8), rows), :] = mine[...]
     residual[pl.ds(pl.multiple_of((1 - core) * rows, 8), rows), :] = theirs[...]
-    out[...] = weights[...] - factor * (own_delta[...] + other_delta[...])
+    out[...] = partly[...] - factor * other_delta[...]
 
 
 def call(kernel, outs, *operands, scratch=(), scalars=0, products=0):
@@ -340,30 +341,30 @@
     opposite, up, down = (permute(value, along_z(step)) for step in (4, 2, -2))
     resid_list = quarters(spread((value + opposite) + (up + down), PLANES))
 
-    def delta_of(start, *outs):
+    def delta_of(start, factor, extra, *outs):
         return call(
-            functools.partial(delta_kernel, start),
+            functools.partial(delta_kernel, start, factor),
             (((outputs, here), jnp.float32), *outs),
             place,
             *resid_list,
             *(part[1] for part in done),
             *(part[2] for part in done),
+            *extra,
             scratch=(((4 * quarter, lanes), jnp.bfloat16),) * 2
             + (((4 * quarter, here), jnp.bfloat16),) * 2,
             scalars=1,
             products=3 * 4 * quarter * here * lanes,
         )
 
-    first, mine = delta_of(here, ((half_block, outputs), jnp.float32))
+    first, mine = delta_of(here, 0.0, (), ((half_block, outputs), jnp.float32))
     received, theirs = permute(first, SWAP), permute(mine, SWAP)
     *resid_list, first = lax.optimization_barrier((*resid_list, first))
-    (second,) = delta_of(0)
+    (partly,) = delta_of(0, step_size / batch, (weights.T,))
     new_weights, residual = call(
         functools.partial(update_kernel, step_size / batch),
         (((outputs, here), jnp.float32), ((block, outputs), jnp.float32)),
         place,
-        weights.T,
-        second,
+        partly,
         received,
         mine,
         theirs,

time: 116 us -> 116 us (level)
  no operation moved by 1% of the time
where the time goes in v17:
time: 116 us
  blocking collectives  49 us (42%)
  starting transfers between devices  30.6 us (26%)
  waiting for transfers between devices  20.9 us (18%)
  Pallas kernels  12 us (10%)
  local copies, waits for them, and re-layouts  1.55 us (1%)
  other arithmetic  1.17 us (1%)
    all_to_all x3, blocking collectives, exchange(): lax.all_to_all(array, AXES, 0, 0, axis_index_groups=groups, tiled=True)  49 us
    ppermute x16, starting transfers between devices, permute(): return lax.ppermute(array, AXES, pairs)  30.6 us
    ppermute x16, waiting for transfers between devices, permute(): return lax.ppermute(array, AXES, pairs)  20.9 us
    pallas_call x10, Pallas kernels, call(): pl.pallas_call(kernel, in_specs=[pl.BlockSpec(memory_space=pltpu.SMEM)] *...  12 us
  transfers between devices with their start and end apart: 16, of which 9 were waited for; matrix products, arithmetic and copies ran while one was open for 0% of the time, Pallas kernels for 7%

profile of v17, /device:TPU:1, one launch (start us, length us, event | category | flops | bytes accessed | tf_op | source)
XLA Modules:
  0.0 116.0 jit_solution(17601033379189833141)
XLA Ops:
  0.7 1.0 select_reduce_fusion
  1.7 0.7 dynamic_slice.3.index
  3.1 3.3 %collective-permute-start = (f32[256,1024]{1,0:T(8,128)}, f32[256,1024]{1,0:T(8,128)S(1)}, u32[]{:S(2)}, u32[]{:S(2)}) collective-permute-start(f32[256,1024]{1,0:T(8,128)} %own_centers), channel_id=1, source_target_pairs={{0,16},{16,0},{2,18},{18,2},{4,20},{20,4},{6,22},{22,6},{8,24},{24... | collective-permute-start | bytes 3145736 | tf_op jit(solution)/shard_map/ppermute | solution.py:92
  6.6 23.4 %all_to_all.29 = f32[16,8,1024]{2,1,0:T(8,128)S(1)} all-to-all(f32[16,8,1024]{2,1,0:T(8,128)S(1)} %bitcast.30), channel_id=1, replica_groups={{0,2,4,6,8,10,12,14,129,131,133,135,137,139,141,143},{16,18,20,22,24,26..., dimensions={0} | all-to-all | bytes 1048576 | tf_op jit(solution)/shard_map/all_to_all | solution.py:96
  30.1 2.6 %collective-permute-start.4 = (f32[128,1024]{1,0:T(8,128)S(1)}, f32[128,1024]{1,0:T(8,128)S(1)}, u32[]{:S(2)}, u32[]{:S(2)}) collective-permute-start(f32[128,1024]{1,0:T(8,128)S(1)} %shard_map.68.rows), channel_id=1, source_target_pairs={{0,32},{16,112},{2,34},{18,114},{4,36},{20,116},{6,38},{22,118},{8... | collective-permute-start | bytes 1572872 | tf_op jit(solution)/shard_map/ppermute | solution.py:92
  33.3 3.2 %collective-permute-start.2 = (f32[128,1024]{1,0:T(8,128)S(1)}, f32[128,1024]{1,0:T(8,128)S(1)}, u32[]{:S(2)}, u32[]{:S(2)}) collective-permute-start(f32[128,1024]{1,0:T(8,128)S(1)} %shard_map.68.rows), channel_id=1, source_target_pairs={{0,2},{16,30},{2,0},{18,20},{4,6},{20,18},{6,4},{22,24},{8,10},{24... | collective-permute-start | bytes 1572872 | tf_op jit(solution)/shard_map/ppermute | solution.py:92
  36.6 2.1 %shard_map.69 = (bf16[1024,512]{1,0:T(8,128)(2,1)S(1)}, bf16[1024,512]{1,0:T(8,128)(2,1)S(1)}, f32[1,512]{1,0:T(1,128)S(1)}, bf16[512,1024]{1,0:T(8,128)(2,1)S(1...) custom-call(s32[4]{0:T(128)S(1)} %dynamic_slice.3.index, s32[5]{0:T(128)S(1)} %stack.23.place, ...), custom_call_target="tpu_custom_call" | custom-call | bytes 2097152 | tf_op jit(solution)/shard_map/pallas_call | solution.py:238
  38.7 1.1 shard_map.70
  39.8 1.1 shard_map.71
  40.9 2.2 %collective-permute-start.5 = (f32[128,1024]{1,0:T(8,128)S(1)}, f32[128,1024]{1,0:T(8,128)S(1)}, u32[]{:S(2)}, u32[]{:S(2)}) collective-permute-start(f32[128,1024]{1,0:T(8,128)S(1)} %get-tuple-element.66), channel_id=1, source_target_pairs={{0,32},{16,112},{2,34},{18,114},{4,36},{20,116},{6,38},{22,118},{8... | collective-permute-start | bytes 1572872 | tf_op jit(solution)/shard_map/ppermute | solution.py:92
  43.1 1.1 shard_map.72
  44.3 0.7 collective-permute-start.6
  45.0 1.2 shard_map.73
  46.2 3.3 %collective-permute-start.7 = (f32[128,1024]{1,0:T(8,128)S(1)}, f32[128,1024]{1,0:T(8,128)S(1)}, u32[]{:S(2)}, u32[]{:S(2)}) collective-permute-start(f32[128,1024]{1,0:T(8,128)S(1)} %get-tuple-element.70), channel_id=1, source_target_pairs={{0,2},{16,30},{2,0},{18,20},{4,6},{20,18},{6,4},{22,24},{8,10},{24... | collective-permute-start | bytes 1572872 | tf_op jit(solution)/shard_map/ppermute | solution.py:92
  49.5 0.7 collective-permute-done.5
  50.3 3.3 %collective-permute-done.6 = f32[128,1024]{1,0:T(8,128)S(1)} collective-permute-done((f32[128,1024]{1,0:T(8,128)S(1)}, f32[128,1024]{1,0:T(8,128)S(1)}, u32[]{:S(2)}, u32[]{:S(2)}) %collective-permute-start.6) | collective-permute-done | bytes 524320 | tf_op jit(solution)/shard_map/ppermute | solution.py:92
  53.6 2.5 %collective-permute-done.7 = f32[128,1024]{1,0:T(8,128)S(1)} collective-permute-done((f32[128,1024]{1,0:T(8,128)S(1)}, f32[128,1024]{1,0:T(8,128)S(1)}, u32[]{:S(2)}, u32[]{:S(2)}) %collective-permute-start.7) | collective-permute-done | bytes 524320 | tf_op jit(solution)/shard_map/ppermute | solution.py:92
  56.2 12.7 %all_to_all.30.sums = f32[8,16,1024]{2,1,0:T(8,128)S(1)} all-to-all(f32[8,16,1024]{2,1,0:T(8,128)S(1)} %bitcast.29), channel_id=1, replica_groups={{0,162,1,163,64,226,65,227},{16,178,17,179,80,242,81,243},{4,166,5,167,..., dimensions={0} | all-to-all | bytes 1048576 | tf_op jit(solution)/shard_map/all_to_all | solution.py:96
  69.0 2.8 %collective-permute-start.10 = (f32[16,1024]{1,0:T(8,128)S(1)}, f32[16,1024]{1,0:T(8,128)S(1)}, u32[]{:S(2)}, u32[]{:S(2)}) collective-permute-start(f32[16,1024]{1,0:T(8,128)S(1)} %shard_map.74), channel_id=1, source_target_pairs={{0,12},{16,28},{2,14},{18,30},{4,0},{20,16},{6,2},{22,18},{8,4},{2... | collective-permute-start | bytes 196616 | tf_op jit(solution)/shard_map/ppermute | solution.py:92
  71.8 3.0 %collective-permute-start.8 = (f32[16,1024]{1,0:T(8,128)S(1)}, f32[16,1024]{1,0:T(8,128)S(1)}, u32[]{:S(2)}, u32[]{:S(2)}) collective-permute-start(f32[16,1024]{1,0:T(8,128)S(1)} %shard_map.74), channel_id=1, source_target_pairs={{0,8},{16,24},{2,10},{18,26},{4,12},{20,28},{6,14},{22,30},{8,0},{... | collective-permute-start | bytes 196616 | tf_op jit(solution)/shard_map/ppermute | solution.py:92
  74.8 1.2 %collective-permute-start.9 = (f32[16,1024]{1,0:T(8,128)S(1)}, f32[16,1024]{1,0:T(8,128)S(1)}, u32[]{:S(2)}, u32[]{:S(2)}) collective-permute-start(f32[16,1024]{1,0:T(8,128)S(1)} %shard_map.74), channel_id=1, source_target_pairs={{0,4},{16,20},{2,6},{18,22},{4,8},{20,24},{6,10},{22,26},{8,12},{2... | collective-permute-start | bytes 196616 | tf_op jit(solution)/shard_map/ppermute | solution.py:92
  76.0 2.9 %collective-permute-done.8 = f32[16,1024]{1,0:T(8,128)S(1)} collective-permute-done((f32[16,1024]{1,0:T(8,128)S(1)}, f32[16,1024]{1,0:T(8,128)S(1)}, u32[]{:S(2)}, u32[]{:S(2)}) %collective-permute-start.8) | collective-permute-done | bytes 65568 | tf_op jit(solution)/shard_map/ppermute | solution.py:92
  78.9 1.6 %collective-permute-done.9 = f32[16,1024]{1,0:T(8,128)S(1)} collective-permute-done((f32[16,1024]{1,0:T(8,128)S(1)}, f32[16,1024]{1,0:T(8,128)S(1)}, u32[]{:S(2)}, u32[]{:S(2)}) %collective-permute-start.9) | collective-permute-done | bytes 65568 | tf_op jit(solution)/shard_map/ppermute | solution.py:92
  80.5 12.9 %all_to_all.31 = f32[8,16,1024]{2,1,0:T(8,128)S(1)} all-to-all(f32[8,16,1024]{2,1,0:T(8,128)S(1)} %broadcast_in_dim.33), channel_id=1, replica_groups={{0,162,1,163,64,226,65,227},{16,178,17,179,80,242,81,243},{4,166,5,167,..., dimensions={0} | all-to-all | bytes 1048576 | tf_op jit(solution)/shard_map/all_to_all | solution.py:96
  93.4 2.7 %collective-permute-start.12 = (f32[128,1024]{1,0:T(8,128)S(1)}, f32[128,1024]{1,0:T(8,128)S(1)}, u32[]{:S(2)}, u32[]{:S(2)}) collective-permute-start(f32[128,1024]{1,0:T(8,128)S(1)} %bitcast.20), channel_id=1, source_target_pairs={{0,128},{16,145},{2,130},{18,147},{4,132},{20,149},{6,134},{22,151... | collective-permute-start | bytes 1572872 | tf_op jit(solution)/shard_map/ppermute | solution.py:92
  96.2 6.7 %collective-permute-done.11.refs_1_ = f32[128,1024]{1,0:T(8,128)S(1)} collective-permute-done((f32[128,1024]{1,0:T(8,128)S(1)}, f32[128,1024]{1,0:T(8,128)S(1)}, u32[]{:S(2)}, u32[]{:S(2)}) %collective-permute-start.11) | collective-permute-done | bytes 524320 | tf_op jit(solution)/shard_map/ppermute | solution.py:92
  102.9 1.3 %collective-permute-done.12.refs_2_ = f32[128,1024]{1,0:T(8,128)S(1)} collective-permute-done((f32[128,1024]{1,0:T(8,128)S(1)}, f32[128,1024]{1,0:T(8,128)S(1)}, u32[]{:S(2)}, u32[]{:S(2)}) %collective-permute-start.12) | collective-permute-done | bytes 524320 | tf_op jit(solution)/shard_map/ppermute | solution.py:92
  104.2 1.2 %collective-permute-done.13.refs_3_ = f32[128,1024]{1,0:T(8,128)S(1)} collective-permute-done((f32[128,1024]{1,0:T(8,128)S(1)}, f32[128,1024]{1,0:T(8,128)S(1)}, u32[]{:S(2)}, u32[]{:S(2)}) %collective-permute-start.13) | collective-permute-done | bytes 524320 | tf_op jit(solution)/shard_map/ppermute | solution.py:92
  105.4 1.8 %shard_map.75 = (f32[1000,256]{1,0:T(8,128)S(1)}, f32[32,1000]{1,0:T(8,128)S(1)}) custom-call(s32[5]{0:T(128)S(1)} %stack.23.place, f32[128,1024]{1,0:T(8,128)S(1)} %bitcast.22, f32[128,1024]{1,0:T(8,128)S(1)} %collective-permute-done.11.refs_1_, f32[128,1024]{1,0:T(8,128)S(1)} %collective-permute-done.12.refs_2_, ...), custom_call_target="tpu_custom_call" | custom-call | flops 805306368 | bytes 2097152 | tf_op jit(solution)/shard_map/pallas_call | solution.py:238
  107.2 4.7 %collective-permute-start.14 = (f32[1000,256]{1,0:T(8,128)S(1)}, f32[1000,256]{1,0:T(8,128)S(1)}, u32[]{:S(2)}, u32[]{:S(2)}) collective-permute-start(f32[1000,256]{1,0:T(8,128)S(1)} %get-tuple-element.80), channel_id=1, source_target_pairs={{0,16},{16,0},{2,18},{18,2},{4,20},{20,4},{6,22},{22,6},{8,24},{24... | collective-permute-start | bytes 3072008 | tf_op jit(solution)/shard_map/ppermute | solution.py:92
  111.9 1.7 %shard_map.76.partly = f32[1000,256]{1,0:T(8,128)S(1)} custom-call(s32[5]{0:T(128)S(1)} %stack.23.place, f32[128,1024]{1,0:T(8,128)S(1)} %bitcast.23, f32[128,1024]{1,0:T(8,128)S(1)} %collective-permute-done.11.refs_1_, f32[128,1024]{1,0:T(8,128)S(1)} %collective-permute-done.12.refs_2_, f32[128,1024]{1,0:T(8,128)S(1)} %collective-permute-done.13.refs_3_, ...), custom_call_target="tpu_custom_call" | custom-call | flops 805306368 | bytes 2097152 | tf_op jit(solution)/shard_map/pallas_call | solution.py:238
  114.3 1.7 %shard_map.77 = (f32[1000,256]{1,0:T(8,128)}, f32[64,1000]{1,0:T(8,128)}) custom-call(s32[5]{0:T(128)S(1)} %stack.23.place, f32[1000,256]{1,0:T(8,128)S(1)} %shard_map.76.partly, f32[1000,256]{1,0:T(8,128)S(1)} %collective-permute-done.14.other_delta, f32[32,1000]{1,0:T(8,128)S(1)} %get-tuple-element.85.mine, f32[32,1000]{1,0:T(8,128)S(1)} %collective-permute-done.15.theirs), custom_call_target="tpu_custom_call" | custom-call | bytes 2097152 | tf_op jit(solution)/shard_map/pallas_call | solution.py:238
  (32 shorter events, 2.6 us)
Async XLA Ops:
  0.6 1.8 %copy-start = (f32[256,1024]{1,0:T(8,128)S(1)}, f32[256,1024]{1,0:T(8,128)}, u32[]{:S(2)}) copy-start(f32[256,1024]{1,0:T(8,128)} %param.6) | copy-start | bytes 3145732
  0.6 5.8 %copy-start.1 = (f32[256,1000]{0,1:T(8,128)S(1)}, f32[256,1000]{0,1:T(8,128)}, u32[]{:S(2)}) copy-start(f32[256,1000]{0,1:T(8,128)} %param.9) | copy-start | bytes 3072004
  3.1 26.9 %collective-permute-start = (f32[256,1024]{1,0:T(8,128)}, f32[256,1024]{1,0:T(8,128)S(1)}, u32[]{:S(2)}, u32[]{:S(2)}) collective-permute-start(f32[256,1024]{1,0:T(8,128)} %own_centers), channel_id=1, source_target_pairs={{0,16},{16,0},{2,18},{18,2},{4,20},{20,4},{6,22},{22,6},{8,24},{24... | collective-permute-start | bytes 3145736 | tf_op jit(solution)/shard_map/ppermute | solution.py:92
  6.4 23.6 %collective-permute-start.1 = (f32[256,1000]{0,1:T(8,128)S(1)}, f32[256,1000]{0,1:T(8,128)S(1)}, u32[]{:S(2)}, u32[]{:S(2)}) collective-permute-start(f32[256,1000]{0,1:T(8,128)S(1)} %copy-done.1), channel_id=1, source_target_pairs={{0,16},{16,0},{2,18},{18,2},{4,20},{20,4},{6,22},{22,6},{8,24},{24... | collective-permute-start | bytes 3072008 | tf_op jit(solution)/shard_map/ppermute | solution.py:92
  6.6 30.0 %copy-start.2 = (f32[256,1024]{1,0:T(8,128)S(1)}, f32[256,1024]{1,0:T(8,128)}, u32[]{:S(2)}) copy-start(f32[256,1024]{1,0:T(8,128)} %own_centers) | copy-start | bytes 3145732
  6.6 30.0 %copy-start.3 = (f32[256,1000]{0,1:T(8,128)S(1)}, f32[256,1000]{0,1:T(8,128)}, u32[]{:S(2)}) copy-start(f32[256,1000]{0,1:T(8,128)} %param.7) | copy-start | bytes 3072004
  30.1 9.7 %collective-permute-start.4 = (f32[128,1024]{1,0:T(8,128)S(1)}, f32[128,1024]{1,0:T(8,128)S(1)}, u32[]{:S(2)}, u32[]{:S(2)}) collective-permute-start(f32[128,1024]{1,0:T(8,128)S(1)} %shard_map.68.rows), channel_id=1, source_target_pairs={{0,32},{16,112},{2,34},{18,114},{4,36},{20,116},{6,38},{22,118},{8... | collective-permute-start | bytes 1572872 | tf_op jit(solution)/shard_map/ppermute | solution.py:92
  32.7 10.5 %collective-permute-start.3 = (f32[128,1024]{1,0:T(8,128)S(1)}, f32[128,1024]{1,0:T(8,128)S(1)}, u32[]{:S(2)}, u32[]{:S(2)}) collective-permute-start(f32[128,1024]{1,0:T(8,128)S(1)} %shard_map.68.rows), channel_id=1, source_target_pairs={{0,128},{16,145},{2,130},{18,147},{4,132},{20,149},{6,134},{22,151... | collective-permute-start | bytes 1572872 | tf_op jit(solution)/shard_map/ppermute | solution.py:92
  33.3 11.7 %collective-permute-start.2 = (f32[128,1024]{1,0:T(8,128)S(1)}, f32[128,1024]{1,0:T(8,128)S(1)}, u32[]{:S(2)}, u32[]{:S(2)}) collective-permute-start(f32[128,1024]{1,0:T(8,128)S(1)} %shard_map.68.rows), channel_id=1, source_target_pairs={{0,2},{16,30},{2,0},{18,20},{4,6},{20,18},{6,4},{22,24},{8,10},{24... | collective-permute-start | bytes 1572872 | tf_op jit(solution)/shard_map/ppermute | solution.py:92
  40.9 9.3 %collective-permute-start.5 = (f32[128,1024]{1,0:T(8,128)S(1)}, f32[128,1024]{1,0:T(8,128)S(1)}, u32[]{:S(2)}, u32[]{:S(2)}) collective-permute-start(f32[128,1024]{1,0:T(8,128)S(1)} %get-tuple-element.66), channel_id=1, source_target_pairs={{0,32},{16,112},{2,34},{18,114},{4,36},{20,116},{6,38},{22,118},{8... | collective-permute-start | bytes 1572872 | tf_op jit(solution)/shard_map/ppermute | solution.py:92
  44.3 9.3 %collective-permute-start.6 = (f32[128,1024]{1,0:T(8,128)S(1)}, f32[128,1024]{1,0:T(8,128)S(1)}, u32[]{:S(2)}, u32[]{:S(2)}) collective-permute-start(f32[128,1024]{1,0:T(8,128)S(1)} %get-tuple-element.68), channel_id=1, source_target_pairs={{0,128},{16,145},{2,130},{18,147},{4,132},{20,149},{6,134},{22,151... | collective-permute-start | bytes 1572872 | tf_op jit(solution)/shard_map/ppermute | solution.py:92
  46.2 9.9 %collective-permute-start.7 = (f32[128,1024]{1,0:T(8,128)S(1)}, f32[128,1024]{1,0:T(8,128)S(1)}, u32[]{:S(2)}, u32[]{:S(2)}) collective-permute-start(f32[128,1024]{1,0:T(8,128)S(1)} %get-tuple-element.70), channel_id=1, source_target_pairs={{0,2},{16,30},{2,0},{18,20},{4,6},{20,18},{6,4},{22,24},{8,10},{24... | collective-permute-start | bytes 1572872 | tf_op jit(solution)/shard_map/ppermute | solution.py:92
  69.0 7.0 %collective-permute-start.10 = (f32[16,1024]{1,0:T(8,128)S(1)}, f32[16,1024]{1,0:T(8,128)S(1)}, u32[]{:S(2)}, u32[]{:S(2)}) collective-permute-start(f32[16,1024]{1,0:T(8,128)S(1)} %shard_map.74), channel_id=1, source_target_pairs={{0,12},{16,28},{2,14},{18,30},{4,0},{20,16},{6,2},{22,18},{8,4},{2... | collective-permute-start | bytes 196616 | tf_op jit(solution)/shard_map/ppermute | solution.py:92
  71.8 7.0 %collective-permute-start.8 = (f32[16,1024]{1,0:T(8,128)S(1)}, f32[16,1024]{1,0:T(8,128)S(1)}, u32[]{:S(2)}, u32[]{:S(2)}) collective-permute-start(f32[16,1024]{1,0:T(8,128)S(1)} %shard_map.74), channel_id=1, source_target_pairs={{0,8},{16,24},{2,10},{18,26},{4,12},{20,28},{6,14},{22,30},{8,0},{... | collective-permute-start | bytes 196616 | tf_op jit(solution)/shard_map/ppermute | solution.py:92
  74.8 5.7 %collective-permute-start.9 = (f32[16,1024]{1,0:T(8,128)S(1)}, f32[16,1024]{1,0:T(8,128)S(1)}, u32[]{:S(2)}, u32[]{:S(2)}) collective-permute-start(f32[16,1024]{1,0:T(8,128)S(1)} %shard_map.74), channel_id=1, source_target_pairs={{0,4},{16,20},{2,6},{18,22},{4,8},{20,24},{6,10},{22,26},{8,12},{2... | collective-permute-start | bytes 196616 | tf_op jit(solution)/shard_map/ppermute | solution.py:92
  93.4 9.4 %collective-permute-start.11 = (f32[128,1024]{1,0:T(8,128)S(1)}, f32[128,1024]{1,0:T(8,128)S(1)}, u32[]{:S(2)}, u32[]{:S(2)}) collective-permute-start(f32[128,1024]{1,0:T(8,128)S(1)} %bitcast.19), channel_id=1, source_target_pairs={{0,32},{16,112},{2,34},{18,114},{4,36},{20,116},{6,38},{22,118},{8... | collective-permute-start | bytes 1572872 | tf_op jit(solution)/shard_map/ppermute | solution.py:92
  93.4 10.8 %collective-permute-start.12 = (f32[128,1024]{1,0:T(8,128)S(1)}, f32[128,1024]{1,0:T(8,128)S(1)}, u32[]{:S(2)}, u32[]{:S(2)}) collective-permute-start(f32[128,1024]{1,0:T(8,128)S(1)} %bitcast.20), channel_id=1, source_target_pairs={{0,128},{16,145},{2,130},{18,147},{4,132},{20,149},{6,134},{22,151... | collective-permute-start | bytes 1572872 | tf_op jit(solution)/shard_map/ppermute | solution.py:92
  96.2 9.2 %collective-permute-start.13 = (f32[128,1024]{1,0:T(8,128)S(1)}, f32[128,1024]{1,0:T(8,128)S(1)}, u32[]{:S(2)}, u32[]{:S(2)}) collective-permute-start(f32[128,1024]{1,0:T(8,128)S(1)} %bitcast.21), channel_id=1, source_target_pairs={{0,2},{16,30},{2,0},{18,20},{4,6},{20,18},{6,4},{22,24},{8,10},{24... | collective-permute-start | bytes 1572872 | tf_op jit(solution)/shard_map/ppermute | solution.py:92
  107.2 7.1 %collective-permute-start.14 = (f32[1000,256]{1,0:T(8,128)S(1)}, f32[1000,256]{1,0:T(8,128)S(1)}, u32[]{:S(2)}, u32[]{:S(2)}) collective-permute-start(f32[1000,256]{1,0:T(8,128)S(1)} %get-tuple-element.80), channel_id=1, source_target_pairs={{0,16},{16,0},{2,18},{18,2},{4,20},{20,4},{6,22},{22,6},{8,24},{24... | collective-permute-start | bytes 3072008 | tf_op jit(solution)/shard_map/ppermute | solution.py:92
  111.8 2.4 %collective-permute-start.15 = (f32[32,1000]{1,0:T(8,128)S(1)}, f32[32,1000]{1,0:T(8,128)S(1)}, u32[]{:S(2)}, u32[]{:S(2)}) collective-permute-start(f32[32,1000]{1,0:T(8,128)S(1)} %get-tuple-element.85.mine), channel_id=1, source_target_pairs={{0,16},{16,0},{2,18},{18,2},{4,20},{20,4},{6,22},{22,6},{8,24},{24... | collective-permute-start | bytes 384008 | tf_op jit(solution)/shard_map/ppermute | solution.py:92
